TPU v7x, 32 devices: a whole 2x2x4 slice. The times are simulated.
32 devices in a mesh: seq: 8 (over y, x, core), tensor: 4 (over z).
Axes of the slice: x: 2, y: 2, z: 4, core: 2. Of those that a mesh axis runs over, the one named last changes fastest.
Arguments:
- byte_states: bfloat16 [8192, 1024], P('seq'), may hold values from -6 to 6
- byte_patch: int32 [8192], P('seq'), may hold values from 0 to 1023, as said below
- patch_len: int32 [1024], replicated, may hold values from 1 to 1024, as said below
- cross_query: bfloat16 [1024, 4096], P('seq', 'tensor'), may hold values from -0.75 to 0.75
- cross_key: bfloat16 [1024, 4096], P('seq', 'tensor'), may hold values from -0.375 to 0.375
- cross_value: bfloat16 [1024, 4096], P('seq', 'tensor'), may hold values from -0.1875 to 0.1875
- cross_out: bfloat16 [4096, 4096], P('tensor', 'seq'), may hold values from -0.09375 to 0.09375
- norm_gain: float32 [4096], replicated, may hold values from 0.5 to 1.5
- latent_query: bfloat16 [4096, 4096], P('seq', 'tensor'), may hold values from -0.1875 to 0.1875
- latent_key: bfloat16 [4096, 4096], P('seq', 'tensor'), may hold values from -0.1875 to 0.1875
- latent_value: bfloat16 [4096, 4096], P('seq', 'tensor'), may hold values from -0.09375 to 0.09375
- latent_out: bfloat16 [4096, 4096], P('tensor', 'seq'), may hold values from -0.09375 to 0.09375
Outputs:
- patch_latent: bfloat16 [1024, 4096], P('seq', 'tensor')
Inputs may be any that keep to these rules, and one draw needn't show every extreme that they name: `byte_patch`: within each aligned block of 1024 bytes the numbers never fall and rise by at most one from byte to byte, and the block's first byte starts a new patch, so no patch spans two blocks. Block k begins with patch number k * 128 + r with -64 <= r < 64; the first block begins with 0 and the last ends with 1023. A block holds 1 to 255 patches; some block holds exactly 255 and the block after it exactly one. patch_len[p] is the number of bytes b with byte_patch[b] = p.
All inputs are finite; a program needn't handle non-finite values.
Results may differ from a plain program's by a relative error of at most 0.028.
Values may be sent and summed in bfloat16 or wider, within the bound.
No kernel may reach another device: no remote copies, remote signals or barrier semaphores. Data moves between devices by JAX's collectives and lax.ppermute only.
A program may use at most 128 MiB of HBM per device.

v0:
```python
import math

import jax
import jax.numpy as jnp
from jax import lax
from jax.sharding import PartitionSpec as P

HEAD_DIM = 128
PATCH_DEV = 128


score_cap = 30.0
norm_eps = 1e-05


def shifted(block, axis, distance):
    devices = range(lax.axis_size(axis))
    route = [(i - distance, i) for i in devices if i - distance in devices]
    return lax.ppermute(block, axis, route)


def capped_exp(scores):
    return jnp.exp(score_cap * jnp.tanh(scores / score_cap))


def contract_rows(left, right):
    return lax.dot_general(
        left,
        right,
        (((0,), (0,)), ((), ())),
        precision=lax.Precision.HIGHEST,
        preferred_element_type=jnp.float32,
    )


def per_device(
    byte_states,
    byte_patch,
    patch_len,
    cross_query,
    cross_key,
    cross_value,
    cross_out,
    norm_gain,
    latent_query,
    latent_key,
    latent_value,
    latent_out,
):
    seq_index = lax.axis_index("seq")
    tensor_count = lax.axis_size("tensor")
    (
        cross_query,
        cross_key,
        cross_value,
        latent_query,
        latent_key,
        latent_value,
        cross_out,
        latent_out,
    ) = (
        lax.all_gather(cross_query, "seq", axis=0, tiled=True),
        lax.all_gather(cross_key, "seq", axis=0, tiled=True),
        lax.all_gather(cross_value, "seq", axis=0, tiled=True),
        lax.all_gather(latent_query, "seq", axis=0, tiled=True),
        lax.all_gather(latent_key, "seq", axis=0, tiled=True),
        lax.all_gather(latent_value, "seq", axis=0, tiled=True),
        lax.all_gather(cross_out, "seq", axis=1, tiled=True),
        lax.all_gather(latent_out, "seq", axis=1, tiled=True),
    )
    latent_width = cross_out.shape[1]
    local_width = cross_out.shape[0]
    head_count = local_width // HEAD_DIM
    slot_count = 2 * PATCH_DEV
    byte_count = byte_states.shape[0]
    first_patch = byte_patch[0]
    slot_of = byte_patch - first_patch
    onehot_mask = slot_of[:, None] == jnp.arange(slot_count, dtype=jnp.int32)[None, :]
    onehot = onehot_mask.astype(jnp.bfloat16)
    onehot_float = onehot_mask.astype(jnp.float32)
    byte_sums = lax.dot_general(
        onehot, byte_states, (((0,), (0,)), ((), ())), preferred_element_type=jnp.float32
    )
    lengths_all = jnp.concatenate([patch_len, jnp.ones((slot_count,), jnp.int32)])
    lengths = lax.dynamic_slice_in_dim(lengths_all, first_patch, slot_count)
    pooled = (byte_sums / lengths.astype(jnp.float32)[:, None]).astype(jnp.bfloat16)
    query_slots = jnp.dot(pooled, cross_query, preferred_element_type=jnp.float32).astype(
        jnp.bfloat16
    )
    byte_keys = jnp.dot(byte_states, cross_key, preferred_element_type=jnp.float32).astype(
        jnp.bfloat16
    )
    byte_values = jnp.dot(byte_states, cross_value, preferred_element_type=jnp.float32).astype(
        jnp.bfloat16
    )
    query_bytes = jnp.dot(onehot, query_slots, preferred_element_type=jnp.float32)
    scores = (query_bytes * byte_keys.astype(jnp.float32)).reshape(
        byte_count, head_count, HEAD_DIM
    ).sum(axis=2) / math.sqrt(HEAD_DIM)
    byte_raw = capped_exp(scores)
    totals = contract_rows(onehot_float, byte_raw)
    totals = jnp.where(totals > 0.0, totals, 1.0)
    totals_bytes = jnp.dot(
        onehot_float, totals, precision=lax.Precision.HIGHEST, preferred_element_type=jnp.float32
    )
    byte_weight = (byte_raw / totals_bytes).astype(jnp.bfloat16)
    weighted = (
        byte_weight.astype(jnp.float32)[:, :, None]
        * byte_values.astype(jnp.float32).reshape(byte_count, head_count, HEAD_DIM)
    ).reshape(byte_count, local_width)
    cross_heads = contract_rows(onehot_float, weighted).astype(jnp.bfloat16)
    padding = jnp.zeros((2 * PATCH_DEV, cross_heads.shape[1]), cross_heads.dtype)
    padded = jnp.concatenate([padding, cross_heads, padding], axis=0)
    offset = seq_index * PATCH_DEV - first_patch + 2 * PATCH_DEV
    padded, offset = (padded, offset)
    owned_heads = lax.dynamic_slice_in_dim(padded, offset, PATCH_DEV, 0)
    for offset_step in (-1, 1):
        window = lax.dynamic_slice_in_dim(padded, offset + offset_step * PATCH_DEV, PATCH_DEV, 0)
        owned_heads = owned_heads + shifted(window, "seq", offset_step)
    partial_value = jnp.dot(owned_heads, cross_out, preferred_element_type=jnp.float32)
    latent_in = lax.psum(partial_value, "tensor").astype(jnp.bfloat16)
    hidden = latent_in.astype(jnp.float32)
    mean_square = jnp.mean(hidden * hidden, axis=1, keepdims=True)
    normed = (hidden * lax.rsqrt(mean_square + norm_eps) * norm_gain[None, :]).astype(jnp.bfloat16)
    query = (
        jnp.dot(normed, latent_query, preferred_element_type=jnp.float32)
        .astype(jnp.bfloat16)
        .reshape(PATCH_DEV, head_count, HEAD_DIM)
    )
    key_rows = jnp.dot(normed, latent_key, preferred_element_type=jnp.float32).astype(jnp.bfloat16)
    value_rows = jnp.dot(normed, latent_value, preferred_element_type=jnp.float32).astype(
        jnp.bfloat16
    )
    positions = seq_index * PATCH_DEV + jnp.arange(PATCH_DEV, dtype=jnp.int32)
    key_piece = lax.all_gather(key_rows, "seq", axis=0, tiled=True)
    value_piece = lax.all_gather(value_rows, "seq", axis=0, tiled=True)
    piece_rows = key_piece.shape[0]
    key_piece = key_piece.reshape(piece_rows, head_count, HEAD_DIM)
    value_piece = value_piece.reshape(piece_rows, head_count, HEAD_DIM)
    piece_scores = jnp.einsum(
        "qhd,khd->hqk", query, key_piece, preferred_element_type=jnp.float32
    ) / math.sqrt(HEAD_DIM)
    key_positions = jnp.arange(piece_rows, dtype=jnp.int32)
    allowed = key_positions[None, :] <= positions[:, None]
    exp_scores = jnp.where(allowed[None, :, :], capped_exp(piece_scores), 0.0)
    denominator = jnp.sum(exp_scores, axis=2)
    numerator = jnp.einsum(
        "hqk,khd->hqd",
        exp_scores.astype(jnp.bfloat16),
        value_piece,
        preferred_element_type=jnp.float32,
    )
    numerator, denominator = (numerator, denominator)
    attended = (numerator / denominator[:, :, None]).astype(jnp.bfloat16)
    attended = attended.transpose(1, 0, 2).reshape(PATCH_DEV, local_width)
    projected = jnp.dot(attended, latent_out, preferred_element_type=jnp.float32)
    mixed_sum = lax.psum_scatter(projected, "tensor", scatter_dimension=1, tiled=True)
    column_width = latent_width // tensor_count
    residual = lax.dynamic_slice_in_dim(
        hidden, lax.axis_index("tensor") * column_width, column_width, 1
    )
    return (residual + mixed_sum).astype(jnp.bfloat16)


def solution(mesh):
    return jax.shard_map(
        per_device,
        mesh=mesh,
        in_specs=(
            P("seq", None),
            P("seq"),
            P(),
            P("seq", "tensor"),
            P("seq", "tensor"),
            P("seq", "tensor"),
            P("tensor", "seq"),
            P(),
            P("seq", "tensor"),
            P("seq", "tensor"),
            P("seq", "tensor"),
            P("tensor", "seq"),
        ),
        out_specs=P("seq", "tensor"),
        check_vma=False,
    )
```

profile of v0, /device:TPU:9, one launch (start us, length us, event | category | flops | bytes accessed | tf_op | source)
XLA Modules:
  0.0 502.9 jit_solution(11857208999369262361)
XLA Ops:
  6.5 0.7 all-gather.13.cloned.1.call-update
  10.5 0.7 all-gather.19.cloned.1.call-update
  15.2 0.9 fusion.16
  16.1 22.6 %all-gather.13.cloned.1.call-done = bf16[1024,1024]{1,0:T(8,128)(2,1)} async-done(((bf16[128,1024]{1,0:T(8,128)(2,1)}), bf16[1024,1024]{1,0:T(8,128)(2,1)}) %all-gather.13.cloned.1.call-update) | async-done | bytes 2097168 | tf_op jit(solution)/shard_map/all_gather | solution.py:63
  38.8 5.4 %fusion.50 = bf16[1024,1024]{0,1:T(8,128)(2,1)} fusion(bf16[1024,1024]{1,0:T(8,128)(2,1)S(1)} %copy-done, bf16[1024,1024]{1,0:T(8,128)(2,1)} %all-gather.13.cloned.1.call-done), kind=kOutput, calls=%fused_computation.68 | convolution fusion | flops 2147483648 | bytes 6291456 | tf_op jit(solution)/shard_map/dot_general | solution.py:90
  44.1 24.5 %all-gather.11.cloned.1.call-done = bf16[1024,1024]{1,0:T(8,128)(2,1)} async-done(((bf16[128,1024]{1,0:T(8,128)(2,1)}), bf16[1024,1024]{1,0:T(8,128)(2,1)}) %all-gather.11.cloned.1.call-update) | async-done | bytes 2097168 | tf_op jit(solution)/shard_map/all_gather | solution.py:62
  68.6 3.6 bitcast_reduce_fusion
  73.5 24.9 %all-gather.15.cloned.1.call-done = bf16[1024,1024]{1,0:T(8,128)(2,1)} async-done(((bf16[128,1024]{1,0:T(8,128)(2,1)}), bf16[1024,1024]{1,0:T(8,128)(2,1)}) %all-gather.15.cloned.1.call-update) | async-done | bytes 2097168 | tf_op jit(solution)/shard_map/all_gather | solution.py:64
  98.4 3.9 fusion.51
  102.3 1.1 mul.48
  103.5 2.8 fusion.15
  106.7 2.2 collective-permute-start
  108.9 3.6 collective-permute-start.1
  112.5 9.3 %collective-permute-done = bf16[128,1024]{1,0:T(8,128)(2,1)S(1)} collective-permute-done((bf16[128,1024]{1,0:T(8,128)(2,1)S(1)}, bf16[128,1024]{1,0:T(8,128)(2,1)S(1)}, u32[]{:S(2)}, u32[]{:S(2)}) %collective-permute-start) | collective-permute-done | bytes 262176 | tf_op jit(solution)/shard_map/ppermute | solution.py:19
  121.8 39.4 %all-gather.17.cloned.1.call-done = bf16[1024,4096]{1,0:T(8,128)(2,1)} async-done(((bf16[1024,512]{1,0:T(8,128)(2,1)}), bf16[1024,4096]{1,0:T(8,128)(2,1)}) %all-gather.17.cloned.1.call-update) | async-done | bytes 8388624 | tf_op jit(solution)/shard_map/all_gather | solution.py:68
  161.2 4.8 fusion.37
  166.0 73.7 %all-reduce.2 = bf16[128,4096]{1,0:T(8,128)(2,1)S(1)} all-reduce(f32[128,4096]{1,0:T(8,128)S(1)} %fusion.37), channel_id=1, replica_groups=mesh['seq'=8,'tensor'=4] {'tensor'}, use_global_device_ids=true, to_apply=%region_1.2 | all-reduce | flops 524288 | bytes 3145728 | tf_op jit(solution)/shard_map/psum | solution.py:121
  240.0 5.4 %convolution_convert_fusion.1 = bf16[128,1024]{1,0:T(8,128)(2,1)} fusion(bf16[4096,1024]{1,0:T(8,128)(2,1)} %all-gather.25.cloned.1.call-done, f32[4096]{0:T(1024)S(1)} %copy-done.5, f32[128]{0:T(128)S(1)} %add_rsqrt_fusion, bf16[128,4096]{1,0:T(8,128)(2,1)S(1)} %all-reduce.2), kind=kOutput, calls=%fused_computation.26 | convolution fusion | flops 1075970048 | bytes 9716224 | tf_op jit(solution)/shard_map/dot_general | solution.py:131
  245.5 28.1 %all-gather.21.cloned.1.call-done = bf16[4096,1024]{1,0:T(8,128)(2,1)} async-done(((bf16[512,1024]{1,0:T(8,128)(2,1)}), bf16[4096,1024]{1,0:T(8,128)(2,1)}) %all-gather.21.cloned.1.call-update) | async-done | bytes 8388624 | tf_op jit(solution)/shard_map/all_gather | solution.py:66
  273.5 5.4 %convolution_convert_fusion.2 = bf16[128,1024]{1,0:T(8,128)(2,1)} fusion(bf16[4096,1024]{1,0:T(8,128)(2,1)} %all-gather.21.cloned.1.call-done, f32[4096]{0:T(1024)S(1)} %copy-done.5, f32[128]{0:T(128)S(1)} %add_rsqrt_fusion, bf16[128,4096]{1,0:T(8,128)(2,1)S(1)} %all-reduce.2), kind=kOutput, calls=%fused_computation.27 | convolution fusion | flops 1075970048 | bytes 9716224 | tf_op jit(solution)/shard_map/dot_general | solution.py:130
  279.7 50.1 %all-gather.19.cloned.1.call-done = bf16[4096,1024]{1,0:T(8,128)(2,1)} async-done(((bf16[512,1024]{1,0:T(8,128)(2,1)}), bf16[4096,1024]{1,0:T(8,128)(2,1)}) %all-gather.19.cloned.1.call-update) | async-done | bytes 8388624 | tf_op jit(solution)/shard_map/all_gather | solution.py:65
  329.8 5.4 %fusion.20 = bf16[16,8,8,128]{3,2,1,0:T(8,128)(2,1)} fusion(bf16[4096,1024]{1,0:T(8,128)(2,1)} %all-gather.19.cloned.1.call-done, f32[4096]{0:T(1024)S(1)} %copy-done.5, f32[128]{0:T(128)S(1)} %add_rsqrt_fusion, bf16[128,4096]{1,0:T(8,128)(2,1)S(1)} %all-reduce.2), kind=kOutput, calls=%fused_computation.29 | convolution fusion | flops 1075970048 | bytes 9716224 | tf_op jit(solution)/shard_map/dot_general | solution.py:126
  335.2 24.4 %all-gather.27.cloned.1.call-done = bf16[1024,1024]{1,0:T(8,128)(2,1)} async-done(((bf16[128,1024]{1,0:T(8,128)(2,1)}), bf16[1024,1024]{1,0:T(8,128)(2,1)}) %all-gather.27.cloned.1.call-update) | async-done | bytes 2097168 | tf_op jit(solution)/shard_map/all_gather | solution.py:136
  359.6 2.9 copy.17
  362.5 27.0 %all-gather.23.cloned.1.call-done = bf16[1024,1024]{1,0:T(8,128)(2,1)} async-done(((bf16[128,1024]{1,0:T(8,128)(2,1)}), bf16[1024,1024]{1,0:T(8,128)(2,1)}) %all-gather.23.cloned.1.call-update) | async-done | bytes 2097168 | tf_op jit(solution)/shard_map/all_gather | solution.py:135
  389.5 3.3 fusion.3
  392.8 1.7 fusion.27
  394.4 52.8 %all-gather.29.cloned.1.call-done = bf16[1024,4096]{1,0:T(8,128)(2,1)} async-done(((bf16[1024,512]{1,0:T(8,128)(2,1)}), bf16[1024,4096]{1,0:T(8,128)(2,1)}) %all-gather.29.cloned.1.call-update) | async-done | bytes 8388624 | tf_op jit(solution)/shard_map/all_gather | solution.py:69
  447.2 6.0 %fusion.52 = f32[128,4096]{1,0:T(8,128)} fusion(bf16[128,1024]{0,1:T(8,128)(2,1)S(1)} %bitcast.51, bf16[1024,4096]{1,0:T(8,128)(2,1)} %all-gather.29.cloned.1.call-done), kind=kOutput, calls=%fused_computation.70 | convolution fusion | flops 1073741824 | bytes 10747904 | tf_op jit(solution)/shard_map/dot_general | solution.py:156
  453.2 1.5 convert_element_type.127
  454.7 39.7 %reduce-scatter.2.cloned.1.call-done = f32[128,1024]{1,0:T(8,128)} async-done(((f32[128,4096]{1,0:T(8,128)}), f32[128,1024]{1,0:T(8,128)}) %reduce-scatter.2.cloned.1.call-update) | async-done | bytes 524304 | tf_op jit(solution)/shard_map/reduce_scatter | solution.py:157
  494.4 2.0 add_convert_fusion
  (49 shorter events, 7.4 us)
Async XLA Ops:
  6.5 8.6 %copy-start = (bf16[1024,1024]{1,0:T(8,128)(2,1)S(1)}, bf16[1024,1024]{1,0:T(8,128)(2,1)}, u32[]{:S(2)}) copy-start(bf16[1024,1024]{1,0:T(8,128)(2,1)} %param.12) | copy-start | bytes 6291460
  6.5 32.2 %all-gather.13.cloned.1.call-start = ((), (), s32[]{:S(2)}) async-start(), calls=%async_computation.2 | async-start | bytes 2359296 | tf_op jit(solution)/shard_map/all_gather | solution.py:63
  7.3 61.3 %all-gather.11.cloned.1.call-start = ((), (), s32[]{:S(2)}) async-start(), calls=%async_computation.1 | async-start | bytes 2359296 | tf_op jit(solution)/shard_map/all_gather | solution.py:62
  8.0 90.4 %all-gather.15.cloned.1.call-start = ((), (), s32[]{:S(2)}) async-start(), calls=%async_computation.3 | async-start | bytes 2359296 | tf_op jit(solution)/shard_map/all_gather | solution.py:64
  8.7 2.6 copy-start.4
  8.8 5.7 %copy-start.3 = (s32[1024]{0:T(1024)S(1)}, s32[1024]{0:T(1024)}, u32[]{:S(2)}) copy-start(s32[1024]{0:T(1024)} %param.14) | copy-start | bytes 12292
  8.8 152.4 %all-gather.17.cloned.1.call-start = ((), (), s32[]{:S(2)}) async-start(), calls=%async_computation.4 | async-start | bytes 9437184 | tf_op jit(solution)/shard_map/all_gather | solution.py:68
  9.3 230.6 %all-gather.25.cloned.1.call-start = ((), (), s32[]{:S(2)}) async-start(), calls=%async_computation.8 | async-start | bytes 9437184 | tf_op jit(solution)/shard_map/all_gather | solution.py:67
  9.9 263.6 %all-gather.21.cloned.1.call-start = ((), (), s32[]{:S(2)}) async-start(), calls=%async_computation.6 | async-start | bytes 9437184 | tf_op jit(solution)/shard_map/all_gather | solution.py:66
  10.5 319.3 %all-gather.19.cloned.1.call-start = ((), (), s32[]{:S(2)}) async-start(), calls=%async_computation.5 | async-start | bytes 9437184 | tf_op jit(solution)/shard_map/all_gather | solution.py:65
  11.3 348.4 %all-gather.27.cloned.1.call-start = ((), (), s32[]{:S(2)}) async-start(), calls=%async_computation.9 | async-start | bytes 2359296 | tf_op jit(solution)/shard_map/all_gather | solution.py:136
  106.6 15.2 %copy-start.2 = (bf16[768,1024]{1,0:T(8,128)(2,1)}, bf16[768,1024]{1,0:T(8,128)(2,1)S(1)}, u32[]{:S(2)}) copy-start(bf16[768,1024]{1,0:T(8,128)(2,1)S(1)} %pad_maximum_fusion) | copy-start | bytes 4718596
  106.7 15.0 %collective-permute-start = (bf16[128,1024]{1,0:T(8,128)(2,1)S(1)}, bf16[128,1024]{1,0:T(8,128)(2,1)S(1)}, u32[]{:S(2)}, u32[]{:S(2)}) collective-permute-start(bf16[128,1024]{1,0:T(8,128)(2,1)S(1)} %get-tuple-element.5), channel_id=1, source_target_pairs={{4,0},{8,4},{12,8},{16,12},{20,16},{24,20},{28,24},{5,1},{9,5},{13... | collective-permute-start | bytes 786440 | tf_op jit(solution)/shard_map/ppermute | solution.py:19
  108.9 12.9 %collective-permute-start.1 = (bf16[128,1024]{1,0:T(8,128)(2,1)S(1)}, bf16[128,1024]{1,0:T(8,128)(2,1)S(1)}, u32[]{:S(2)}, u32[]{:S(2)}) collective-permute-start(bf16[128,1024]{1,0:T(8,128)(2,1)S(1)} %get-tuple-element.6), channel_id=1, source_target_pairs={{0,4},{4,8},{8,12},{12,16},{16,20},{20,24},{24,28},{1,5},{5,9},{9,... | collective-permute-start | bytes 786440 | tf_op jit(solution)/shard_map/ppermute | solution.py:19
  166.0 74.0 %copy-start.5 = (f32[4096]{0:T(1024)S(1)}, f32[4096]{0:T(1024)}, u32[]{:S(2)}) copy-start(f32[4096]{0:T(1024)} %param.19) | copy-start | bytes 49156
  245.4 144.1 %all-gather.23.cloned.1.call-start = ((), (), s32[]{:S(2)}) async-start(), calls=%async_computation.7 | async-start | bytes 2359296 | tf_op jit(solution)/shard_map/all_gather | solution.py:135
  278.9 168.2 %all-gather.29.cloned.1.call-start = ((), (), s32[]{:S(2)}) async-start(), calls=%async_computation.10 | async-start | bytes 9437184 | tf_op jit(solution)/shard_map/all_gather | solution.py:69
  279.5 214.9 %reduce-scatter.2.cloned.1.call-start = ((), (), s32[]{:S(2)}) async-start(), calls=%async_computation.11 | async-start | bytes 2621440 | tf_op jit(solution)/shard_map/reduce_scatter | solution.py:157
  335.2 54.2 %copy-start.6 = (bf16[16,8,8,128]{3,2,1,0:T(8,128)(2,1)S(1)}, bf16[16,8,8,128]{3,2,1,0:T(8,128)(2,1)}, u32[]{:S(2)}) copy-start(bf16[16,8,8,128]{3,2,1,0:T(8,128)(2,1)} %fusion.20) | copy-start | bytes 786436
  453.2 43.2 %copy-start.1 = (bf16[1024,1024]{1,0:T(8,128)(2,1)S(1)}, bf16[1024,1024]{1,0:T(8,128)(2,1)}, u32[]{:S(2)}) copy-start(bf16[1024,1024]{1,0:T(8,128)(2,1)} %param.12) | copy-start | bytes 6291460
Sparse Core Ops, SparseCore 0:
  9.2 29.4 all-gather.12
  40.7 27.8 all-gather.10
  70.5 27.8 all-gather.14
  100.1 61.0 all-gather.16
  162.9 54.3 all-gather.24
  219.1 54.3 all-gather.20
  275.4 54.3 all-gather.18
  331.7 27.8 all-gather.26
  361.5 27.8 all-gather.22
  391.2 55.9 all-gather.28
  453.3 41.0 reduce-scatter.1
where the time goes:
time: 507 us; the launch traced here: 503 us
  waiting for transfers between devices  348 us (69%)
  blocking collectives  73.7 us (15%)
  matrix products  49.7 us (10%)
  between operations  16.1 us (3%)
  starting transfers between devices  6.13 us (1%)
    psum x1, blocking collectives, per_device(): latent_in = lax.psum(partial_value, 'tensor').astype(jnp.bfloat16)  73.7 us
    all_gather x1, waiting for transfers between devices, per_device(): lax.all_gather(latent_out, 'seq', axis=1, tiled=True)  52.8 us
    all_gather x1, waiting for transfers between devices, per_device(): lax.all_gather(latent_query, 'seq', axis=0, tiled=True)  50.1 us
    reduce_scatter x1, waiting for transfers between devices, per_device(): lax.psum_scatter(projected, 'tensor', scatter_dimension=1, tiled=True)  39.7 us
    all_gather x1, waiting for transfers between devices, per_device(): lax.all_gather(cross_out, 'seq', axis=1, tiled=True)  39.4 us
    all_gather x1, waiting for transfers between devices, per_device(): lax.all_gather(latent_key, 'seq', axis=0, tiled=True)  28.1 us
    all_gather x1, waiting for transfers between devices, per_device(): key_piece = lax.all_gather(key_rows, 'seq', axis=0, tiled=True)  27 us
    all_gather x1, waiting for transfers between devices, per_device(): lax.all_gather(cross_value, 'seq', axis=0, tiled=True)  24.9 us
  transfers between devices with their start and end apart: 13, of which 11 were waited for; matrix products, arithmetic and copies ran while one was open for 10% of the time, Pallas kernels for 0%

commit v1 on v0

--- a/solution.py
+++ b/solution.py
@@ -33,7 +33,7 @@
     )
 
 
-def per_device(
+def per_device_gathered(
     byte_states,
     byte_patch,
     patch_len,
@@ -162,24 +162,247 @@
     return (residual + mixed_sum).astype(jnp.bfloat16)
 
 
+def dot(left, right):
+    return jnp.dot(left, right, preferred_element_type=jnp.float32)
+
+
+def exchanged(block, axis, distance):
+    route = [(i, i ^ distance) for i in range(lax.axis_size(axis))]
+    return lax.ppermute(block, axis, route)
+
+
+def core_swapped(block):
+    return exchanged(block, "seq", 1)
+
+
+def columns(matrix, index, width):
+    return lax.dynamic_slice_in_dim(matrix, index * width, width, 1)
+
+
+def rows(matrix, index, height):
+    return lax.dynamic_slice_in_dim(matrix, index * height, height, 0)
+
+
+def per_device(
+    byte_states,
+    byte_patch,
+    patch_len,
+    cross_query,
+    cross_key,
+    cross_value,
+    cross_out,
+    norm_gain,
+    latent_query,
+    latent_key,
+    latent_value,
+    latent_out,
+):
+    seq = lax.axis_index("seq")
+    tensor = lax.axis_index("tensor")
+    seq_count = lax.axis_size("seq")
+    tensor_count = lax.axis_size("tensor")
+    chip_count = seq_count // 2
+    chip, core = seq // 2, seq % 2
+    other = 1 - core
+    patch_count = patch_len.shape[0]
+    patch_dev = patch_count // seq_count
+    chip_patches = 2 * patch_dev
+    spill = patch_dev // 2
+    slot_count = chip_patches + 2 * spill
+    local_width = cross_query.shape[1]
+    half_width = local_width // 2
+    half_heads = half_width // HEAD_DIM
+    key_rows = cross_query.shape[0]
+    out_width = cross_out.shape[1]
+    bf16 = jnp.bfloat16
+
+    cross_weights = []
+    for weight in (cross_query, cross_key, cross_value):
+        received = core_swapped(columns(weight, other, half_width))
+        block = jnp.concatenate([columns(weight, core, half_width), received], axis=0)
+        cross_weights.append(
+            jnp.concatenate(
+                [block] + [exchanged(block, "seq", 2 * d) for d in range(1, chip_count)], axis=0
+            )
+        )
+    states = jnp.concatenate([byte_states, core_swapped(byte_states)], axis=0)
+    patches = jnp.concatenate([byte_patch, core_swapped(byte_patch)], axis=0)
+    states = jnp.concatenate(
+        [
+            columns(states, 2 * (chip ^ d) + (core ^ e), key_rows)
+            for d in range(chip_count)
+            for e in range(2)
+        ],
+        axis=1,
+    )
+
+    cross_out = jnp.concatenate(
+        [rows(cross_out, core, half_width), rows(cross_out, other, half_width)], axis=0
+    )
+    latent_out = jnp.concatenate(
+        [
+            rows(latent_out, half_heads * e + (chip ^ d), HEAD_DIM)
+            for e in (core, other)
+            for d in range(chip_count)
+        ],
+        axis=0,
+    )
+    paired = []
+    for weight in (latent_query, latent_key, latent_value):
+        received = core_swapped(columns(weight, other, half_width))
+        paired.append(jnp.concatenate([columns(weight, core, half_width), received], axis=0))
+    head_weights = [
+        jnp.concatenate([columns(weight, chip ^ d, HEAD_DIM) for weight in paired], axis=1)
+        for d in range(chip_count)
+    ]
+    gain_own = lax.dynamic_slice_in_dim(norm_gain, seq * out_width, out_width)
+    gain_other = lax.dynamic_slice_in_dim(norm_gain, (seq ^ 1) * out_width, out_width)
+
+    slot_of = patches - (chip * chip_patches - spill)
+    onehot = (slot_of[:, None] == jnp.arange(slot_count, dtype=jnp.int32)[None, :]).astype(bf16)
+    edge = jnp.ones((spill,), jnp.int32)
+    lengths = lax.dynamic_slice_in_dim(
+        jnp.concatenate([edge, patch_len, edge]), chip * chip_patches, slot_count
+    )
+    byte_sums = lax.dot_general(
+        onehot, states, (((0,), (0,)), ((), ())), preferred_element_type=jnp.float32
+    )
+    pooled = (byte_sums / lengths.astype(jnp.float32)[:, None]).astype(bf16)
+    query_slots = dot(pooled, cross_weights[0]).astype(bf16)
+    byte_keys = dot(states, cross_weights[1]).astype(bf16)
+    byte_values = dot(states, cross_weights[2]).astype(bf16)
+    byte_count = states.shape[0]
+    query_bytes = dot(onehot, query_slots)
+    scores = (query_bytes * byte_keys.astype(jnp.float32)).reshape(
+        byte_count, half_heads, HEAD_DIM
+    ).sum(axis=2) / math.sqrt(HEAD_DIM)
+    byte_raw = capped_exp(scores)
+    totals = contract_rows(onehot.astype(jnp.float32), byte_raw)
+    totals = jnp.where(totals > 0.0, totals, 1.0)
+    weighted = (
+        byte_raw[:, :, None]
+        * byte_values.astype(jnp.float32).reshape(byte_count, half_heads, HEAD_DIM)
+    ).reshape(byte_count, half_width)
+    summed = lax.dot_general(
+        onehot, weighted.astype(bf16), (((0,), (0,)), ((), ())), preferred_element_type=jnp.float32
+    )
+    heads = (
+        summed.reshape(slot_count, half_heads, HEAD_DIM) / totals[:, :, None]
+    ).reshape(slot_count, half_width).astype(bf16)
+
+    own_heads = heads[spill : spill + chip_patches]
+    from_above = shifted(heads[:spill], "seq", -2)
+    from_below = shifted(heads[spill + chip_patches :], "seq", 2)
+    own_heads = own_heads + jnp.concatenate(
+        [from_below, jnp.zeros((chip_patches - 2 * spill, half_width), bf16), from_above], axis=0
+    )
+
+    partial = []
+    for d in range(chip_count):
+        block = exchanged(own_heads, "seq", 2 * d) if d else own_heads
+        block = jnp.concatenate([block, core_swapped(block)], axis=1)
+        partial.append(dot(block, cross_out))
+    partial = jnp.stack(partial)
+
+    def quarter(stack, index):
+        return lax.dynamic_index_in_dim(stack, index, 0, keepdims=False)
+
+    total = quarter(partial, chip ^ tensor)
+    partial = partial.astype(bf16)
+    for r in range(1, tensor_count):
+        total = total + exchanged(quarter(partial, chip ^ tensor ^ r), "tensor", r).astype(
+            jnp.float32
+        )
+    latent_in = total.astype(bf16)
+
+    projected = []
+    squares = []
+    for r in range(tensor_count):
+        block = exchanged(latent_in, "tensor", r) if r else latent_in
+        pair = jnp.concatenate([block, core_swapped(block)], axis=1).astype(jnp.float32)
+        squares.append(jnp.sum(pair * pair, axis=1))
+        scaled = (pair * jnp.concatenate([gain_own, gain_other])[None, :]).astype(bf16)
+        share = dot(scaled, head_weights[0])
+        for d in range(1, chip_count):
+            share = share + exchanged(
+                dot(scaled, head_weights[d]).astype(bf16), "seq", 2 * d
+            ).astype(jnp.float32)
+        projected.append(share)
+    squares = jnp.stack(squares)
+    mean_square = squares
+    for d in range(1, chip_count):
+        mean_square = mean_square + exchanged(squares, "seq", 2 * d)
+    mean_square = mean_square / (out_width * seq_count)
+    projected = jnp.stack(projected) * lax.rsqrt(mean_square + norm_eps)[:, :, None]
+    projected = jnp.concatenate(
+        [quarter(projected, tensor ^ a) for a in range(tensor_count)], axis=0
+    ).astype(bf16)
+    query, key, value = jnp.split(projected, 3, axis=1)
+
+    attn_scores = lax.dot_general(
+        query, key, (((1,), (1,)), ((), ())), preferred_element_type=jnp.float32
+    ) / math.sqrt(HEAD_DIM)
+    positions = jnp.arange(patch_count, dtype=jnp.int32)
+    raw = jnp.where(positions[None, :] <= positions[:, None], capped_exp(attn_scores), 0.0)
+    attended = (dot(raw.astype(bf16), value) / jnp.sum(raw, axis=1, keepdims=True)).astype(bf16)
+
+    arrived = [attended] + [exchanged(attended, "seq", 2 * d) for d in range(1, chip_count)]
+    arrived = jnp.concatenate(arrived, axis=1)
+    arrived = jnp.concatenate([arrived, core_swapped(arrived)], axis=1)
+    mixed = dot(arrived, latent_out).reshape(tensor_count, -1, out_width)
+    result = latent_in.astype(jnp.float32) + quarter(mixed, tensor)
+    mixed = mixed.astype(bf16)
+    for r in range(1, tensor_count):
+        result = result + exchanged(quarter(mixed, tensor ^ r), "tensor", r).astype(jnp.float32)
+    result = result.astype(bf16)
+
+    pieces = []
+    for flip in range(2):
+        route = [
+            (s * tensor_count + t, (2 * t + ((s % 2) ^ flip)) * tensor_count + s // 2)
+            for s in range(seq_count)
+            for t in range(tensor_count)
+        ]
+        pieces.append(lax.ppermute(rows(result, core ^ flip, patch_dev), ("seq", "tensor"), route))
+    same, crossed = pieces
+    return jnp.concatenate(
+        [jnp.where(core == 0, same, crossed), jnp.where(core == 0, crossed, same)], axis=1
+    )
+
+
+def head_per_device(mesh, heads):
+    seq_count, tensor_count = mesh.shape["seq"], mesh.shape["tensor"]
+    return (
+        heads == seq_count * tensor_count
+        and seq_count == 2 * tensor_count
+        and tensor_count & (tensor_count - 1) == 0
+    )
+
+
 def solution(mesh):
-    return jax.shard_map(
-        per_device,
-        mesh=mesh,
-        in_specs=(
-            P("seq", None),
-            P("seq"),
-            P(),
-            P("seq", "tensor"),
-            P("seq", "tensor"),
-            P("seq", "tensor"),
-            P("tensor", "seq"),
-            P(),
-            P("seq", "tensor"),
-            P("seq", "tensor"),
-            P("seq", "tensor"),
-            P("tensor", "seq"),
-        ),
-        out_specs=P("seq", "tensor"),
-        check_vma=False,
-    )
+    specs = (
+        P("seq", None),
+        P("seq"),
+        P(),
+        P("seq", "tensor"),
+        P("seq", "tensor"),
+        P("seq", "tensor"),
+        P("tensor", "seq"),
+        P(),
+        P("seq", "tensor"),
+        P("seq", "tensor"),
+        P("seq", "tensor"),
+        P("tensor", "seq"),
+    )
+
+    def whole(*arrays):
+        chosen = (
+            per_device
+            if head_per_device(mesh, arrays[3].shape[1] // HEAD_DIM)
+            else per_device_gathered
+        )
+        return jax.shard_map(
+            chosen, mesh=mesh, in_specs=specs, out_specs=P("seq", "tensor"), check_vma=False
+        )(*arrays)
+
+    return whole

time: 507 us -> 279 us (0.55)
  waiting for transfers between devices: 348 us -> 115 us
  blocking collectives: 73.7 us -> 0 us
  starting transfers between devices: 6.13 us -> 74.2 us
  local copies, waits for them, and re-layouts: 4.93 us -> 40.9 us
  between operations: 16.1 us -> 0.74 us
  matrix products: 49.7 us -> 35.6 us
    all_gather x10 -> x0, waiting for transfers between devices: 294 us -> none  [the longest x1 52.8 us: per_device(): lax.all_gather(latent_out, 'seq', axis=1, tiled=True)]
    ppermute x0 -> x58, waiting for transfers between devices: none -> 110 us  [the longest x56 99.2 us: exchanged(): return lax.ppermute(block, axis, route)]
    psum x1 -> x0, blocking collectives: 73.7 us -> none  [per_device(): latent_in = lax.psum(partial_value, 'tensor').astype(jnp.bfloat16)]
    ppermute x0 -> x58, starting transfers between devices: none -> 67.5 us  [the longest x56 61.8 us: exchanged(): return lax.ppermute(block, axis, route)]
    reduce_scatter x1 -> x0, waiting for transfers between devices: 39.7 us -> none  [per_device(): lax.psum_scatter(projected, 'tensor', scatter_dimension=1, tiled=True)]
    unnamed x14 -> x72, local copies, waits for them, and re-layouts: 0.03 us -> 26.8 us
    dot_general x12 -> x28, matrix products: 46.3 us -> 34.2 us  [the longest x25 30.4 us: dot(): return jnp.dot(left, right, preferred_element_type=jnp.float32)]
    dynamic_slice x1 -> x6, local copies, waits for them, and re-layouts: 0.14 us -> 6.98 us  [the longest x3 5.05 us: columns(): return lax.dynamic_slice_in_dim(matrix, index * width, width, 1)]
  transfers between devices with their start and end apart: 13 -> 60, of which waited for: 11 -> 28; matrix products, arithmetic and copies ran while one was open for 10% -> 27% of each run, Pallas kernels for 0% -> 0%
where the time goes in v1:
time: 279 us; the launch traced here: 276 us
  waiting for transfers between devices  115 us (41%)
  starting transfers between devices  74.2 us (27%)
  local copies, waits for them, and re-layouts  40.9 us (15%)
  matrix products  35.6 us (13%)
  other arithmetic  9.34 us (3%)
    ppermute x56, waiting for transfers between devices, exchanged(): return lax.ppermute(block, axis, route)  99.2 us
    ppermute x56, starting transfers between devices, exchanged(): return lax.ppermute(block, axis, route)  61.8 us
    dot_general x25, matrix products, dot(): return jnp.dot(left, right, preferred_element_type=jnp.float32)  30.4 us
    unnamed x72, local copies, waits for them, and re-layouts  26.8 us
    ppermute x2, waiting for transfers between devices, per_device(): lax.ppermute(rows(result, core ^ flip, patch_dev), ('seq', 'tensor'), route)  11.3 us
    ppermute x2, starting transfers between devices, shifted(): return lax.ppermute(block, axis, route)  6.7 us
    ppermute x2, starting transfers between devices, per_device(): lax.ppermute(rows(result, core ^ flip, patch_dev), ('seq', 'tensor'), route)  5.68 us
  transfers between devices with their start and end apart: 60, of which 28 were waited for; matrix products, arithmetic and copies ran while one was open for 27% of the time, Pallas kernels for 0%

profile of v1, /device:TPU:9, one launch (start us, length us, event | category | flops | bytes accessed | tf_op | source)
XLA Modules:
  0.0 275.8 jit_solution(16525141040340341436)
XLA Ops:
  6.8 3.1 %constant_dynamic-update-slice_fusion.1 = bf16[2048,1024]{1,0:T(8,128)(2,1)} fusion(bf16[1024,1024]{1,0:T(8,128)(2,1)} %param.12), kind=kLoop, calls=%fused_computation.175 | loop fusion | bytes 4194304
  24.5 3.7 %collective-permute-start.4 = (bf16[256,512]{1,0:T(8,128)(2,1)S(1)}, bf16[256,512]{1,0:T(8,128)(2,1)S(1)}, u32[]{:S(2)}, u32[]{:S(2)}) collective-permute-start(bf16[256,512]{1,0:T(8,128)(2,1)S(1)} %pad_maximum_fusion.12), channel_id=1, source_target_pairs={{0,16},{4,20},{8,24},{12,28},{16,0},{20,4},{24,8},{28,12},{1,17},{... | collective-permute-start | bytes 786440 | tf_op jit(solution)/shard_map/ppermute | solution.py:171
  29.8 2.8 %collective-permute-done.3 = bf16[256,512]{1,0:T(8,128)(2,1)S(1)} collective-permute-done((bf16[256,512]{1,0:T(8,128)(2,1)S(1)}, bf16[256,512]{1,0:T(8,128)(2,1)S(1)}, u32[]{:S(2)}, u32[]{:S(2)}) %collective-permute-start.3) | collective-permute-done | bytes 262176 | tf_op jit(solution)/shard_map/ppermute | solution.py:171
  41.1 2.8 %collective-permute-done.11 = bf16[256,512]{1,0:T(8,128)(2,1)S(1)} collective-permute-done((bf16[256,512]{1,0:T(8,128)(2,1)S(1)}, bf16[256,512]{1,0:T(8,128)(2,1)S(1)}, u32[]{:S(2)}, u32[]{:S(2)}) %collective-permute-start.11) | collective-permute-done | bytes 262176 | tf_op jit(solution)/shard_map/ppermute | solution.py:171
  43.9 4.4 %collective-permute-done.13 = bf16[256,512]{1,0:T(8,128)(2,1)S(1)} collective-permute-done((bf16[256,512]{1,0:T(8,128)(2,1)S(1)}, bf16[256,512]{1,0:T(8,128)(2,1)S(1)}, u32[]{:S(2)}, u32[]{:S(2)}) %collective-permute-start.13) | collective-permute-done | bytes 262176 | tf_op jit(solution)/shard_map/ppermute | solution.py:171
  51.8 3.9 %convolution_convert_fusion.1 = bf16[2048,512]{0,1:T(8,128)(2,1)} fusion(bf16[2048,1024]{1,0:T(8,128)(2,1)S(1)} %dynamic-slice_dynamic-update-slice_fusion, bf16[1024,512]{1,0:T(8,128)(2,1)S(1)} %copy-done.13), kind=kOutput, calls=%fused_computation.13 | convolution fusion | flops 2148532224 | bytes 7340032 | tf_op jit(solution)/shard_map/dot_general | solution.py:166
  57.5 3.5 %bitcast_reduce_fusion = f32[2048,4]{0,1:T(4,128)S(1)} fusion(bf16[2048,512]{0,1:T(8,128)(2,1)} %convolution_convert_fusion.1, s32[2048]{0:T(1024)S(1)} %add_subtract_fusion, bf16[384,1024]{1,0:T(8,128)(2,1)S(1)} %divide_convert_fusion, bf16[1024,512]{1,0:T(8,128)(2,1)S(1)} %copy-done.14), kind=kOutput, calls=%fused_computation.2 | convolution fusion | flops 1212080128 | bytes 3973120 | tf_op jit(solution)/shard_map/dot_general | solution.py:166
  62.5 5.1 %fusion = bf16[2048,512]{0,1:T(8,128)(2,1)S(1)} fusion(bf16[2048,1024]{1,0:T(8,128)(2,1)} %copy-done.12, bf16[1024,512]{1,0:T(8,128)(2,1)} %copy-done.16, f32[2048,4]{0,1:T(4,128)S(1)} %multiply_exponential_fusion), kind=kOutput, calls=%fused_computation.1 | convolution fusion | flops 2151677952 | bytes 7372800 | tf_op jit(solution)/shard_map/dot_general | solution.py:166
  70.1 5.4 %collective-permute-start.14 = (bf16[64,512]{0,1:T(8,128)(2,1)}, bf16[64,512]{0,1:T(8,128)(2,1)}, u32[]{:S(2)}, u32[]{:S(2)}) collective-permute-start(bf16[64,512]{0,1:T(8,128)(2,1)} %bitcast.91), channel_id=1, source_target_pairs={{0,8},{4,12},{8,16},{12,20},{16,24},{20,28},{1,9},{5,13},{9,17},{1... | collective-permute-start | bytes 196616 | tf_op jit(solution)/shard_map/ppermute | solution.py:19
  79.8 4.5 %collective-permute-done.15 = bf16[64,512]{0,1:T(8,128)(2,1)} collective-permute-done((bf16[64,512]{0,1:T(8,128)(2,1)}, bf16[64,512]{0,1:T(8,128)(2,1)}, u32[]{:S(2)}, u32[]{:S(2)}) %collective-permute-start.15) | collective-permute-done | bytes 65568 | tf_op jit(solution)/shard_map/ppermute | solution.py:19
  86.8 6.7 %collective-permute-start.16 = (bf16[256,512]{0,1:T(8,128)(2,1)S(1)}, bf16[256,512]{0,1:T(8,128)(2,1)S(1)}, u32[]{:S(2)}, u32[]{:S(2)}) collective-permute-start(bf16[256,512]{0,1:T(8,128)(2,1)S(1)} %maximum_add_fusion), channel_id=1, source_target_pairs={{0,4},{4,0},{8,12},{12,8},{16,20},{20,16},{24,28},{28,24},{1,5},{5... | collective-permute-start | bytes 786440 | tf_op jit(solution)/shard_map/ppermute | solution.py:171
  98.1 6.6 %collective-permute-start.20 = (bf16[256,512]{0,1:T(8,128)(2,1)}, bf16[256,512]{0,1:T(8,128)(2,1)S(1)}, u32[]{:S(2)}, u32[]{:S(2)}) collective-permute-start(bf16[256,512]{0,1:T(8,128)(2,1)} %collective-permute-done.19), channel_id=1, source_target_pairs={{0,4},{4,0},{8,12},{12,8},{16,20},{20,16},{24,28},{28,24},{1,5},{5... | collective-permute-start | bytes 786440 | tf_op jit(solution)/shard_map/ppermute | solution.py:171
  112.3 2.5 collective-permute-start.24
  115.3 7.4 %collective-permute-done.23 = bf16[256,512]{1,0:T(8,128)(2,1)S(1)} collective-permute-done((bf16[256,512]{1,0:T(8,128)(2,1)S(1)}, bf16[256,512]{1,0:T(8,128)(2,1)S(1)}, u32[]{:S(2)}, u32[]{:S(2)}) %collective-permute-start.23) | collective-permute-done | bytes 262176 | tf_op jit(solution)/shard_map/ppermute | solution.py:171
  122.7 3.7 %collective-permute-done.24 = bf16[256,512]{1,0:T(8,128)(2,1)S(1)} collective-permute-done((bf16[256,512]{1,0:T(8,128)(2,1)S(1)}, bf16[256,512]{1,0:T(8,128)(2,1)S(1)}, u32[]{:S(2)}, u32[]{:S(2)}) %collective-permute-start.24) | collective-permute-done | bytes 262176 | tf_op jit(solution)/shard_map/ppermute | solution.py:171
  126.4 11.1 %collective-permute-done.25 = bf16[256,512]{1,0:T(8,128)(2,1)S(1)} collective-permute-done((bf16[256,512]{1,0:T(8,128)(2,1)S(1)}, bf16[256,512]{1,0:T(8,128)(2,1)S(1)}, u32[]{:S(2)}, u32[]{:S(2)}) %collective-permute-start.25) | collective-permute-done | bytes 262176 | tf_op jit(solution)/shard_map/ppermute | solution.py:171
  139.7 2.5 collective-permute-start.38
  144.1 6.8 %collective-permute-done.33 = bf16[256,512]{1,0:T(8,128)(2,1)S(1)} collective-permute-done((bf16[256,512]{1,0:T(8,128)(2,1)S(1)}, bf16[256,512]{1,0:T(8,128)(2,1)S(1)}, u32[]{:S(2)}, u32[]{:S(2)}) %collective-permute-start.33) | collective-permute-done | bytes 262176 | tf_op jit(solution)/shard_map/ppermute | solution.py:171
  151.3 7.5 %collective-permute-done.38 = bf16[256,512]{1,0:T(8,128)(2,1)S(1)} collective-permute-done((bf16[256,512]{1,0:T(8,128)(2,1)S(1)}, bf16[256,512]{1,0:T(8,128)(2,1)S(1)}, u32[]{:S(2)}, u32[]{:S(2)}) %collective-permute-start.38) | collective-permute-done | bytes 262176 | tf_op jit(solution)/shard_map/ppermute | solution.py:171
  160.9 4.5 %collective-permute-done.43 = bf16[256,512]{1,0:T(8,128)(2,1)S(1)} collective-permute-done((bf16[256,512]{1,0:T(8,128)(2,1)S(1)}, bf16[256,512]{1,0:T(8,128)(2,1)S(1)}, u32[]{:S(2)}, u32[]{:S(2)}) %collective-permute-start.43) | collective-permute-done | bytes 262176 | tf_op jit(solution)/shard_map/ppermute | solution.py:171
  184.1 2.9 %collective-permute-done.40 = bf16[256,384]{1,0:T(8,128)(2,1)S(1)} collective-permute-done((bf16[256,384]{1,0:T(8,128)(2,1)S(1)}, bf16[256,384]{1,0:T(8,128)(2,1)S(1)}, u32[]{:S(2)}, u32[]{:S(2)}) %collective-permute-start.40) | collective-permute-done | bytes 196640 | tf_op jit(solution)/shard_map/ppermute | solution.py:171
  190.8 4.7 %collective-permute-done.45 = bf16[256,384]{1,0:T(8,128)(2,1)S(1)} collective-permute-done((bf16[256,384]{1,0:T(8,128)(2,1)S(1)}, bf16[256,384]{1,0:T(8,128)(2,1)S(1)}, u32[]{:S(2)}, u32[]{:S(2)}) %collective-permute-start.45) | collective-permute-done | bytes 196640 | tf_op jit(solution)/shard_map/ppermute | solution.py:171
  209.9 4.4 %collective-permute-done.53 = bf16[1024,128]{0,1:T(8,128)(2,1)S(1)} collective-permute-done((bf16[1024,128]{0,1:T(8,128)(2,1)S(1)}, bf16[1024,128]{0,1:T(8,128)(2,1)S(1)}, u32[]{:S(2)}, u32[]{:S(2)}) %collective-permute-start.53) | collective-permute-done | bytes 262176 | tf_op jit(solution)/shard_map/ppermute | solution.py:171
  215.1 4.6 %collective-permute-start.54 = (bf16[1024,512]{0,1:T(8,128)(2,1)S(1)}, bf16[1024,512]{0,1:T(8,128)(2,1)S(1)}, u32[]{:S(2)}, u32[]{:S(2)}) collective-permute-start(bf16[1024,512]{0,1:T(8,128)(2,1)S(1)} %pad_maximum_fusion.2), channel_id=1, source_target_pairs={{0,4},{4,0},{8,12},{12,8},{16,20},{20,16},{24,28},{28,24},{1,5},{5... | collective-permute-start | bytes 3145736 | tf_op jit(solution)/shard_map/ppermute | solution.py:171
  227.9 2.9 %fusion.104 = f32[1024,512]{1,0:T(8,128)S(1)} fusion(bf16[1024,1024]{0,1:T(8,128)(2,1)} %constant_dynamic-update-slice_fusion.17, bf16[1024,512]{1,0:T(8,128)(2,1)S(1)} %copy-done.17), kind=kOutput, calls=%fused_computation.233 | convolution fusion | flops 1073741824 | bytes 5242880 | tf_op jit(solution)/shard_map/dot_general | solution.py:166
  231.1 2.5 collective-permute-start.56
  233.7 8.4 %collective-permute-done.55 = bf16[256,512]{1,0:T(8,128)(2,1)S(1)} collective-permute-done((bf16[256,512]{1,0:T(8,128)(2,1)S(1)}, bf16[256,512]{1,0:T(8,128)(2,1)S(1)}, u32[]{:S(2)}, u32[]{:S(2)}) %collective-permute-start.55) | collective-permute-done | bytes 262176 | tf_op jit(solution)/shard_map/ppermute | solution.py:171
  242.1 7.9 %collective-permute-done.56 = bf16[256,512]{1,0:T(8,128)(2,1)} collective-permute-done((bf16[256,512]{1,0:T(8,128)(2,1)S(1)}, bf16[256,512]{1,0:T(8,128)(2,1)}, u32[]{:S(2)}, u32[]{:S(2)}) %collective-permute-start.56) | collective-permute-done | bytes 262176 | tf_op jit(solution)/shard_map/ppermute | solution.py:171
  250.0 6.8 %collective-permute-done.57 = bf16[256,512]{1,0:T(8,128)(2,1)} collective-permute-done((bf16[256,512]{1,0:T(8,128)(2,1)S(1)}, bf16[256,512]{1,0:T(8,128)(2,1)}, u32[]{:S(2)}, u32[]{:S(2)}) %collective-permute-start.57) | collective-permute-done | bytes 262176 | tf_op jit(solution)/shard_map/ppermute | solution.py:171
  260.0 3.8 %collective-permute-start.59 = (bf16[128,512]{1,0:T(8,128)(2,1)S(1)}, bf16[128,512]{1,0:T(8,128)(2,1)S(1)}, u32[]{:S(2)}, u32[]{:S(2)}) collective-permute-start(bf16[128,512]{1,0:T(8,128)(2,1)S(1)} %get-tuple-element.46), channel_id=1, source_target_pairs={{0,4},{1,12},{2,20},{3,28},{4,0},{5,8},{6,16},{7,24},{8,5},{9,13},... | collective-permute-start | bytes 393224 | tf_op jit(solution)/shard_map/ppermute | solution.py:366
  263.7 8.5 %collective-permute-done.58 = bf16[128,512]{1,0:T(8,128)(2,1)S(1)} collective-permute-done((bf16[128,512]{1,0:T(8,128)(2,1)S(1)}, bf16[128,512]{1,0:T(8,128)(2,1)S(1)}, u32[]{:S(2)}, u32[]{:S(2)}) %collective-permute-start.58) | collective-permute-done | bytes 131104 | tf_op jit(solution)/shard_map/ppermute | solution.py:366
  272.2 2.8 %collective-permute-done.59 = bf16[128,512]{1,0:T(8,128)(2,1)S(1)} collective-permute-done((bf16[128,512]{1,0:T(8,128)(2,1)S(1)}, bf16[128,512]{1,0:T(8,128)(2,1)S(1)}, u32[]{:S(2)}, u32[]{:S(2)}) %collective-permute-start.59) | collective-permute-done | bytes 131104 | tf_op jit(solution)/shard_map/ppermute | solution.py:366
  (245 shorter events, 116.5 us)
Async XLA Ops:
  0.0 49.4 %collective-permute-start.1 = (bf16[1024,1024]{1,0:T(8,128)(2,1)}, bf16[1024,1024]{1,0:T(8,128)(2,1)S(1)}, u32[]{:S(2)}, u32[]{:S(2)}) collective-permute-start(bf16[1024,1024]{1,0:T(8,128)(2,1)} %param.12), channel_id=1, source_target_pairs={{0,4},{4,0},{8,12},{12,8},{16,20},{20,16},{24,28},{28,24},{1,5},{5... | collective-permute-start | bytes 6291464 | tf_op jit(solution)/shard_map/ppermute | solution.py:171
  6.3 10.9 %collective-permute-start.10 = (bf16[128,512]{1,0:T(8,128)(2,1)}, bf16[128,512]{1,0:T(8,128)(2,1)}, u32[]{:S(2)}, u32[]{:S(2)}) collective-permute-start(bf16[128,512]{1,0:T(8,128)(2,1)} %get-tuple-element.49), channel_id=1, source_target_pairs={{0,4},{4,0},{8,12},{12,8},{16,20},{20,16},{24,28},{28,24},{1,5},{5... | collective-permute-start | bytes 393224 | tf_op jit(solution)/shard_map/ppermute | solution.py:171
  12.7 102.0 %collective-permute-start.27 = (bf16[512,512]{1,0:T(8,128)(2,1)}, bf16[512,512]{1,0:T(8,128)(2,1)S(1)}, u32[]{:S(2)}, u32[]{:S(2)}) collective-permute-start(bf16[512,512]{1,0:T(8,128)(2,1)} %get-tuple-element.26), channel_id=1, source_target_pairs={{0,4},{4,0},{8,12},{12,8},{16,20},{20,16},{24,28},{28,24},{1,5},{5... | collective-permute-start | bytes 1572872 | tf_op jit(solution)/shard_map/ppermute | solution.py:171
  17.2 11.7 %collective-permute-start.9 = (bf16[256,512]{1,0:T(8,128)(2,1)S(1)}, bf16[256,512]{1,0:T(8,128)(2,1)S(1)}, u32[]{:S(2)}, u32[]{:S(2)}) collective-permute-start(bf16[256,512]{1,0:T(8,128)(2,1)S(1)} %pad_maximum_fusion.13), channel_id=1, source_target_pairs={{0,24},{4,28},{8,16},{12,20},{16,8},{20,12},{24,0},{28,4},{1,25},{... | collective-permute-start | bytes 786440 | tf_op jit(solution)/shard_map/ppermute | solution.py:171
  32.6 11.3 %collective-permute-start.11 = (bf16[256,512]{1,0:T(8,128)(2,1)S(1)}, bf16[256,512]{1,0:T(8,128)(2,1)S(1)}, u32[]{:S(2)}, u32[]{:S(2)}) collective-permute-start(bf16[256,512]{1,0:T(8,128)(2,1)S(1)} %pad_maximum_fusion.14), channel_id=1, source_target_pairs={{0,8},{4,12},{8,0},{12,4},{16,24},{20,28},{24,16},{28,20},{1,9},{5... | collective-permute-start | bytes 786440 | tf_op jit(solution)/shard_map/ppermute | solution.py:171
  85.4 11.4 %collective-permute-start.17 = (bf16[256,512]{0,1:T(8,128)(2,1)S(1)}, bf16[256,512]{0,1:T(8,128)(2,1)}, u32[]{:S(2)}, u32[]{:S(2)}) collective-permute-start(bf16[256,512]{0,1:T(8,128)(2,1)S(1)} %maximum_add_fusion), channel_id=1, source_target_pairs={{0,8},{4,12},{8,0},{12,4},{16,24},{20,28},{24,16},{28,20},{1,9},{5... | collective-permute-start | bytes 786440 | tf_op jit(solution)/shard_map/ppermute | solution.py:171
  85.9 12.2 %collective-permute-start.19 = (bf16[256,512]{0,1:T(8,128)(2,1)S(1)}, bf16[256,512]{0,1:T(8,128)(2,1)}, u32[]{:S(2)}, u32[]{:S(2)}) collective-permute-start(bf16[256,512]{0,1:T(8,128)(2,1)S(1)} %maximum_add_fusion), channel_id=1, source_target_pairs={{0,16},{4,20},{8,24},{12,28},{16,0},{20,4},{24,8},{28,12},{1,17},{... | collective-permute-start | bytes 786440 | tf_op jit(solution)/shard_map/ppermute | solution.py:171
  86.8 17.9 %collective-permute-start.16 = (bf16[256,512]{0,1:T(8,128)(2,1)S(1)}, bf16[256,512]{0,1:T(8,128)(2,1)S(1)}, u32[]{:S(2)}, u32[]{:S(2)}) collective-permute-start(bf16[256,512]{0,1:T(8,128)(2,1)S(1)} %maximum_add_fusion), channel_id=1, source_target_pairs={{0,4},{4,0},{8,12},{12,8},{16,20},{20,16},{24,28},{28,24},{1,5},{5... | collective-permute-start | bytes 786440 | tf_op jit(solution)/shard_map/ppermute | solution.py:171
  93.6 11.3 %collective-permute-start.21 = (bf16[256,512]{0,1:T(8,128)(2,1)S(1)}, bf16[256,512]{0,1:T(8,128)(2,1)}, u32[]{:S(2)}, u32[]{:S(2)}) collective-permute-start(bf16[256,512]{0,1:T(8,128)(2,1)S(1)} %maximum_add_fusion), channel_id=1, source_target_pairs={{0,24},{4,28},{8,16},{12,20},{16,8},{20,12},{24,0},{28,4},{1,25},{... | collective-permute-start | bytes 786440 | tf_op jit(solution)/shard_map/ppermute | solution.py:171
  98.1 10.9 %collective-permute-start.20 = (bf16[256,512]{0,1:T(8,128)(2,1)}, bf16[256,512]{0,1:T(8,128)(2,1)S(1)}, u32[]{:S(2)}, u32[]{:S(2)}) collective-permute-start(bf16[256,512]{0,1:T(8,128)(2,1)} %collective-permute-done.19), channel_id=1, source_target_pairs={{0,4},{4,0},{8,12},{12,8},{16,20},{20,16},{24,28},{28,24},{1,5},{5... | collective-permute-start | bytes 786440 | tf_op jit(solution)/shard_map/ppermute | solution.py:171
  104.8 34.5 %collective-permute-start.28 = (bf16[512,512]{1,0:T(8,128)(2,1)}, bf16[512,512]{1,0:T(8,128)(2,1)S(1)}, u32[]{:S(2)}, u32[]{:S(2)}) collective-permute-start(bf16[512,512]{1,0:T(8,128)(2,1)} %get-tuple-element.28), channel_id=1, source_target_pairs={{0,4},{4,0},{8,12},{12,8},{16,20},{20,16},{24,28},{28,24},{1,5},{5... | collective-permute-start | bytes 1572872 | tf_op jit(solution)/shard_map/ppermute | solution.py:171
  107.1 32.4 %collective-permute-start.29 = (bf16[512,512]{1,0:T(8,128)(2,1)S(1)}, bf16[512,512]{1,0:T(8,128)(2,1)S(1)}, u32[]{:S(2)}, u32[]{:S(2)}) collective-permute-start(bf16[512,512]{1,0:T(8,128)(2,1)S(1)} %copy-done.9), channel_id=1, source_target_pairs={{0,4},{4,0},{8,12},{12,8},{16,20},{20,16},{24,28},{28,24},{1,5},{5... | collective-permute-start | bytes 1572872 | tf_op jit(solution)/shard_map/ppermute | solution.py:171
  112.3 14.1 %collective-permute-start.24 = (bf16[256,512]{1,0:T(8,128)(2,1)S(1)}, bf16[256,512]{1,0:T(8,128)(2,1)S(1)}, u32[]{:S(2)}, u32[]{:S(2)}) collective-permute-start(bf16[256,512]{1,0:T(8,128)(2,1)S(1)} %get-tuple-element.34), channel_id=1, source_target_pairs={{0,2},{1,3},{2,0},{3,1},{4,6},{5,7},{6,4},{7,5},{8,10},{9,11},{10,... | collective-permute-start | bytes 786440 | tf_op jit(solution)/shard_map/ppermute | solution.py:171
  114.7 22.8 %collective-permute-start.25 = (bf16[256,512]{1,0:T(8,128)(2,1)S(1)}, bf16[256,512]{1,0:T(8,128)(2,1)S(1)}, u32[]{:S(2)}, u32[]{:S(2)}) collective-permute-start(bf16[256,512]{1,0:T(8,128)(2,1)S(1)} %get-tuple-element.33), channel_id=1, source_target_pairs={{0,3},{1,2},{2,1},{3,0},{4,7},{5,6},{6,5},{7,4},{8,11},{9,10},{10,... | collective-permute-start | bytes 786440 | tf_op jit(solution)/shard_map/ppermute | solution.py:171
  139.7 11.2 %collective-permute-start.33 = (bf16[256,512]{1,0:T(8,128)(2,1)S(1)}, bf16[256,512]{1,0:T(8,128)(2,1)S(1)}, u32[]{:S(2)}, u32[]{:S(2)}) collective-permute-start(bf16[256,512]{1,0:T(8,128)(2,1)S(1)} %fusion.53), channel_id=1, source_target_pairs={{0,1},{1,0},{2,3},{3,2},{4,5},{5,4},{6,7},{7,6},{8,9},{9,8},{10,11... | collective-permute-start | bytes 786440 | tf_op jit(solution)/shard_map/ppermute | solution.py:171
  139.7 19.0 %collective-permute-start.38 = (bf16[256,512]{1,0:T(8,128)(2,1)S(1)}, bf16[256,512]{1,0:T(8,128)(2,1)S(1)}, u32[]{:S(2)}, u32[]{:S(2)}) collective-permute-start(bf16[256,512]{1,0:T(8,128)(2,1)S(1)} %fusion.53), channel_id=1, source_target_pairs={{0,2},{1,3},{2,0},{3,1},{4,6},{5,7},{6,4},{7,5},{8,10},{9,11},{10,... | collective-permute-start | bytes 786440 | tf_op jit(solution)/shard_map/ppermute | solution.py:171
  142.2 23.2 %collective-permute-start.43 = (bf16[256,512]{1,0:T(8,128)(2,1)S(1)}, bf16[256,512]{1,0:T(8,128)(2,1)S(1)}, u32[]{:S(2)}, u32[]{:S(2)}) collective-permute-start(bf16[256,512]{1,0:T(8,128)(2,1)S(1)} %fusion.53), channel_id=1, source_target_pairs={{0,3},{1,2},{2,1},{3,0},{4,7},{5,6},{6,5},{7,4},{8,11},{9,10},{10,... | collective-permute-start | bytes 786440 | tf_op jit(solution)/shard_map/ppermute | solution.py:171
  142.8 23.7 %collective-permute-start.30 = (bf16[256,384]{1,0:T(8,128)(2,1)S(1)}, bf16[256,384]{1,0:T(8,128)(2,1)S(1)}, u32[]{:S(2)}, u32[]{:S(2)}) collective-permute-start(bf16[256,384]{1,0:T(8,128)(2,1)S(1)} %convolution_convert_fusion.14), channel_id=1, source_target_pairs={{0,8},{4,12},{8,0},{12,4},{16,24},{20,28},{24,16},{28,20},{1,9},{5... | collective-permute-start | bytes 589832 | tf_op jit(solution)/shard_map/ppermute | solution.py:171
  143.3 23.2 %collective-permute-start.31 = (bf16[256,384]{1,0:T(8,128)(2,1)S(1)}, bf16[256,384]{1,0:T(8,128)(2,1)S(1)}, u32[]{:S(2)}, u32[]{:S(2)}) collective-permute-start(bf16[256,384]{1,0:T(8,128)(2,1)S(1)} %convolution_convert_fusion.13), channel_id=1, source_target_pairs={{0,16},{4,20},{8,24},{12,28},{16,0},{20,4},{24,8},{28,12},{1,17},{... | collective-permute-start | bytes 589832 | tf_op jit(solution)/shard_map/ppermute | solution.py:171
  150.8 15.7 %collective-permute-start.32 = (bf16[256,384]{1,0:T(8,128)(2,1)S(1)}, bf16[256,384]{1,0:T(8,128)(2,1)S(1)}, u32[]{:S(2)}, u32[]{:S(2)}) collective-permute-start(bf16[256,384]{1,0:T(8,128)(2,1)S(1)} %convolution_convert_fusion.12), channel_id=1, source_target_pairs={{0,24},{4,28},{8,16},{12,20},{16,8},{20,12},{24,0},{28,4},{1,25},{... | collective-permute-start | bytes 589832 | tf_op jit(solution)/shard_map/ppermute | solution.py:171
  168.4 11.0 %collective-permute-start.49 = (f32[4,256]{1,0:T(4,128)S(1)}, f32[4,256]{1,0:T(4,128)S(1)}, u32[]{:S(2)}, u32[]{:S(2)}) collective-permute-start(f32[4,256]{1,0:T(4,128)S(1)} %pad_maximum_fusion.17), channel_id=1, source_target_pairs={{0,16},{4,20},{8,24},{12,28},{16,0},{20,4},{24,8},{28,12},{1,17},{... | collective-permute-start | bytes 12296 | tf_op jit(solution)/shard_map/ppermute | solution.py:171
  168.6 10.8 %collective-permute-start.50 = (f32[4,256]{1,0:T(4,128)S(1)}, f32[4,256]{1,0:T(4,128)S(1)}, u32[]{:S(2)}, u32[]{:S(2)}) collective-permute-start(f32[4,256]{1,0:T(4,128)S(1)} %pad_maximum_fusion.17), channel_id=1, source_target_pairs={{0,24},{4,28},{8,16},{12,20},{16,8},{20,12},{24,0},{28,4},{1,25},{... | collective-permute-start | bytes 12296 | tf_op jit(solution)/shard_map/ppermute | solution.py:171
  179.7 10.9 %collective-permute-start.42 = (bf16[256,384]{1,0:T(8,128)(2,1)S(1)}, bf16[256,384]{1,0:T(8,128)(2,1)S(1)}, u32[]{:S(2)}, u32[]{:S(2)}) collective-permute-start(bf16[256,384]{1,0:T(8,128)(2,1)S(1)} %convolution_convert_fusion.6), channel_id=1, source_target_pairs={{0,24},{4,28},{8,16},{12,20},{16,8},{20,12},{24,0},{28,4},{1,25},{... | collective-permute-start | bytes 589832 | tf_op jit(solution)/shard_map/ppermute | solution.py:171
  182.1 13.4 %collective-permute-start.45 = (bf16[256,384]{1,0:T(8,128)(2,1)S(1)}, bf16[256,384]{1,0:T(8,128)(2,1)S(1)}, u32[]{:S(2)}, u32[]{:S(2)}) collective-permute-start(bf16[256,384]{1,0:T(8,128)(2,1)S(1)} %convolution_convert_fusion.5), channel_id=1, source_target_pairs={{0,8},{4,12},{8,0},{12,4},{16,24},{20,28},{24,16},{28,20},{1,9},{5... | collective-permute-start | bytes 589832 | tf_op jit(solution)/shard_map/ppermute | solution.py:171
  182.5 15.0 %collective-permute-start.46 = (bf16[256,384]{1,0:T(8,128)(2,1)S(1)}, bf16[256,384]{1,0:T(8,128)(2,1)S(1)}, u32[]{:S(2)}, u32[]{:S(2)}) collective-permute-start(bf16[256,384]{1,0:T(8,128)(2,1)S(1)} %convolution_convert_fusion.4), channel_id=1, source_target_pairs={{0,16},{4,20},{8,24},{12,28},{16,0},{20,4},{24,8},{28,12},{1,17},{... | collective-permute-start | bytes 589832 | tf_op jit(solution)/shard_map/ppermute | solution.py:171
  187.1 12.0 %collective-permute-start.47 = (bf16[256,384]{1,0:T(8,128)(2,1)S(1)}, bf16[256,384]{1,0:T(8,128)(2,1)S(1)}, u32[]{:S(2)}, u32[]{:S(2)}) collective-permute-start(bf16[256,384]{1,0:T(8,128)(2,1)S(1)} %convolution_convert_fusion.3), channel_id=1, source_target_pairs={{0,24},{4,28},{8,16},{12,20},{16,8},{20,12},{24,0},{28,4},{1,25},{... | collective-permute-start | bytes 589832 | tf_op jit(solution)/shard_map/ppermute | solution.py:171
  215.1 11.8 %collective-permute-start.54 = (bf16[1024,512]{0,1:T(8,128)(2,1)S(1)}, bf16[1024,512]{0,1:T(8,128)(2,1)S(1)}, u32[]{:S(2)}, u32[]{:S(2)}) collective-permute-start(bf16[1024,512]{0,1:T(8,128)(2,1)S(1)} %pad_maximum_fusion.2), channel_id=1, source_target_pairs={{0,4},{4,0},{8,12},{12,8},{16,20},{20,16},{24,28},{28,24},{1,5},{5... | collective-permute-start | bytes 3145736 | tf_op jit(solution)/shard_map/ppermute | solution.py:171
  231.0 11.1 %collective-permute-start.55 = (bf16[256,512]{1,0:T(8,128)(2,1)S(1)}, bf16[256,512]{1,0:T(8,128)(2,1)S(1)}, u32[]{:S(2)}, u32[]{:S(2)}) collective-permute-start(bf16[256,512]{1,0:T(8,128)(2,1)S(1)} %get-tuple-element.11), channel_id=1, source_target_pairs={{0,1},{1,0},{2,3},{3,2},{4,5},{5,4},{6,7},{7,6},{8,9},{9,8},{10,11... | collective-permute-start | bytes 786440 | tf_op jit(solution)/shard_map/ppermute | solution.py:171
  231.1 18.9 %collective-permute-start.56 = (bf16[256,512]{1,0:T(8,128)(2,1)S(1)}, bf16[256,512]{1,0:T(8,128)(2,1)}, u32[]{:S(2)}, u32[]{:S(2)}) collective-permute-start(bf16[256,512]{1,0:T(8,128)(2,1)S(1)} %get-tuple-element.13), channel_id=1, source_target_pairs={{0,2},{1,3},{2,0},{3,1},{4,6},{5,7},{6,4},{7,5},{8,10},{9,11},{10,... | collective-permute-start | bytes 786440 | tf_op jit(solution)/shard_map/ppermute | solution.py:171
  233.5 23.3 %collective-permute-start.57 = (bf16[256,512]{1,0:T(8,128)(2,1)S(1)}, bf16[256,512]{1,0:T(8,128)(2,1)}, u32[]{:S(2)}, u32[]{:S(2)}) collective-permute-start(bf16[256,512]{1,0:T(8,128)(2,1)S(1)} %get-tuple-element.12), channel_id=1, source_target_pairs={{0,3},{1,2},{2,1},{3,0},{4,7},{5,6},{6,5},{7,4},{8,11},{9,10},{10,... | collective-permute-start | bytes 786440 | tf_op jit(solution)/shard_map/ppermute | solution.py:171
  258.1 14.2 %collective-permute-start.58 = (bf16[128,512]{1,0:T(8,128)(2,1)S(1)}, bf16[128,512]{1,0:T(8,128)(2,1)S(1)}, u32[]{:S(2)}, u32[]{:S(2)}) collective-permute-start(bf16[128,512]{1,0:T(8,128)(2,1)S(1)} %get-tuple-element.45), channel_id=1, source_target_pairs={{0,0},{1,8},{2,16},{3,24},{4,4},{5,12},{6,20},{7,28},{8,1},{9,9},{... | collective-permute-start | bytes 393224 | tf_op jit(solution)/shard_map/ppermute | solution.py:366
  260.0 15.1 %collective-permute-start.59 = (bf16[128,512]{1,0:T(8,128)(2,1)S(1)}, bf16[128,512]{1,0:T(8,128)(2,1)S(1)}, u32[]{:S(2)}, u32[]{:S(2)}) collective-permute-start(bf16[128,512]{1,0:T(8,128)(2,1)S(1)} %get-tuple-element.46), channel_id=1, source_target_pairs={{0,4},{1,12},{2,20},{3,28},{4,0},{5,8},{6,16},{7,24},{8,5},{9,13},... | collective-permute-start | bytes 393224 | tf_op jit(solution)/shard_map/ppermute | solution.py:366
  (49 other events, 358.0 us)

commit v2 on v0

--- a/solution.py
+++ b/solution.py
@@ -1,8 +1,11 @@
+import functools
 import math
 
 import jax
 import jax.numpy as jnp
 from jax import lax
+from jax.experimental import pallas as pl
+from jax.experimental.pallas import tpu as pltpu
 from jax.sharding import PartitionSpec as P
 
 HEAD_DIM = 128
@@ -33,7 +36,7 @@
     )
 
 
-def per_device(
+def per_device_gathered(
     byte_states,
     byte_patch,
     patch_len,
@@ -162,24 +165,424 @@
     return (residual + mixed_sum).astype(jnp.bfloat16)
 
 
+def dot(left, right):
+    return jnp.dot(left, right, preferred_element_type=jnp.float32)
+
+
+def exchanged(block, axis, distance):
+    route = [(i, i ^ distance) for i in range(lax.axis_size(axis))]
+    return lax.ppermute(block, axis, route)
+
+
+def core_swapped(block):
+    return exchanged(block, "seq", 1)
+
+
+def after(value, *earlier):
+    return lax.optimization_barrier((value, *earlier))[0]
+
+
+def place():
+    seq = lax.axis_index("seq")
+    return seq // 2, lax.rem(seq, 2), lax.axis_index("tensor")
+
+
+def aligned(index, size):
+    return pl.ds(pl.multiple_of(index * size, size), size)
+
+
+def call(kernel, outs, *operands, scratch=(), flops=0):
+    shapes = [jax.ShapeDtypeStruct(shape, dtype) for shape, dtype in outs]
+    moved = sum(o.size * o.dtype.itemsize for o in [*operands, *shapes])
+    return pl.pallas_call(
+        kernel,
+        out_shape=shapes,
+        in_specs=[pl.BlockSpec(memory_space=pltpu.VMEM)] * len(operands),
+        out_specs=[pl.BlockSpec(memory_space=pltpu.VMEM)] * len(outs),
+        scratch_shapes=list(scratch),
+        compiler_params=pltpu.CompilerParams(vmem_limit_bytes=28 * 1024 * 1024),
+        cost_estimate=pl.CostEstimate(flops=flops, bytes_accessed=moved, transcendentals=0),
+    )(*operands)
+
+
+def assemble(pieces, whole):
+    chip, core, _ = place()
+    for n, piece in enumerate(pieces):
+        index = 2 * (chip ^ (n // 2)) + (core ^ (n % 2))
+        whole[aligned(index, piece.shape[0]), :] = piece[...]
+
+
+def query_kernel(count, states, slot_row, lengths, *refs):
+    pieces, query, whole = refs[:count], refs[count], refs[count + 1]
+    slots, byte_count = query.shape[0], states.shape[0]
+    assemble(pieces, whole)
+    index = lax.broadcasted_iota(jnp.int32, (slots, byte_count), 0)
+    onehot = (index == slot_row[...]).astype(jnp.bfloat16)
+    pooled = (dot(onehot, states[...]) / lengths[...]).astype(jnp.bfloat16)
+    query[...] = dot(pooled, whole[...]).astype(jnp.bfloat16)
+
+
+def score_kernel(count, tile, states, slot_row, slot_column, query, *refs):
+    pieces, (raw, totals, whole) = refs[:count], refs[count:]
+    slots, width = query.shape
+    head_count = width // HEAD_DIM
+    assemble(pieces, whole)
+    totals[...] = jnp.zeros_like(totals)
+
+    @pl.loop(0, states.shape[0] // tile)
+    def _(step):
+        span = aligned(step, tile)
+        keys = dot(states[span, :], whole[...]).astype(jnp.bfloat16).astype(jnp.float32)
+        slot = lax.broadcasted_iota(jnp.int32, (tile, slots), 1)
+        onehot = (slot == slot_column[span, :]).astype(jnp.bfloat16)
+        product = dot(onehot, query[...]) * keys
+        lane = lax.broadcasted_iota(jnp.int32, (tile, HEAD_DIM), 1)
+        scores = jnp.zeros((tile, HEAD_DIM), jnp.float32)
+        for head in range(head_count):
+            summed = jnp.sum(
+                product[:, head * HEAD_DIM : (head + 1) * HEAD_DIM], axis=1, keepdims=True
+            )
+            scores = jnp.where(lane == head, summed, scores)
+        values = capped_exp(scores / math.sqrt(HEAD_DIM))
+        raw[span, :] = values
+        high = values.astype(jnp.bfloat16)
+        low = (values - high.astype(jnp.float32)).astype(jnp.bfloat16)
+        index = lax.broadcasted_iota(jnp.int32, (slots, tile), 0)
+        turned = (index == slot_row[:, span]).astype(jnp.bfloat16)
+        totals[...] += dot(turned, high) + dot(turned, low)
+
+
+def value_kernel(tile, states, slot_row, weight, raw, totals, own, above, below, summed):
+    slots = totals.shape[0]
+    spill = above.shape[0]
+    head_count = weight.shape[1] // HEAD_DIM
+    summed[...] = jnp.zeros_like(summed)
+
+    @pl.loop(0, states.shape[0] // tile)
+    def _(step):
+        span = aligned(step, tile)
+        values = dot(states[span, :], weight[...]).astype(jnp.bfloat16).astype(jnp.float32)
+        factors = raw[span, :]
+        weighted = jnp.concatenate(
+            [
+                (values[:, h * HEAD_DIM : (h + 1) * HEAD_DIM] * factors[:, h : h + 1]).astype(
+                    jnp.bfloat16
+                )
+                for h in range(head_count)
+            ],
+            axis=1,
+        )
+        index = lax.broadcasted_iota(jnp.int32, (slots, tile), 0)
+        turned = (index == slot_row[:, span]).astype(jnp.bfloat16)
+        summed[...] += dot(turned, weighted)
+
+    total = totals[...]
+    inverse = 1.0 / jnp.where(total > 0.0, total, 1.0)
+    for h in range(head_count):
+        part = slice(h * HEAD_DIM, (h + 1) * HEAD_DIM)
+        heads = (summed[:, part] * inverse[:, h : h + 1]).astype(jnp.bfloat16)
+        above[:, part] = heads[:spill]
+        own[:, part] = heads[spill : slots - spill]
+        below[:, part] = heads[slots - spill :]
+
+
+def quarters(left, weight, outs):
+    _, _, tensor = place()
+    height = outs[0].shape[0]
+    for r, out in enumerate(outs):
+        block = left[aligned(tensor ^ r, height), :]
+        out[...] = dot(block, weight[...]).astype(out.dtype)
+
+
+def cross_out_kernel(count, weight, *refs):
+    pieces, outs, whole = refs[:count], refs[count:-1], refs[-1]
+    assemble(pieces, whole)
+    quarters(whole, weight, outs)
+
+
+def latent_out_kernel(count, weight, *refs):
+    pieces, outs, whole = refs[:count], refs[count:-1], refs[-1]
+    chip, core, _ = place()
+    for n, piece in enumerate(pieces):
+        index = (count // 2) * (core ^ (n % 2)) + (chip ^ (n // 2))
+        whole[:, aligned(index, HEAD_DIM)] = piece[...]
+    quarters(whole, weight, outs)
+
+
+def project_kernel(rows_own, rows_other, gain, *refs):
+    weights, (stats, *outs), (left, right) = refs[:6], refs[6:-2], refs[-2:]
+    chip, core, _ = place()
+    seq = lax.axis_index("seq")
+    width = rows_own.shape[1]
+    total = jnp.zeros((8, rows_own.shape[0]), jnp.float32)
+    for n, block in enumerate((rows_own, rows_other)):
+        hidden = block[...].astype(jnp.float32)
+        total += lax.dot_general(
+            jnp.ones((8, width), jnp.float32),
+            hidden * hidden,
+            (((1,), (1,)), ((), ())),
+            precision=lax.Precision.HIGHEST,
+            preferred_element_type=jnp.float32,
+        )
+        left[:, n * width : (n + 1) * width] = (
+            hidden * gain[:, aligned(seq ^ n, width)]
+        ).astype(jnp.bfloat16)
+    stats[...] = total
+    for d, out in enumerate(outs):
+        head = len(outs) * core + (chip ^ d)
+        for m in range(3):
+            for n in range(2):
+                right[n * width : (n + 1) * width, m * HEAD_DIM : (m + 1) * HEAD_DIM] = weights[
+                    2 * m + n
+                ][:, aligned(head, HEAD_DIM)]
+        out[...] = dot(left[...], right[...]).astype(out.dtype)
+
+
+def attention_kernel(parts, chips, depth, stats, *refs):
+    shares, attended, (query, key, value) = refs[: parts * chips], refs[-4], refs[-3:]
+    _, _, tensor = place()
+    height = shares[0].shape[0]
+    diagonal = lax.broadcasted_iota(jnp.int32, (height, height), 0) == lax.broadcasted_iota(
+        jnp.int32, (height, height), 1
+    )
+    for r in range(parts):
+        total = shares[r * chips][...]
+        for d in range(1, chips):
+            total += shares[r * chips + d][...].astype(jnp.float32)
+        row = stats[r * 8 : r * 8 + 1, :]
+        column = jnp.sum(jnp.where(diagonal, row, 0.0), axis=1, keepdims=True)
+        total = (total * lax.rsqrt(column / depth + norm_eps)).astype(jnp.bfloat16)
+        span = aligned(tensor ^ r, height)
+        for m, kept in enumerate((query, key, value)):
+            kept[span, :] = total[:, m * HEAD_DIM : (m + 1) * HEAD_DIM]
+    causal = lax.broadcasted_iota(jnp.int32, (height, height), 0) >= lax.broadcasted_iota(
+        jnp.int32, (height, height), 1
+    )
+    for i in range(parts):
+        block = query[i * height : (i + 1) * height, :]
+        numerator = jnp.zeros((height, HEAD_DIM), jnp.float32)
+        denominator = jnp.zeros((height, 1), jnp.float32)
+        for j in range(i + 1):
+            span = slice(j * height, (j + 1) * height)
+            scores = lax.dot_general(
+                block, key[span, :], (((1,), (1,)), ((), ())), preferred_element_type=jnp.float32
+            )
+            raw = capped_exp(scores / math.sqrt(HEAD_DIM))
+            if i == j:
+                raw = jnp.where(causal, raw, 0.0)
+            denominator += jnp.sum(raw, axis=1, keepdims=True)
+            numerator += dot(raw.astype(jnp.bfloat16), value[span, :])
+        attended[i * height : (i + 1) * height, :] = (numerator / denominator).astype(jnp.bfloat16)
+
+
+def final_kernel(own, hidden, *refs):
+    received, outs, whole = refs[:-3], refs[-3:-1], refs[-1]
+    _, core, _ = place()
+    total = own[...] + hidden[...].astype(jnp.float32)
+    for block in received:
+        total += block[...].astype(jnp.float32)
+    whole[...] = total
+    height = outs[0].shape[0]
+    for flip, out in enumerate(outs):
+        out[...] = whole[aligned(core ^ flip, height), :].astype(jnp.bfloat16)
+
+
+def per_device(
+    byte_states,
+    byte_patch,
+    patch_len,
+    cross_query,
+    cross_key,
+    cross_value,
+    cross_out,
+    norm_gain,
+    latent_query,
+    latent_key,
+    latent_value,
+    latent_out,
+):
+    seq = lax.axis_index("seq")
+    core = lax.rem(seq, 2)
+    seq_count = lax.axis_size("seq")
+    tensor_count = lax.axis_size("tensor")
+    chip_count = seq_count // 2
+    patch_count = patch_len.shape[0]
+    patch_dev = patch_count // seq_count
+    spill = patch_dev // 2
+    slot_count = patch_dev + 2 * spill
+    byte_count, byte_width = byte_states.shape
+    local_width = cross_query.shape[1]
+    out_width = cross_out.shape[1]
+    quarter = patch_count // tensor_count
+    bf16, f32 = jnp.bfloat16, jnp.float32
+    tile = min(256, byte_count)
+
+    def over_plane(block):
+        pieces = []
+        for d in range(chip_count):
+            moved = exchanged(block, "seq", 2 * d) if d else block
+            pieces += [moved, core_swapped(moved)]
+        return pieces
+
+    value_weight = lax.all_gather(cross_value, "seq", axis=0, tiled=True)
+    slot_of = byte_patch - (seq * patch_dev - spill)
+    slot_row, slot_column = slot_of[None, :], slot_of[:, None]
+    edge = jnp.ones((spill,), jnp.int32)
+    lengths = lax.dynamic_slice_in_dim(
+        jnp.concatenate([edge, patch_len, edge]), seq * patch_dev, slot_count
+    ).astype(f32)[:, None]
+    query_pieces = over_plane(cross_query)
+    key_pieces = over_plane(cross_key)
+    (query_slots,) = call(
+        functools.partial(query_kernel, seq_count),
+        [((slot_count, local_width), bf16)],
+        byte_states,
+        slot_row,
+        lengths,
+        *query_pieces,
+        scratch=[pltpu.VMEM((byte_width, local_width), bf16)],
+        flops=2 * slot_count * byte_width * (byte_count + local_width),
+    )
+    raw, totals = call(
+        functools.partial(score_kernel, seq_count, tile),
+        [((byte_count, HEAD_DIM), f32), ((slot_count, HEAD_DIM), f32)],
+        byte_states,
+        slot_row,
+        slot_column,
+        query_slots,
+        *key_pieces,
+        scratch=[pltpu.VMEM((byte_width, local_width), bf16)],
+        flops=2 * byte_count * local_width * (byte_width + 2 * slot_count),
+    )
+    weights = []
+    for weight in (latent_query, latent_key, latent_value):
+        weights += [weight, core_swapped(after(weight, query_slots))]
+    raw, *weights = lax.optimization_barrier((raw, *weights))
+    own, above, below = call(
+        functools.partial(value_kernel, tile),
+        [((rows, local_width), bf16) for rows in (patch_dev, spill, spill)],
+        byte_states,
+        slot_row,
+        value_weight,
+        raw,
+        totals,
+        scratch=[pltpu.VMEM((slot_count, local_width), f32)],
+        flops=2 * byte_count * local_width * (byte_width + slot_count),
+    )
+
+    own = own + jnp.concatenate([shifted(below, "seq", 1), shifted(above, "seq", -1)], axis=0)
+
+    total, *sent = call(
+        functools.partial(cross_out_kernel, seq_count),
+        [((quarter, out_width), f32 if r == 0 else bf16) for r in range(tensor_count)],
+        cross_out,
+        *over_plane(own),
+        scratch=[pltpu.VMEM((patch_count, local_width), bf16)],
+        flops=2 * patch_count * local_width * out_width,
+    )
+    for r, block in enumerate(sent, 1):
+        total = total + exchanged(block, "tensor", r).astype(f32)
+    latent_in = total.astype(bf16)
+
+    gain = norm_gain[None, :]
+    blocks = [latent_in]
+    for r in range(1, tensor_count):
+        blocks.append(exchanged(after(latent_in, *blocks[r - 2 : r - 1]), "tensor", r))
+    shares, squares = [], []
+    for block in blocks:
+        square, share, *sent = call(
+            project_kernel,
+            [((8, quarter), f32)]
+            + [((quarter, 3 * HEAD_DIM), f32 if d == 0 else bf16) for d in range(chip_count)],
+            block,
+            core_swapped(block),
+            gain,
+            *weights,
+            scratch=[
+                pltpu.VMEM((quarter, 2 * out_width), bf16),
+                pltpu.VMEM((2 * out_width, 3 * HEAD_DIM), bf16),
+            ],
+            flops=2 * quarter * 2 * out_width * 3 * HEAD_DIM * chip_count,
+        )
+        squares.append(square)
+        shares += [share] + [exchanged(part, "seq", 2 * d) for d, part in enumerate(sent, 1)]
+    squares = jnp.concatenate(squares, axis=0)
+    square_sum = squares
+    for d in range(1, chip_count):
+        square_sum = square_sum + exchanged(squares, "seq", 2 * d)
+    (attended,) = call(
+        functools.partial(attention_kernel, tensor_count, chip_count, out_width * seq_count),
+        [((patch_count, HEAD_DIM), bf16)],
+        square_sum,
+        *shares,
+        scratch=[pltpu.VMEM((patch_count, HEAD_DIM), bf16)] * 3,
+        flops=2 * patch_count * patch_count * HEAD_DIM,
+    )
+
+    total, *sent = call(
+        functools.partial(latent_out_kernel, seq_count),
+        [((quarter, out_width), f32 if r == 0 else bf16) for r in range(tensor_count)],
+        latent_out,
+        *over_plane(attended),
+        scratch=[pltpu.VMEM((patch_count, local_width), bf16)],
+        flops=2 * patch_count * local_width * out_width,
+    )
+    pieces = call(
+        final_kernel,
+        [((patch_dev, out_width), bf16)] * 2,
+        total,
+        latent_in,
+        *[exchanged(block, "tensor", r) for r, block in enumerate(sent, 1)],
+        scratch=[pltpu.VMEM((quarter, out_width), f32)],
+    )
+
+    moved = []
+    for flip in range(2):
+        route = [
+            (s * tensor_count + t, (2 * t + ((s % 2) ^ flip)) * tensor_count + s // 2)
+            for s in range(seq_count)
+            for t in range(tensor_count)
+        ]
+        moved.append(lax.ppermute(pieces[flip], ("seq", "tensor"), route))
+    same, crossed = moved
+    return jnp.concatenate(
+        [jnp.where(core == 0, same, crossed), jnp.where(core == 0, crossed, same)], axis=1
+    )
+
+
+def head_per_device(mesh, heads):
+    seq_count, tensor_count = mesh.shape["seq"], mesh.shape["tensor"]
+    return (
+        heads == seq_count * tensor_count
+        and seq_count == 2 * tensor_count
+        and tensor_count & (tensor_count - 1) == 0
+    )
+
+
 def solution(mesh):
-    return jax.shard_map(
-        per_device,
-        mesh=mesh,
-        in_specs=(
-            P("seq", None),
-            P("seq"),
-            P(),
-            P("seq", "tensor"),
-            P("seq", "tensor"),
-            P("seq", "tensor"),
-            P("tensor", "seq"),
-            P(),
-            P("seq", "tensor"),
-            P("seq", "tensor"),
-            P("seq", "tensor"),
-            P("tensor", "seq"),
-        ),
-        out_specs=P("seq", "tensor"),
-        check_vma=False,
-    )
+    specs = (
+        P("seq", None),
+        P("seq"),
+        P(),
+        P("seq", "tensor"),
+        P("seq", "tensor"),
+        P("seq", "tensor"),
+        P("tensor", "seq"),
+        P(),
+        P("seq", "tensor"),
+        P("seq", "tensor"),
+        P("seq", "tensor"),
+        P("tensor", "seq"),
+    )
+
+    def whole(*arrays):
+        chosen = (
+            per_device
+            if head_per_device(mesh, arrays[3].shape[1] // HEAD_DIM)
+            else per_device_gathered
+        )
+        return jax.shard_map(
+            chosen, mesh=mesh, in_specs=specs, out_specs=P("seq", "tensor"), check_vma=False
+        )(*arrays)
+
+    return whole

time: 507 us -> 273 us (0.54)
  waiting for transfers between devices: 348 us -> 115 us
  blocking collectives: 73.7 us -> 0 us
  starting transfers between devices: 6.13 us -> 76.3 us
  matrix products: 49.7 us -> 0 us
  Pallas kernels: 0 us -> 34.9 us
  local copies, waits for them, and re-layouts: 4.93 us -> 28.1 us
    all_gather x10 -> x1, waiting for transfers between devices: 294 us -> 0.02 us  [per_device(): value_weight = lax.all_gather(cross_value, 'seq', axis=0, tiled=True)]
    ppermute x0 -> x61, waiting for transfers between devices: none -> 110 us  [the longest x59 99.6 us: exchanged(): return lax.ppermute(block, axis, route)]
    psum x1 -> x0, blocking collectives: 73.7 us -> none  [per_device(): latent_in = lax.psum(partial_value, 'tensor').astype(jnp.bfloat16)]
    ppermute x0 -> x61, starting transfers between devices: none -> 71.8 us  [the longest x59 65.8 us: exchanged(): return lax.ppermute(block, axis, route)]
    dot_general x14 -> x0, matrix products: 49.7 us -> none  [the longest x1 6 us: per_device(): jnp.dot(attended, latent_out, preferred_element_type=jnp.float32)]
    reduce_scatter x1 -> x0, waiting for transfers between devices: 39.7 us -> none  [per_device(): lax.psum_scatter(projected, 'tensor', scatter_dimension=1, tiled=True)]
    pallas_call x0 -> x11, Pallas kernels: none -> 34.9 us  [call(): pl.pallas_call(kernel, out_shape=shapes, in_specs=[pl.BlockSpec(memory_sp...]
    unnamed x14 -> x71, local copies, waits for them, and re-layouts: 0.03 us -> 26.2 us
  transfers between devices with their start and end apart: 13 -> 64, of which waited for: 11 -> 28; matrix products, arithmetic and copies ran while one was open for 10% -> 1% of each run, Pallas kernels for 0% -> 9%
where the time goes in v2:
time: 273 us; the launch traced here: 270 us
  waiting for transfers between devices  115 us (42%)
  starting transfers between devices  76.3 us (28%)
  Pallas kernels  34.9 us (13%)
  local copies, waits for them, and re-layouts  28.1 us (10%)
  between operations  13.7 us (5%)
    ppermute x59, waiting for transfers between devices, exchanged(): return lax.ppermute(block, axis, route)  99.6 us
    ppermute x59, starting transfers between devices, exchanged(): return lax.ppermute(block, axis, route)  65.8 us
    pallas_call x11, Pallas kernels, call(): pl.pallas_call(kernel, out_shape=shapes, in_specs=[pl.BlockSpec(memory_sp...  34.9 us
    unnamed x71, local copies, waits for them, and re-layouts  26.2 us
    ppermute x2, waiting for transfers between devices, per_device(): moved.append(lax.ppermute(pieces[flip], ('seq', 'tensor'), route))  10.7 us
    ppermute x2, starting transfers between devices, per_device(): moved.append(lax.ppermute(pieces[flip], ('seq', 'tensor'), route))  5.97 us
  transfers between devices with their start and end apart: 64, of which 28 were waited for; matrix products, arithmetic and copies ran while one was open for 1% of the time, Pallas kernels for 9%

profile of v2, /device:TPU:9, one launch (start us, length us, event | category | flops | bytes accessed | tf_op | source)
XLA Modules:
  0.0 269.5 jit_solution(4529031588833044893)
XLA Ops:
  14.7 4.1 %collective-permute-start.4 = (bf16[128,1024]{1,0:T(8,128)(2,1)S(1)}, bf16[128,1024]{1,0:T(8,128)(2,1)S(1)}, u32[]{:S(2)}, u32[]{:S(2)}) collective-permute-start(bf16[128,1024]{1,0:T(8,128)(2,1)S(1)} %collective-permute-done.3.refs_4_), channel_id=1, source_target_pairs={{0,4},{4,0},{8,12},{12,8},{16,20},{20,16},{24,28},{28,24},{1,5},{5... | collective-permute-start | bytes 786440 | tf_op jit(solution)/shard_map/ppermute | solution.py:174
  21.7 3.4 %collective-permute-start.6 = (bf16[128,1024]{1,0:T(8,128)(2,1)S(1)}, bf16[128,1024]{1,0:T(8,128)(2,1)S(1)}, u32[]{:S(2)}, u32[]{:S(2)}) collective-permute-start(bf16[128,1024]{1,0:T(8,128)(2,1)S(1)} %collective-permute-done.5.refs_6_), channel_id=1, source_target_pairs={{0,4},{4,0},{8,12},{12,8},{16,20},{20,16},{24,28},{28,24},{1,5},{5... | collective-permute-start | bytes 786440 | tf_op jit(solution)/shard_map/ppermute | solution.py:174
  45.5 6.1 %collective-permute-done.12.refs_6_ = bf16[128,1024]{1,0:T(8,128)(2,1)S(1)} collective-permute-done((bf16[128,1024]{1,0:T(8,128)(2,1)S(1)}, bf16[128,1024]{1,0:T(8,128)(2,1)S(1)}, u32[]{:S(2)}, u32[]{:S(2)}) %collective-permute-start.12) | collective-permute-done | bytes 262176 | tf_op jit(solution)/shard_map/ppermute | solution.py:174
  61.6 6.5 %shard_map.119 = (f32[1024,128]{1,0:T(8,128)S(1)}, f32[256,128]{1,0:T(8,128)S(1)}) custom-call(bf16[1024,1024]{1,0:T(8,128)(2,1)S(1)} %copy-done.4, s32[1,1024]{1,0:T(1,128)S(1)} %bitcast.10, s32[1024,1]{1,0:T(8,128)S(1)} %copy-done.6, bf16[256,1024]{1,0:T(8,128)(2,1)S(1)} %copy-done.8, bf16[128,1024]{1,0:T(8,128)(2,1)S(1)} %copy-done.27, ...), custom_call_target="tpu_custom_call" | custom-call | flops 3221225472 | bytes 5382144 | tf_op jit(solution)/shard_map/pallas_call | solution.py:197
  73.1 4.2 %shard_map.120 = (bf16[128,1024]{1,0:T(8,128)(2,1)S(1)}, bf16[64,1024]{1,0:T(8,128)(2,1)S(1)}, bf16[64,1024]{1,0:T(8,128)(2,1)S(1)}) custom-call(bf16[1024,1024]{1,0:T(8,128)(2,1)S(1)} %copy-done.5, s32[1,1024]{1,0:T(1,128)S(1)} %bitcast.11, bf16[1024,1024]{1,0:T(8,128)(2,1)S(1)} %copy-done.23, f32[1024,128]{1,0:T(8,128)S(1)} %copy-done.33, ...), custom_call_target="tpu_custom_call" | custom-call | flops 2684354560 | bytes 5378048 | tf_op jit(solution)/shard_map/pallas_call | solution.py:197
  79.3 2.5 collective-permute-start.18
  81.8 3.8 %collective-permute-done.18 = bf16[64,1024]{1,0:T(8,128)(2,1)S(1)} collective-permute-done((bf16[64,1024]{1,0:T(8,128)(2,1)S(1)}, bf16[64,1024]{1,0:T(8,128)(2,1)S(1)}, u32[]{:S(2)}, u32[]{:S(2)}) %collective-permute-start.18) | collective-permute-done | bytes 131104 | tf_op jit(solution)/shard_map/ppermute | solution.py:22
  85.8 4.4 %collective-permute-start.22 = (bf16[128,1024]{1,0:T(8,128)(2,1)S(1)}, bf16[128,1024]{1,0:T(8,128)(2,1)S(1)}, u32[]{:S(2)}, u32[]{:S(2)}) collective-permute-start(bf16[128,1024]{1,0:T(8,128)(2,1)S(1)} %maximum_add_fusion.refs_0_), channel_id=1, source_target_pairs={{0,16},{4,20},{8,24},{12,28},{16,0},{20,4},{24,8},{28,12},{1,17},{... | collective-permute-start | bytes 786440 | tf_op jit(solution)/shard_map/ppermute | solution.py:174
  90.2 4.5 %collective-permute-done.24.refs_6_ = bf16[128,1024]{1,0:T(8,128)(2,1)S(1)} collective-permute-done((bf16[128,1024]{1,0:T(8,128)(2,1)S(1)}, bf16[128,1024]{1,0:T(8,128)(2,1)S(1)}, u32[]{:S(2)}, u32[]{:S(2)}) %collective-permute-start.24) | collective-permute-done | bytes 262176 | tf_op jit(solution)/shard_map/ppermute | solution.py:174
  94.7 5.4 %collective-permute-done.22.refs_4_ = bf16[128,1024]{1,0:T(8,128)(2,1)S(1)} collective-permute-done((bf16[128,1024]{1,0:T(8,128)(2,1)S(1)}, bf16[128,1024]{1,0:T(8,128)(2,1)S(1)}, u32[]{:S(2)}, u32[]{:S(2)}) %collective-permute-start.22) | collective-permute-done | bytes 262176 | tf_op jit(solution)/shard_map/ppermute | solution.py:174
  107.2 7.9 %collective-permute-done.26 = bf16[256,512]{1,0:T(8,128)(2,1)S(1)} collective-permute-done((bf16[256,512]{1,0:T(8,128)(2,1)S(1)}, bf16[256,512]{1,0:T(8,128)(2,1)S(1)}, u32[]{:S(2)}, u32[]{:S(2)}) %collective-permute-start.26) | collective-permute-done | bytes 262176 | tf_op jit(solution)/shard_map/ppermute | solution.py:174
  115.1 3.7 %collective-permute-done.27 = bf16[256,512]{1,0:T(8,128)(2,1)S(1)} collective-permute-done((bf16[256,512]{1,0:T(8,128)(2,1)S(1)}, bf16[256,512]{1,0:T(8,128)(2,1)S(1)}, u32[]{:S(2)}, u32[]{:S(2)}) %collective-permute-start.27) | collective-permute-done | bytes 262176 | tf_op jit(solution)/shard_map/ppermute | solution.py:174
  118.8 11.1 %collective-permute-done.28 = bf16[256,512]{1,0:T(8,128)(2,1)S(1)} collective-permute-done((bf16[256,512]{1,0:T(8,128)(2,1)S(1)}, bf16[256,512]{1,0:T(8,128)(2,1)S(1)}, u32[]{:S(2)}, u32[]{:S(2)}) %collective-permute-start.28) | collective-permute-done | bytes 262176 | tf_op jit(solution)/shard_map/ppermute | solution.py:174
  131.7 2.7 collective-permute-start.32
  137.7 4.7 %collective-permute-start.31 = (bf16[256,512]{1,0:T(8,128)(2,1)S(1)}, bf16[256,512]{1,0:T(8,128)(2,1)S(1)}, u32[]{:S(2)}, u32[]{:S(2)}) collective-permute-start(bf16[256,512]{1,0:T(8,128)(2,1)S(1)} %collective-permute-done.30.rows_own), channel_id=1, source_target_pairs={{0,4},{4,0},{8,12},{12,8},{16,20},{20,16},{24,28},{28,24},{1,5},{5... | collective-permute-start | bytes 786440 | tf_op jit(solution)/shard_map/ppermute | solution.py:174
  142.4 4.3 %shard_map.122 = (f32[8,256]{1,0:T(8,128)S(1)}, f32[256,384]{1,0:T(8,128)S(1)}, bf16[256,384]{1,0:T(8,128)(2,1)S(1)}, bf16[256,384]{1,0:T(8,128)(2,1)S(1)}, bf16[256,384]{1,0:T(8,128)(2,1)S(1)}) custom-call(bf16[256,512]{1,0:T(8,128)(2,1)S(1)} %add_convert_fusion.rows_own.hidden, bf16[256,512]{1,0:T(8,128)(2,1)S(1)} %collective-permute-done.29.rows_other, ...), custom_call_target="tpu_custom_call" | custom-call | flops 805306368 | bytes 7823360 | tf_op jit(solution)/shard_map/pallas_call | solution.py:197
  147.7 3.6 %collective-permute-done.32.rows_own = bf16[256,512]{1,0:T(8,128)(2,1)S(1)} collective-permute-done((bf16[256,512]{1,0:T(8,128)(2,1)S(1)}, bf16[256,512]{1,0:T(8,128)(2,1)S(1)}, u32[]{:S(2)}, u32[]{:S(2)}) %collective-permute-start.32) | collective-permute-done | bytes 262176 | tf_op jit(solution)/shard_map/ppermute | solution.py:174
  152.5 5.4 %collective-permute-done.34.rows_own = bf16[256,512]{1,0:T(8,128)(2,1)S(1)} collective-permute-done((bf16[256,512]{1,0:T(8,128)(2,1)S(1)}, bf16[256,512]{1,0:T(8,128)(2,1)S(1)}, u32[]{:S(2)}, u32[]{:S(2)}) %collective-permute-start.34) | collective-permute-done | bytes 262176 | tf_op jit(solution)/shard_map/ppermute | solution.py:174
  158.8 4.3 %shard_map.123 = (f32[8,256]{1,0:T(8,128)S(1)}, f32[256,384]{1,0:T(8,128)S(1)}, bf16[256,384]{1,0:T(8,128)(2,1)S(1)}, bf16[256,384]{1,0:T(8,128)(2,1)S(1)}, bf16[256,384]{1,0:T(8,128)(2,1)S(1)}) custom-call(bf16[256,512]{1,0:T(8,128)(2,1)S(1)} %collective-permute-done.30.rows_own, bf16[256,512]{1,0:T(8,128)(2,1)S(1)} %collective-permute-done.31.rows_other, ...), custom_call_target="tpu_custom_call" | custom-call | flops 805306368 | bytes 7823360 | tf_op jit(solution)/shard_map/pallas_call | solution.py:197
  165.4 4.3 %shard_map.124 = (f32[8,256]{1,0:T(8,128)S(1)}, f32[256,384]{1,0:T(8,128)S(1)}, bf16[256,384]{1,0:T(8,128)(2,1)S(1)}, bf16[256,384]{1,0:T(8,128)(2,1)S(1)}, bf16[256,384]{1,0:T(8,128)(2,1)S(1)}) custom-call(bf16[256,512]{1,0:T(8,128)(2,1)S(1)} %collective-permute-done.32.rows_own, bf16[256,512]{1,0:T(8,128)(2,1)S(1)} %collective-permute-done.33.rows_other, ...), custom_call_target="tpu_custom_call" | custom-call | flops 805306368 | bytes 7823360 | tf_op jit(solution)/shard_map/pallas_call | solution.py:197
  172.5 4.3 %shard_map.125 = (f32[8,256]{1,0:T(8,128)S(1)}, f32[256,384]{1,0:T(8,128)S(1)}, bf16[256,384]{1,0:T(8,128)(2,1)S(1)}, bf16[256,384]{1,0:T(8,128)(2,1)S(1)}, bf16[256,384]{1,0:T(8,128)(2,1)S(1)}) custom-call(bf16[256,512]{1,0:T(8,128)(2,1)S(1)} %collective-permute-done.34.rows_own, bf16[256,512]{1,0:T(8,128)(2,1)S(1)} %collective-permute-done.35.rows_other, ...), custom_call_target="tpu_custom_call" | custom-call | flops 805306368 | bytes 7823360 | tf_op jit(solution)/shard_map/pallas_call | solution.py:197
  185.7 3.7 %collective-permute-done.46.refs_10_ = bf16[256,384]{1,0:T(8,128)(2,1)S(1)} collective-permute-done((bf16[256,384]{1,0:T(8,128)(2,1)S(1)}, bf16[256,384]{1,0:T(8,128)(2,1)S(1)}, u32[]{:S(2)}, u32[]{:S(2)}) %collective-permute-start.46) | collective-permute-done | bytes 196640 | tf_op jit(solution)/shard_map/ppermute | solution.py:174
  191.8 7.0 %collective-permute-done.49.refs_14_ = bf16[256,384]{1,0:T(8,128)(2,1)S(1)} collective-permute-done((bf16[256,384]{1,0:T(8,128)(2,1)S(1)}, bf16[256,384]{1,0:T(8,128)(2,1)S(1)}, u32[]{:S(2)}, u32[]{:S(2)}) %collective-permute-start.49) | collective-permute-done | bytes 196640 | tf_op jit(solution)/shard_map/ppermute | solution.py:174
  203.5 2.7 %collective-permute-start.51 = (bf16[1024,128]{1,0:T(8,128)(2,1)S(1)}, bf16[1024,128]{1,0:T(8,128)(2,1)S(1)}, u32[]{:S(2)}, u32[]{:S(2)}) collective-permute-start(bf16[1024,128]{1,0:T(8,128)(2,1)S(1)} %shard_map.126.refs_0_), channel_id=1, source_target_pairs={{0,4},{4,0},{8,12},{12,8},{16,20},{20,16},{24,28},{28,24},{1,5},{5... | collective-permute-start | bytes 786440 | tf_op jit(solution)/shard_map/ppermute | solution.py:174
  207.7 5.1 %collective-permute-start.57 = (bf16[1024,128]{1,0:T(8,128)(2,1)S(1)}, bf16[1024,128]{1,0:T(8,128)(2,1)S(1)}, u32[]{:S(2)}, u32[]{:S(2)}) collective-permute-start(bf16[1024,128]{1,0:T(8,128)(2,1)S(1)} %collective-permute-done.56.refs_6_), channel_id=1, source_target_pairs={{0,4},{4,0},{8,12},{12,8},{16,20},{20,16},{24,28},{28,24},{1,5},{5... | collective-permute-start | bytes 786440 | tf_op jit(solution)/shard_map/ppermute | solution.py:174
  212.8 2.7 %collective-permute-done.54.refs_4_ = bf16[1024,128]{1,0:T(8,128)(2,1)S(1)} collective-permute-done((bf16[1024,128]{1,0:T(8,128)(2,1)S(1)}, bf16[1024,128]{1,0:T(8,128)(2,1)S(1)}, u32[]{:S(2)}, u32[]{:S(2)}) %collective-permute-start.54) | collective-permute-done | bytes 262176 | tf_op jit(solution)/shard_map/ppermute | solution.py:174
  222.2 8.0 %collective-permute-done.58.refs_0_ = bf16[256,512]{1,0:T(8,128)(2,1)S(1)} collective-permute-done((bf16[256,512]{1,0:T(8,128)(2,1)S(1)}, bf16[256,512]{1,0:T(8,128)(2,1)S(1)}, u32[]{:S(2)}, u32[]{:S(2)}) %collective-permute-start.58) | collective-permute-done | bytes 262176 | tf_op jit(solution)/shard_map/ppermute | solution.py:174
  230.2 3.5 %collective-permute-done.59.refs_1_ = bf16[256,512]{1,0:T(8,128)(2,1)S(1)} collective-permute-done((bf16[256,512]{1,0:T(8,128)(2,1)S(1)}, bf16[256,512]{1,0:T(8,128)(2,1)S(1)}, u32[]{:S(2)}, u32[]{:S(2)}) %collective-permute-start.59) | collective-permute-done | bytes 262176 | tf_op jit(solution)/shard_map/ppermute | solution.py:174
  233.8 11.2 %collective-permute-done.60.refs_2_ = bf16[256,512]{1,0:T(8,128)(2,1)S(1)} collective-permute-done((bf16[256,512]{1,0:T(8,128)(2,1)S(1)}, bf16[256,512]{1,0:T(8,128)(2,1)S(1)}, u32[]{:S(2)}, u32[]{:S(2)}) %collective-permute-start.60) | collective-permute-done | bytes 262176 | tf_op jit(solution)/shard_map/ppermute | solution.py:174
  247.1 4.1 %collective-permute-start.62 = (bf16[128,512]{1,0:T(8,128)(2,1)S(1)}, bf16[128,512]{1,0:T(8,128)(2,1)S(1)}, u32[]{:S(2)}, u32[]{:S(2)}) collective-permute-start(bf16[128,512]{1,0:T(8,128)(2,1)S(1)} %get-tuple-element.98), channel_id=1, source_target_pairs={{0,4},{1,12},{2,20},{3,28},{4,0},{5,8},{6,16},{7,24},{8,5},{9,13},... | collective-permute-start | bytes 393224 | tf_op jit(solution)/shard_map/ppermute | solution.py:546
  251.2 7.8 %collective-permute-done.61 = bf16[128,512]{1,0:T(8,128)(2,1)S(1)} collective-permute-done((bf16[128,512]{1,0:T(8,128)(2,1)S(1)}, bf16[128,512]{1,0:T(8,128)(2,1)S(1)}, u32[]{:S(2)}, u32[]{:S(2)}) %collective-permute-start.61) | collective-permute-done | bytes 131104 | tf_op jit(solution)/shard_map/ppermute | solution.py:546
  259.0 3.0 %collective-permute-done.62 = bf16[128,512]{1,0:T(8,128)(2,1)S(1)} collective-permute-done((bf16[128,512]{1,0:T(8,128)(2,1)S(1)}, bf16[128,512]{1,0:T(8,128)(2,1)S(1)}, u32[]{:S(2)}, u32[]{:S(2)}) %collective-permute-start.62) | collective-permute-done | bytes 131104 | tf_op jit(solution)/shard_map/ppermute | solution.py:546
  (191 shorter events, 95.9 us)
Async XLA Ops:
  6.5 62.3 %all-gather.2.cloned.1.call-start = ((), (), s32[]{:S(2)}) async-start(), calls=%async_computation | async-start | bytes 2359296 | tf_op jit(solution)/shard_map/all_gather | solution.py:427
  9.8 11.9 %collective-permute-start.5 = (bf16[128,1024]{1,0:T(8,128)(2,1)}, bf16[128,1024]{1,0:T(8,128)(2,1)S(1)}, u32[]{:S(2)}, u32[]{:S(2)}) collective-permute-start(bf16[128,1024]{1,0:T(8,128)(2,1)} %refs_0_.2), channel_id=1, source_target_pairs={{0,24},{4,28},{8,16},{12,20},{16,8},{20,12},{24,0},{28,4},{1,25},{... | collective-permute-start | bytes 786440 | tf_op jit(solution)/shard_map/ppermute | solution.py:174
  10.0 16.7 %collective-permute-start = (bf16[128,1024]{1,0:T(8,128)(2,1)}, bf16[128,1024]{1,0:T(8,128)(2,1)S(1)}, u32[]{:S(2)}, u32[]{:S(2)}) collective-permute-start(bf16[128,1024]{1,0:T(8,128)(2,1)} %refs_0_.2), channel_id=1, source_target_pairs={{0,4},{4,0},{8,12},{12,8},{16,20},{20,16},{24,28},{28,24},{1,5},{5... | collective-permute-start | bytes 786440 | tf_op jit(solution)/shard_map/ppermute | solution.py:174
  11.5 31.3 %collective-permute-start.10 = (bf16[128,1024]{1,0:T(8,128)(2,1)}, bf16[128,1024]{1,0:T(8,128)(2,1)}, u32[]{:S(2)}, u32[]{:S(2)}) collective-permute-start(bf16[128,1024]{1,0:T(8,128)(2,1)} %refs_0_.3), channel_id=1, source_target_pairs={{0,16},{4,20},{8,24},{12,28},{16,0},{20,4},{24,8},{28,12},{1,17},{... | collective-permute-start | bytes 786440 | tf_op jit(solution)/shard_map/ppermute | solution.py:174
  14.7 14.7 %collective-permute-start.4 = (bf16[128,1024]{1,0:T(8,128)(2,1)S(1)}, bf16[128,1024]{1,0:T(8,128)(2,1)S(1)}, u32[]{:S(2)}, u32[]{:S(2)}) collective-permute-start(bf16[128,1024]{1,0:T(8,128)(2,1)S(1)} %collective-permute-done.3.refs_4_), channel_id=1, source_target_pairs={{0,4},{4,0},{8,12},{12,8},{16,20},{20,16},{24,28},{28,24},{1,5},{5... | collective-permute-start | bytes 786440 | tf_op jit(solution)/shard_map/ppermute | solution.py:174
  27.4 15.6 %collective-permute-start.8 = (bf16[128,1024]{1,0:T(8,128)(2,1)}, bf16[128,1024]{1,0:T(8,128)(2,1)}, u32[]{:S(2)}, u32[]{:S(2)}) collective-permute-start(bf16[128,1024]{1,0:T(8,128)(2,1)} %refs_0_.3), channel_id=1, source_target_pairs={{0,8},{4,12},{8,0},{12,4},{16,24},{20,28},{24,16},{28,20},{1,9},{5... | collective-permute-start | bytes 786440 | tf_op jit(solution)/shard_map/ppermute | solution.py:174
  30.2 14.1 %collective-permute-start.7 = (bf16[128,1024]{1,0:T(8,128)(2,1)}, bf16[128,1024]{1,0:T(8,128)(2,1)S(1)}, u32[]{:S(2)}, u32[]{:S(2)}) collective-permute-start(bf16[128,1024]{1,0:T(8,128)(2,1)} %refs_0_.3), channel_id=1, source_target_pairs={{0,4},{4,0},{8,12},{12,8},{16,20},{20,16},{24,28},{28,24},{1,5},{5... | collective-permute-start | bytes 786440 | tf_op jit(solution)/shard_map/ppermute | solution.py:174
  42.2 26.6 %collective-permute-start.14 = (bf16[512,1024]{1,0:T(8,128)(2,1)S(1)}, bf16[512,1024]{1,0:T(8,128)(2,1)}, u32[]{:S(2)}, u32[]{:S(2)}) collective-permute-start(bf16[512,1024]{1,0:T(8,128)(2,1)S(1)} %copy-done), channel_id=1, source_target_pairs={{0,4},{4,0},{8,12},{12,8},{16,20},{20,16},{24,28},{28,24},{1,5},{5... | collective-permute-start | bytes 3145736 | tf_op jit(solution)/shard_map/ppermute | solution.py:174
  42.5 26.3 %collective-permute-start.15 = (bf16[512,1024]{1,0:T(8,128)(2,1)S(1)}, bf16[512,1024]{1,0:T(8,128)(2,1)}, u32[]{:S(2)}, u32[]{:S(2)}) collective-permute-start(bf16[512,1024]{1,0:T(8,128)(2,1)S(1)} %copy-done.1), channel_id=1, source_target_pairs={{0,4},{4,0},{8,12},{12,8},{16,20},{20,16},{24,28},{28,24},{1,5},{5... | collective-permute-start | bytes 3145736 | tf_op jit(solution)/shard_map/ppermute | solution.py:174
  42.8 26.1 %collective-permute-start.16 = (bf16[512,1024]{1,0:T(8,128)(2,1)S(1)}, bf16[512,1024]{1,0:T(8,128)(2,1)}, u32[]{:S(2)}, u32[]{:S(2)}) collective-permute-start(bf16[512,1024]{1,0:T(8,128)(2,1)S(1)} %copy-done.2), channel_id=1, source_target_pairs={{0,4},{4,0},{8,12},{12,8},{16,20},{20,16},{24,28},{28,24},{1,5},{5... | collective-permute-start | bytes 3145736 | tf_op jit(solution)/shard_map/ppermute | solution.py:174
  85.8 14.3 %collective-permute-start.22 = (bf16[128,1024]{1,0:T(8,128)(2,1)S(1)}, bf16[128,1024]{1,0:T(8,128)(2,1)S(1)}, u32[]{:S(2)}, u32[]{:S(2)}) collective-permute-start(bf16[128,1024]{1,0:T(8,128)(2,1)S(1)} %maximum_add_fusion.refs_0_), channel_id=1, source_target_pairs={{0,16},{4,20},{8,24},{12,28},{16,0},{20,4},{24,8},{28,12},{1,17},{... | collective-permute-start | bytes 786440 | tf_op jit(solution)/shard_map/ppermute | solution.py:174
  104.8 14.0 %collective-permute-start.27 = (bf16[256,512]{1,0:T(8,128)(2,1)S(1)}, bf16[256,512]{1,0:T(8,128)(2,1)S(1)}, u32[]{:S(2)}, u32[]{:S(2)}) collective-permute-start(bf16[256,512]{1,0:T(8,128)(2,1)S(1)} %get-tuple-element.63), channel_id=1, source_target_pairs={{0,2},{1,3},{2,0},{3,1},{4,6},{5,7},{6,4},{7,5},{8,10},{9,11},{10,... | collective-permute-start | bytes 786440 | tf_op jit(solution)/shard_map/ppermute | solution.py:174
  107.1 22.8 %collective-permute-start.28 = (bf16[256,512]{1,0:T(8,128)(2,1)S(1)}, bf16[256,512]{1,0:T(8,128)(2,1)S(1)}, u32[]{:S(2)}, u32[]{:S(2)}) collective-permute-start(bf16[256,512]{1,0:T(8,128)(2,1)S(1)} %get-tuple-element.64), channel_id=1, source_target_pairs={{0,3},{1,2},{2,1},{3,0},{4,7},{5,6},{6,5},{7,4},{8,11},{9,10},{10,... | collective-permute-start | bytes 786440 | tf_op jit(solution)/shard_map/ppermute | solution.py:174
  130.1 12.3 %collective-permute-start.29 = (bf16[256,512]{1,0:T(8,128)(2,1)S(1)}, bf16[256,512]{1,0:T(8,128)(2,1)S(1)}, u32[]{:S(2)}, u32[]{:S(2)}) collective-permute-start(bf16[256,512]{1,0:T(8,128)(2,1)S(1)} %add_convert_fusion.rows_own.hidden), channel_id=1, source_target_pairs={{0,4},{4,0},{8,12},{12,8},{16,20},{20,16},{24,28},{28,24},{1,5},{5... | collective-permute-start | bytes 786440 | tf_op jit(solution)/shard_map/ppermute | solution.py:174
  131.7 19.7 %collective-permute-start.32 = (bf16[256,512]{1,0:T(8,128)(2,1)S(1)}, bf16[256,512]{1,0:T(8,128)(2,1)S(1)}, u32[]{:S(2)}, u32[]{:S(2)}) collective-permute-start(bf16[256,512]{1,0:T(8,128)(2,1)S(1)} %add_convert_fusion.rows_own.hidden), channel_id=1, source_target_pairs={{0,2},{1,3},{2,0},{3,1},{4,6},{5,7},{6,4},{7,5},{8,10},{9,11},{10,... | collective-permute-start | bytes 786440 | tf_op jit(solution)/shard_map/ppermute | solution.py:174
  136.4 21.5 %collective-permute-start.34 = (bf16[256,512]{1,0:T(8,128)(2,1)S(1)}, bf16[256,512]{1,0:T(8,128)(2,1)S(1)}, u32[]{:S(2)}, u32[]{:S(2)}) collective-permute-start(bf16[256,512]{1,0:T(8,128)(2,1)S(1)} %add_convert_fusion.rows_own.hidden), channel_id=1, source_target_pairs={{0,3},{1,2},{2,1},{3,0},{4,7},{5,6},{6,5},{7,4},{8,11},{9,10},{10,... | collective-permute-start | bytes 786440 | tf_op jit(solution)/shard_map/ppermute | solution.py:174
  137.7 20.2 %collective-permute-start.31 = (bf16[256,512]{1,0:T(8,128)(2,1)S(1)}, bf16[256,512]{1,0:T(8,128)(2,1)S(1)}, u32[]{:S(2)}, u32[]{:S(2)}) collective-permute-start(bf16[256,512]{1,0:T(8,128)(2,1)S(1)} %collective-permute-done.30.rows_own), channel_id=1, source_target_pairs={{0,4},{4,0},{8,12},{12,8},{16,20},{20,16},{24,28},{28,24},{1,5},{5... | collective-permute-start | bytes 786440 | tf_op jit(solution)/shard_map/ppermute | solution.py:174
  146.8 23.0 %collective-permute-start.39 = (bf16[256,384]{1,0:T(8,128)(2,1)S(1)}, bf16[256,384]{1,0:T(8,128)(2,1)S(1)}, u32[]{:S(2)}, u32[]{:S(2)}) collective-permute-start(bf16[256,384]{1,0:T(8,128)(2,1)S(1)} %get-tuple-element.78), channel_id=1, source_target_pairs={{0,8},{4,12},{8,0},{12,4},{16,24},{20,28},{24,16},{28,20},{1,9},{5... | collective-permute-start | bytes 589832 | tf_op jit(solution)/shard_map/ppermute | solution.py:174
  147.3 23.1 %collective-permute-start.40 = (bf16[256,384]{1,0:T(8,128)(2,1)S(1)}, bf16[256,384]{1,0:T(8,128)(2,1)S(1)}, u32[]{:S(2)}, u32[]{:S(2)}) collective-permute-start(bf16[256,384]{1,0:T(8,128)(2,1)S(1)} %get-tuple-element.79), channel_id=1, source_target_pairs={{0,16},{4,20},{8,24},{12,28},{16,0},{20,4},{24,8},{28,12},{1,17},{... | collective-permute-start | bytes 589832 | tf_op jit(solution)/shard_map/ppermute | solution.py:174
  151.3 11.8 %collective-permute-start.33 = (bf16[256,512]{1,0:T(8,128)(2,1)S(1)}, bf16[256,512]{1,0:T(8,128)(2,1)S(1)}, u32[]{:S(2)}, u32[]{:S(2)}) collective-permute-start(bf16[256,512]{1,0:T(8,128)(2,1)S(1)} %collective-permute-done.32.rows_own), channel_id=1, source_target_pairs={{0,4},{4,0},{8,12},{12,8},{16,20},{20,16},{24,28},{28,24},{1,5},{5... | collective-permute-start | bytes 786440 | tf_op jit(solution)/shard_map/ppermute | solution.py:174
  157.9 18.9 %collective-permute-start.41 = (bf16[256,384]{1,0:T(8,128)(2,1)S(1)}, bf16[256,384]{1,0:T(8,128)(2,1)S(1)}, u32[]{:S(2)}, u32[]{:S(2)}) collective-permute-start(bf16[256,384]{1,0:T(8,128)(2,1)S(1)} %get-tuple-element.80), channel_id=1, source_target_pairs={{0,24},{4,28},{8,16},{12,20},{16,8},{20,12},{24,0},{28,4},{1,25},{... | collective-permute-start | bytes 589832 | tf_op jit(solution)/shard_map/ppermute | solution.py:174
  157.9 13.1 %collective-permute-start.35 = (bf16[256,512]{1,0:T(8,128)(2,1)S(1)}, bf16[256,512]{1,0:T(8,128)(2,1)S(1)}, u32[]{:S(2)}, u32[]{:S(2)}) collective-permute-start(bf16[256,512]{1,0:T(8,128)(2,1)S(1)} %collective-permute-done.34.rows_own), channel_id=1, source_target_pairs={{0,4},{4,0},{8,12},{12,8},{16,20},{20,16},{24,28},{28,24},{1,5},{5... | collective-permute-start | bytes 786440 | tf_op jit(solution)/shard_map/ppermute | solution.py:174
  163.2 14.8 %collective-permute-start.42 = (bf16[256,384]{1,0:T(8,128)(2,1)S(1)}, bf16[256,384]{1,0:T(8,128)(2,1)S(1)}, u32[]{:S(2)}, u32[]{:S(2)}) collective-permute-start(bf16[256,384]{1,0:T(8,128)(2,1)S(1)} %get-tuple-element.82), channel_id=1, source_target_pairs={{0,8},{4,12},{8,0},{12,4},{16,24},{20,28},{24,16},{28,20},{1,9},{5... | collective-permute-start | bytes 589832 | tf_op jit(solution)/shard_map/ppermute | solution.py:174
  183.4 15.4 %collective-permute-start.49 = (bf16[256,384]{1,0:T(8,128)(2,1)S(1)}, bf16[256,384]{1,0:T(8,128)(2,1)S(1)}, u32[]{:S(2)}, u32[]{:S(2)}) collective-permute-start(bf16[256,384]{1,0:T(8,128)(2,1)S(1)} %get-tuple-element.91), channel_id=1, source_target_pairs={{0,16},{4,20},{8,24},{12,28},{16,0},{20,4},{24,8},{28,12},{1,17},{... | collective-permute-start | bytes 589832 | tf_op jit(solution)/shard_map/ppermute | solution.py:174
  184.2 14.6 %collective-permute-start.50 = (bf16[256,384]{1,0:T(8,128)(2,1)S(1)}, bf16[256,384]{1,0:T(8,128)(2,1)S(1)}, u32[]{:S(2)}, u32[]{:S(2)}) collective-permute-start(bf16[256,384]{1,0:T(8,128)(2,1)S(1)} %get-tuple-element.92), channel_id=1, source_target_pairs={{0,24},{4,28},{8,16},{12,20},{16,8},{20,12},{24,0},{28,4},{1,25},{... | collective-permute-start | bytes 589832 | tf_op jit(solution)/shard_map/ppermute | solution.py:174
  201.9 13.7 %collective-permute-start.54 = (bf16[1024,128]{1,0:T(8,128)(2,1)S(1)}, bf16[1024,128]{1,0:T(8,128)(2,1)S(1)}, u32[]{:S(2)}, u32[]{:S(2)}) collective-permute-start(bf16[1024,128]{1,0:T(8,128)(2,1)S(1)} %shard_map.126.refs_0_), channel_id=1, source_target_pairs={{0,16},{4,20},{8,24},{12,28},{16,0},{20,4},{24,8},{28,12},{1,17},{... | collective-permute-start | bytes 786440 | tf_op jit(solution)/shard_map/ppermute | solution.py:174
  202.9 13.2 %collective-permute-start.52 = (bf16[1024,128]{1,0:T(8,128)(2,1)S(1)}, bf16[1024,128]{1,0:T(8,128)(2,1)S(1)}, u32[]{:S(2)}, u32[]{:S(2)}) collective-permute-start(bf16[1024,128]{1,0:T(8,128)(2,1)S(1)} %shard_map.126.refs_0_), channel_id=1, source_target_pairs={{0,8},{4,12},{8,0},{12,4},{16,24},{20,28},{24,16},{28,20},{1,9},{5... | collective-permute-start | bytes 786440 | tf_op jit(solution)/shard_map/ppermute | solution.py:174
  203.5 12.6 %collective-permute-start.51 = (bf16[1024,128]{1,0:T(8,128)(2,1)S(1)}, bf16[1024,128]{1,0:T(8,128)(2,1)S(1)}, u32[]{:S(2)}, u32[]{:S(2)}) collective-permute-start(bf16[1024,128]{1,0:T(8,128)(2,1)S(1)} %shard_map.126.refs_0_), channel_id=1, source_target_pairs={{0,4},{4,0},{8,12},{12,8},{16,20},{20,16},{24,28},{28,24},{1,5},{5... | collective-permute-start | bytes 786440 | tf_op jit(solution)/shard_map/ppermute | solution.py:174
  219.6 14.1 %collective-permute-start.59 = (bf16[256,512]{1,0:T(8,128)(2,1)S(1)}, bf16[256,512]{1,0:T(8,128)(2,1)S(1)}, u32[]{:S(2)}, u32[]{:S(2)}) collective-permute-start(bf16[256,512]{1,0:T(8,128)(2,1)S(1)} %get-tuple-element.95), channel_id=1, source_target_pairs={{0,2},{1,3},{2,0},{3,1},{4,6},{5,7},{6,4},{7,5},{8,10},{9,11},{10,... | collective-permute-start | bytes 786440 | tf_op jit(solution)/shard_map/ppermute | solution.py:174
  222.0 22.9 %collective-permute-start.60 = (bf16[256,512]{1,0:T(8,128)(2,1)S(1)}, bf16[256,512]{1,0:T(8,128)(2,1)S(1)}, u32[]{:S(2)}, u32[]{:S(2)}) collective-permute-start(bf16[256,512]{1,0:T(8,128)(2,1)S(1)} %get-tuple-element.96), channel_id=1, source_target_pairs={{0,3},{1,2},{2,1},{3,0},{4,7},{5,6},{6,5},{7,4},{8,11},{9,10},{10,... | collective-permute-start | bytes 786440 | tf_op jit(solution)/shard_map/ppermute | solution.py:174
  245.2 13.8 %collective-permute-start.61 = (bf16[128,512]{1,0:T(8,128)(2,1)S(1)}, bf16[128,512]{1,0:T(8,128)(2,1)S(1)}, u32[]{:S(2)}, u32[]{:S(2)}) collective-permute-start(bf16[128,512]{1,0:T(8,128)(2,1)S(1)} %get-tuple-element.97), channel_id=1, source_target_pairs={{0,0},{1,8},{2,16},{3,24},{4,4},{5,12},{6,20},{7,28},{8,1},{9,9},{... | collective-permute-start | bytes 393224 | tf_op jit(solution)/shard_map/ppermute | solution.py:546
  247.1 14.8 %collective-permute-start.62 = (bf16[128,512]{1,0:T(8,128)(2,1)S(1)}, bf16[128,512]{1,0:T(8,128)(2,1)S(1)}, u32[]{:S(2)}, u32[]{:S(2)}) collective-permute-start(bf16[128,512]{1,0:T(8,128)(2,1)S(1)} %get-tuple-element.98), channel_id=1, source_target_pairs={{0,4},{1,12},{2,20},{3,28},{4,0},{5,8},{6,16},{7,24},{8,5},{9,13},... | collective-permute-start | bytes 393224 | tf_op jit(solution)/shard_map/ppermute | solution.py:546
  (66 other events, 373.2 us)
Sparse Core Ops, SparseCore 0:
  9.2 36.1 all-gather.1

commit v3 on v2

--- a/solution.py
+++ b/solution.py
@@ -191,13 +191,24 @@
     return pl.ds(pl.multiple_of(index * size, size), size)
 
 
-def call(kernel, outs, *operands, scratch=(), flops=0):
+def fetched(pairs, semaphores):
+    copies = [
+        pltpu.make_async_copy(source, target, semaphores.at[n])
+        for n, (source, target) in enumerate(pairs)
+    ]
+    for copy in copies:
+        copy.start()
+    return copies
+
+
+def call(kernel, outs, *operands, far=0, scratch=(), flops=0):
     shapes = [jax.ShapeDtypeStruct(shape, dtype) for shape, dtype in outs]
     moved = sum(o.size * o.dtype.itemsize for o in [*operands, *shapes])
     return pl.pallas_call(
         kernel,
         out_shape=shapes,
-        in_specs=[pl.BlockSpec(memory_space=pltpu.VMEM)] * len(operands),
+        in_specs=[pl.BlockSpec(memory_space=pltpu.VMEM)] * (len(operands) - far)
+        + [pl.BlockSpec(memory_space=pl.ANY)] * far,
         out_specs=[pl.BlockSpec(memory_space=pltpu.VMEM)] * len(outs),
         scratch_shapes=list(scratch),
         compiler_params=pltpu.CompilerParams(vmem_limit_bytes=28 * 1024 * 1024),
@@ -212,30 +223,45 @@
         whole[aligned(index, piece.shape[0]), :] = piece[...]
 
 
-def query_kernel(count, states, slot_row, lengths, *refs):
-    pieces, query, whole = refs[:count], refs[count], refs[count + 1]
+def plane_rows(pieces, whole):
+    chip, core, _ = place()
+    return [
+        (piece, whole.at[aligned(2 * (chip ^ (n // 2)) + (core ^ (n % 2)), piece.shape[0]), :])
+        for n, piece in enumerate(pieces)
+    ]
+
+
+def query_kernel(count, slot_row, lengths, states, *refs):
+    pieces, (query, held, whole, semaphores) = refs[:count], refs[count:]
     slots, byte_count = query.shape[0], states.shape[0]
-    assemble(pieces, whole)
+    copies = fetched([(states, held), *plane_rows(pieces, whole)], semaphores)
     index = lax.broadcasted_iota(jnp.int32, (slots, byte_count), 0)
     onehot = (index == slot_row[...]).astype(jnp.bfloat16)
-    pooled = (dot(onehot, states[...]) / lengths[...]).astype(jnp.bfloat16)
+    copies[0].wait()
+    pooled = (dot(onehot, held[...]) / lengths[...]).astype(jnp.bfloat16)
+    for copy in copies[1:]:
+        copy.wait()
     query[...] = dot(pooled, whole[...]).astype(jnp.bfloat16)
 
 
-def score_kernel(count, tile, states, slot_row, slot_column, query, *refs):
-    pieces, (raw, totals, whole) = refs[:count], refs[count:]
+def score_kernel(count, tile, slot_row, query, states, *refs):
+    pieces, (raw, totals, held, whole, semaphores) = refs[:count], refs[count:]
     slots, width = query.shape
     head_count = width // HEAD_DIM
-    assemble(pieces, whole)
+    copies = fetched([(states, held), *plane_rows(pieces, whole)], semaphores)
     totals[...] = jnp.zeros_like(totals)
+    for copy in copies:
+        copy.wait()
 
     @pl.loop(0, states.shape[0] // tile)
     def _(step):
         span = aligned(step, tile)
-        keys = dot(states[span, :], whole[...]).astype(jnp.bfloat16).astype(jnp.float32)
-        slot = lax.broadcasted_iota(jnp.int32, (tile, slots), 1)
-        onehot = (slot == slot_column[span, :]).astype(jnp.bfloat16)
-        product = dot(onehot, query[...]) * keys
+        keys = dot(held[span, :], whole[...]).astype(jnp.bfloat16).astype(jnp.float32)
+        index = lax.broadcasted_iota(jnp.int32, (slots, tile), 0)
+        turned = (index == slot_row[:, span]).astype(jnp.bfloat16)
+        product = keys * lax.dot_general(
+            turned, query[...], (((0,), (0,)), ((), ())), preferred_element_type=jnp.float32
+        )
         lane = lax.broadcasted_iota(jnp.int32, (tile, HEAD_DIM), 1)
         scores = jnp.zeros((tile, HEAD_DIM), jnp.float32)
         for head in range(head_count):
@@ -247,21 +273,23 @@
         raw[span, :] = values
         high = values.astype(jnp.bfloat16)
         low = (values - high.astype(jnp.float32)).astype(jnp.bfloat16)
-        index = lax.broadcasted_iota(jnp.int32, (slots, tile), 0)
-        turned = (index == slot_row[:, span]).astype(jnp.bfloat16)
         totals[...] += dot(turned, high) + dot(turned, low)
 
 
-def value_kernel(tile, states, slot_row, weight, raw, totals, own, above, below, summed):
+def value_kernel(tile, slot_row, raw, totals, states, weight, *refs):
+    own, above, below, held, whole, summed, semaphores = refs
     slots = totals.shape[0]
+    copies = fetched([(states, held), (weight, whole)], semaphores)
     spill = above.shape[0]
     head_count = weight.shape[1] // HEAD_DIM
     summed[...] = jnp.zeros_like(summed)
+    for copy in copies:
+        copy.wait()
 
     @pl.loop(0, states.shape[0] // tile)
     def _(step):
         span = aligned(step, tile)
-        values = dot(states[span, :], weight[...]).astype(jnp.bfloat16).astype(jnp.float32)
+        values = dot(held[span, :], whole[...]).astype(jnp.bfloat16).astype(jnp.float32)
         factors = raw[span, :]
         weighted = jnp.concatenate(
             [
@@ -309,48 +337,71 @@
     quarters(whole, weight, outs)
 
 
+def arrange_kernel(*refs):
+    weights, outs, semaphores = refs[:6], refs[6:-1], refs[-1]
+    chip, core, _ = place()
+    height = weights[0].shape[0]
+    copies = fetched(
+        [
+            (
+                weights[2 * m + n].at[:, aligned(len(outs) * core + (chip ^ d), HEAD_DIM)],
+                out.at[n * height : (n + 1) * height, m * HEAD_DIM : (m + 1) * HEAD_DIM],
+            )
+            for d, out in enumerate(outs)
+            for m in range(3)
+            for n in range(2)
+        ],
+        semaphores,
+    )
+    for copy in copies:
+        copy.wait()
+
+
+def diagonal(size):
+    return lax.broadcasted_iota(jnp.int32, (size, size), 0) == lax.broadcasted_iota(
+        jnp.int32, (size, size), 1
+    )
+
+
 def project_kernel(rows_own, rows_other, gain, *refs):
-    weights, (stats, *outs), (left, right) = refs[:6], refs[6:-2], refs[-2:]
-    chip, core, _ = place()
+    chips = (len(refs) - 1) // 2
+    weights, outs, left = refs[:chips], refs[chips:-1], refs[-1]
     seq = lax.axis_index("seq")
-    width = rows_own.shape[1]
-    total = jnp.zeros((8, rows_own.shape[0]), jnp.float32)
+    height, width = rows_own.shape
+    total = jnp.zeros((height, 1), jnp.float32)
     for n, block in enumerate((rows_own, rows_other)):
         hidden = block[...].astype(jnp.float32)
-        total += lax.dot_general(
-            jnp.ones((8, width), jnp.float32),
-            hidden * hidden,
-            (((1,), (1,)), ((), ())),
-            precision=lax.Precision.HIGHEST,
-            preferred_element_type=jnp.float32,
-        )
+        total += jnp.sum(hidden * hidden, axis=1, keepdims=True)
         left[:, n * width : (n + 1) * width] = (
             hidden * gain[:, aligned(seq ^ n, width)]
         ).astype(jnp.bfloat16)
-    stats[...] = total
-    for d, out in enumerate(outs):
-        head = len(outs) * core + (chip ^ d)
-        for m in range(3):
-            for n in range(2):
-                right[n * width : (n + 1) * width, m * HEAD_DIM : (m + 1) * HEAD_DIM] = weights[
-                    2 * m + n
-                ][:, aligned(head, HEAD_DIM)]
-        out[...] = dot(left[...], right[...]).astype(out.dtype)
-
-
-def attention_kernel(parts, chips, depth, stats, *refs):
+    for weight, out in reversed(list(zip(weights, outs))):
+        out[:height, :] = dot(left[...], weight[...]).astype(out.dtype)
+    row = jnp.sum(jnp.where(diagonal(height), total, 0.0), axis=0, keepdims=True)
+    outs[0][height:, :height] = jnp.broadcast_to(row, (outs[0].shape[0] - height, height))
+    high = row.astype(jnp.bfloat16).astype(jnp.float32)
+    middle = (row - high).astype(jnp.bfloat16).astype(jnp.float32)
+    low = row - high - middle
+    index = lax.broadcasted_iota(jnp.int32, (outs[1].shape[0] - height, height), 0)
+    terms = jnp.where(index == 0, high, jnp.where(index == 1, middle, low)).astype(jnp.bfloat16)
+    for out in outs[1:]:
+        out[height:, :height] = terms
+
+
+def attention_kernel(parts, chips, depth, *refs):
     shares, attended, (query, key, value) = refs[: parts * chips], refs[-4], refs[-3:]
     _, _, tensor = place()
-    height = shares[0].shape[0]
-    diagonal = lax.broadcasted_iota(jnp.int32, (height, height), 0) == lax.broadcasted_iota(
-        jnp.int32, (height, height), 1
-    )
+    height = attended.shape[0] // parts
+    own_place = diagonal(height)
     for r in range(parts):
-        total = shares[r * chips][...]
+        total = shares[r * chips][:height, :]
+        row = shares[r * chips][height : height + 1, :height]
         for d in range(1, chips):
-            total += shares[r * chips + d][...].astype(jnp.float32)
-        row = stats[r * 8 : r * 8 + 1, :]
-        column = jnp.sum(jnp.where(diagonal, row, 0.0), axis=1, keepdims=True)
+            share = shares[r * chips + d]
+            total += share[:height, :].astype(jnp.float32)
+            terms = share[height:, :height].astype(jnp.float32)
+            row += terms[0:1] + terms[1:2] + terms[2:3]
+        column = jnp.sum(jnp.where(own_place, row, 0.0), axis=1, keepdims=True)
         total = (total * lax.rsqrt(column / depth + norm_eps)).astype(jnp.bfloat16)
         span = aligned(tensor ^ r, height)
         for m, kept in enumerate((query, key, value)):
@@ -426,7 +477,7 @@
 
     value_weight = lax.all_gather(cross_value, "seq", axis=0, tiled=True)
     slot_of = byte_patch - (seq * patch_dev - spill)
-    slot_row, slot_column = slot_of[None, :], slot_of[:, None]
+    slot_row = slot_of[None, :]
     edge = jnp.ones((spill,), jnp.int32)
     lengths = lax.dynamic_slice_in_dim(
         jnp.concatenate([edge, patch_len, edge]), seq * patch_dev, slot_count
@@ -436,37 +487,59 @@
     (query_slots,) = call(
         functools.partial(query_kernel, seq_count),
         [((slot_count, local_width), bf16)],
-        byte_states,
         slot_row,
         lengths,
+        byte_states,
         *query_pieces,
-        scratch=[pltpu.VMEM((byte_width, local_width), bf16)],
+        far=1 + seq_count,
+        scratch=[
+            pltpu.VMEM((byte_count, byte_width), bf16),
+            pltpu.VMEM((byte_width, local_width), bf16),
+            pltpu.SemaphoreType.DMA((1 + seq_count,)),
+        ],
         flops=2 * slot_count * byte_width * (byte_count + local_width),
     )
     raw, totals = call(
         functools.partial(score_kernel, seq_count, tile),
         [((byte_count, HEAD_DIM), f32), ((slot_count, HEAD_DIM), f32)],
+        slot_row,
+        query_slots,
         byte_states,
-        slot_row,
-        slot_column,
-        query_slots,
         *key_pieces,
-        scratch=[pltpu.VMEM((byte_width, local_width), bf16)],
+        far=1 + seq_count,
+        scratch=[
+            pltpu.VMEM((byte_count, byte_width), bf16),
+            pltpu.VMEM((byte_width, local_width), bf16),
+            pltpu.SemaphoreType.DMA((1 + seq_count,)),
+        ],
         flops=2 * byte_count * local_width * (byte_width + 2 * slot_count),
     )
     weights = []
     for weight in (latent_query, latent_key, latent_value):
         weights += [weight, core_swapped(after(weight, query_slots))]
-    raw, *weights = lax.optimization_barrier((raw, *weights))
+    head_weights = call(
+        arrange_kernel,
+        [((2 * out_width, 3 * HEAD_DIM), bf16)] * chip_count,
+        *weights,
+        far=6,
+        scratch=[pltpu.SemaphoreType.DMA((6 * chip_count,))],
+    )
+    raw, *head_weights = lax.optimization_barrier((raw, *head_weights))
     own, above, below = call(
         functools.partial(value_kernel, tile),
         [((rows, local_width), bf16) for rows in (patch_dev, spill, spill)],
-        byte_states,
         slot_row,
-        value_weight,
         raw,
         totals,
-        scratch=[pltpu.VMEM((slot_count, local_width), f32)],
+        byte_states,
+        value_weight,
+        far=2,
+        scratch=[
+            pltpu.VMEM((byte_count, byte_width), bf16),
+            pltpu.VMEM((byte_width, local_width), bf16),
+            pltpu.VMEM((slot_count, local_width), f32),
+            pltpu.SemaphoreType.DMA((2,)),
+        ],
         flops=2 * byte_count * local_width * (byte_width + slot_count),
     )
 
@@ -485,35 +558,32 @@
     latent_in = total.astype(bf16)
 
     gain = norm_gain[None, :]
-    blocks = [latent_in]
-    for r in range(1, tensor_count):
-        blocks.append(exchanged(after(latent_in, *blocks[r - 2 : r - 1]), "tensor", r))
-    shares, squares = [], []
-    for block in blocks:
-        square, share, *sent = call(
+    shares, blocks = [], [latent_in]
+    for r in range(tensor_count):
+        if r == 1:
+            near = [exchanged(latent_in, "tensor", d) for d in (1, 2)]
+            blocks += [after(block, shares[0]) for block in near]
+        elif r > 2:
+            earlier = shares[: (r - 2) * chip_count]
+            blocks.append(exchanged(after(latent_in, blocks[r - 2], *earlier), "tensor", r))
+        swapped = core_swapped(blocks[r])
+        if r > 2:
+            blocks[r] = after(blocks[r], *shares[(r - 2) * chip_count :])
+        share, *sent = call(
             project_kernel,
-            [((8, quarter), f32)]
-            + [((quarter, 3 * HEAD_DIM), f32 if d == 0 else bf16) for d in range(chip_count)],
-            block,
-            core_swapped(block),
+            [((quarter + 8, 3 * HEAD_DIM), f32)]
+            + [((quarter + 16, 3 * HEAD_DIM), bf16)] * (chip_count - 1),
+            blocks[r],
+            swapped,
             gain,
-            *weights,
-            scratch=[
-                pltpu.VMEM((quarter, 2 * out_width), bf16),
-                pltpu.VMEM((2 * out_width, 3 * HEAD_DIM), bf16),
-            ],
+            *head_weights,
+            scratch=[pltpu.VMEM((quarter, 2 * out_width), bf16)],
             flops=2 * quarter * 2 * out_width * 3 * HEAD_DIM * chip_count,
         )
-        squares.append(square)
         shares += [share] + [exchanged(part, "seq", 2 * d) for d, part in enumerate(sent, 1)]
-    squares = jnp.concatenate(squares, axis=0)
-    square_sum = squares
-    for d in range(1, chip_count):
-        square_sum = square_sum + exchanged(squares, "seq", 2 * d)
     (attended,) = call(
         functools.partial(attention_kernel, tensor_count, chip_count, out_width * seq_count),
         [((patch_count, HEAD_DIM), bf16)],
-        square_sum,
         *shares,
         scratch=[pltpu.VMEM((patch_count, HEAD_DIM), bf16)] * 3,
         flops=2 * patch_count * patch_count * HEAD_DIM,

time: 273 us -> 249 us (0.912)
  local copies, waits for them, and re-layouts: 28.1 us -> 7.7 us
  Pallas kernels: 34.9 us -> 23.7 us
  waiting for transfers between devices: 115 us -> 120 us
  starting transfers between devices: 76.3 us -> 80 us
    unnamed x71 -> x28, local copies, waits for them, and re-layouts: 26.2 us -> 6.8 us
    pallas_call x11 -> x12, Pallas kernels: 34.9 us -> 23.7 us  [call(): pl.pallas_call(kernel, out_shape=shapes, in_specs=[pl.BlockSpec(memory_sp...]
    ppermute x59 -> x56, waiting for transfers between devices: 99.6 us -> 104 us  [exchanged(): return lax.ppermute(block, axis, route)]
    ppermute x59 -> x56, starting transfers between devices: 65.8 us -> 69.5 us  [exchanged(): return lax.ppermute(block, axis, route)]
  transfers between devices with their start and end apart: 64 -> 61, of which waited for: 28 -> 29; matrix products, arithmetic and copies ran while one was open for 1% -> 1% of each run, Pallas kernels for 9% -> 5%
where the time goes in v3:
time: 249 us; the launch traced here: 246 us
  waiting for transfers between devices  120 us (48%)
  starting transfers between devices  80 us (32%)
  Pallas kernels  23.7 us (10%)
  between operations  13.7 us (6%)
  local copies, waits for them, and re-layouts  7.7 us (3%)
    ppermute x56, waiting for transfers between devices, exchanged(): return lax.ppermute(block, axis, route)  104 us
    ppermute x56, starting transfers between devices, exchanged(): return lax.ppermute(block, axis, route)  69.5 us
    pallas_call x12, Pallas kernels, call(): pl.pallas_call(kernel, out_shape=shapes, in_specs=[pl.BlockSpec(memory_sp...  23.7 us
    ppermute x2, waiting for transfers between devices, per_device(): moved.append(lax.ppermute(pieces[flip], ('seq', 'tensor'), route))  11.7 us
    unnamed x28, local copies, waits for them, and re-layouts  6.8 us
    ppermute x2, starting transfers between devices, per_device(): moved.append(lax.ppermute(pieces[flip], ('seq', 'tensor'), route))  5.97 us
  transfers between devices with their start and end apart: 61, of which 29 were waited for; matrix products, arithmetic and copies ran while one was open for 1% of the time, Pallas kernels for 5%

profile of v3, /device:TPU:9, one launch (start us, length us, event | category | flops | bytes accessed | tf_op | source)
XLA Modules:
  0.0 246.5 jit_solution(6666777661290411986)
XLA Ops:
  14.7 2.7 %collective-permute-start.2 = (bf16[128,1024]{1,0:T(8,128)(2,1)S(1)}, bf16[128,1024]{1,0:T(8,128)(2,1)S(1)}, u32[]{:S(2)}, u32[]{:S(2)}) collective-permute-start(bf16[128,1024]{1,0:T(8,128)(2,1)S(1)} %collective-permute-done.1.refs_2_), channel_id=1, source_target_pairs={{0,4},{4,0},{8,12},{12,8},{16,20},{20,16},{24,28},{28,24},{1,5},{5... | collective-permute-start | bytes 786440 | tf_op jit(solution)/shard_map/ppermute | solution.py:174
  17.4 8.8 %collective-permute-start.4 = (bf16[128,1024]{1,0:T(8,128)(2,1)S(1)}, bf16[128,1024]{1,0:T(8,128)(2,1)S(1)}, u32[]{:S(2)}, u32[]{:S(2)}) collective-permute-start(bf16[128,1024]{1,0:T(8,128)(2,1)S(1)} %collective-permute-done.3.refs_4_), channel_id=1, source_target_pairs={{0,4},{4,0},{8,12},{12,8},{16,20},{20,16},{24,28},{28,24},{1,5},{5... | collective-permute-start | bytes 786440 | tf_op jit(solution)/shard_map/ppermute | solution.py:174
  28.2 2.2 collective-permute-start.8
  38.4 9.4 %collective-permute-done.8.refs_2_ = bf16[128,1024]{1,0:T(8,128)(2,1)S(1)} collective-permute-done((bf16[128,1024]{1,0:T(8,128)(2,1)}, bf16[128,1024]{1,0:T(8,128)(2,1)S(1)}, u32[]{:S(2)}, u32[]{:S(2)}) %collective-permute-start.8) | collective-permute-done | bytes 262176 | tf_op jit(solution)/shard_map/ppermute | solution.py:174
  51.8 5.5 %shard_map.119 = (f32[1024,128]{1,0:T(8,128)S(1)}, f32[256,128]{1,0:T(8,128)S(1)}) custom-call(s32[1,1024]{1,0:T(1,128)S(1)} %bitcast.8, bf16[256,1024]{1,0:T(8,128)(2,1)S(1)} %shard_map.118.query, bf16[1024,1024]{1,0:T(8,128)(2,1)S(1)} %copy-done.1, bf16[128,1024]{1,0:T(8,128)(2,1)S(1)} %copy-done.11, bf16[128,1024]{1,0:T(8,128)(2,1)S(1)} %collective-permute-done.7.refs_1_, ...), custom_call_target="tpu_custom_call" | custom-call | flops 3221225472 | bytes 5378048 | tf_op jit(solution)/shard_map/pallas_call | solution.py:207
  62.8 4.5 %shard_map.121 = (bf16[128,1024]{1,0:T(8,128)(2,1)S(1)}, bf16[64,1024]{1,0:T(8,128)(2,1)S(1)}, bf16[64,1024]{1,0:T(8,128)(2,1)S(1)}) custom-call(s32[1,1024]{1,0:T(1,128)S(1)} %bitcast.9, f32[1024,128]{1,0:T(8,128)S(1)} %copy-done.13, f32[256,128]{1,0:T(8,128)S(1)} %get-tuple-element.61.totals, bf16[1024,1024]{1,0:T(8,128)(2,1)S(1)} %copy-done.2, ...), custom_call_target="tpu_custom_call" | custom-call | flops 2684354560 | bytes 5378048 | tf_op jit(solution)/shard_map/pallas_call | solution.py:207
  69.2 2.6 %collective-permute-start.18 = (bf16[64,1024]{1,0:T(8,128)(2,1)S(1)}, bf16[64,1024]{1,0:T(8,128)(2,1)S(1)}, u32[]{:S(2)}, u32[]{:S(2)}) collective-permute-start(bf16[64,1024]{1,0:T(8,128)(2,1)S(1)} %get-tuple-element.64), channel_id=1, source_target_pairs={{4,0},{8,4},{12,8},{16,12},{20,16},{24,20},{28,24},{5,1},{9,5},{13... | collective-permute-start | bytes 393224 | tf_op jit(solution)/shard_map/ppermute | solution.py:22
  71.8 3.7 %collective-permute-done.18 = bf16[64,1024]{1,0:T(8,128)(2,1)S(1)} collective-permute-done((bf16[64,1024]{1,0:T(8,128)(2,1)S(1)}, bf16[64,1024]{1,0:T(8,128)(2,1)S(1)}, u32[]{:S(2)}, u32[]{:S(2)}) %collective-permute-start.18) | collective-permute-done | bytes 131104 | tf_op jit(solution)/shard_map/ppermute | solution.py:22
  78.6 5.4 %collective-permute-done.20.refs_2_ = bf16[128,1024]{1,0:T(8,128)(2,1)S(1)} collective-permute-done((bf16[128,1024]{1,0:T(8,128)(2,1)S(1)}, bf16[128,1024]{1,0:T(8,128)(2,1)S(1)}, u32[]{:S(2)}, u32[]{:S(2)}) %collective-permute-start.20) | collective-permute-done | bytes 262176 | tf_op jit(solution)/shard_map/ppermute | solution.py:174
  84.0 6.0 %collective-permute-done.22.refs_4_ = bf16[128,1024]{1,0:T(8,128)(2,1)S(1)} collective-permute-done((bf16[128,1024]{1,0:T(8,128)(2,1)S(1)}, bf16[128,1024]{1,0:T(8,128)(2,1)S(1)}, u32[]{:S(2)}, u32[]{:S(2)}) %collective-permute-start.22) | collective-permute-done | bytes 262176 | tf_op jit(solution)/shard_map/ppermute | solution.py:174
  93.8 2.1 collective-permute-start.27
  96.0 8.4 %collective-permute-done.26 = bf16[256,512]{1,0:T(8,128)(2,1)S(1)} collective-permute-done((bf16[256,512]{1,0:T(8,128)(2,1)S(1)}, bf16[256,512]{1,0:T(8,128)(2,1)S(1)}, u32[]{:S(2)}, u32[]{:S(2)}) %collective-permute-start.26) | collective-permute-done | bytes 262176 | tf_op jit(solution)/shard_map/ppermute | solution.py:174
  104.5 3.3 %collective-permute-done.27 = bf16[256,512]{1,0:T(8,128)(2,1)S(1)} collective-permute-done((bf16[256,512]{1,0:T(8,128)(2,1)S(1)}, bf16[256,512]{1,0:T(8,128)(2,1)S(1)}, u32[]{:S(2)}, u32[]{:S(2)}) %collective-permute-start.27) | collective-permute-done | bytes 262176 | tf_op jit(solution)/shard_map/ppermute | solution.py:174
  107.8 11.1 %collective-permute-done.28 = bf16[256,512]{1,0:T(8,128)(2,1)S(1)} collective-permute-done((bf16[256,512]{1,0:T(8,128)(2,1)S(1)}, bf16[256,512]{1,0:T(8,128)(2,1)S(1)}, u32[]{:S(2)}, u32[]{:S(2)}) %collective-permute-start.28) | collective-permute-done | bytes 262176 | tf_op jit(solution)/shard_map/ppermute | solution.py:174
  120.4 2.5 %collective-permute-start.33 = (bf16[256,512]{1,0:T(8,128)(2,1)S(1)}, bf16[256,512]{1,0:T(8,128)(2,1)S(1)}, u32[]{:S(2)}, u32[]{:S(2)}) collective-permute-start(bf16[256,512]{1,0:T(8,128)(2,1)S(1)} %add_convert_fusion.rows_own.hidden), channel_id=1, source_target_pairs={{0,1},{1,0},{2,3},{3,2},{4,5},{5,4},{6,7},{7,6},{8,9},{9,8},{10,11... | collective-permute-start | bytes 786440 | tf_op jit(solution)/shard_map/ppermute | solution.py:174
  126.9 5.0 %collective-permute-done.38.rows_own = bf16[256,512]{1,0:T(8,128)(2,1)S(1)} collective-permute-done((bf16[256,512]{1,0:T(8,128)(2,1)S(1)}, bf16[256,512]{1,0:T(8,128)(2,1)S(1)}, u32[]{:S(2)}, u32[]{:S(2)}) %collective-permute-start.38) | collective-permute-done | bytes 262176 | tf_op jit(solution)/shard_map/ppermute | solution.py:174
  132.6 2.4 collective-permute-done.33.rows_own
  141.0 6.3 %collective-permute-done.43.rows_own = bf16[256,512]{1,0:T(8,128)(2,1)S(1)} collective-permute-done((bf16[256,512]{1,0:T(8,128)(2,1)S(1)}, bf16[256,512]{1,0:T(8,128)(2,1)S(1)}, u32[]{:S(2)}, u32[]{:S(2)}) %collective-permute-start.43) | collective-permute-done | bytes 262176 | tf_op jit(solution)/shard_map/ppermute | solution.py:174
  147.3 2.1 collective-permute-start.44
  153.4 4.1 %collective-permute-done.35.refs_5_ = bf16[272,384]{1,0:T(8,128)(2,1)S(1)} collective-permute-done((bf16[272,384]{1,0:T(8,128)(2,1)S(1)}, bf16[272,384]{1,0:T(8,128)(2,1)S(1)}, u32[]{:S(2)}, u32[]{:S(2)}) %collective-permute-start.35) | collective-permute-done | bytes 208928 | tf_op jit(solution)/shard_map/ppermute | solution.py:174
  158.4 4.3 %collective-permute-done.37.refs_7_ = bf16[272,384]{1,0:T(8,128)(2,1)S(1)} collective-permute-done((bf16[272,384]{1,0:T(8,128)(2,1)S(1)}, bf16[272,384]{1,0:T(8,128)(2,1)S(1)}, u32[]{:S(2)}, u32[]{:S(2)}) %collective-permute-start.37) | collective-permute-done | bytes 208928 | tf_op jit(solution)/shard_map/ppermute | solution.py:174
  166.7 2.9 %collective-permute-done.45.refs_13_ = bf16[272,384]{1,0:T(8,128)(2,1)S(1)} collective-permute-done((bf16[272,384]{1,0:T(8,128)(2,1)S(1)}, bf16[272,384]{1,0:T(8,128)(2,1)S(1)}, u32[]{:S(2)}, u32[]{:S(2)}) %collective-permute-start.45) | collective-permute-done | bytes 208928 | tf_op jit(solution)/shard_map/ppermute | solution.py:174
  170.5 3.8 %collective-permute-done.47.refs_15_ = bf16[272,384]{1,0:T(8,128)(2,1)S(1)} collective-permute-done((bf16[272,384]{1,0:T(8,128)(2,1)S(1)}, bf16[272,384]{1,0:T(8,128)(2,1)S(1)}, u32[]{:S(2)}, u32[]{:S(2)}) %collective-permute-start.47) | collective-permute-done | bytes 208928 | tf_op jit(solution)/shard_map/ppermute | solution.py:174
  179.0 3.3 %collective-permute-start.48 = (bf16[1024,128]{1,0:T(8,128)(2,1)S(1)}, bf16[1024,128]{1,0:T(8,128)(2,1)S(1)}, u32[]{:S(2)}, u32[]{:S(2)}) collective-permute-start(bf16[1024,128]{1,0:T(8,128)(2,1)S(1)} %shard_map.127.refs_0_), channel_id=1, source_target_pairs={{0,4},{4,0},{8,12},{12,8},{16,20},{20,16},{24,28},{28,24},{1,5},{5... | collective-permute-start | bytes 786440 | tf_op jit(solution)/shard_map/ppermute | solution.py:174
  182.3 5.6 %collective-permute-start.50 = (bf16[1024,128]{1,0:T(8,128)(2,1)S(1)}, bf16[1024,128]{1,0:T(8,128)(2,1)S(1)}, u32[]{:S(2)}, u32[]{:S(2)}) collective-permute-start(bf16[1024,128]{1,0:T(8,128)(2,1)S(1)} %collective-permute-done.49.refs_2_), channel_id=1, source_target_pairs={{0,4},{4,0},{8,12},{12,8},{16,20},{20,16},{24,28},{28,24},{1,5},{5... | collective-permute-start | bytes 786440 | tf_op jit(solution)/shard_map/ppermute | solution.py:174
  187.9 4.2 %collective-permute-start.52 = (bf16[1024,128]{1,0:T(8,128)(2,1)S(1)}, bf16[1024,128]{1,0:T(8,128)(2,1)S(1)}, u32[]{:S(2)}, u32[]{:S(2)}) collective-permute-start(bf16[1024,128]{1,0:T(8,128)(2,1)S(1)} %collective-permute-done.51.refs_4_), channel_id=1, source_target_pairs={{0,4},{4,0},{8,12},{12,8},{16,20},{20,16},{24,28},{28,24},{1,5},{5... | collective-permute-start | bytes 786440 | tf_op jit(solution)/shard_map/ppermute | solution.py:174
  198.3 7.4 %collective-permute-done.55.refs_0_ = bf16[256,512]{1,0:T(8,128)(2,1)S(1)} collective-permute-done((bf16[256,512]{1,0:T(8,128)(2,1)S(1)}, bf16[256,512]{1,0:T(8,128)(2,1)S(1)}, u32[]{:S(2)}, u32[]{:S(2)}) %collective-permute-start.55) | collective-permute-done | bytes 262176 | tf_op jit(solution)/shard_map/ppermute | solution.py:174
  205.6 3.1 %collective-permute-done.56.refs_1_ = bf16[256,512]{1,0:T(8,128)(2,1)S(1)} collective-permute-done((bf16[256,512]{1,0:T(8,128)(2,1)S(1)}, bf16[256,512]{1,0:T(8,128)(2,1)S(1)}, u32[]{:S(2)}, u32[]{:S(2)}) %collective-permute-start.56) | collective-permute-done | bytes 262176 | tf_op jit(solution)/shard_map/ppermute | solution.py:174
  208.7 12.3 %collective-permute-done.57.refs_2_ = bf16[256,512]{1,0:T(8,128)(2,1)S(1)} collective-permute-done((bf16[256,512]{1,0:T(8,128)(2,1)S(1)}, bf16[256,512]{1,0:T(8,128)(2,1)S(1)}, u32[]{:S(2)}, u32[]{:S(2)}) %collective-permute-start.57) | collective-permute-done | bytes 262176 | tf_op jit(solution)/shard_map/ppermute | solution.py:174
  223.1 4.1 %collective-permute-start.59 = (bf16[128,512]{1,0:T(8,128)(2,1)S(1)}, bf16[128,512]{1,0:T(8,128)(2,1)S(1)}, u32[]{:S(2)}, u32[]{:S(2)}) collective-permute-start(bf16[128,512]{1,0:T(8,128)(2,1)S(1)} %get-tuple-element.98), channel_id=1, source_target_pairs={{0,4},{1,12},{2,20},{3,28},{4,0},{5,8},{6,16},{7,24},{8,5},{9,13},... | collective-permute-start | bytes 393224 | tf_op jit(solution)/shard_map/ppermute | solution.py:616
  227.2 8.9 %collective-permute-done.58 = bf16[128,512]{1,0:T(8,128)(2,1)S(1)} collective-permute-done((bf16[128,512]{1,0:T(8,128)(2,1)S(1)}, bf16[128,512]{1,0:T(8,128)(2,1)S(1)}, u32[]{:S(2)}, u32[]{:S(2)}) %collective-permute-start.58) | collective-permute-done | bytes 131104 | tf_op jit(solution)/shard_map/ppermute | solution.py:616
  236.0 2.8 %collective-permute-done.59 = bf16[128,512]{1,0:T(8,128)(2,1)S(1)} collective-permute-done((bf16[128,512]{1,0:T(8,128)(2,1)S(1)}, bf16[128,512]{1,0:T(8,128)(2,1)S(1)}, u32[]{:S(2)}, u32[]{:S(2)}) %collective-permute-start.59) | collective-permute-done | bytes 131104 | tf_op jit(solution)/shard_map/ppermute | solution.py:616
  (140 shorter events, 72.3 us)
Async XLA Ops:
  6.5 52.0 %all-gather.2.cloned.1.call-start = ((), (), s32[]{:S(2)}) async-start(), calls=%async_computation | async-start | bytes 2359296 | tf_op jit(solution)/shard_map/all_gather | solution.py:478
  9.8 16.4 %collective-permute-start.5 = (bf16[128,1024]{1,0:T(8,128)(2,1)}, bf16[128,1024]{1,0:T(8,128)(2,1)S(1)}, u32[]{:S(2)}, u32[]{:S(2)}) collective-permute-start(bf16[128,1024]{1,0:T(8,128)(2,1)} %refs_0_.3), channel_id=1, source_target_pairs={{0,24},{4,28},{8,16},{12,20},{16,8},{20,12},{24,0},{28,4},{1,25},{... | collective-permute-start | bytes 786440 | tf_op jit(solution)/shard_map/ppermute | solution.py:174
  10.0 17.2 %collective-permute-start = (bf16[128,1024]{1,0:T(8,128)(2,1)}, bf16[128,1024]{1,0:T(8,128)(2,1)S(1)}, u32[]{:S(2)}, u32[]{:S(2)}) collective-permute-start(bf16[128,1024]{1,0:T(8,128)(2,1)} %refs_0_.3), channel_id=1, source_target_pairs={{0,4},{4,0},{8,12},{12,8},{16,20},{20,16},{24,28},{28,24},{1,5},{5... | collective-permute-start | bytes 786440 | tf_op jit(solution)/shard_map/ppermute | solution.py:174
  11.5 24.7 %collective-permute-start.10 = (bf16[128,1024]{1,0:T(8,128)(2,1)}, bf16[128,1024]{1,0:T(8,128)(2,1)S(1)}, u32[]{:S(2)}, u32[]{:S(2)}) collective-permute-start(bf16[128,1024]{1,0:T(8,128)(2,1)} %refs_0_.4), channel_id=1, source_target_pairs={{0,16},{4,20},{8,24},{12,28},{16,0},{20,4},{24,8},{28,12},{1,17},{... | collective-permute-start | bytes 786440 | tf_op jit(solution)/shard_map/ppermute | solution.py:174
  14.7 13.5 %collective-permute-start.2 = (bf16[128,1024]{1,0:T(8,128)(2,1)S(1)}, bf16[128,1024]{1,0:T(8,128)(2,1)S(1)}, u32[]{:S(2)}, u32[]{:S(2)}) collective-permute-start(bf16[128,1024]{1,0:T(8,128)(2,1)S(1)} %collective-permute-done.1.refs_2_), channel_id=1, source_target_pairs={{0,4},{4,0},{8,12},{12,8},{16,20},{20,16},{24,28},{28,24},{1,5},{5... | collective-permute-start | bytes 786440 | tf_op jit(solution)/shard_map/ppermute | solution.py:174
  17.4 13.0 %collective-permute-start.4 = (bf16[128,1024]{1,0:T(8,128)(2,1)S(1)}, bf16[128,1024]{1,0:T(8,128)(2,1)S(1)}, u32[]{:S(2)}, u32[]{:S(2)}) collective-permute-start(bf16[128,1024]{1,0:T(8,128)(2,1)S(1)} %collective-permute-done.3.refs_4_), channel_id=1, source_target_pairs={{0,4},{4,0},{8,12},{12,8},{16,20},{20,16},{24,28},{28,24},{1,5},{5... | collective-permute-start | bytes 786440 | tf_op jit(solution)/shard_map/ppermute | solution.py:174
  28.2 19.5 %collective-permute-start.8 = (bf16[128,1024]{1,0:T(8,128)(2,1)}, bf16[128,1024]{1,0:T(8,128)(2,1)S(1)}, u32[]{:S(2)}, u32[]{:S(2)}) collective-permute-start(bf16[128,1024]{1,0:T(8,128)(2,1)} %refs_0_.4), channel_id=1, source_target_pairs={{0,8},{4,12},{8,0},{12,4},{16,24},{20,28},{24,16},{28,20},{1,9},{5... | collective-permute-start | bytes 786440 | tf_op jit(solution)/shard_map/ppermute | solution.py:174
  35.0 22.4 %collective-permute-start.14 = (bf16[512,1024]{1,0:T(8,128)(2,1)S(1)}, bf16[512,1024]{1,0:T(8,128)(2,1)S(1)}, u32[]{:S(2)}, u32[]{:S(2)}) collective-permute-start(bf16[512,1024]{1,0:T(8,128)(2,1)S(1)} %copy-done.3), channel_id=1, source_target_pairs={{0,4},{4,0},{8,12},{12,8},{16,20},{20,16},{24,28},{28,24},{1,5},{5... | collective-permute-start | bytes 3145736 | tf_op jit(solution)/shard_map/ppermute | solution.py:174
  36.1 21.3 %collective-permute-start.15 = (bf16[512,1024]{1,0:T(8,128)(2,1)S(1)}, bf16[512,1024]{1,0:T(8,128)(2,1)S(1)}, u32[]{:S(2)}, u32[]{:S(2)}) collective-permute-start(bf16[512,1024]{1,0:T(8,128)(2,1)S(1)} %copy-done.4), channel_id=1, source_target_pairs={{0,4},{4,0},{8,12},{12,8},{16,20},{20,16},{24,28},{28,24},{1,5},{5... | collective-permute-start | bytes 3145736 | tf_op jit(solution)/shard_map/ppermute | solution.py:174
  36.2 21.2 %collective-permute-start.16 = (bf16[512,1024]{1,0:T(8,128)(2,1)}, bf16[512,1024]{1,0:T(8,128)(2,1)S(1)}, u32[]{:S(2)}, u32[]{:S(2)}) collective-permute-start(bf16[512,1024]{1,0:T(8,128)(2,1)} %refs_4_.1), channel_id=1, source_target_pairs={{0,4},{4,0},{8,12},{12,8},{16,20},{20,16},{24,28},{28,24},{1,5},{5... | collective-permute-start | bytes 3145736 | tf_op jit(solution)/shard_map/ppermute | solution.py:174
  36.6 12.5 %collective-permute-start.7 = (bf16[128,1024]{1,0:T(8,128)(2,1)S(1)}, bf16[128,1024]{1,0:T(8,128)(2,1)S(1)}, u32[]{:S(2)}, u32[]{:S(2)}) collective-permute-start(bf16[128,1024]{1,0:T(8,128)(2,1)S(1)} %copy-done.11), channel_id=1, source_target_pairs={{0,4},{4,0},{8,12},{12,8},{16,20},{20,16},{24,28},{28,24},{1,5},{5... | collective-permute-start | bytes 786440 | tf_op jit(solution)/shard_map/ppermute | solution.py:174
  77.4 12.6 %collective-permute-start.22 = (bf16[128,1024]{1,0:T(8,128)(2,1)S(1)}, bf16[128,1024]{1,0:T(8,128)(2,1)S(1)}, u32[]{:S(2)}, u32[]{:S(2)}) collective-permute-start(bf16[128,1024]{1,0:T(8,128)(2,1)S(1)} %maximum_add_fusion.refs_0_), channel_id=1, source_target_pairs={{0,16},{4,20},{8,24},{12,28},{16,0},{20,4},{24,8},{28,12},{1,17},{... | collective-permute-start | bytes 786440 | tf_op jit(solution)/shard_map/ppermute | solution.py:174
  77.4 12.6 %collective-permute-start.24 = (bf16[128,1024]{1,0:T(8,128)(2,1)S(1)}, bf16[128,1024]{1,0:T(8,128)(2,1)S(1)}, u32[]{:S(2)}, u32[]{:S(2)}) collective-permute-start(bf16[128,1024]{1,0:T(8,128)(2,1)S(1)} %maximum_add_fusion.refs_0_), channel_id=1, source_target_pairs={{0,24},{4,28},{8,16},{12,20},{16,8},{20,12},{24,0},{28,4},{1,25},{... | collective-permute-start | bytes 786440 | tf_op jit(solution)/shard_map/ppermute | solution.py:174
  78.6 11.9 %collective-permute-start.19 = (bf16[128,1024]{1,0:T(8,128)(2,1)S(1)}, bf16[128,1024]{1,0:T(8,128)(2,1)S(1)}, u32[]{:S(2)}, u32[]{:S(2)}) collective-permute-start(bf16[128,1024]{1,0:T(8,128)(2,1)S(1)} %maximum_add_fusion.refs_0_), channel_id=1, source_target_pairs={{0,4},{4,0},{8,12},{12,8},{16,20},{20,16},{24,28},{28,24},{1,5},{5... | collective-permute-start | bytes 786440 | tf_op jit(solution)/shard_map/ppermute | solution.py:174
  93.3 11.2 %collective-permute-start.26 = (bf16[256,512]{1,0:T(8,128)(2,1)S(1)}, bf16[256,512]{1,0:T(8,128)(2,1)S(1)}, u32[]{:S(2)}, u32[]{:S(2)}) collective-permute-start(bf16[256,512]{1,0:T(8,128)(2,1)S(1)} %get-tuple-element.66), channel_id=1, source_target_pairs={{0,1},{1,0},{2,3},{3,2},{4,5},{5,4},{6,7},{7,6},{8,9},{9,8},{10,11... | collective-permute-start | bytes 786440 | tf_op jit(solution)/shard_map/ppermute | solution.py:174
  93.8 14.0 %collective-permute-start.27 = (bf16[256,512]{1,0:T(8,128)(2,1)S(1)}, bf16[256,512]{1,0:T(8,128)(2,1)S(1)}, u32[]{:S(2)}, u32[]{:S(2)}) collective-permute-start(bf16[256,512]{1,0:T(8,128)(2,1)S(1)} %get-tuple-element.67), channel_id=1, source_target_pairs={{0,2},{1,3},{2,0},{3,1},{4,6},{5,7},{6,4},{7,5},{8,10},{9,11},{10,... | collective-permute-start | bytes 786440 | tf_op jit(solution)/shard_map/ppermute | solution.py:174
  95.9 23.1 %collective-permute-start.28 = (bf16[256,512]{1,0:T(8,128)(2,1)S(1)}, bf16[256,512]{1,0:T(8,128)(2,1)S(1)}, u32[]{:S(2)}, u32[]{:S(2)}) collective-permute-start(bf16[256,512]{1,0:T(8,128)(2,1)S(1)} %get-tuple-element.68), channel_id=1, source_target_pairs={{0,3},{1,2},{2,1},{3,0},{4,7},{5,6},{6,5},{7,4},{8,11},{9,10},{10,... | collective-permute-start | bytes 786440 | tf_op jit(solution)/shard_map/ppermute | solution.py:174
  120.4 11.5 %collective-permute-start.38 = (bf16[256,512]{1,0:T(8,128)(2,1)S(1)}, bf16[256,512]{1,0:T(8,128)(2,1)S(1)}, u32[]{:S(2)}, u32[]{:S(2)}) collective-permute-start(bf16[256,512]{1,0:T(8,128)(2,1)S(1)} %add_convert_fusion.rows_own.hidden), channel_id=1, source_target_pairs={{0,2},{1,3},{2,0},{3,1},{4,6},{5,7},{6,4},{7,5},{8,10},{9,11},{10,... | collective-permute-start | bytes 786440 | tf_op jit(solution)/shard_map/ppermute | solution.py:174
  120.4 14.5 %collective-permute-start.33 = (bf16[256,512]{1,0:T(8,128)(2,1)S(1)}, bf16[256,512]{1,0:T(8,128)(2,1)S(1)}, u32[]{:S(2)}, u32[]{:S(2)}) collective-permute-start(bf16[256,512]{1,0:T(8,128)(2,1)S(1)} %add_convert_fusion.rows_own.hidden), channel_id=1, source_target_pairs={{0,1},{1,0},{2,3},{3,2},{4,5},{5,4},{6,7},{7,6},{8,9},{9,8},{10,11... | collective-permute-start | bytes 786440 | tf_op jit(solution)/shard_map/ppermute | solution.py:174
  124.2 10.8 %collective-permute-start.30 = (bf16[272,384]{1,0:T(8,128)(2,1)S(1)}, bf16[272,384]{1,0:T(8,128)(2,1)S(1)}, u32[]{:S(2)}, u32[]{:S(2)}) collective-permute-start(bf16[272,384]{1,0:T(8,128)(2,1)S(1)} %get-tuple-element.74), channel_id=1, source_target_pairs={{0,8},{4,12},{8,0},{12,4},{16,24},{20,28},{24,16},{28,20},{1,9},{5... | collective-permute-start | bytes 626696 | tf_op jit(solution)/shard_map/ppermute | solution.py:174
  135.0 12.3 %collective-permute-start.43 = (bf16[256,512]{1,0:T(8,128)(2,1)S(1)}, bf16[256,512]{1,0:T(8,128)(2,1)S(1)}, u32[]{:S(2)}, u32[]{:S(2)}) collective-permute-start(bf16[256,512]{1,0:T(8,128)(2,1)S(1)} %add_convert_fusion.rows_own.hidden), channel_id=1, source_target_pairs={{0,3},{1,2},{2,1},{3,0},{4,7},{5,6},{6,5},{7,4},{8,11},{9,10},{10,... | collective-permute-start | bytes 786440 | tf_op jit(solution)/shard_map/ppermute | solution.py:174
  135.2 14.2 %collective-permute-start.34 = (bf16[256,512]{1,0:T(8,128)(2,1)S(1)}, bf16[256,512]{1,0:T(8,128)(2,1)S(1)}, u32[]{:S(2)}, u32[]{:S(2)}) collective-permute-start(bf16[256,512]{1,0:T(8,128)(2,1)S(1)} %collective-permute-done.33.rows_own), channel_id=1, source_target_pairs={{0,4},{4,0},{8,12},{12,8},{16,20},{20,16},{24,28},{28,24},{1,5},{5... | collective-permute-start | bytes 786440 | tf_op jit(solution)/shard_map/ppermute | solution.py:174
  138.3 13.5 %collective-permute-start.40 = (bf16[272,384]{1,0:T(8,128)(2,1)S(1)}, bf16[272,384]{1,0:T(8,128)(2,1)S(1)}, u32[]{:S(2)}, u32[]{:S(2)}) collective-permute-start(bf16[272,384]{1,0:T(8,128)(2,1)S(1)} %get-tuple-element.84), channel_id=1, source_target_pairs={{0,8},{4,12},{8,0},{12,4},{16,24},{20,28},{24,16},{28,20},{1,9},{5... | collective-permute-start | bytes 626696 | tf_op jit(solution)/shard_map/ppermute | solution.py:174
  139.5 12.8 %collective-permute-start.41 = (bf16[272,384]{1,0:T(8,128)(2,1)S(1)}, bf16[272,384]{1,0:T(8,128)(2,1)S(1)}, u32[]{:S(2)}, u32[]{:S(2)}) collective-permute-start(bf16[272,384]{1,0:T(8,128)(2,1)S(1)} %get-tuple-element.85), channel_id=1, source_target_pairs={{0,16},{4,20},{8,24},{12,28},{16,0},{20,4},{24,8},{28,12},{1,17},{... | collective-permute-start | bytes 626696 | tf_op jit(solution)/shard_map/ppermute | solution.py:174
  140.1 13.3 %collective-permute-start.42 = (bf16[272,384]{1,0:T(8,128)(2,1)S(1)}, bf16[272,384]{1,0:T(8,128)(2,1)S(1)}, u32[]{:S(2)}, u32[]{:S(2)}) collective-permute-start(bf16[272,384]{1,0:T(8,128)(2,1)S(1)} %get-tuple-element.86), channel_id=1, source_target_pairs={{0,24},{4,28},{8,16},{12,20},{16,8},{20,12},{24,0},{28,4},{1,25},{... | collective-permute-start | bytes 626696 | tf_op jit(solution)/shard_map/ppermute | solution.py:174
  147.3 15.4 %collective-permute-start.44 = (bf16[256,512]{1,0:T(8,128)(2,1)S(1)}, bf16[256,512]{1,0:T(8,128)(2,1)S(1)}, u32[]{:S(2)}, u32[]{:S(2)}) collective-permute-start(bf16[256,512]{1,0:T(8,128)(2,1)S(1)} %collective-permute-done.43.rows_own), channel_id=1, source_target_pairs={{0,4},{4,0},{8,12},{12,8},{16,20},{20,16},{24,28},{28,24},{1,5},{5... | collective-permute-start | bytes 786440 | tf_op jit(solution)/shard_map/ppermute | solution.py:174
  178.2 13.9 %collective-permute-start.53 = (bf16[1024,128]{1,0:T(8,128)(2,1)S(1)}, bf16[1024,128]{1,0:T(8,128)(2,1)S(1)}, u32[]{:S(2)}, u32[]{:S(2)}) collective-permute-start(bf16[1024,128]{1,0:T(8,128)(2,1)S(1)} %shard_map.127.refs_0_), channel_id=1, source_target_pairs={{0,24},{4,28},{8,16},{12,20},{16,8},{20,12},{24,0},{28,4},{1,25},{... | collective-permute-start | bytes 786440 | tf_op jit(solution)/shard_map/ppermute | solution.py:174
  179.0 13.1 %collective-permute-start.48 = (bf16[1024,128]{1,0:T(8,128)(2,1)S(1)}, bf16[1024,128]{1,0:T(8,128)(2,1)S(1)}, u32[]{:S(2)}, u32[]{:S(2)}) collective-permute-start(bf16[1024,128]{1,0:T(8,128)(2,1)S(1)} %shard_map.127.refs_0_), channel_id=1, source_target_pairs={{0,4},{4,0},{8,12},{12,8},{16,20},{20,16},{24,28},{28,24},{1,5},{5... | collective-permute-start | bytes 786440 | tf_op jit(solution)/shard_map/ppermute | solution.py:174
  195.6 13.1 %collective-permute-start.56 = (bf16[256,512]{1,0:T(8,128)(2,1)S(1)}, bf16[256,512]{1,0:T(8,128)(2,1)S(1)}, u32[]{:S(2)}, u32[]{:S(2)}) collective-permute-start(bf16[256,512]{1,0:T(8,128)(2,1)S(1)} %get-tuple-element.95), channel_id=1, source_target_pairs={{0,2},{1,3},{2,0},{3,1},{4,6},{5,7},{6,4},{7,5},{8,10},{9,11},{10,... | collective-permute-start | bytes 786440 | tf_op jit(solution)/shard_map/ppermute | solution.py:174
  197.0 24.0 %collective-permute-start.57 = (bf16[256,512]{1,0:T(8,128)(2,1)S(1)}, bf16[256,512]{1,0:T(8,128)(2,1)S(1)}, u32[]{:S(2)}, u32[]{:S(2)}) collective-permute-start(bf16[256,512]{1,0:T(8,128)(2,1)S(1)} %get-tuple-element.96), channel_id=1, source_target_pairs={{0,3},{1,2},{2,1},{3,0},{4,7},{5,6},{6,5},{7,4},{8,11},{9,10},{10,... | collective-permute-start | bytes 786440 | tf_op jit(solution)/shard_map/ppermute | solution.py:174
  221.2 14.8 %collective-permute-start.58 = (bf16[128,512]{1,0:T(8,128)(2,1)S(1)}, bf16[128,512]{1,0:T(8,128)(2,1)S(1)}, u32[]{:S(2)}, u32[]{:S(2)}) collective-permute-start(bf16[128,512]{1,0:T(8,128)(2,1)S(1)} %get-tuple-element.97), channel_id=1, source_target_pairs={{0,0},{1,8},{2,16},{3,24},{4,4},{5,12},{6,20},{7,28},{8,1},{9,9},{... | collective-permute-start | bytes 393224 | tf_op jit(solution)/shard_map/ppermute | solution.py:616
  223.1 15.7 %collective-permute-start.59 = (bf16[128,512]{1,0:T(8,128)(2,1)S(1)}, bf16[128,512]{1,0:T(8,128)(2,1)S(1)}, u32[]{:S(2)}, u32[]{:S(2)}) collective-permute-start(bf16[128,512]{1,0:T(8,128)(2,1)S(1)} %get-tuple-element.98), channel_id=1, source_target_pairs={{0,4},{1,12},{2,20},{3,28},{4,0},{5,8},{6,16},{7,24},{8,5},{9,13},... | collective-permute-start | bytes 393224 | tf_op jit(solution)/shard_map/ppermute | solution.py:616
  (43 other events, 334.1 us)
Sparse Core Ops, SparseCore 0:
  9.2 39.8 all-gather.1

commit v4 on v3

--- a/solution.py
+++ b/solution.py
@@ -276,12 +276,12 @@
         totals[...] += dot(turned, high) + dot(turned, low)
 
 
-def value_kernel(tile, slot_row, raw, totals, states, weight, *refs):
-    own, above, below, held, whole, summed, semaphores = refs
+def value_kernel(count, tile, slot_row, raw, totals, states, *refs):
+    pieces, (own, above, below, held, whole, summed, semaphores) = refs[:count], refs[count:]
     slots = totals.shape[0]
-    copies = fetched([(states, held), (weight, whole)], semaphores)
+    copies = fetched([(states, held), *plane_rows(pieces, whole)], semaphores)
     spill = above.shape[0]
-    head_count = weight.shape[1] // HEAD_DIM
+    head_count = whole.shape[1] // HEAD_DIM
     summed[...] = jnp.zeros_like(summed)
     for copy in copies:
         copy.wait()
@@ -475,7 +475,6 @@
             pieces += [moved, core_swapped(moved)]
         return pieces
 
-    value_weight = lax.all_gather(cross_value, "seq", axis=0, tiled=True)
     slot_of = byte_patch - (seq * patch_dev - spill)
     slot_row = slot_of[None, :]
     edge = jnp.ones((spill,), jnp.int32)
@@ -484,6 +483,7 @@
     ).astype(f32)[:, None]
     query_pieces = over_plane(cross_query)
     key_pieces = over_plane(cross_key)
+    value_pieces = over_plane(cross_value)
     (query_slots,) = call(
         functools.partial(query_kernel, seq_count),
         [((slot_count, local_width), bf16)],
@@ -526,19 +526,19 @@
     )
     raw, *head_weights = lax.optimization_barrier((raw, *head_weights))
     own, above, below = call(
-        functools.partial(value_kernel, tile),
+        functools.partial(value_kernel, seq_count, tile),
         [((rows, local_width), bf16) for rows in (patch_dev, spill, spill)],
         slot_row,
         raw,
         totals,
         byte_states,
-        value_weight,
-        far=2,
+        *value_pieces,
+        far=1 + seq_count,
         scratch=[
             pltpu.VMEM((byte_count, byte_width), bf16),
             pltpu.VMEM((byte_width, local_width), bf16),
             pltpu.VMEM((slot_count, local_width), f32),
-            pltpu.SemaphoreType.DMA((2,)),
+            pltpu.SemaphoreType.DMA((1 + seq_count,)),
         ],
         flops=2 * byte_count * local_width * (byte_width + slot_count),
     )
@@ -558,22 +558,22 @@
     latent_in = total.astype(bf16)
 
     gain = norm_gain[None, :]
-    shares, blocks = [], [latent_in]
+    shares, block = [], latent_in
     for r in range(tensor_count):
+        if r:
+            done = shares[(r - 2) * chip_count] if r > 1 else block
+            block = exchanged(after(latent_in, block, done), "tensor", r)
+        ready = block
         if r == 1:
-            near = [exchanged(latent_in, "tensor", d) for d in (1, 2)]
-            blocks += [after(block, shares[0]) for block in near]
-        elif r > 2:
-            earlier = shares[: (r - 2) * chip_count]
-            blocks.append(exchanged(after(latent_in, blocks[r - 2], *earlier), "tensor", r))
-        swapped = core_swapped(blocks[r])
-        if r > 2:
-            blocks[r] = after(blocks[r], *shares[(r - 2) * chip_count :])
+            ready = after(block, shares[0])
+        swapped = core_swapped(ready)
+        if r > 1:
+            ready = after(block, *shares[(r - 2) * chip_count : (r - 1) * chip_count + 2])
         share, *sent = call(
             project_kernel,
             [((quarter + 8, 3 * HEAD_DIM), f32)]
             + [((quarter + 16, 3 * HEAD_DIM), bf16)] * (chip_count - 1),
-            blocks[r],
+            ready,
             swapped,
             gain,
             *head_weights,

time: 249 us -> 246 us (0.988)
  between operations: 13.7 us -> 0.31 us
  starting transfers between devices: 80 us -> 91.8 us
  local copies, waits for them, and re-layouts: 7.7 us -> 3.48 us
  waiting for transfers between devices: 120 us -> 123 us
    ppermute x56 -> x63, starting transfers between devices: 69.5 us -> 80.3 us  [exchanged(): return lax.ppermute(block, axis, route)]
    ppermute x56 -> x63, waiting for transfers between devices: 104 us -> 109 us  [exchanged(): return lax.ppermute(block, axis, route)]
    unnamed x28 -> x22, local copies, waits for them, and re-layouts: 6.8 us -> 2.58 us
  transfers between devices with their start and end apart: 61 -> 67, of which waited for: 29 -> 28; matrix products, arithmetic and copies ran while one was open for 1% -> 1% of each run, Pallas kernels for 5% -> 6%
where the time goes in v4:
time: 246 us; the launch traced here: 244 us
  waiting for transfers between devices  123 us (50%)
  starting transfers between devices  91.8 us (37%)
  Pallas kernels  23.7 us (10%)
  local copies, waits for them, and re-layouts  3.48 us (1%)
    ppermute x63, waiting for transfers between devices, exchanged(): return lax.ppermute(block, axis, route)  109 us
    ppermute x63, starting transfers between devices, exchanged(): return lax.ppermute(block, axis, route)  80.3 us
    pallas_call x12, Pallas kernels, call(): pl.pallas_call(kernel, out_shape=shapes, in_specs=[pl.BlockSpec(memory_sp...  23.7 us
    ppermute x2, waiting for transfers between devices, per_device(): moved.append(lax.ppermute(pieces[flip], ('seq', 'tensor'), route))  12 us
    ppermute x2, starting transfers between devices, shifted(): return lax.ppermute(block, axis, route)  5.74 us
    ppermute x2, starting transfers between devices, per_device(): moved.append(lax.ppermute(pieces[flip], ('seq', 'tensor'), route))  5.71 us
  transfers between devices with their start and end apart: 67, of which 28 were waited for; matrix products, arithmetic and copies ran while one was open for 1% of the time, Pallas kernels for 6%

profile of v4, /device:TPU:9, one launch (start us, length us, event | category | flops | bytes accessed | tf_op | source)
XLA Modules:
  0.0 243.5 jit_solution(14863097812750390662)
XLA Ops:
  4.9 2.5 %collective-permute-done.1.refs_2_ = bf16[128,1024]{1,0:T(8,128)(2,1)S(1)} collective-permute-done((bf16[128,1024]{1,0:T(8,128)(2,1)}, bf16[128,1024]{1,0:T(8,128)(2,1)S(1)}, u32[]{:S(2)}, u32[]{:S(2)}) %collective-permute-start.1) | collective-permute-done | bytes 262176 | tf_op jit(solution)/shard_map/ppermute | solution.py:174
  7.4 2.7 %collective-permute-start.2 = (bf16[128,1024]{1,0:T(8,128)(2,1)S(1)}, bf16[128,1024]{1,0:T(8,128)(2,1)S(1)}, u32[]{:S(2)}, u32[]{:S(2)}) collective-permute-start(bf16[128,1024]{1,0:T(8,128)(2,1)S(1)} %collective-permute-done.1.refs_2_), channel_id=1, source_target_pairs={{0,4},{4,0},{8,12},{12,8},{16,20},{20,16},{24,28},{28,24},{1,5},{5... | collective-permute-start | bytes 786440 | tf_op jit(solution)/shard_map/ppermute | solution.py:174
  10.1 5.7 %collective-permute-start.4 = (bf16[128,1024]{1,0:T(8,128)(2,1)S(1)}, bf16[128,1024]{1,0:T(8,128)(2,1)S(1)}, u32[]{:S(2)}, u32[]{:S(2)}) collective-permute-start(bf16[128,1024]{1,0:T(8,128)(2,1)S(1)} %collective-permute-done.3.refs_4_), channel_id=1, source_target_pairs={{0,4},{4,0},{8,12},{12,8},{16,20},{20,16},{24,28},{28,24},{1,5},{5... | collective-permute-start | bytes 786440 | tf_op jit(solution)/shard_map/ppermute | solution.py:174
  26.6 5.7 %collective-permute-done.12.refs_6_ = bf16[128,1024]{1,0:T(8,128)(2,1)S(1)} collective-permute-done((bf16[128,1024]{1,0:T(8,128)(2,1)S(1)}, bf16[128,1024]{1,0:T(8,128)(2,1)S(1)}, u32[]{:S(2)}, u32[]{:S(2)}) %collective-permute-start.12) | collective-permute-done | bytes 262176 | tf_op jit(solution)/shard_map/ppermute | solution.py:174
  32.4 2.1 collective-permute-start.16
  34.5 2.7 %collective-permute-done.18.refs_2_ = bf16[128,1024]{1,0:T(8,128)(2,1)S(1)} collective-permute-done((bf16[128,1024]{1,0:T(8,128)(2,1)S(1)}, bf16[128,1024]{1,0:T(8,128)(2,1)S(1)}, u32[]{:S(2)}, u32[]{:S(2)}) %collective-permute-start.18) | collective-permute-done | bytes 262176 | tf_op jit(solution)/shard_map/ppermute | solution.py:174
  40.8 3.9 %collective-permute-done.22.refs_6_ = bf16[128,1024]{1,0:T(8,128)(2,1)S(1)} collective-permute-done((bf16[128,1024]{1,0:T(8,128)(2,1)S(1)}, bf16[128,1024]{1,0:T(8,128)(2,1)S(1)}, u32[]{:S(2)}, u32[]{:S(2)}) %collective-permute-start.22) | collective-permute-done | bytes 262176 | tf_op jit(solution)/shard_map/ppermute | solution.py:174
  44.7 2.2 collective-permute-start.11
  49.3 5.5 %shard_map.119 = (f32[1024,128]{1,0:T(8,128)S(1)}, f32[256,128]{1,0:T(8,128)S(1)}) custom-call(s32[1,1024]{1,0:T(1,128)S(1)} %bitcast.8, bf16[256,1024]{1,0:T(8,128)(2,1)S(1)} %shard_map.118.query, bf16[1024,1024]{1,0:T(8,128)(2,1)S(1)} %copy-done.1, bf16[128,1024]{1,0:T(8,128)(2,1)S(1)} %copy-done.9, bf16[128,1024]{1,0:T(8,128)(2,1)S(1)} %collective-permute-done.7.refs_1_, ...), custom_call_target="tpu_custom_call" | custom-call | flops 3221225472 | bytes 5378048 | tf_op jit(solution)/shard_map/pallas_call | solution.py:207
  56.0 4.5 %shard_map.121 = (bf16[128,1024]{1,0:T(8,128)(2,1)S(1)}, bf16[64,1024]{1,0:T(8,128)(2,1)S(1)}, bf16[64,1024]{1,0:T(8,128)(2,1)S(1)}) custom-call(s32[1,1024]{1,0:T(1,128)S(1)} %bitcast.9, f32[1024,128]{1,0:T(8,128)S(1)} %get-tuple-element.62.raw, f32[256,128]{1,0:T(8,128)S(1)} %get-tuple-element.63.totals, bf16[1024,1024]{1,0:T(8,128)(2,1)S(1)} %copy-done.1, ...), custom_call_target="tpu_custom_call" | custom-call | flops 2684354560 | bytes 5378048 | tf_op jit(solution)/shard_map/pallas_call | solution.py:207
  62.6 3.7 %collective-permute-start.24 = (bf16[64,1024]{1,0:T(8,128)(2,1)S(1)}, bf16[64,1024]{1,0:T(8,128)(2,1)S(1)}, u32[]{:S(2)}, u32[]{:S(2)}) collective-permute-start(bf16[64,1024]{1,0:T(8,128)(2,1)S(1)} %get-tuple-element.65), channel_id=1, source_target_pairs={{0,4},{4,8},{8,12},{12,16},{16,20},{20,24},{24,28},{1,5},{5,9},{9,... | collective-permute-start | bytes 393224 | tf_op jit(solution)/shard_map/ppermute | solution.py:22
  71.4 2.8 %collective-permute-start.26 = (bf16[128,1024]{1,0:T(8,128)(2,1)S(1)}, bf16[128,1024]{1,0:T(8,128)(2,1)S(1)}, u32[]{:S(2)}, u32[]{:S(2)}) collective-permute-start(bf16[128,1024]{1,0:T(8,128)(2,1)S(1)} %maximum_add_fusion.refs_0_), channel_id=1, source_target_pairs={{0,4},{4,0},{8,12},{12,8},{16,20},{20,16},{24,28},{28,24},{1,5},{5... | collective-permute-start | bytes 786440 | tf_op jit(solution)/shard_map/ppermute | solution.py:174
  79.8 4.6 %collective-permute-start.30 = (bf16[128,1024]{1,0:T(8,128)(2,1)S(1)}, bf16[128,1024]{1,0:T(8,128)(2,1)S(1)}, u32[]{:S(2)}, u32[]{:S(2)}) collective-permute-start(bf16[128,1024]{1,0:T(8,128)(2,1)S(1)} %collective-permute-done.29.refs_4_), channel_id=1, source_target_pairs={{0,4},{4,0},{8,12},{12,8},{16,20},{20,16},{24,28},{28,24},{1,5},{5... | collective-permute-start | bytes 786440 | tf_op jit(solution)/shard_map/ppermute | solution.py:174
  90.9 15.3 %collective-permute-done.35 = bf16[256,512]{1,0:T(8,128)(2,1)S(1)} collective-permute-done((bf16[256,512]{1,0:T(8,128)(2,1)S(1)}, bf16[256,512]{1,0:T(8,128)(2,1)S(1)}, u32[]{:S(2)}, u32[]{:S(2)}) %collective-permute-start.35) | collective-permute-done | bytes 262176 | tf_op jit(solution)/shard_map/ppermute | solution.py:174
  106.2 4.7 %collective-permute-done.34 = bf16[256,512]{1,0:T(8,128)(2,1)S(1)} collective-permute-done((bf16[256,512]{1,0:T(8,128)(2,1)S(1)}, bf16[256,512]{1,0:T(8,128)(2,1)S(1)}, u32[]{:S(2)}, u32[]{:S(2)}) %collective-permute-start.34) | collective-permute-done | bytes 262176 | tf_op jit(solution)/shard_map/ppermute | solution.py:174
  115.7 5.3 %collective-permute-done.40.rows_own = bf16[256,512]{1,0:T(8,128)(2,1)S(1)} collective-permute-done((bf16[256,512]{1,0:T(8,128)(2,1)S(1)}, bf16[256,512]{1,0:T(8,128)(2,1)S(1)}, u32[]{:S(2)}, u32[]{:S(2)}) %collective-permute-start.40) | collective-permute-done | bytes 262176 | tf_op jit(solution)/shard_map/ppermute | solution.py:174
  121.7 2.5 %collective-permute-start.45 = (bf16[256,512]{1,0:T(8,128)(2,1)S(1)}, bf16[256,512]{1,0:T(8,128)(2,1)S(1)}, u32[]{:S(2)}, u32[]{:S(2)}) collective-permute-start(bf16[256,512]{1,0:T(8,128)(2,1)S(1)} %add_convert_fusion.rows_own.hidden), channel_id=1, source_target_pairs={{0,2},{1,3},{2,0},{3,1},{4,6},{5,7},{6,4},{7,5},{8,10},{9,11},{10,... | collective-permute-start | bytes 786440 | tf_op jit(solution)/shard_map/ppermute | solution.py:174
  125.5 10.1 %collective-permute-done.45.rows_own = bf16[256,512]{1,0:T(8,128)(2,1)S(1)} collective-permute-done((bf16[256,512]{1,0:T(8,128)(2,1)S(1)}, bf16[256,512]{1,0:T(8,128)(2,1)S(1)}, u32[]{:S(2)}, u32[]{:S(2)}) %collective-permute-start.45) | collective-permute-done | bytes 262176 | tf_op jit(solution)/shard_map/ppermute | solution.py:174
  139.2 8.6 %collective-permute-done.38.refs_2_ = bf16[272,384]{1,0:T(8,128)(2,1)S(1)} collective-permute-done((bf16[272,384]{1,0:T(8,128)(2,1)S(1)}, bf16[272,384]{1,0:T(8,128)(2,1)S(1)}, u32[]{:S(2)}, u32[]{:S(2)}) %collective-permute-start.38) | collective-permute-done | bytes 208928 | tf_op jit(solution)/shard_map/ppermute | solution.py:174
  153.5 5.0 %collective-permute-done.43.refs_6_ = bf16[272,384]{1,0:T(8,128)(2,1)S(1)} collective-permute-done((bf16[272,384]{1,0:T(8,128)(2,1)S(1)}, bf16[272,384]{1,0:T(8,128)(2,1)S(1)}, u32[]{:S(2)}, u32[]{:S(2)}) %collective-permute-start.43) | collective-permute-done | bytes 208928 | tf_op jit(solution)/shard_map/ppermute | solution.py:174
  165.3 2.8 %collective-permute-done.52.refs_13_ = bf16[272,384]{1,0:T(8,128)(2,1)S(1)} collective-permute-done((bf16[272,384]{1,0:T(8,128)(2,1)S(1)}, bf16[272,384]{1,0:T(8,128)(2,1)S(1)}, u32[]{:S(2)}, u32[]{:S(2)}) %collective-permute-start.52) | collective-permute-done | bytes 208928 | tf_op jit(solution)/shard_map/ppermute | solution.py:174
  168.1 8.3 %collective-permute-done.53.refs_14_ = bf16[272,384]{1,0:T(8,128)(2,1)S(1)} collective-permute-done((bf16[272,384]{1,0:T(8,128)(2,1)S(1)}, bf16[272,384]{1,0:T(8,128)(2,1)S(1)}, u32[]{:S(2)}, u32[]{:S(2)}) %collective-permute-start.53) | collective-permute-done | bytes 208928 | tf_op jit(solution)/shard_map/ppermute | solution.py:174
  181.1 2.3 collective-permute-start.55
  184.8 4.3 %collective-permute-start.57 = (bf16[1024,128]{1,0:T(8,128)(2,1)S(1)}, bf16[1024,128]{1,0:T(8,128)(2,1)S(1)}, u32[]{:S(2)}, u32[]{:S(2)}) collective-permute-start(bf16[1024,128]{1,0:T(8,128)(2,1)S(1)} %collective-permute-done.56.refs_2_), channel_id=1, source_target_pairs={{0,4},{4,0},{8,12},{12,8},{16,20},{20,16},{24,28},{28,24},{1,5},{5... | collective-permute-start | bytes 786440 | tf_op jit(solution)/shard_map/ppermute | solution.py:174
  189.2 3.8 %collective-permute-start.59 = (bf16[1024,128]{1,0:T(8,128)(2,1)S(1)}, bf16[1024,128]{1,0:T(8,128)(2,1)S(1)}, u32[]{:S(2)}, u32[]{:S(2)}) collective-permute-start(bf16[1024,128]{1,0:T(8,128)(2,1)S(1)} %collective-permute-done.58.refs_4_), channel_id=1, source_target_pairs={{0,4},{4,0},{8,12},{12,8},{16,20},{20,16},{24,28},{28,24},{1,5},{5... | collective-permute-start | bytes 786440 | tf_op jit(solution)/shard_map/ppermute | solution.py:174
  196.5 4.0 %collective-permute-start.62 = (bf16[256,512]{1,0:T(8,128)(2,1)S(1)}, bf16[256,512]{1,0:T(8,128)(2,1)S(1)}, u32[]{:S(2)}, u32[]{:S(2)}) collective-permute-start(bf16[256,512]{1,0:T(8,128)(2,1)S(1)} %get-tuple-element.98), channel_id=1, source_target_pairs={{0,1},{1,0},{2,3},{3,2},{4,5},{5,4},{6,7},{7,6},{8,9},{9,8},{10,11... | collective-permute-start | bytes 786440 | tf_op jit(solution)/shard_map/ppermute | solution.py:174
  201.8 8.5 %collective-permute-done.62.refs_0_ = bf16[256,512]{1,0:T(8,128)(2,1)S(1)} collective-permute-done((bf16[256,512]{1,0:T(8,128)(2,1)S(1)}, bf16[256,512]{1,0:T(8,128)(2,1)S(1)}, u32[]{:S(2)}, u32[]{:S(2)}) %collective-permute-start.62) | collective-permute-done | bytes 262176 | tf_op jit(solution)/shard_map/ppermute | solution.py:174
  210.3 2.3 collective-permute-done.63.refs_1_
  212.6 12.2 %collective-permute-done.64.refs_2_ = bf16[256,512]{1,0:T(8,128)(2,1)S(1)} collective-permute-done((bf16[256,512]{1,0:T(8,128)(2,1)S(1)}, bf16[256,512]{1,0:T(8,128)(2,1)S(1)}, u32[]{:S(2)}, u32[]{:S(2)}) %collective-permute-start.64) | collective-permute-done | bytes 262176 | tf_op jit(solution)/shard_map/ppermute | solution.py:174
  227.0 3.8 %collective-permute-start.66 = (bf16[128,512]{1,0:T(8,128)(2,1)S(1)}, bf16[128,512]{1,0:T(8,128)(2,1)S(1)}, u32[]{:S(2)}, u32[]{:S(2)}) collective-permute-start(bf16[128,512]{1,0:T(8,128)(2,1)S(1)} %get-tuple-element.102), channel_id=1, source_target_pairs={{0,4},{1,12},{2,20},{3,28},{4,0},{5,8},{6,16},{7,24},{8,5},{9,13},... | collective-permute-start | bytes 393224 | tf_op jit(solution)/shard_map/ppermute | solution.py:616
  230.7 9.2 %collective-permute-done.65 = bf16[128,512]{1,0:T(8,128)(2,1)S(1)} collective-permute-done((bf16[128,512]{1,0:T(8,128)(2,1)S(1)}, bf16[128,512]{1,0:T(8,128)(2,1)S(1)}, u32[]{:S(2)}, u32[]{:S(2)}) %collective-permute-start.65) | collective-permute-done | bytes 131104 | tf_op jit(solution)/shard_map/ppermute | solution.py:616
  240.0 2.8 %collective-permute-done.66 = bf16[128,512]{1,0:T(8,128)(2,1)S(1)} collective-permute-done((bf16[128,512]{1,0:T(8,128)(2,1)S(1)}, bf16[128,512]{1,0:T(8,128)(2,1)S(1)}, u32[]{:S(2)}, u32[]{:S(2)}) %collective-permute-start.66) | collective-permute-done | bytes 131104 | tf_op jit(solution)/shard_map/ppermute | solution.py:616
  (145 shorter events, 78.8 us)
Async XLA Ops:
  2.5 13.3 %collective-permute-start.5 = (bf16[128,1024]{1,0:T(8,128)(2,1)}, bf16[128,1024]{1,0:T(8,128)(2,1)S(1)}, u32[]{:S(2)}, u32[]{:S(2)}) collective-permute-start(bf16[128,1024]{1,0:T(8,128)(2,1)} %refs_0_.4), channel_id=1, source_target_pairs={{0,24},{4,28},{8,16},{12,20},{16,8},{20,12},{24,0},{28,4},{1,25},{... | collective-permute-start | bytes 786440 | tf_op jit(solution)/shard_map/ppermute | solution.py:174
  2.6 14.0 %collective-permute-start = (bf16[128,1024]{1,0:T(8,128)(2,1)}, bf16[128,1024]{1,0:T(8,128)(2,1)S(1)}, u32[]{:S(2)}, u32[]{:S(2)}) collective-permute-start(bf16[128,1024]{1,0:T(8,128)(2,1)} %refs_0_.4), channel_id=1, source_target_pairs={{0,4},{4,0},{8,12},{12,8},{16,20},{20,16},{24,28},{28,24},{1,5},{5... | collective-permute-start | bytes 786440 | tf_op jit(solution)/shard_map/ppermute | solution.py:174
  4.2 19.8 %collective-permute-start.7 = (bf16[128,1024]{1,0:T(8,128)(2,1)}, bf16[128,1024]{1,0:T(8,128)(2,1)S(1)}, u32[]{:S(2)}, u32[]{:S(2)}) collective-permute-start(bf16[128,1024]{1,0:T(8,128)(2,1)} %refs_0_.5), channel_id=1, source_target_pairs={{0,4},{4,0},{8,12},{12,8},{16,20},{20,16},{24,28},{28,24},{1,5},{5... | collective-permute-start | bytes 786440 | tf_op jit(solution)/shard_map/ppermute | solution.py:174
  22.8 26.0 %collective-permute-start.14 = (bf16[512,1024]{1,0:T(8,128)(2,1)S(1)}, bf16[512,1024]{1,0:T(8,128)(2,1)S(1)}, u32[]{:S(2)}, u32[]{:S(2)}) collective-permute-start(bf16[512,1024]{1,0:T(8,128)(2,1)S(1)} %copy-done.2), channel_id=1, source_target_pairs={{0,4},{4,0},{8,12},{12,8},{16,20},{20,16},{24,28},{28,24},{1,5},{5... | collective-permute-start | bytes 3145736 | tf_op jit(solution)/shard_map/ppermute | solution.py:174
  23.9 25.0 %collective-permute-start.15 = (bf16[512,1024]{1,0:T(8,128)(2,1)S(1)}, bf16[512,1024]{1,0:T(8,128)(2,1)S(1)}, u32[]{:S(2)}, u32[]{:S(2)}) collective-permute-start(bf16[512,1024]{1,0:T(8,128)(2,1)S(1)} %copy-done.3), channel_id=1, source_target_pairs={{0,4},{4,0},{8,12},{12,8},{16,20},{20,16},{24,28},{28,24},{1,5},{5... | collective-permute-start | bytes 3145736 | tf_op jit(solution)/shard_map/ppermute | solution.py:174
  25.1 12.1 %collective-permute-start.18 = (bf16[128,1024]{1,0:T(8,128)(2,1)S(1)}, bf16[128,1024]{1,0:T(8,128)(2,1)S(1)}, u32[]{:S(2)}, u32[]{:S(2)}) collective-permute-start(bf16[128,1024]{1,0:T(8,128)(2,1)S(1)} %copy-done.10), channel_id=1, source_target_pairs={{0,8},{4,12},{8,0},{12,4},{16,24},{20,28},{24,16},{28,20},{1,9},{5... | collective-permute-start | bytes 786440 | tf_op jit(solution)/shard_map/ppermute | solution.py:174
  25.8 13.4 %collective-permute-start.20 = (bf16[128,1024]{1,0:T(8,128)(2,1)S(1)}, bf16[128,1024]{1,0:T(8,128)(2,1)S(1)}, u32[]{:S(2)}, u32[]{:S(2)}) collective-permute-start(bf16[128,1024]{1,0:T(8,128)(2,1)S(1)} %copy-done.10), channel_id=1, source_target_pairs={{0,16},{4,20},{8,24},{12,28},{16,0},{20,4},{24,8},{28,12},{1,17},{... | collective-permute-start | bytes 786440 | tf_op jit(solution)/shard_map/ppermute | solution.py:174
  32.4 22.4 %collective-permute-start.16 = (bf16[512,1024]{1,0:T(8,128)(2,1)}, bf16[512,1024]{1,0:T(8,128)(2,1)S(1)}, u32[]{:S(2)}, u32[]{:S(2)}) collective-permute-start(bf16[512,1024]{1,0:T(8,128)(2,1)} %refs_4_.1), channel_id=1, source_target_pairs={{0,4},{4,0},{8,12},{12,8},{16,20},{20,16},{24,28},{28,24},{1,5},{5... | collective-permute-start | bytes 3145736 | tf_op jit(solution)/shard_map/ppermute | solution.py:174
  70.1 14.3 %collective-permute-start.31 = (bf16[128,1024]{1,0:T(8,128)(2,1)S(1)}, bf16[128,1024]{1,0:T(8,128)(2,1)S(1)}, u32[]{:S(2)}, u32[]{:S(2)}) collective-permute-start(bf16[128,1024]{1,0:T(8,128)(2,1)S(1)} %maximum_add_fusion.refs_0_), channel_id=1, source_target_pairs={{0,24},{4,28},{8,16},{12,20},{16,8},{20,12},{24,0},{28,4},{1,25},{... | collective-permute-start | bytes 786440 | tf_op jit(solution)/shard_map/ppermute | solution.py:174
  71.4 13.1 %collective-permute-start.26 = (bf16[128,1024]{1,0:T(8,128)(2,1)S(1)}, bf16[128,1024]{1,0:T(8,128)(2,1)S(1)}, u32[]{:S(2)}, u32[]{:S(2)}) collective-permute-start(bf16[128,1024]{1,0:T(8,128)(2,1)S(1)} %maximum_add_fusion.refs_0_), channel_id=1, source_target_pairs={{0,4},{4,0},{8,12},{12,8},{16,20},{20,16},{24,28},{28,24},{1,5},{5... | collective-permute-start | bytes 786440 | tf_op jit(solution)/shard_map/ppermute | solution.py:174
  87.4 18.8 %collective-permute-start.35 = (bf16[256,512]{1,0:T(8,128)(2,1)S(1)}, bf16[256,512]{1,0:T(8,128)(2,1)S(1)}, u32[]{:S(2)}, u32[]{:S(2)}) collective-permute-start(bf16[256,512]{1,0:T(8,128)(2,1)S(1)} %get-tuple-element.70), channel_id=1, source_target_pairs={{0,3},{1,2},{2,1},{3,0},{4,7},{5,6},{6,5},{7,4},{8,11},{9,10},{10,... | collective-permute-start | bytes 786440 | tf_op jit(solution)/shard_map/ppermute | solution.py:174
  88.7 22.2 %collective-permute-start.34 = (bf16[256,512]{1,0:T(8,128)(2,1)S(1)}, bf16[256,512]{1,0:T(8,128)(2,1)S(1)}, u32[]{:S(2)}, u32[]{:S(2)}) collective-permute-start(bf16[256,512]{1,0:T(8,128)(2,1)S(1)} %get-tuple-element.69), channel_id=1, source_target_pairs={{0,2},{1,3},{2,0},{3,1},{4,6},{5,7},{6,4},{7,5},{8,10},{9,11},{10,... | collective-permute-start | bytes 786440 | tf_op jit(solution)/shard_map/ppermute | solution.py:174
  89.8 21.1 %collective-permute-start.33 = (bf16[256,512]{1,0:T(8,128)(2,1)S(1)}, bf16[256,512]{1,0:T(8,128)(2,1)S(1)}, u32[]{:S(2)}, u32[]{:S(2)}) collective-permute-start(bf16[256,512]{1,0:T(8,128)(2,1)S(1)} %get-tuple-element.68), channel_id=1, source_target_pairs={{0,1},{1,0},{2,3},{3,2},{4,5},{5,4},{6,7},{7,6},{8,9},{9,8},{10,11... | collective-permute-start | bytes 786440 | tf_op jit(solution)/shard_map/ppermute | solution.py:174
  121.7 13.9 %collective-permute-start.45 = (bf16[256,512]{1,0:T(8,128)(2,1)S(1)}, bf16[256,512]{1,0:T(8,128)(2,1)S(1)}, u32[]{:S(2)}, u32[]{:S(2)}) collective-permute-start(bf16[256,512]{1,0:T(8,128)(2,1)S(1)} %add_convert_fusion.rows_own.hidden), channel_id=1, source_target_pairs={{0,2},{1,3},{2,0},{3,1},{4,6},{5,7},{6,4},{7,5},{8,10},{9,11},{10,... | collective-permute-start | bytes 786440 | tf_op jit(solution)/shard_map/ppermute | solution.py:174
  124.1 13.8 %collective-permute-start.37 = (bf16[272,384]{1,0:T(8,128)(2,1)S(1)}, bf16[272,384]{1,0:T(8,128)(2,1)S(1)}, u32[]{:S(2)}, u32[]{:S(2)}) collective-permute-start(bf16[272,384]{1,0:T(8,128)(2,1)S(1)} %get-tuple-element.76), channel_id=1, source_target_pairs={{0,8},{4,12},{8,0},{12,4},{16,24},{20,28},{24,16},{28,20},{1,9},{5... | collective-permute-start | bytes 626696 | tf_op jit(solution)/shard_map/ppermute | solution.py:174
  135.5 13.8 %collective-permute-start.50 = (bf16[256,512]{1,0:T(8,128)(2,1)S(1)}, bf16[256,512]{1,0:T(8,128)(2,1)S(1)}, u32[]{:S(2)}, u32[]{:S(2)}) collective-permute-start(bf16[256,512]{1,0:T(8,128)(2,1)S(1)} %add_convert_fusion.rows_own.hidden), channel_id=1, source_target_pairs={{0,3},{1,2},{2,1},{3,0},{4,7},{5,6},{6,5},{7,4},{8,11},{9,10},{10,... | collective-permute-start | bytes 786440 | tf_op jit(solution)/shard_map/ppermute | solution.py:174
  135.8 14.8 %collective-permute-start.46 = (bf16[256,512]{1,0:T(8,128)(2,1)S(1)}, bf16[256,512]{1,0:T(8,128)(2,1)S(1)}, u32[]{:S(2)}, u32[]{:S(2)}) collective-permute-start(bf16[256,512]{1,0:T(8,128)(2,1)S(1)} %collective-permute-done.45.rows_own), channel_id=1, source_target_pairs={{0,4},{4,0},{8,12},{12,8},{16,20},{20,16},{24,28},{28,24},{1,5},{5... | collective-permute-start | bytes 786440 | tf_op jit(solution)/shard_map/ppermute | solution.py:174
  136.6 11.3 %collective-permute-start.38 = (bf16[272,384]{1,0:T(8,128)(2,1)S(1)}, bf16[272,384]{1,0:T(8,128)(2,1)S(1)}, u32[]{:S(2)}, u32[]{:S(2)}) collective-permute-start(bf16[272,384]{1,0:T(8,128)(2,1)S(1)} %get-tuple-element.77), channel_id=1, source_target_pairs={{0,16},{4,20},{8,24},{12,28},{16,0},{20,4},{24,8},{28,12},{1,17},{... | collective-permute-start | bytes 626696 | tf_op jit(solution)/shard_map/ppermute | solution.py:174
  136.6 11.3 %collective-permute-start.39 = (bf16[272,384]{1,0:T(8,128)(2,1)S(1)}, bf16[272,384]{1,0:T(8,128)(2,1)S(1)}, u32[]{:S(2)}, u32[]{:S(2)}) collective-permute-start(bf16[272,384]{1,0:T(8,128)(2,1)S(1)} %get-tuple-element.78), channel_id=1, source_target_pairs={{0,24},{4,28},{8,16},{12,20},{16,8},{20,12},{24,0},{28,4},{1,25},{... | collective-permute-start | bytes 626696 | tf_op jit(solution)/shard_map/ppermute | solution.py:174
  138.0 11.3 %collective-permute-start.42 = (bf16[272,384]{1,0:T(8,128)(2,1)S(1)}, bf16[272,384]{1,0:T(8,128)(2,1)S(1)}, u32[]{:S(2)}, u32[]{:S(2)}) collective-permute-start(bf16[272,384]{1,0:T(8,128)(2,1)S(1)} %get-tuple-element.82), channel_id=1, source_target_pairs={{0,8},{4,12},{8,0},{12,4},{16,24},{20,28},{24,16},{28,20},{1,9},{5... | collective-permute-start | bytes 626696 | tf_op jit(solution)/shard_map/ppermute | solution.py:174
  147.9 10.6 %collective-permute-start.43 = (bf16[272,384]{1,0:T(8,128)(2,1)S(1)}, bf16[272,384]{1,0:T(8,128)(2,1)S(1)}, u32[]{:S(2)}, u32[]{:S(2)}) collective-permute-start(bf16[272,384]{1,0:T(8,128)(2,1)S(1)} %get-tuple-element.83), channel_id=1, source_target_pairs={{0,16},{4,20},{8,24},{12,28},{16,0},{20,4},{24,8},{28,12},{1,17},{... | collective-permute-start | bytes 626696 | tf_op jit(solution)/shard_map/ppermute | solution.py:174
  147.9 11.9 %collective-permute-start.44 = (bf16[272,384]{1,0:T(8,128)(2,1)S(1)}, bf16[272,384]{1,0:T(8,128)(2,1)S(1)}, u32[]{:S(2)}, u32[]{:S(2)}) collective-permute-start(bf16[272,384]{1,0:T(8,128)(2,1)S(1)} %get-tuple-element.84), channel_id=1, source_target_pairs={{0,24},{4,28},{8,16},{12,20},{16,8},{20,12},{24,0},{28,4},{1,25},{... | collective-permute-start | bytes 626696 | tf_op jit(solution)/shard_map/ppermute | solution.py:174
  153.2 12.1 %collective-permute-start.48 = (bf16[272,384]{1,0:T(8,128)(2,1)S(1)}, bf16[272,384]{1,0:T(8,128)(2,1)S(1)}, u32[]{:S(2)}, u32[]{:S(2)}) collective-permute-start(bf16[272,384]{1,0:T(8,128)(2,1)S(1)} %get-tuple-element.89), channel_id=1, source_target_pairs={{0,16},{4,20},{8,24},{12,28},{16,0},{20,4},{24,8},{28,12},{1,17},{... | collective-permute-start | bytes 626696 | tf_op jit(solution)/shard_map/ppermute | solution.py:174
  161.8 14.6 %collective-permute-start.53 = (bf16[272,384]{1,0:T(8,128)(2,1)S(1)}, bf16[272,384]{1,0:T(8,128)(2,1)S(1)}, u32[]{:S(2)}, u32[]{:S(2)}) collective-permute-start(bf16[272,384]{1,0:T(8,128)(2,1)S(1)} %get-tuple-element.95), channel_id=1, source_target_pairs={{0,16},{4,20},{8,24},{12,28},{16,0},{20,4},{24,8},{28,12},{1,17},{... | collective-permute-start | bytes 626696 | tf_op jit(solution)/shard_map/ppermute | solution.py:174
  162.5 13.9 %collective-permute-start.54 = (bf16[272,384]{1,0:T(8,128)(2,1)S(1)}, bf16[272,384]{1,0:T(8,128)(2,1)S(1)}, u32[]{:S(2)}, u32[]{:S(2)}) collective-permute-start(bf16[272,384]{1,0:T(8,128)(2,1)S(1)} %get-tuple-element.96), channel_id=1, source_target_pairs={{0,24},{4,28},{8,16},{12,20},{16,8},{20,12},{24,0},{28,4},{1,25},{... | collective-permute-start | bytes 626696 | tf_op jit(solution)/shard_map/ppermute | solution.py:174
  180.1 12.9 %collective-permute-start.60 = (bf16[1024,128]{1,0:T(8,128)(2,1)S(1)}, bf16[1024,128]{1,0:T(8,128)(2,1)S(1)}, u32[]{:S(2)}, u32[]{:S(2)}) collective-permute-start(bf16[1024,128]{1,0:T(8,128)(2,1)S(1)} %shard_map.127.refs_0_), channel_id=1, source_target_pairs={{0,24},{4,28},{8,16},{12,20},{16,8},{20,12},{24,0},{28,4},{1,25},{... | collective-permute-start | bytes 786440 | tf_op jit(solution)/shard_map/ppermute | solution.py:174
  181.1 11.9 %collective-permute-start.55 = (bf16[1024,128]{1,0:T(8,128)(2,1)S(1)}, bf16[1024,128]{1,0:T(8,128)(2,1)S(1)}, u32[]{:S(2)}, u32[]{:S(2)}) collective-permute-start(bf16[1024,128]{1,0:T(8,128)(2,1)S(1)} %shard_map.127.refs_0_), channel_id=1, source_target_pairs={{0,4},{4,0},{8,12},{12,8},{16,20},{20,16},{24,28},{28,24},{1,5},{5... | collective-permute-start | bytes 786440 | tf_op jit(solution)/shard_map/ppermute | solution.py:174
  196.5 13.8 %collective-permute-start.62 = (bf16[256,512]{1,0:T(8,128)(2,1)S(1)}, bf16[256,512]{1,0:T(8,128)(2,1)S(1)}, u32[]{:S(2)}, u32[]{:S(2)}) collective-permute-start(bf16[256,512]{1,0:T(8,128)(2,1)S(1)} %get-tuple-element.98), channel_id=1, source_target_pairs={{0,1},{1,0},{2,3},{3,2},{4,5},{5,4},{6,7},{7,6},{8,9},{9,8},{10,11... | collective-permute-start | bytes 786440 | tf_op jit(solution)/shard_map/ppermute | solution.py:174
  200.6 12.1 %collective-permute-start.63 = (bf16[256,512]{1,0:T(8,128)(2,1)S(1)}, bf16[256,512]{1,0:T(8,128)(2,1)S(1)}, u32[]{:S(2)}, u32[]{:S(2)}) collective-permute-start(bf16[256,512]{1,0:T(8,128)(2,1)S(1)} %get-tuple-element.99), channel_id=1, source_target_pairs={{0,2},{1,3},{2,0},{3,1},{4,6},{5,7},{6,4},{7,5},{8,10},{9,11},{10,... | collective-permute-start | bytes 786440 | tf_op jit(solution)/shard_map/ppermute | solution.py:174
  200.7 24.1 %collective-permute-start.64 = (bf16[256,512]{1,0:T(8,128)(2,1)S(1)}, bf16[256,512]{1,0:T(8,128)(2,1)S(1)}, u32[]{:S(2)}, u32[]{:S(2)}) collective-permute-start(bf16[256,512]{1,0:T(8,128)(2,1)S(1)} %get-tuple-element.100), channel_id=1, source_target_pairs={{0,3},{1,2},{2,1},{3,0},{4,7},{5,6},{6,5},{7,4},{8,11},{9,10},{10,... | collective-permute-start | bytes 786440 | tf_op jit(solution)/shard_map/ppermute | solution.py:174
  225.0 14.9 %collective-permute-start.65 = (bf16[128,512]{1,0:T(8,128)(2,1)S(1)}, bf16[128,512]{1,0:T(8,128)(2,1)S(1)}, u32[]{:S(2)}, u32[]{:S(2)}) collective-permute-start(bf16[128,512]{1,0:T(8,128)(2,1)S(1)} %get-tuple-element.101), channel_id=1, source_target_pairs={{0,0},{1,8},{2,16},{3,24},{4,4},{5,12},{6,20},{7,28},{8,1},{9,9},{... | collective-permute-start | bytes 393224 | tf_op jit(solution)/shard_map/ppermute | solution.py:616
  227.0 15.8 %collective-permute-start.66 = (bf16[128,512]{1,0:T(8,128)(2,1)S(1)}, bf16[128,512]{1,0:T(8,128)(2,1)S(1)}, u32[]{:S(2)}, u32[]{:S(2)}) collective-permute-start(bf16[128,512]{1,0:T(8,128)(2,1)S(1)} %get-tuple-element.102), channel_id=1, source_target_pairs={{0,4},{1,12},{2,20},{3,28},{4,0},{5,8},{6,16},{7,24},{8,5},{9,13},... | collective-permute-start | bytes 393224 | tf_op jit(solution)/shard_map/ppermute | solution.py:616
  (46 other events, 406.6 us)

commit v5 on v4

--- a/solution.py
+++ b/solution.py
@@ -223,10 +223,25 @@
         whole[aligned(index, piece.shape[0]), :] = piece[...]
 
 
-def plane_rows(pieces, whole):
+def stack_kernel(*refs):
+    sources, stacked, semaphores = refs[:-2], refs[-2], refs[-1]
+    height = sources[0].shape[0]
+    copies = fetched(
+        [(s, stacked.at[n * height : (n + 1) * height, :]) for n, s in enumerate(sources)],
+        semaphores,
+    )
+    for copy in copies:
+        copy.wait()
+
+
+def plane_rows(pieces, whole, part=0):
     chip, core, _ = place()
+    height = whole.shape[0] // len(pieces)
     return [
-        (piece, whole.at[aligned(2 * (chip ^ (n // 2)) + (core ^ (n % 2)), piece.shape[0]), :])
+        (
+            piece.at[part * height : (part + 1) * height, :],
+            whole.at[aligned(2 * (chip ^ (n // 2)) + (core ^ (n % 2)), height), :],
+        )
         for n, piece in enumerate(pieces)
     ]
 
@@ -244,65 +259,53 @@
     query[...] = dot(pooled, whole[...]).astype(jnp.bfloat16)
 
 
-def score_kernel(count, tile, slot_row, query, states, *refs):
-    pieces, (raw, totals, held, whole, semaphores) = refs[:count], refs[count:]
+def cross_kernel(count, tile, slot_row, query, states, *refs):
+    pieces, (own, above, below, *scratch) = refs[:count], refs[count:]
+    held, key_weight, value_weight, totals, summed, semaphores = scratch
     slots, width = query.shape
+    spill = above.shape[0]
     head_count = width // HEAD_DIM
-    copies = fetched([(states, held), *plane_rows(pieces, whole)], semaphores)
+    pairs = [(states, held)]
+    for part, weight in enumerate((key_weight, value_weight)):
+        pairs += plane_rows(pieces, weight, part)
+    copies = fetched(pairs, semaphores)
     totals[...] = jnp.zeros_like(totals)
+    summed[...] = jnp.zeros_like(summed)
     for copy in copies:
         copy.wait()
 
     @pl.loop(0, states.shape[0] // tile)
     def _(step):
         span = aligned(step, tile)
-        keys = dot(held[span, :], whole[...]).astype(jnp.bfloat16).astype(jnp.float32)
+        block = held[span, :]
+        keys = dot(block, key_weight[...]).astype(jnp.bfloat16).astype(jnp.float32)
         index = lax.broadcasted_iota(jnp.int32, (slots, tile), 0)
-        turned = (index == slot_row[:, span]).astype(jnp.bfloat16)
+        onehot = (index == slot_row[:, span]).astype(jnp.bfloat16)
         product = keys * lax.dot_general(
-            turned, query[...], (((0,), (0,)), ((), ())), preferred_element_type=jnp.float32
+            onehot, query[...], (((0,), (0,)), ((), ())), preferred_element_type=jnp.float32
         )
         lane = lax.broadcasted_iota(jnp.int32, (tile, HEAD_DIM), 1)
         scores = jnp.zeros((tile, HEAD_DIM), jnp.float32)
         for head in range(head_count):
-            summed = jnp.sum(
+            total = jnp.sum(
                 product[:, head * HEAD_DIM : (head + 1) * HEAD_DIM], axis=1, keepdims=True
             )
-            scores = jnp.where(lane == head, summed, scores)
-        values = capped_exp(scores / math.sqrt(HEAD_DIM))
-        raw[span, :] = values
-        high = values.astype(jnp.bfloat16)
-        low = (values - high.astype(jnp.float32)).astype(jnp.bfloat16)
-        totals[...] += dot(turned, high) + dot(turned, low)
-
-
-def value_kernel(count, tile, slot_row, raw, totals, states, *refs):
-    pieces, (own, above, below, held, whole, summed, semaphores) = refs[:count], refs[count:]
-    slots = totals.shape[0]
-    copies = fetched([(states, held), *plane_rows(pieces, whole)], semaphores)
-    spill = above.shape[0]
-    head_count = whole.shape[1] // HEAD_DIM
-    summed[...] = jnp.zeros_like(summed)
-    for copy in copies:
-        copy.wait()
-
-    @pl.loop(0, states.shape[0] // tile)
-    def _(step):
-        span = aligned(step, tile)
-        values = dot(held[span, :], whole[...]).astype(jnp.bfloat16).astype(jnp.float32)
-        factors = raw[span, :]
+            scores = jnp.where(lane == head, total, scores)
+        raw = capped_exp(scores / math.sqrt(HEAD_DIM))
+        high = raw.astype(jnp.bfloat16)
+        low = (raw - high.astype(jnp.float32)).astype(jnp.bfloat16)
+        totals[...] += dot(onehot, high) + dot(onehot, low)
+        values = dot(block, value_weight[...]).astype(jnp.bfloat16).astype(jnp.float32)
         weighted = jnp.concatenate(
             [
-                (values[:, h * HEAD_DIM : (h + 1) * HEAD_DIM] * factors[:, h : h + 1]).astype(
+                (values[:, h * HEAD_DIM : (h + 1) * HEAD_DIM] * raw[:, h : h + 1]).astype(
                     jnp.bfloat16
                 )
                 for h in range(head_count)
             ],
             axis=1,
         )
-        index = lax.broadcasted_iota(jnp.int32, (slots, tile), 0)
-        turned = (index == slot_row[:, span]).astype(jnp.bfloat16)
-        summed[...] += dot(turned, weighted)
+        summed[...] += dot(onehot, weighted)
 
     total = totals[...]
     inverse = 1.0 / jnp.where(total > 0.0, total, 1.0)
@@ -363,49 +366,63 @@
     )
 
 
-def project_kernel(rows_own, rows_other, gain, *refs):
+def project_kernel(count, gain, *refs):
+    blocks, refs = refs[: 2 * count], refs[2 * count :]
     chips = (len(refs) - 1) // 2
     weights, outs, left = refs[:chips], refs[chips:-1], refs[-1]
     seq = lax.axis_index("seq")
-    height, width = rows_own.shape
-    total = jnp.zeros((height, 1), jnp.float32)
-    for n, block in enumerate((rows_own, rows_other)):
-        hidden = block[...].astype(jnp.float32)
-        total += jnp.sum(hidden * hidden, axis=1, keepdims=True)
-        left[:, n * width : (n + 1) * width] = (
-            hidden * gain[:, aligned(seq ^ n, width)]
-        ).astype(jnp.bfloat16)
+    part, width = blocks[0].shape
+    height = count * part
+    totals = []
+    for q in range(count):
+        total = jnp.zeros((part, 1), jnp.float32)
+        for n, block in enumerate(blocks[2 * q : 2 * q + 2]):
+            hidden = block[...].astype(jnp.float32)
+            total += jnp.sum(hidden * hidden, axis=1, keepdims=True)
+            left[q * part : (q + 1) * part, n * width : (n + 1) * width] = (
+                hidden * gain[:, aligned(seq ^ n, width)]
+            ).astype(jnp.bfloat16)
+        totals.append(jnp.sum(jnp.where(diagonal(part), total, 0.0), axis=0, keepdims=True))
     for weight, out in reversed(list(zip(weights, outs))):
         out[:height, :] = dot(left[...], weight[...]).astype(out.dtype)
-    row = jnp.sum(jnp.where(diagonal(height), total, 0.0), axis=0, keepdims=True)
-    outs[0][height:, :height] = jnp.broadcast_to(row, (outs[0].shape[0] - height, height))
-    high = row.astype(jnp.bfloat16).astype(jnp.float32)
-    middle = (row - high).astype(jnp.bfloat16).astype(jnp.float32)
-    low = row - high - middle
-    index = lax.broadcasted_iota(jnp.int32, (outs[1].shape[0] - height, height), 0)
-    terms = jnp.where(index == 0, high, jnp.where(index == 1, middle, low)).astype(jnp.bfloat16)
+    outs[0][height:, :] = jnp.zeros((outs[0].shape[0] - height, outs[0].shape[1]), jnp.float32)
     for out in outs[1:]:
-        out[height:, :height] = terms
-
-
-def attention_kernel(parts, chips, depth, *refs):
-    shares, attended, (query, key, value) = refs[: parts * chips], refs[-4], refs[-3:]
+        out[height:, :] = jnp.zeros((out.shape[0] - height, out.shape[1]), jnp.bfloat16)
+    index = lax.broadcasted_iota(jnp.int32, (16, part), 0)
+    own_sums, sent_sums = jnp.zeros((8, part), jnp.float32), jnp.zeros((16, part), jnp.float32)
+    for q, row in enumerate(totals):
+        high = row.astype(jnp.bfloat16).astype(jnp.float32)
+        middle = (row - high).astype(jnp.bfloat16).astype(jnp.float32)
+        own_sums = jnp.where(index[:8] == q, row, own_sums)
+        for m, term in enumerate((high, middle, row - high - middle)):
+            sent_sums = jnp.where(index == 3 * q + m, term, sent_sums)
+    outs[0][height:, :part] = own_sums
+    for out in outs[1:]:
+        out[height:, :part] = sent_sums.astype(jnp.bfloat16)
+
+
+def attention_kernel(groups, chips, depth, *refs):
+    shares, attended, (query, key, value) = refs[: len(groups) * chips], refs[-4], refs[-3:]
     _, _, tensor = place()
+    parts = sum(len(group) for group in groups)
     height = attended.shape[0] // parts
     own_place = diagonal(height)
-    for r in range(parts):
-        total = shares[r * chips][:height, :]
-        row = shares[r * chips][height : height + 1, :height]
-        for d in range(1, chips):
-            share = shares[r * chips + d]
-            total += share[:height, :].astype(jnp.float32)
-            terms = share[height:, :height].astype(jnp.float32)
-            row += terms[0:1] + terms[1:2] + terms[2:3]
-        column = jnp.sum(jnp.where(own_place, row, 0.0), axis=1, keepdims=True)
-        total = (total * lax.rsqrt(column / depth + norm_eps)).astype(jnp.bfloat16)
-        span = aligned(tensor ^ r, height)
-        for m, kept in enumerate((query, key, value)):
-            kept[span, :] = total[:, m * HEAD_DIM : (m + 1) * HEAD_DIM]
+    for g, group in enumerate(groups):
+        end = len(group) * height
+        own, *received = shares[g * chips : (g + 1) * chips]
+        for q, r in enumerate(group):
+            rows = slice(q * height, (q + 1) * height)
+            total = own[rows, :]
+            row = own[end:, :height][q : q + 1]
+            for share in received:
+                total += share[rows, :].astype(jnp.float32)
+                terms = share[end:, :height].astype(jnp.float32)
+                row += sum(terms[3 * q + m : 3 * q + m + 1] for m in range(3))
+            column = jnp.sum(jnp.where(own_place, row, 0.0), axis=1, keepdims=True)
+            total = (total * lax.rsqrt(column / depth + norm_eps)).astype(jnp.bfloat16)
+            span = aligned(tensor ^ r, height)
+            for m, kept in enumerate((query, key, value)):
+                kept[span, :] = total[:, m * HEAD_DIM : (m + 1) * HEAD_DIM]
     causal = lax.broadcasted_iota(jnp.int32, (height, height), 0) >= lax.broadcasted_iota(
         jnp.int32, (height, height), 1
     )
@@ -468,11 +485,11 @@
     bf16, f32 = jnp.bfloat16, jnp.float32
     tile = min(256, byte_count)
 
-    def over_plane(block):
+    def over_plane(block, earlier=()):
         pieces = []
         for d in range(chip_count):
             moved = exchanged(block, "seq", 2 * d) if d else block
-            pieces += [moved, core_swapped(moved)]
+            pieces += [moved, core_swapped(after(moved, *earlier) if d else moved)]
         return pieces
 
     slot_of = byte_patch - (seq * patch_dev - spill)
@@ -482,8 +499,14 @@
         jnp.concatenate([edge, patch_len, edge]), seq * patch_dev, slot_count
     ).astype(f32)[:, None]
     query_pieces = over_plane(cross_query)
-    key_pieces = over_plane(cross_key)
-    value_pieces = over_plane(cross_value)
+    (stacked,) = call(
+        stack_kernel,
+        [((2 * cross_key.shape[0], local_width), bf16)],
+        cross_key,
+        cross_value,
+        far=2,
+        scratch=[pltpu.SemaphoreType.DMA((2,))],
+    )
     (query_slots,) = call(
         functools.partial(query_kernel, seq_count),
         [((slot_count, local_width), bf16)],
@@ -499,24 +522,29 @@
         ],
         flops=2 * slot_count * byte_width * (byte_count + local_width),
     )
-    raw, totals = call(
-        functools.partial(score_kernel, seq_count, tile),
-        [((byte_count, HEAD_DIM), f32), ((slot_count, HEAD_DIM), f32)],
+    own, above, below = call(
+        functools.partial(cross_kernel, seq_count, tile),
+        [((height, local_width), bf16) for height in (patch_dev, spill, spill)],
         slot_row,
         query_slots,
         byte_states,
-        *key_pieces,
+        *over_plane(stacked, (query_slots,)),
         far=1 + seq_count,
         scratch=[
             pltpu.VMEM((byte_count, byte_width), bf16),
             pltpu.VMEM((byte_width, local_width), bf16),
-            pltpu.SemaphoreType.DMA((1 + seq_count,)),
+            pltpu.VMEM((byte_width, local_width), bf16),
+            pltpu.VMEM((slot_count, HEAD_DIM), f32),
+            pltpu.VMEM((slot_count, local_width), f32),
+            pltpu.SemaphoreType.DMA((1 + 2 * seq_count,)),
         ],
-        flops=2 * byte_count * local_width * (byte_width + 2 * slot_count),
-    )
+        flops=4 * byte_count * local_width * (byte_width + slot_count),
+    )
+
+    spilled = [shifted(below, "seq", 1), shifted(above, "seq", -1)]
     weights = []
     for weight in (latent_query, latent_key, latent_value):
-        weights += [weight, core_swapped(after(weight, query_slots))]
+        weights += [weight, core_swapped(after(weight, own))]
     head_weights = call(
         arrange_kernel,
         [((2 * out_width, 3 * HEAD_DIM), bf16)] * chip_count,
@@ -524,26 +552,8 @@
         far=6,
         scratch=[pltpu.SemaphoreType.DMA((6 * chip_count,))],
     )
-    raw, *head_weights = lax.optimization_barrier((raw, *head_weights))
-    own, above, below = call(
-        functools.partial(value_kernel, seq_count, tile),
-        [((rows, local_width), bf16) for rows in (patch_dev, spill, spill)],
-        slot_row,
-        raw,
-        totals,
-        byte_states,
-        *value_pieces,
-        far=1 + seq_count,
-        scratch=[
-            pltpu.VMEM((byte_count, byte_width), bf16),
-            pltpu.VMEM((byte_width, local_width), bf16),
-            pltpu.VMEM((slot_count, local_width), f32),
-            pltpu.SemaphoreType.DMA((1 + seq_count,)),
-        ],
-        flops=2 * byte_count * local_width * (byte_width + slot_count),
-    )
-
-    own = own + jnp.concatenate([shifted(below, "seq", 1), shifted(above, "seq", -1)], axis=0)
+    own, *head_weights = lax.optimization_barrier((own, *head_weights))
+    own = own + jnp.concatenate(spilled, axis=0)
 
     total, *sent = call(
         functools.partial(cross_out_kernel, seq_count),
@@ -558,31 +568,31 @@
     latent_in = total.astype(bf16)
 
     gain = norm_gain[None, :]
-    shares, block = [], latent_in
-    for r in range(tensor_count):
-        if r:
-            done = shares[(r - 2) * chip_count] if r > 1 else block
-            block = exchanged(after(latent_in, block, done), "tensor", r)
-        ready = block
-        if r == 1:
-            ready = after(block, shares[0])
-        swapped = core_swapped(ready)
-        if r > 1:
-            ready = after(block, *shares[(r - 2) * chip_count : (r - 1) * chip_count + 2])
+    groups = [[0], list(range(1, min(3, tensor_count))), list(range(3, tensor_count))]
+    groups = [group for group in groups if group]
+    shares, arrived = [], []
+    for g, group in enumerate(groups):
+        blocks = [latent_in]
+        if g:
+            start = after(latent_in, *arrived, *shares[:chip_count]) if g > 1 else latent_in
+            arrived = [exchanged(start, "tensor", r) for r in group]
+            blocks = [after(block, *shares[:chip_count]) for block in arrived]
+        height = len(group) * quarter
         share, *sent = call(
-            project_kernel,
-            [((quarter + 8, 3 * HEAD_DIM), f32)]
-            + [((quarter + 16, 3 * HEAD_DIM), bf16)] * (chip_count - 1),
-            ready,
-            swapped,
+            functools.partial(project_kernel, len(group)),
+            [((height + 8, 3 * HEAD_DIM), f32)]
+            + [((height + 16, 3 * HEAD_DIM), bf16)] * (chip_count - 1),
             gain,
+            *[piece for block in blocks for piece in (block, core_swapped(block))],
             *head_weights,
-            scratch=[pltpu.VMEM((quarter, 2 * out_width), bf16)],
-            flops=2 * quarter * 2 * out_width * 3 * HEAD_DIM * chip_count,
+            scratch=[pltpu.VMEM((height, 2 * out_width), bf16)],
+            flops=2 * height * 2 * out_width * 3 * HEAD_DIM * chip_count,
         )
+        if g > 1:
+            sent = [after(part, *shares[(g - 1) * chip_count + 1 :]) for part in sent]
         shares += [share] + [exchanged(part, "seq", 2 * d) for d, part in enumerate(sent, 1)]
     (attended,) = call(
-        functools.partial(attention_kernel, tensor_count, chip_count, out_width * seq_count),
+        functools.partial(attention_kernel, groups, chip_count, out_width * seq_count),
         [((patch_count, HEAD_DIM), bf16)],
         *shares,
         scratch=[pltpu.VMEM((patch_count, HEAD_DIM), bf16)] * 3,

time: 246 us -> 223 us (0.907)
  waiting for transfers between devices: 123 us -> 98.9 us
    ppermute x63 -> x53, waiting for transfers between devices: 109 us -> 86.5 us  [exchanged(): return lax.ppermute(block, axis, route)]
    ppermute x63 -> x53, starting transfers between devices: 80.3 us -> 78.4 us  [exchanged(): return lax.ppermute(block, axis, route)]
    pallas_call x12 -> x11, Pallas kernels: 23.7 us -> 23.8 us  [call(): pl.pallas_call(kernel, out_shape=shapes, in_specs=[pl.BlockSpec(memory_sp...]
  transfers between devices with their start and end apart: 67 -> 57, of which waited for: 28 -> 28; matrix products, arithmetic and copies ran while one was open for 1% -> 1% of each run, Pallas kernels for 6% -> 4%
where the time goes in v5:
time: 223 us; the launch traced here: 220 us
  waiting for transfers between devices  98.9 us (44%)
  starting transfers between devices  90.2 us (40%)
  Pallas kernels  23.8 us (11%)
  local copies, waits for them, and re-layouts  5.38 us (2%)
    ppermute x53, waiting for transfers between devices, exchanged(): return lax.ppermute(block, axis, route)  86.5 us
    ppermute x53, starting transfers between devices, exchanged(): return lax.ppermute(block, axis, route)  78.4 us
    pallas_call x11, Pallas kernels, call(): pl.pallas_call(kernel, out_shape=shapes, in_specs=[pl.BlockSpec(memory_sp...  23.8 us
    ppermute x2, waiting for transfers between devices, per_device(): moved.append(lax.ppermute(pieces[flip], ('seq', 'tensor'), route))  11.8 us
    ppermute x2, starting transfers between devices, per_device(): moved.append(lax.ppermute(pieces[flip], ('seq', 'tensor'), route))  5.88 us
    ppermute x2, starting transfers between devices, shifted(): return lax.ppermute(block, axis, route)  5.86 us
    unnamed x22, local copies, waits for them, and re-layouts  4.48 us
  transfers between devices with their start and end apart: 57, of which 28 were waited for; matrix products, arithmetic and copies ran while one was open for 1% of the time, Pallas kernels for 4%

profile of v5, /device:TPU:9, one launch (start us, length us, event | category | flops | bytes accessed | tf_op | source)
XLA Modules:
  0.0 220.3 jit_solution(5101700984444968666)
XLA Ops:
  4.2 3.2 %collective-permute-done.1.refs_2_ = bf16[128,1024]{1,0:T(8,128)(2,1)S(1)} collective-permute-done((bf16[128,1024]{1,0:T(8,128)(2,1)}, bf16[128,1024]{1,0:T(8,128)(2,1)S(1)}, u32[]{:S(2)}, u32[]{:S(2)}) %collective-permute-start.1) | collective-permute-done | bytes 262176 | tf_op jit(solution)/shard_map/ppermute | solution.py:174
  7.4 2.7 %collective-permute-start.2 = (bf16[128,1024]{1,0:T(8,128)(2,1)S(1)}, bf16[128,1024]{1,0:T(8,128)(2,1)S(1)}, u32[]{:S(2)}, u32[]{:S(2)}) collective-permute-start(bf16[128,1024]{1,0:T(8,128)(2,1)S(1)} %collective-permute-done.1.refs_2_), channel_id=1, source_target_pairs={{0,4},{4,0},{8,12},{12,8},{16,20},{20,16},{24,28},{28,24},{1,5},{5... | collective-permute-start | bytes 786440 | tf_op jit(solution)/shard_map/ppermute | solution.py:174
  15.9 2.1 collective-permute-start.4
  26.8 12.1 %collective-permute-start.11 = (bf16[256,1024]{1,0:T(8,128)(2,1)S(1)}, bf16[256,1024]{1,0:T(8,128)(2,1)S(1)}, u32[]{:S(2)}, u32[]{:S(2)}) collective-permute-start(bf16[256,1024]{1,0:T(8,128)(2,1)S(1)} %collective-permute-done.10.refs_4_), channel_id=1, source_target_pairs={{0,4},{4,0},{8,12},{12,8},{16,20},{20,16},{24,28},{28,24},{1,5},{5... | collective-permute-start | bytes 1572872 | tf_op jit(solution)/shard_map/ppermute | solution.py:174
  38.9 2.2 collective-permute-done.11.refs_5_
  41.4 10.2 %shard_map.120 = (bf16[128,1024]{1,0:T(8,128)(2,1)S(1)}, bf16[64,1024]{1,0:T(8,128)(2,1)S(1)}, bf16[64,1024]{1,0:T(8,128)(2,1)S(1)}) custom-call(s32[1,1024]{1,0:T(1,128)S(1)} %bitcast.7, bf16[256,1024]{1,0:T(8,128)(2,1)S(1)} %shard_map.118.query, bf16[1024,1024]{1,0:T(8,128)(2,1)S(1)} %copy-done.1, bf16[256,1024]{1,0:T(8,128)(2,1)S(1)} %shard_map.119.refs_0_, ...), custom_call_target="tpu_custom_call" | custom-call | flops 5368709120 | bytes 7344128 | tf_op jit(solution)/shard_map/pallas_call | solution.py:207
  52.6 2.0 collective-permute-start.18
  54.7 3.8 %collective-permute-start.17 = (bf16[64,1024]{1,0:T(8,128)(2,1)S(1)}, bf16[64,1024]{1,0:T(8,128)(2,1)S(1)}, u32[]{:S(2)}, u32[]{:S(2)}) collective-permute-start(bf16[64,1024]{1,0:T(8,128)(2,1)S(1)} %get-tuple-element.64), channel_id=1, source_target_pairs={{0,4},{4,8},{8,12},{12,16},{16,20},{20,24},{24,28},{1,5},{5,9},{9,... | collective-permute-start | bytes 393224 | tf_op jit(solution)/shard_map/ppermute | solution.py:22
  63.0 2.6 %collective-permute-start.19 = (bf16[128,1024]{1,0:T(8,128)(2,1)S(1)}, bf16[128,1024]{1,0:T(8,128)(2,1)S(1)}, u32[]{:S(2)}, u32[]{:S(2)}) collective-permute-start(bf16[128,1024]{1,0:T(8,128)(2,1)S(1)} %maximum_add_fusion.refs_0_), channel_id=1, source_target_pairs={{0,4},{4,0},{8,12},{12,8},{16,20},{20,16},{24,28},{28,24},{1,5},{5... | collective-permute-start | bytes 786440 | tf_op jit(solution)/shard_map/ppermute | solution.py:174
  67.4 3.0 %collective-permute-start.21 = (bf16[128,1024]{1,0:T(8,128)(2,1)S(1)}, bf16[128,1024]{1,0:T(8,128)(2,1)S(1)}, u32[]{:S(2)}, u32[]{:S(2)}) collective-permute-start(bf16[128,1024]{1,0:T(8,128)(2,1)S(1)} %collective-permute-done.20.refs_2_), channel_id=1, source_target_pairs={{0,4},{4,0},{8,12},{12,8},{16,20},{20,16},{24,28},{28,24},{1,5},{5... | collective-permute-start | bytes 786440 | tf_op jit(solution)/shard_map/ppermute | solution.py:174
  70.4 5.5 %collective-permute-start.23 = (bf16[128,1024]{1,0:T(8,128)(2,1)S(1)}, bf16[128,1024]{1,0:T(8,128)(2,1)S(1)}, u32[]{:S(2)}, u32[]{:S(2)}) collective-permute-start(bf16[128,1024]{1,0:T(8,128)(2,1)S(1)} %collective-permute-done.22.refs_4_), channel_id=1, source_target_pairs={{0,4},{4,0},{8,12},{12,8},{16,20},{20,16},{24,28},{28,24},{1,5},{5... | collective-permute-start | bytes 786440 | tf_op jit(solution)/shard_map/ppermute | solution.py:174
  82.5 15.3 %collective-permute-done.28 = bf16[256,512]{1,0:T(8,128)(2,1)S(1)} collective-permute-done((bf16[256,512]{1,0:T(8,128)(2,1)S(1)}, bf16[256,512]{1,0:T(8,128)(2,1)S(1)}, u32[]{:S(2)}, u32[]{:S(2)}) %collective-permute-start.28) | collective-permute-done | bytes 262176 | tf_op jit(solution)/shard_map/ppermute | solution.py:174
  97.7 4.7 %collective-permute-done.27 = bf16[256,512]{1,0:T(8,128)(2,1)S(1)} collective-permute-done((bf16[256,512]{1,0:T(8,128)(2,1)S(1)}, bf16[256,512]{1,0:T(8,128)(2,1)S(1)}, u32[]{:S(2)}, u32[]{:S(2)}) %collective-permute-start.27) | collective-permute-done | bytes 262176 | tf_op jit(solution)/shard_map/ppermute | solution.py:174
  103.8 2.1 collective-permute-start.33
  110.9 6.1 %collective-permute-done.33.refs_0_ = bf16[256,512]{1,0:T(8,128)(2,1)S(1)} collective-permute-done((bf16[256,512]{1,0:T(8,128)(2,1)S(1)}, bf16[256,512]{1,0:T(8,128)(2,1)S(1)}, u32[]{:S(2)}, u32[]{:S(2)}) %collective-permute-start.33) | collective-permute-done | bytes 262176 | tf_op jit(solution)/shard_map/ppermute | solution.py:174
  117.0 2.3 %collective-permute-done.32.refs_3_ = bf16[272,384]{1,0:T(8,128)(2,1)S(1)} collective-permute-done((bf16[272,384]{1,0:T(8,128)(2,1)S(1)}, bf16[272,384]{1,0:T(8,128)(2,1)S(1)}, u32[]{:S(2)}, u32[]{:S(2)}) %collective-permute-start.32) | collective-permute-done | bytes 208928 | tf_op jit(solution)/shard_map/ppermute | solution.py:174
  122.1 2.3 %shard_map.124 = (f32[520,384]{1,0:T(8,128)S(1)}, bf16[528,384]{1,0:T(8,128)(2,1)S(1)}, bf16[528,384]{1,0:T(8,128)(2,1)S(1)}, bf16[528,384]{1,0:T(8,128)(2,1)S(1)}) custom-call(f32[1,4096]{1,0:T(1,128)S(1)} %bitcast.4, bf16[256,512]{1,0:T(8,128)(2,1)S(1)} %collective-permute-done.33.refs_0_, bf16[256,512]{1,0:T(8,128)(2,1)S(1)} %collective-permute-done.34.refs_1_, ...), custom_call_target="tpu_custom_call" | custom-call | flops 1610612736 | bytes 6225920 | tf_op jit(solution)/shard_map/pallas_call | solution.py:207
  127.2 6.4 %collective-permute-done.40.refs_0_ = bf16[256,512]{1,0:T(8,128)(2,1)S(1)} collective-permute-done((bf16[256,512]{1,0:T(8,128)(2,1)S(1)}, bf16[256,512]{1,0:T(8,128)(2,1)S(1)}, u32[]{:S(2)}, u32[]{:S(2)}) %collective-permute-start.40) | collective-permute-done | bytes 262176 | tf_op jit(solution)/shard_map/ppermute | solution.py:174
  137.4 7.6 %collective-permute-done.39.refs_7_ = bf16[528,384]{1,0:T(8,128)(2,1)S(1)} collective-permute-done((bf16[528,384]{1,0:T(8,128)(2,1)S(1)}, bf16[528,384]{1,0:T(8,128)(2,1)S(1)}, u32[]{:S(2)}, u32[]{:S(2)}) %collective-permute-start.39) | collective-permute-done | bytes 405536 | tf_op jit(solution)/shard_map/ppermute | solution.py:174
  147.6 2.8 %collective-permute-done.42.refs_9_ = bf16[272,384]{1,0:T(8,128)(2,1)S(1)} collective-permute-done((bf16[272,384]{1,0:T(8,128)(2,1)S(1)}, bf16[272,384]{1,0:T(8,128)(2,1)S(1)}, u32[]{:S(2)}, u32[]{:S(2)}) %collective-permute-start.42) | collective-permute-done | bytes 208928 | tf_op jit(solution)/shard_map/ppermute | solution.py:174
  151.1 3.3 %collective-permute-done.44.refs_11_ = bf16[272,384]{1,0:T(8,128)(2,1)S(1)} collective-permute-done((bf16[272,384]{1,0:T(8,128)(2,1)S(1)}, bf16[272,384]{1,0:T(8,128)(2,1)S(1)}, u32[]{:S(2)}, u32[]{:S(2)}) %collective-permute-start.44) | collective-permute-done | bytes 208928 | tf_op jit(solution)/shard_map/ppermute | solution.py:174
  154.4 2.0 shard_map.126.refs_0_
  159.3 3.6 %collective-permute-start.45 = (bf16[1024,128]{1,0:T(8,128)(2,1)S(1)}, bf16[1024,128]{1,0:T(8,128)(2,1)S(1)}, u32[]{:S(2)}, u32[]{:S(2)}) collective-permute-start(bf16[1024,128]{1,0:T(8,128)(2,1)S(1)} %shard_map.126.refs_0_), channel_id=1, source_target_pairs={{0,4},{4,0},{8,12},{12,8},{16,20},{20,16},{24,28},{28,24},{1,5},{5... | collective-permute-start | bytes 786440 | tf_op jit(solution)/shard_map/ppermute | solution.py:174
  162.9 5.0 %collective-permute-start.47 = (bf16[1024,128]{1,0:T(8,128)(2,1)S(1)}, bf16[1024,128]{1,0:T(8,128)(2,1)S(1)}, u32[]{:S(2)}, u32[]{:S(2)}) collective-permute-start(bf16[1024,128]{1,0:T(8,128)(2,1)S(1)} %collective-permute-done.46.refs_2_), channel_id=1, source_target_pairs={{0,4},{4,0},{8,12},{12,8},{16,20},{20,16},{24,28},{28,24},{1,5},{5... | collective-permute-start | bytes 786440 | tf_op jit(solution)/shard_map/ppermute | solution.py:174
  168.0 4.5 %collective-permute-start.49 = (bf16[1024,128]{1,0:T(8,128)(2,1)S(1)}, bf16[1024,128]{1,0:T(8,128)(2,1)S(1)}, u32[]{:S(2)}, u32[]{:S(2)}) collective-permute-start(bf16[1024,128]{1,0:T(8,128)(2,1)S(1)} %collective-permute-done.48.refs_4_), channel_id=1, source_target_pairs={{0,4},{4,0},{8,12},{12,8},{16,20},{20,16},{24,28},{28,24},{1,5},{5... | collective-permute-start | bytes 786440 | tf_op jit(solution)/shard_map/ppermute | solution.py:174
  174.0 2.0 shard_map.127
  178.8 8.3 %collective-permute-done.52.refs_0_ = bf16[256,512]{1,0:T(8,128)(2,1)S(1)} collective-permute-done((bf16[256,512]{1,0:T(8,128)(2,1)S(1)}, bf16[256,512]{1,0:T(8,128)(2,1)S(1)}, u32[]{:S(2)}, u32[]{:S(2)}) %collective-permute-start.52) | collective-permute-done | bytes 262176 | tf_op jit(solution)/shard_map/ppermute | solution.py:174
  187.1 2.0 collective-permute-done.53.refs_1_
  189.1 12.5 %collective-permute-done.54.refs_2_ = bf16[256,512]{1,0:T(8,128)(2,1)S(1)} collective-permute-done((bf16[256,512]{1,0:T(8,128)(2,1)S(1)}, bf16[256,512]{1,0:T(8,128)(2,1)S(1)}, u32[]{:S(2)}, u32[]{:S(2)}) %collective-permute-start.54) | collective-permute-done | bytes 262176 | tf_op jit(solution)/shard_map/ppermute | solution.py:174
  203.7 4.0 %collective-permute-start.56 = (bf16[128,512]{1,0:T(8,128)(2,1)S(1)}, bf16[128,512]{1,0:T(8,128)(2,1)S(1)}, u32[]{:S(2)}, u32[]{:S(2)}) collective-permute-start(bf16[128,512]{1,0:T(8,128)(2,1)S(1)} %get-tuple-element.98), channel_id=1, source_target_pairs={{0,4},{1,12},{2,20},{3,28},{4,0},{5,8},{6,16},{7,24},{8,5},{9,13},... | collective-permute-start | bytes 393224 | tf_op jit(solution)/shard_map/ppermute | solution.py:626
  207.7 9.0 %collective-permute-done.55 = bf16[128,512]{1,0:T(8,128)(2,1)S(1)} collective-permute-done((bf16[128,512]{1,0:T(8,128)(2,1)S(1)}, bf16[128,512]{1,0:T(8,128)(2,1)S(1)}, u32[]{:S(2)}, u32[]{:S(2)}) %collective-permute-start.55) | collective-permute-done | bytes 131104 | tf_op jit(solution)/shard_map/ppermute | solution.py:626
  216.7 2.8 %collective-permute-done.56 = bf16[128,512]{1,0:T(8,128)(2,1)S(1)} collective-permute-done((bf16[128,512]{1,0:T(8,128)(2,1)S(1)}, bf16[128,512]{1,0:T(8,128)(2,1)S(1)}, u32[]{:S(2)}, u32[]{:S(2)}) %collective-permute-start.56) | collective-permute-done | bytes 131104 | tf_op jit(solution)/shard_map/ppermute | solution.py:626
  (124 shorter events, 62.0 us)
Async XLA Ops:
  1.2 12.1 %collective-permute-start.3 = (bf16[128,1024]{1,0:T(8,128)(2,1)}, bf16[128,1024]{1,0:T(8,128)(2,1)S(1)}, u32[]{:S(2)}, u32[]{:S(2)}) collective-permute-start(bf16[128,1024]{1,0:T(8,128)(2,1)} %refs_0_.3), channel_id=1, source_target_pairs={{0,16},{4,20},{8,24},{12,28},{16,0},{20,4},{24,8},{28,12},{1,17},{... | collective-permute-start | bytes 786440 | tf_op jit(solution)/shard_map/ppermute | solution.py:174
  2.5 12.1 %collective-permute-start.5 = (bf16[128,1024]{1,0:T(8,128)(2,1)}, bf16[128,1024]{1,0:T(8,128)(2,1)S(1)}, u32[]{:S(2)}, u32[]{:S(2)}) collective-permute-start(bf16[128,1024]{1,0:T(8,128)(2,1)} %refs_0_.3), channel_id=1, source_target_pairs={{0,24},{4,28},{8,16},{12,20},{16,8},{20,12},{24,0},{28,4},{1,25},{... | collective-permute-start | bytes 786440 | tf_op jit(solution)/shard_map/ppermute | solution.py:174
  2.6 13.3 %collective-permute-start = (bf16[128,1024]{1,0:T(8,128)(2,1)}, bf16[128,1024]{1,0:T(8,128)(2,1)S(1)}, u32[]{:S(2)}, u32[]{:S(2)}) collective-permute-start(bf16[128,1024]{1,0:T(8,128)(2,1)} %refs_0_.3), channel_id=1, source_target_pairs={{0,4},{4,0},{8,12},{12,8},{16,20},{20,16},{24,28},{28,24},{1,5},{5... | collective-permute-start | bytes 786440 | tf_op jit(solution)/shard_map/ppermute | solution.py:174
  7.4 10.7 %collective-permute-start.2 = (bf16[128,1024]{1,0:T(8,128)(2,1)S(1)}, bf16[128,1024]{1,0:T(8,128)(2,1)S(1)}, u32[]{:S(2)}, u32[]{:S(2)}) collective-permute-start(bf16[128,1024]{1,0:T(8,128)(2,1)S(1)} %collective-permute-done.1.refs_2_), channel_id=1, source_target_pairs={{0,4},{4,0},{8,12},{12,8},{16,20},{20,16},{24,28},{28,24},{1,5},{5... | collective-permute-start | bytes 786440 | tf_op jit(solution)/shard_map/ppermute | solution.py:174
  12.0 13.6 %collective-permute-start.8 = (bf16[256,1024]{1,0:T(8,128)(2,1)S(1)}, bf16[256,1024]{1,0:T(8,128)(2,1)S(1)}, u32[]{:S(2)}, u32[]{:S(2)}) collective-permute-start(bf16[256,1024]{1,0:T(8,128)(2,1)S(1)} %shard_map.119.refs_0_), channel_id=1, source_target_pairs={{0,8},{4,12},{8,0},{12,4},{16,24},{20,28},{24,16},{28,20},{1,9},{5... | collective-permute-start | bytes 1572872 | tf_op jit(solution)/shard_map/ppermute | solution.py:174
  13.3 13.5 %collective-permute-start.10 = (bf16[256,1024]{1,0:T(8,128)(2,1)S(1)}, bf16[256,1024]{1,0:T(8,128)(2,1)S(1)}, u32[]{:S(2)}, u32[]{:S(2)}) collective-permute-start(bf16[256,1024]{1,0:T(8,128)(2,1)S(1)} %shard_map.119.refs_0_), channel_id=1, source_target_pairs={{0,16},{4,20},{8,24},{12,28},{16,0},{20,4},{24,8},{28,12},{1,17},{... | collective-permute-start | bytes 1572872 | tf_op jit(solution)/shard_map/ppermute | solution.py:174
  14.6 24.3 %collective-permute-start.12 = (bf16[256,1024]{1,0:T(8,128)(2,1)S(1)}, bf16[256,1024]{1,0:T(8,128)(2,1)}, u32[]{:S(2)}, u32[]{:S(2)}) collective-permute-start(bf16[256,1024]{1,0:T(8,128)(2,1)S(1)} %shard_map.119.refs_0_), channel_id=1, source_target_pairs={{0,24},{4,28},{8,16},{12,20},{16,8},{20,12},{24,0},{28,4},{1,25},{... | collective-permute-start | bytes 1572872 | tf_op jit(solution)/shard_map/ppermute | solution.py:174
  19.2 19.7 %collective-permute-start.7 = (bf16[256,1024]{1,0:T(8,128)(2,1)S(1)}, bf16[256,1024]{1,0:T(8,128)(2,1)S(1)}, u32[]{:S(2)}, u32[]{:S(2)}) collective-permute-start(bf16[256,1024]{1,0:T(8,128)(2,1)S(1)} %shard_map.119.refs_0_), channel_id=1, source_target_pairs={{0,4},{4,0},{8,12},{12,8},{16,20},{20,16},{24,28},{28,24},{1,5},{5... | collective-permute-start | bytes 1572872 | tf_op jit(solution)/shard_map/ppermute | solution.py:174
  25.7 13.2 %collective-permute-start.9 = (bf16[256,1024]{1,0:T(8,128)(2,1)S(1)}, bf16[256,1024]{1,0:T(8,128)(2,1)S(1)}, u32[]{:S(2)}, u32[]{:S(2)}) collective-permute-start(bf16[256,1024]{1,0:T(8,128)(2,1)S(1)} %collective-permute-done.8.refs_2_), channel_id=1, source_target_pairs={{0,4},{4,0},{8,12},{12,8},{16,20},{20,16},{24,28},{28,24},{1,5},{5... | collective-permute-start | bytes 1572872 | tf_op jit(solution)/shard_map/ppermute | solution.py:174
  26.8 14.3 %collective-permute-start.11 = (bf16[256,1024]{1,0:T(8,128)(2,1)S(1)}, bf16[256,1024]{1,0:T(8,128)(2,1)S(1)}, u32[]{:S(2)}, u32[]{:S(2)}) collective-permute-start(bf16[256,1024]{1,0:T(8,128)(2,1)S(1)} %collective-permute-done.10.refs_4_), channel_id=1, source_target_pairs={{0,4},{4,0},{8,12},{12,8},{16,20},{20,16},{24,28},{28,24},{1,5},{5... | collective-permute-start | bytes 1572872 | tf_op jit(solution)/shard_map/ppermute | solution.py:174
  61.6 8.8 %collective-permute-start.22 = (bf16[128,1024]{1,0:T(8,128)(2,1)S(1)}, bf16[128,1024]{1,0:T(8,128)(2,1)S(1)}, u32[]{:S(2)}, u32[]{:S(2)}) collective-permute-start(bf16[128,1024]{1,0:T(8,128)(2,1)S(1)} %maximum_add_fusion.refs_0_), channel_id=1, source_target_pairs={{0,16},{4,20},{8,24},{12,28},{16,0},{20,4},{24,8},{28,12},{1,17},{... | collective-permute-start | bytes 786440 | tf_op jit(solution)/shard_map/ppermute | solution.py:174
  61.7 14.2 %collective-permute-start.24 = (bf16[128,1024]{1,0:T(8,128)(2,1)S(1)}, bf16[128,1024]{1,0:T(8,128)(2,1)S(1)}, u32[]{:S(2)}, u32[]{:S(2)}) collective-permute-start(bf16[128,1024]{1,0:T(8,128)(2,1)S(1)} %maximum_add_fusion.refs_0_), channel_id=1, source_target_pairs={{0,24},{4,28},{8,16},{12,20},{16,8},{20,12},{24,0},{28,4},{1,25},{... | collective-permute-start | bytes 786440 | tf_op jit(solution)/shard_map/ppermute | solution.py:174
  63.0 12.9 %collective-permute-start.19 = (bf16[128,1024]{1,0:T(8,128)(2,1)S(1)}, bf16[128,1024]{1,0:T(8,128)(2,1)S(1)}, u32[]{:S(2)}, u32[]{:S(2)}) collective-permute-start(bf16[128,1024]{1,0:T(8,128)(2,1)S(1)} %maximum_add_fusion.refs_0_), channel_id=1, source_target_pairs={{0,4},{4,0},{8,12},{12,8},{16,20},{20,16},{24,28},{28,24},{1,5},{5... | collective-permute-start | bytes 786440 | tf_op jit(solution)/shard_map/ppermute | solution.py:174
  78.9 18.8 %collective-permute-start.28 = (bf16[256,512]{1,0:T(8,128)(2,1)S(1)}, bf16[256,512]{1,0:T(8,128)(2,1)S(1)}, u32[]{:S(2)}, u32[]{:S(2)}) collective-permute-start(bf16[256,512]{1,0:T(8,128)(2,1)S(1)} %get-tuple-element.69), channel_id=1, source_target_pairs={{0,3},{1,2},{2,1},{3,0},{4,7},{5,6},{6,5},{7,4},{8,11},{9,10},{10,... | collective-permute-start | bytes 786440 | tf_op jit(solution)/shard_map/ppermute | solution.py:174
  80.3 22.2 %collective-permute-start.27 = (bf16[256,512]{1,0:T(8,128)(2,1)S(1)}, bf16[256,512]{1,0:T(8,128)(2,1)S(1)}, u32[]{:S(2)}, u32[]{:S(2)}) collective-permute-start(bf16[256,512]{1,0:T(8,128)(2,1)S(1)} %get-tuple-element.68), channel_id=1, source_target_pairs={{0,2},{1,3},{2,0},{3,1},{4,6},{5,7},{6,4},{7,5},{8,10},{9,11},{10,... | collective-permute-start | bytes 786440 | tf_op jit(solution)/shard_map/ppermute | solution.py:174
  81.4 21.1 %collective-permute-start.26 = (bf16[256,512]{1,0:T(8,128)(2,1)S(1)}, bf16[256,512]{1,0:T(8,128)(2,1)S(1)}, u32[]{:S(2)}, u32[]{:S(2)}) collective-permute-start(bf16[256,512]{1,0:T(8,128)(2,1)S(1)} %get-tuple-element.67), channel_id=1, source_target_pairs={{0,1},{1,0},{2,3},{3,2},{4,5},{5,4},{6,7},{7,6},{8,9},{9,8},{10,11... | collective-permute-start | bytes 786440 | tf_op jit(solution)/shard_map/ppermute | solution.py:174
  103.8 13.2 %collective-permute-start.33 = (bf16[256,512]{1,0:T(8,128)(2,1)S(1)}, bf16[256,512]{1,0:T(8,128)(2,1)S(1)}, u32[]{:S(2)}, u32[]{:S(2)}) collective-permute-start(bf16[256,512]{1,0:T(8,128)(2,1)S(1)} %add_convert_fusion.refs_0_.hidden), channel_id=1, source_target_pairs={{0,1},{1,0},{2,3},{3,2},{4,5},{5,4},{6,7},{7,6},{8,9},{9,8},{10,11... | collective-permute-start | bytes 786440 | tf_op jit(solution)/shard_map/ppermute | solution.py:174
  106.0 14.7 %collective-permute-start.35 = (bf16[256,512]{1,0:T(8,128)(2,1)S(1)}, bf16[256,512]{1,0:T(8,128)(2,1)S(1)}, u32[]{:S(2)}, u32[]{:S(2)}) collective-permute-start(bf16[256,512]{1,0:T(8,128)(2,1)S(1)} %add_convert_fusion.refs_0_.hidden), channel_id=1, source_target_pairs={{0,2},{1,3},{2,0},{3,1},{4,6},{5,7},{6,4},{7,5},{8,10},{9,11},{10,... | collective-permute-start | bytes 786440 | tf_op jit(solution)/shard_map/ppermute | solution.py:174
  110.0 9.3 %collective-permute-start.32 = (bf16[272,384]{1,0:T(8,128)(2,1)S(1)}, bf16[272,384]{1,0:T(8,128)(2,1)S(1)}, u32[]{:S(2)}, u32[]{:S(2)}) collective-permute-start(bf16[272,384]{1,0:T(8,128)(2,1)S(1)} %get-tuple-element.77), channel_id=1, source_target_pairs={{0,24},{4,28},{8,16},{12,20},{16,8},{20,12},{24,0},{28,4},{1,25},{... | collective-permute-start | bytes 626696 | tf_op jit(solution)/shard_map/ppermute | solution.py:174
  120.6 13.0 %collective-permute-start.40 = (bf16[256,512]{1,0:T(8,128)(2,1)S(1)}, bf16[256,512]{1,0:T(8,128)(2,1)S(1)}, u32[]{:S(2)}, u32[]{:S(2)}) collective-permute-start(bf16[256,512]{1,0:T(8,128)(2,1)S(1)} %add_convert_fusion.refs_0_.hidden), channel_id=1, source_target_pairs={{0,3},{1,2},{2,1},{3,0},{4,7},{5,6},{6,5},{7,4},{8,11},{9,10},{10,... | collective-permute-start | bytes 786440 | tf_op jit(solution)/shard_map/ppermute | solution.py:174
  124.5 12.9 %collective-permute-start.37 = (bf16[528,384]{1,0:T(8,128)(2,1)S(1)}, bf16[528,384]{1,0:T(8,128)(2,1)S(1)}, u32[]{:S(2)}, u32[]{:S(2)}) collective-permute-start(bf16[528,384]{1,0:T(8,128)(2,1)S(1)} %get-tuple-element.81), channel_id=1, source_target_pairs={{0,8},{4,12},{8,0},{12,4},{16,24},{20,28},{24,16},{28,20},{1,9},{5... | collective-permute-start | bytes 1216520 | tf_op jit(solution)/shard_map/ppermute | solution.py:174
  125.8 11.6 %collective-permute-start.38 = (bf16[528,384]{1,0:T(8,128)(2,1)S(1)}, bf16[528,384]{1,0:T(8,128)(2,1)S(1)}, u32[]{:S(2)}, u32[]{:S(2)}) collective-permute-start(bf16[528,384]{1,0:T(8,128)(2,1)S(1)} %get-tuple-element.82), channel_id=1, source_target_pairs={{0,16},{4,20},{8,24},{12,28},{16,0},{20,4},{24,8},{28,12},{1,17},{... | collective-permute-start | bytes 1216520 | tf_op jit(solution)/shard_map/ppermute | solution.py:174
  126.3 18.7 %collective-permute-start.39 = (bf16[528,384]{1,0:T(8,128)(2,1)S(1)}, bf16[528,384]{1,0:T(8,128)(2,1)S(1)}, u32[]{:S(2)}, u32[]{:S(2)}) collective-permute-start(bf16[528,384]{1,0:T(8,128)(2,1)S(1)} %get-tuple-element.83), channel_id=1, source_target_pairs={{0,24},{4,28},{8,16},{12,20},{16,8},{20,12},{24,0},{28,4},{1,25},{... | collective-permute-start | bytes 1216520 | tf_op jit(solution)/shard_map/ppermute | solution.py:174
  157.6 10.4 %collective-permute-start.48 = (bf16[1024,128]{1,0:T(8,128)(2,1)S(1)}, bf16[1024,128]{1,0:T(8,128)(2,1)S(1)}, u32[]{:S(2)}, u32[]{:S(2)}) collective-permute-start(bf16[1024,128]{1,0:T(8,128)(2,1)S(1)} %shard_map.126.refs_0_), channel_id=1, source_target_pairs={{0,16},{4,20},{8,24},{12,28},{16,0},{20,4},{24,8},{28,12},{1,17},{... | collective-permute-start | bytes 786440 | tf_op jit(solution)/shard_map/ppermute | solution.py:174
  158.5 13.9 %collective-permute-start.50 = (bf16[1024,128]{1,0:T(8,128)(2,1)S(1)}, bf16[1024,128]{1,0:T(8,128)(2,1)S(1)}, u32[]{:S(2)}, u32[]{:S(2)}) collective-permute-start(bf16[1024,128]{1,0:T(8,128)(2,1)S(1)} %shard_map.126.refs_0_), channel_id=1, source_target_pairs={{0,24},{4,28},{8,16},{12,20},{16,8},{20,12},{24,0},{28,4},{1,25},{... | collective-permute-start | bytes 786440 | tf_op jit(solution)/shard_map/ppermute | solution.py:174
  159.3 13.1 %collective-permute-start.45 = (bf16[1024,128]{1,0:T(8,128)(2,1)S(1)}, bf16[1024,128]{1,0:T(8,128)(2,1)S(1)}, u32[]{:S(2)}, u32[]{:S(2)}) collective-permute-start(bf16[1024,128]{1,0:T(8,128)(2,1)S(1)} %shard_map.126.refs_0_), channel_id=1, source_target_pairs={{0,4},{4,0},{8,12},{12,8},{16,20},{20,16},{24,28},{28,24},{1,5},{5... | collective-permute-start | bytes 786440 | tf_op jit(solution)/shard_map/ppermute | solution.py:174
  162.9 9.5 %collective-permute-start.47 = (bf16[1024,128]{1,0:T(8,128)(2,1)S(1)}, bf16[1024,128]{1,0:T(8,128)(2,1)S(1)}, u32[]{:S(2)}, u32[]{:S(2)}) collective-permute-start(bf16[1024,128]{1,0:T(8,128)(2,1)S(1)} %collective-permute-done.46.refs_2_), channel_id=1, source_target_pairs={{0,4},{4,0},{8,12},{12,8},{16,20},{20,16},{24,28},{28,24},{1,5},{5... | collective-permute-start | bytes 786440 | tf_op jit(solution)/shard_map/ppermute | solution.py:174
  176.0 11.1 %collective-permute-start.52 = (bf16[256,512]{1,0:T(8,128)(2,1)S(1)}, bf16[256,512]{1,0:T(8,128)(2,1)S(1)}, u32[]{:S(2)}, u32[]{:S(2)}) collective-permute-start(bf16[256,512]{1,0:T(8,128)(2,1)S(1)} %get-tuple-element.94), channel_id=1, source_target_pairs={{0,1},{1,0},{2,3},{3,2},{4,5},{5,4},{6,7},{7,6},{8,9},{9,8},{10,11... | collective-permute-start | bytes 786440 | tf_op jit(solution)/shard_map/ppermute | solution.py:174
  177.5 11.6 %collective-permute-start.53 = (bf16[256,512]{1,0:T(8,128)(2,1)S(1)}, bf16[256,512]{1,0:T(8,128)(2,1)S(1)}, u32[]{:S(2)}, u32[]{:S(2)}) collective-permute-start(bf16[256,512]{1,0:T(8,128)(2,1)S(1)} %get-tuple-element.95), channel_id=1, source_target_pairs={{0,2},{1,3},{2,0},{3,1},{4,6},{5,7},{6,4},{7,5},{8,10},{9,11},{10,... | collective-permute-start | bytes 786440 | tf_op jit(solution)/shard_map/ppermute | solution.py:174
  177.5 24.0 %collective-permute-start.54 = (bf16[256,512]{1,0:T(8,128)(2,1)S(1)}, bf16[256,512]{1,0:T(8,128)(2,1)S(1)}, u32[]{:S(2)}, u32[]{:S(2)}) collective-permute-start(bf16[256,512]{1,0:T(8,128)(2,1)S(1)} %get-tuple-element.96), channel_id=1, source_target_pairs={{0,3},{1,2},{2,1},{3,0},{4,7},{5,6},{6,5},{7,4},{8,11},{9,10},{10,... | collective-permute-start | bytes 786440 | tf_op jit(solution)/shard_map/ppermute | solution.py:174
  201.8 14.9 %collective-permute-start.55 = (bf16[128,512]{1,0:T(8,128)(2,1)S(1)}, bf16[128,512]{1,0:T(8,128)(2,1)S(1)}, u32[]{:S(2)}, u32[]{:S(2)}) collective-permute-start(bf16[128,512]{1,0:T(8,128)(2,1)S(1)} %get-tuple-element.97), channel_id=1, source_target_pairs={{0,0},{1,8},{2,16},{3,24},{4,4},{5,12},{6,20},{7,28},{8,1},{9,9},{... | collective-permute-start | bytes 393224 | tf_op jit(solution)/shard_map/ppermute | solution.py:626
  203.7 15.8 %collective-permute-start.56 = (bf16[128,512]{1,0:T(8,128)(2,1)S(1)}, bf16[128,512]{1,0:T(8,128)(2,1)S(1)}, u32[]{:S(2)}, u32[]{:S(2)}) collective-permute-start(bf16[128,512]{1,0:T(8,128)(2,1)S(1)} %get-tuple-element.98), channel_id=1, source_target_pairs={{0,4},{1,12},{2,20},{3,28},{4,0},{5,8},{6,16},{7,24},{8,5},{9,13},... | collective-permute-start | bytes 393224 | tf_op jit(solution)/shard_map/ppermute | solution.py:626
  (36 other events, 328.4 us)

commit v6 on v5

--- a/solution.py
+++ b/solution.py
@@ -216,13 +216,6 @@
     )(*operands)
 
 
-def assemble(pieces, whole):
-    chip, core, _ = place()
-    for n, piece in enumerate(pieces):
-        index = 2 * (chip ^ (n // 2)) + (core ^ (n % 2))
-        whole[aligned(index, piece.shape[0]), :] = piece[...]
-
-
 def stack_kernel(*refs):
     sources, stacked, semaphores = refs[:-2], refs[-2], refs[-1]
     height = sources[0].shape[0]
@@ -317,18 +310,41 @@
         below[:, part] = heads[slots - spill :]
 
 
-def quarters(left, weight, outs):
+def spill_kernel(halves, own, first, last, *refs):
+    outs, whole = refs[:-1], refs[-1]
     _, _, tensor = place()
+    spill = first.shape[0]
+    whole[:spill, :] = own[:spill, :] + first[...]
+    whole[spill:, :] = own[spill:, :] + last[...]
+    for half, out in zip(halves, outs):
+        height = out.shape[0] // len(half)
+        for n, r in enumerate(half):
+            out[n * height : (n + 1) * height, :] = whole[aligned(tensor ^ r, height), :]
+
+
+def products(whole, weight, outs):
     height = outs[0].shape[0]
-    for r, out in enumerate(outs):
-        block = left[aligned(tensor ^ r, height), :]
+    for n, out in enumerate(outs):
+        block = whole[n * height : (n + 1) * height, :]
         out[...] = dot(block, weight[...]).astype(out.dtype)
+
+
+def add_kernel(*refs):
+    total = refs[0][...].astype(jnp.float32)
+    for share in refs[1:-1]:
+        total += share[...].astype(jnp.float32)
+    refs[-1][...] = total
 
 
 def cross_out_kernel(count, weight, *refs):
     pieces, outs, whole = refs[:count], refs[count:-1], refs[-1]
-    assemble(pieces, whole)
-    quarters(whole, weight, outs)
+    chip, core, _ = place()
+    height = pieces[0].shape[0] // len(outs)
+    for n, piece in enumerate(pieces):
+        index = 2 * (chip ^ (n // 2)) + (core ^ (n % 2))
+        for m in range(len(outs)):
+            whole[aligned(m * count + index, height), :] = piece[m * height : (m + 1) * height, :]
+    products(whole, weight, outs)
 
 
 def latent_out_kernel(count, weight, *refs):
@@ -337,7 +353,7 @@
     for n, piece in enumerate(pieces):
         index = (count // 2) * (core ^ (n % 2)) + (chip ^ (n // 2))
         whole[:, aligned(index, HEAD_DIM)] = piece[...]
-    quarters(whole, weight, outs)
+    products(whole, weight, outs)
 
 
 def arrange_kernel(*refs):
@@ -401,11 +417,13 @@
         out[height:, :part] = sent_sums.astype(jnp.bfloat16)
 
 
-def attention_kernel(groups, chips, depth, *refs):
-    shares, attended, (query, key, value) = refs[: len(groups) * chips], refs[-4], refs[-3:]
+def attention_kernel(groups, halves, chips, depth, *refs):
+    shares, refs = refs[: len(groups) * chips], refs[len(groups) * chips :]
+    outs, (query, key, value, attended) = refs[: len(halves)], refs[len(halves) :]
     _, _, tensor = place()
     parts = sum(len(group) for group in groups)
     height = attended.shape[0] // parts
+    piece = height // (2 * chips)
     own_place = diagonal(height)
     for g, group in enumerate(groups):
         end = len(group) * height
@@ -420,9 +438,11 @@
                 row += sum(terms[3 * q + m : 3 * q + m + 1] for m in range(3))
             column = jnp.sum(jnp.where(own_place, row, 0.0), axis=1, keepdims=True)
             total = (total * lax.rsqrt(column / depth + norm_eps)).astype(jnp.bfloat16)
-            span = aligned(tensor ^ r, height)
             for m, kept in enumerate((query, key, value)):
-                kept[span, :] = total[:, m * HEAD_DIM : (m + 1) * HEAD_DIM]
+                for n in range(2 * chips):
+                    kept[aligned(n * parts + (tensor ^ r), piece), :] = total[
+                        n * piece : (n + 1) * piece, m * HEAD_DIM : (m + 1) * HEAD_DIM
+                    ]
     causal = lax.broadcasted_iota(jnp.int32, (height, height), 0) >= lax.broadcasted_iota(
         jnp.int32, (height, height), 1
     )
@@ -441,16 +461,25 @@
             denominator += jnp.sum(raw, axis=1, keepdims=True)
             numerator += dot(raw.astype(jnp.bfloat16), value[span, :])
         attended[i * height : (i + 1) * height, :] = (numerator / denominator).astype(jnp.bfloat16)
-
-
-def final_kernel(own, hidden, *refs):
-    received, outs, whole = refs[:-3], refs[-3:-1], refs[-1]
-    _, core, _ = place()
-    total = own[...] + hidden[...].astype(jnp.float32)
-    for block in received:
-        total += block[...].astype(jnp.float32)
+    for half, out in zip(halves, outs):
+        for n, r in enumerate(half):
+            out[n * height : (n + 1) * height, :] = attended[aligned(tensor ^ r, height), :]
+
+
+def final_kernel(parts, own, *refs):
+    blocks, received, outs, whole = refs[:parts], refs[parts:-3], refs[-3:-1], refs[-1]
+    _, core, tensor = place()
+    total = own[...]
+    for share in received:
+        total += share[...].astype(jnp.float32)
     whole[...] = total
     height = outs[0].shape[0]
+    piece = height // parts
+    for n in range(2):
+        for r, block in enumerate(blocks):
+            span = aligned(n * parts + (tensor ^ r), piece)
+            rows = aligned(2 * tensor + n, piece)
+            whole[span, :] += block[rows, :].astype(jnp.float32)
     for flip, out in enumerate(outs):
         out[...] = whole[aligned(core ^ flip, height), :].astype(jnp.bfloat16)
 
@@ -541,10 +570,47 @@
         flops=4 * byte_count * local_width * (byte_width + slot_count),
     )
 
-    spilled = [shifted(below, "seq", 1), shifted(above, "seq", -1)]
+    half = max(1, tensor_count // 2)
+    halves = [list(range(half, tensor_count)), list(range(half))]
+    first, last = shifted(below, "seq", 1), shifted(above, "seq", -1)
+    sorted_heads = call(
+        functools.partial(spill_kernel, halves),
+        [((patch_dev * len(group) // tensor_count, local_width), bf16) for group in halves],
+        own,
+        first,
+        last,
+        scratch=[pltpu.VMEM((patch_dev, local_width), bf16)],
+    )
+
+    def summed_shares(kernel, weight, operands, width):
+        shares, earlier = [], ()
+        for group, operand in zip(halves, operands):
+            pieces = over_plane(after(operand, *earlier))
+            height = len(group) * quarter
+            outs = call(
+                functools.partial(kernel, seq_count),
+                [((quarter, out_width), bf16 if r else f32) for r in group],
+                weight,
+                *pieces,
+                scratch=[pltpu.VMEM((height, width), bf16)],
+                flops=2 * height * width * out_width,
+            )
+            earlier = outs[:1]
+            shares += [exchanged(out, "tensor", r) if r else out for r, out in zip(group, outs)]
+        far, (own_share, *near) = shares[: len(halves[0])], shares[len(halves[0]) :]
+        (far_sum,) = call(
+            add_kernel,
+            [((quarter, out_width), f32)],
+            *[after(share, own_share, *near) for share in far],
+            flops=32 * patch_count * width * out_width,
+        )
+        return own_share, [far_sum, *near]
+
+    total, received = summed_shares(cross_out_kernel, cross_out, sorted_heads, local_width)
+
     weights = []
     for weight in (latent_query, latent_key, latent_value):
-        weights += [weight, core_swapped(after(weight, own))]
+        weights += [weight, core_swapped(after(weight, total))]
     head_weights = call(
         arrange_kernel,
         [((2 * out_width, 3 * HEAD_DIM), bf16)] * chip_count,
@@ -552,30 +618,21 @@
         far=6,
         scratch=[pltpu.SemaphoreType.DMA((6 * chip_count,))],
     )
-    own, *head_weights = lax.optimization_barrier((own, *head_weights))
-    own = own + jnp.concatenate(spilled, axis=0)
-
-    total, *sent = call(
-        functools.partial(cross_out_kernel, seq_count),
-        [((quarter, out_width), f32 if r == 0 else bf16) for r in range(tensor_count)],
-        cross_out,
-        *over_plane(own),
-        scratch=[pltpu.VMEM((patch_count, local_width), bf16)],
-        flops=2 * patch_count * local_width * out_width,
-    )
-    for r, block in enumerate(sent, 1):
-        total = total + exchanged(block, "tensor", r).astype(f32)
+    total, *head_weights = lax.optimization_barrier((total, *head_weights))
+    for share in received:
+        total = total + share.astype(f32)
     latent_in = total.astype(bf16)
 
     gain = norm_gain[None, :]
     groups = [[0], list(range(1, min(3, tensor_count))), list(range(3, tensor_count))]
     groups = [group for group in groups if group]
-    shares, arrived = [], []
+    shares, arrived, latent_blocks = [], [], [latent_in]
     for g, group in enumerate(groups):
         blocks = [latent_in]
         if g:
             start = after(latent_in, *arrived, *shares[:chip_count]) if g > 1 else latent_in
             arrived = [exchanged(start, "tensor", r) for r in group]
+            latent_blocks += arrived
             blocks = [after(block, *shares[:chip_count]) for block in arrived]
         height = len(group) * quarter
         share, *sent = call(
@@ -589,30 +646,23 @@
             flops=2 * height * 2 * out_width * 3 * HEAD_DIM * chip_count,
         )
         if g > 1:
-            sent = [after(part, *shares[(g - 1) * chip_count + 1 :]) for part in sent]
+            sent[-1] = after(sent[-1], *shares[(g - 1) * chip_count + 1 :])
         shares += [share] + [exchanged(part, "seq", 2 * d) for d, part in enumerate(sent, 1)]
-    (attended,) = call(
-        functools.partial(attention_kernel, groups, chip_count, out_width * seq_count),
-        [((patch_count, HEAD_DIM), bf16)],
+    attended = call(
+        functools.partial(attention_kernel, groups, halves, chip_count, out_width * seq_count),
+        [((len(group) * quarter, HEAD_DIM), bf16) for group in halves],
         *shares,
-        scratch=[pltpu.VMEM((patch_count, HEAD_DIM), bf16)] * 3,
+        scratch=[pltpu.VMEM((patch_count, HEAD_DIM), bf16)] * 4,
         flops=2 * patch_count * patch_count * HEAD_DIM,
     )
 
-    total, *sent = call(
-        functools.partial(latent_out_kernel, seq_count),
-        [((quarter, out_width), f32 if r == 0 else bf16) for r in range(tensor_count)],
-        latent_out,
-        *over_plane(attended),
-        scratch=[pltpu.VMEM((patch_count, local_width), bf16)],
-        flops=2 * patch_count * local_width * out_width,
-    )
+    total, received = summed_shares(latent_out_kernel, latent_out, attended, local_width)
     pieces = call(
-        final_kernel,
+        functools.partial(final_kernel, tensor_count),
         [((patch_dev, out_width), bf16)] * 2,
         total,
-        latent_in,
-        *[exchanged(block, "tensor", r) for r, block in enumerate(sent, 1)],
+        *latent_blocks,
+        *received,
         scratch=[pltpu.VMEM((quarter, out_width), f32)],
     )
 

time: 223 us -> 229 us (1.027)
  waiting for transfers between devices: 98.9 us -> 105 us
    ppermute x2, waiting for transfers between devices: 0.57 us -> 4.17 us  [shifted(): return lax.ppermute(block, axis, route)]
    ppermute x53 -> x67, waiting for transfers between devices: 86.5 us -> 90 us  [exchanged(): return lax.ppermute(block, axis, route)]
    ppermute x53 -> x67, starting transfers between devices: 78.4 us -> 79.2 us  [exchanged(): return lax.ppermute(block, axis, route)]
    pallas_call x11 -> x16, Pallas kernels: 23.8 us -> 24.1 us  [call(): pl.pallas_call(kernel, out_shape=shapes, in_specs=[pl.BlockSpec(memory_sp...]
  transfers between devices with their start and end apart: 57 -> 71, of which waited for: 28 -> 32; matrix products, arithmetic and copies ran while one was open for 1% -> 1% of each run, Pallas kernels for 4% -> 4%
where the time goes in v6:
time: 229 us; the launch traced here: 226 us
  waiting for transfers between devices  105 us (46%)
  starting transfers between devices  89.4 us (39%)
  Pallas kernels  24.1 us (11%)
  local copies, waits for them, and re-layouts  5.38 us (2%)
    ppermute x67, waiting for transfers between devices, exchanged(): return lax.ppermute(block, axis, route)  90 us
    ppermute x67, starting transfers between devices, exchanged(): return lax.ppermute(block, axis, route)  79.2 us
    pallas_call x16, Pallas kernels, call(): pl.pallas_call(kernel, out_shape=shapes, in_specs=[pl.BlockSpec(memory_sp...  24.1 us
    ppermute x2, waiting for transfers between devices, per_device(): moved.append(lax.ppermute(pieces[flip], ('seq', 'tensor'), route))  11.3 us
    ppermute x2, starting transfers between devices, per_device(): moved.append(lax.ppermute(pieces[flip], ('seq', 'tensor'), route))  5.69 us
  transfers between devices with their start and end apart: 71, of which 32 were waited for; matrix products, arithmetic and copies ran while one was open for 1% of the time, Pallas kernels for 4%

profile of v6, /device:TPU:9, one launch (start us, length us, event | category | flops | bytes accessed | tf_op | source)
XLA Modules:
  0.0 226.4 jit_solution(14224860249020167268)
XLA Ops:
  4.2 3.2 %collective-permute-done.1.refs_2_ = bf16[128,1024]{1,0:T(8,128)(2,1)S(1)} collective-permute-done((bf16[128,1024]{1,0:T(8,128)(2,1)}, bf16[128,1024]{1,0:T(8,128)(2,1)S(1)}, u32[]{:S(2)}, u32[]{:S(2)}) %collective-permute-start.1) | collective-permute-done | bytes 262176 | tf_op jit(solution)/shard_map/ppermute | solution.py:174
  7.4 2.7 %collective-permute-start.2 = (bf16[128,1024]{1,0:T(8,128)(2,1)S(1)}, bf16[128,1024]{1,0:T(8,128)(2,1)S(1)}, u32[]{:S(2)}, u32[]{:S(2)}) collective-permute-start(bf16[128,1024]{1,0:T(8,128)(2,1)S(1)} %collective-permute-done.1.refs_2_), channel_id=1, source_target_pairs={{0,4},{4,0},{8,12},{12,8},{16,20},{20,16},{24,28},{28,24},{1,5},{5... | collective-permute-start | bytes 786440 | tf_op jit(solution)/shard_map/ppermute | solution.py:174
  15.9 2.1 collective-permute-start.4
  26.8 12.1 %collective-permute-start.11 = (bf16[256,1024]{1,0:T(8,128)(2,1)S(1)}, bf16[256,1024]{1,0:T(8,128)(2,1)S(1)}, u32[]{:S(2)}, u32[]{:S(2)}) collective-permute-start(bf16[256,1024]{1,0:T(8,128)(2,1)S(1)} %collective-permute-done.10.refs_4_), channel_id=1, source_target_pairs={{0,4},{4,0},{8,12},{12,8},{16,20},{20,16},{24,28},{28,24},{1,5},{5... | collective-permute-start | bytes 1572872 | tf_op jit(solution)/shard_map/ppermute | solution.py:174
  38.9 2.2 collective-permute-done.11.refs_5_
  41.4 10.2 %shard_map.120 = (bf16[128,1024]{1,0:T(8,128)(2,1)S(1)}, bf16[64,1024]{1,0:T(8,128)(2,1)S(1)}, bf16[64,1024]{1,0:T(8,128)(2,1)S(1)}) custom-call(s32[1,1024]{1,0:T(1,128)S(1)} %bitcast.7, bf16[256,1024]{1,0:T(8,128)(2,1)S(1)} %shard_map.118.query, bf16[1024,1024]{1,0:T(8,128)(2,1)S(1)} %copy-done.3, bf16[256,1024]{1,0:T(8,128)(2,1)S(1)} %shard_map.119.refs_0_, ...), custom_call_target="tpu_custom_call" | custom-call | flops 5368709120 | bytes 7344128 | tf_op jit(solution)/shard_map/pallas_call | solution.py:207
  51.6 2.5 %collective-permute-start.14 = (bf16[64,1024]{1,0:T(8,128)(2,1)S(1)}, bf16[64,1024]{1,0:T(8,128)(2,1)S(1)}, u32[]{:S(2)}, u32[]{:S(2)}) collective-permute-start(bf16[64,1024]{1,0:T(8,128)(2,1)S(1)} %get-tuple-element.64), channel_id=1, source_target_pairs={{0,4},{4,8},{8,12},{12,16},{16,20},{20,24},{24,28},{1,5},{5,9},{9,... | collective-permute-start | bytes 393224 | tf_op jit(solution)/shard_map/ppermute | solution.py:22
  54.1 2.1 collective-permute-start.15
  56.2 4.2 %collective-permute-done.15.last = bf16[64,1024]{1,0:T(8,128)(2,1)S(1)} collective-permute-done((bf16[64,1024]{1,0:T(8,128)(2,1)S(1)}, bf16[64,1024]{1,0:T(8,128)(2,1)S(1)}, u32[]{:S(2)}, u32[]{:S(2)}) %collective-permute-start.15) | collective-permute-done | bytes 131104 | tf_op jit(solution)/shard_map/ppermute | solution.py:22
  60.5 3.1 %collective-permute-start.17 = (bf16[64,1024]{1,0:T(8,128)(2,1)S(1)}, bf16[64,1024]{1,0:T(8,128)(2,1)S(1)}, u32[]{:S(2)}, u32[]{:S(2)}) collective-permute-start(bf16[64,1024]{1,0:T(8,128)(2,1)S(1)} %get-tuple-element.67.refs_0_), channel_id=1, source_target_pairs={{0,8},{4,12},{8,0},{12,4},{16,24},{20,28},{24,16},{28,20},{1,9},{5... | collective-permute-start | bytes 393224 | tf_op jit(solution)/shard_map/ppermute | solution.py:174
  66.3 3.9 %collective-permute-done.19.refs_4_ = bf16[64,1024]{1,0:T(8,128)(2,1)S(1)} collective-permute-done((bf16[64,1024]{1,0:T(8,128)(2,1)S(1)}, bf16[64,1024]{1,0:T(8,128)(2,1)S(1)}, u32[]{:S(2)}, u32[]{:S(2)}) %collective-permute-start.19) | collective-permute-done | bytes 131104 | tf_op jit(solution)/shard_map/ppermute | solution.py:174
  79.3 2.7 %collective-permute-start.27 = (bf16[64,1024]{1,0:T(8,128)(2,1)S(1)}, bf16[64,1024]{1,0:T(8,128)(2,1)S(1)}, u32[]{:S(2)}, u32[]{:S(2)}) collective-permute-start(bf16[64,1024]{1,0:T(8,128)(2,1)S(1)} %collective-permute-done.26.refs_4_), channel_id=1, source_target_pairs={{0,4},{4,0},{8,12},{12,8},{16,20},{20,16},{24,28},{28,24},{1,5},{5... | collective-permute-start | bytes 393224 | tf_op jit(solution)/shard_map/ppermute | solution.py:174
  82.0 2.3 %collective-permute-start.33 = (bf16[256,512]{1,0:T(8,128)(2,1)S(1)}, bf16[256,512]{1,0:T(8,128)(2,1)S(1)}, u32[]{:S(2)}, u32[]{:S(2)}) collective-permute-start(bf16[256,512]{1,0:T(8,128)(2,1)S(1)} %get-tuple-element.68), channel_id=1, source_target_pairs={{0,2},{1,3},{2,0},{3,1},{4,6},{5,7},{6,4},{7,5},{8,10},{9,11},{10,... | collective-permute-start | bytes 786440 | tf_op jit(solution)/shard_map/ppermute | solution.py:174
  87.6 8.7 %collective-permute-done.33.refs_0_ = bf16[256,512]{1,0:T(8,128)(2,1)S(1)} collective-permute-done((bf16[256,512]{1,0:T(8,128)(2,1)S(1)}, bf16[256,512]{1,0:T(8,128)(2,1)S(1)}, u32[]{:S(2)}, u32[]{:S(2)}) %collective-permute-start.33) | collective-permute-done | bytes 262176 | tf_op jit(solution)/shard_map/ppermute | solution.py:174
  97.2 9.9 %collective-permute-done.35.refs_1_ = bf16[256,512]{1,0:T(8,128)(2,1)S(1)} collective-permute-done((bf16[256,512]{1,0:T(8,128)(2,1)S(1)}, bf16[256,512]{1,0:T(8,128)(2,1)S(1)}, u32[]{:S(2)}, u32[]{:S(2)}) %collective-permute-start.35) | collective-permute-done | bytes 262176 | tf_op jit(solution)/shard_map/ppermute | solution.py:174
  109.1 3.4 %collective-permute-start.42 = (bf16[256,512]{1,0:T(8,128)(2,1)S(1)}, bf16[256,512]{1,0:T(8,128)(2,1)S(1)}, u32[]{:S(2)}, u32[]{:S(2)}) collective-permute-start(bf16[256,512]{1,0:T(8,128)(2,1)S(1)} %add_convert_fusion.refs_0_), channel_id=1, source_target_pairs={{0,2},{1,3},{2,0},{3,1},{4,6},{5,7},{6,4},{7,5},{8,10},{9,11},{10,... | collective-permute-start | bytes 786440 | tf_op jit(solution)/shard_map/ppermute | solution.py:174
  116.4 4.1 %collective-permute-done.40.refs_0_.refs_1_ = bf16[256,512]{1,0:T(8,128)(2,1)S(1)} collective-permute-done((bf16[256,512]{1,0:T(8,128)(2,1)S(1)}, bf16[256,512]{1,0:T(8,128)(2,1)S(1)}, u32[]{:S(2)}, u32[]{:S(2)}) %collective-permute-start.40) | collective-permute-done | bytes 262176 | tf_op jit(solution)/shard_map/ppermute | solution.py:174
  120.6 4.8 %collective-permute-done.39.refs_3_ = bf16[272,384]{1,0:T(8,128)(2,1)S(1)} collective-permute-done((bf16[272,384]{1,0:T(8,128)(2,1)S(1)}, bf16[272,384]{1,0:T(8,128)(2,1)S(1)}, u32[]{:S(2)}, u32[]{:S(2)}) %collective-permute-start.39) | collective-permute-done | bytes 208928 | tf_op jit(solution)/shard_map/ppermute | solution.py:174
  128.4 2.3 %shard_map.127 = (f32[520,384]{1,0:T(8,128)S(1)}, bf16[528,384]{1,0:T(8,128)(2,1)S(1)}, bf16[528,384]{1,0:T(8,128)(2,1)S(1)}, bf16[528,384]{1,0:T(8,128)(2,1)S(1)}) custom-call(f32[1,4096]{1,0:T(1,128)S(1)} %bitcast.4, bf16[256,512]{1,0:T(8,128)(2,1)S(1)} %collective-permute-done.40.refs_0_.refs_1_, bf16[256,512]{1,0:T(8,128)(2,1)S(1)} %collective-permute-done.41.refs_1_, ...), custom_call_target="tpu_custom_call" | custom-call | flops 1610612736 | bytes 6225920 | tf_op jit(solution)/shard_map/pallas_call | solution.py:207
  133.5 6.7 %collective-permute-done.47.refs_0_.refs_3_ = bf16[256,512]{1,0:T(8,128)(2,1)S(1)} collective-permute-done((bf16[256,512]{1,0:T(8,128)(2,1)S(1)}, bf16[256,512]{1,0:T(8,128)(2,1)S(1)}, u32[]{:S(2)}, u32[]{:S(2)}) %collective-permute-start.47) | collective-permute-done | bytes 262176 | tf_op jit(solution)/shard_map/ppermute | solution.py:174
  145.6 4.8 %collective-permute-done.46.refs_7_ = bf16[528,384]{1,0:T(8,128)(2,1)S(1)} collective-permute-done((bf16[528,384]{1,0:T(8,128)(2,1)S(1)}, bf16[528,384]{1,0:T(8,128)(2,1)S(1)}, u32[]{:S(2)}, u32[]{:S(2)}) %collective-permute-start.46) | collective-permute-done | bytes 405536 | tf_op jit(solution)/shard_map/ppermute | solution.py:174
  151.5 3.1 %collective-permute-done.49.refs_9_ = bf16[272,384]{1,0:T(8,128)(2,1)S(1)} collective-permute-done((bf16[272,384]{1,0:T(8,128)(2,1)S(1)}, bf16[272,384]{1,0:T(8,128)(2,1)S(1)}, u32[]{:S(2)}, u32[]{:S(2)}) %collective-permute-start.49) | collective-permute-done | bytes 208928 | tf_op jit(solution)/shard_map/ppermute | solution.py:174
  154.6 5.6 %collective-permute-done.50.refs_10_ = bf16[272,384]{1,0:T(8,128)(2,1)S(1)} collective-permute-done((bf16[272,384]{1,0:T(8,128)(2,1)S(1)}, bf16[272,384]{1,0:T(8,128)(2,1)S(1)}, u32[]{:S(2)}, u32[]{:S(2)}) %collective-permute-start.50) | collective-permute-done | bytes 208928 | tf_op jit(solution)/shard_map/ppermute | solution.py:174
  160.3 2.0 shard_map.129
  167.0 2.1 collective-permute-start.54
  169.2 2.8 %collective-permute-start.56 = (bf16[512,128]{1,0:T(8,128)(2,1)S(1)}, bf16[512,128]{1,0:T(8,128)(2,1)S(1)}, u32[]{:S(2)}, u32[]{:S(2)}) collective-permute-start(bf16[512,128]{1,0:T(8,128)(2,1)S(1)} %collective-permute-done.55.refs_4_), channel_id=1, source_target_pairs={{0,4},{4,0},{8,12},{12,8},{16,20},{20,16},{24,28},{28,24},{1,5},{5... | collective-permute-start | bytes 393224 | tf_op jit(solution)/shard_map/ppermute | solution.py:174
  180.9 2.8 %collective-permute-start.63 = (bf16[512,128]{1,0:T(8,128)(2,1)S(1)}, bf16[512,128]{1,0:T(8,128)(2,1)S(1)}, u32[]{:S(2)}, u32[]{:S(2)}) collective-permute-start(bf16[512,128]{1,0:T(8,128)(2,1)S(1)} %collective-permute-done.62.refs_4_), channel_id=1, source_target_pairs={{0,4},{4,0},{8,12},{12,8},{16,20},{20,16},{24,28},{28,24},{1,5},{5... | collective-permute-start | bytes 393224 | tf_op jit(solution)/shard_map/ppermute | solution.py:174
  187.5 9.0 %collective-permute-done.66.refs_0_ = bf16[256,512]{1,0:T(8,128)(2,1)S(1)} collective-permute-done((bf16[256,512]{1,0:T(8,128)(2,1)S(1)}, bf16[256,512]{1,0:T(8,128)(2,1)S(1)}, u32[]{:S(2)}, u32[]{:S(2)}) %collective-permute-start.66) | collective-permute-done | bytes 262176 | tf_op jit(solution)/shard_map/ppermute | solution.py:174
  196.5 11.8 %collective-permute-done.68.refs_1_ = bf16[256,512]{1,0:T(8,128)(2,1)S(1)} collective-permute-done((bf16[256,512]{1,0:T(8,128)(2,1)S(1)}, bf16[256,512]{1,0:T(8,128)(2,1)S(1)}, u32[]{:S(2)}, u32[]{:S(2)}) %collective-permute-start.68) | collective-permute-done | bytes 262176 | tf_op jit(solution)/shard_map/ppermute | solution.py:174
  210.5 3.8 %collective-permute-start.70 = (bf16[128,512]{1,0:T(8,128)(2,1)S(1)}, bf16[128,512]{1,0:T(8,128)(2,1)S(1)}, u32[]{:S(2)}, u32[]{:S(2)}) collective-permute-start(bf16[128,512]{1,0:T(8,128)(2,1)S(1)} %get-tuple-element.114), channel_id=1, source_target_pairs={{0,4},{1,12},{2,20},{3,28},{4,0},{5,8},{6,16},{7,24},{8,5},{9,13},... | collective-permute-start | bytes 393224 | tf_op jit(solution)/shard_map/ppermute | solution.py:676
  214.3 8.5 %collective-permute-done.69 = bf16[128,512]{1,0:T(8,128)(2,1)S(1)} collective-permute-done((bf16[128,512]{1,0:T(8,128)(2,1)S(1)}, bf16[128,512]{1,0:T(8,128)(2,1)S(1)}, u32[]{:S(2)}, u32[]{:S(2)}) %collective-permute-start.69) | collective-permute-done | bytes 131104 | tf_op jit(solution)/shard_map/ppermute | solution.py:676
  222.8 2.8 %collective-permute-done.70 = bf16[128,512]{1,0:T(8,128)(2,1)S(1)} collective-permute-done((bf16[128,512]{1,0:T(8,128)(2,1)S(1)}, bf16[128,512]{1,0:T(8,128)(2,1)S(1)}, u32[]{:S(2)}, u32[]{:S(2)}) %collective-permute-start.70) | collective-permute-done | bytes 131104 | tf_op jit(solution)/shard_map/ppermute | solution.py:676
  (156 shorter events, 73.5 us)
Async XLA Ops:
  1.2 12.1 %collective-permute-start.3 = (bf16[128,1024]{1,0:T(8,128)(2,1)}, bf16[128,1024]{1,0:T(8,128)(2,1)S(1)}, u32[]{:S(2)}, u32[]{:S(2)}) collective-permute-start(bf16[128,1024]{1,0:T(8,128)(2,1)} %refs_0_.3), channel_id=1, source_target_pairs={{0,16},{4,20},{8,24},{12,28},{16,0},{20,4},{24,8},{28,12},{1,17},{... | collective-permute-start | bytes 786440 | tf_op jit(solution)/shard_map/ppermute | solution.py:174
  2.5 12.1 %collective-permute-start.5 = (bf16[128,1024]{1,0:T(8,128)(2,1)}, bf16[128,1024]{1,0:T(8,128)(2,1)S(1)}, u32[]{:S(2)}, u32[]{:S(2)}) collective-permute-start(bf16[128,1024]{1,0:T(8,128)(2,1)} %refs_0_.3), channel_id=1, source_target_pairs={{0,24},{4,28},{8,16},{12,20},{16,8},{20,12},{24,0},{28,4},{1,25},{... | collective-permute-start | bytes 786440 | tf_op jit(solution)/shard_map/ppermute | solution.py:174
  2.6 13.3 %collective-permute-start = (bf16[128,1024]{1,0:T(8,128)(2,1)}, bf16[128,1024]{1,0:T(8,128)(2,1)S(1)}, u32[]{:S(2)}, u32[]{:S(2)}) collective-permute-start(bf16[128,1024]{1,0:T(8,128)(2,1)} %refs_0_.3), channel_id=1, source_target_pairs={{0,4},{4,0},{8,12},{12,8},{16,20},{20,16},{24,28},{28,24},{1,5},{5... | collective-permute-start | bytes 786440 | tf_op jit(solution)/shard_map/ppermute | solution.py:174
  7.4 10.7 %collective-permute-start.2 = (bf16[128,1024]{1,0:T(8,128)(2,1)S(1)}, bf16[128,1024]{1,0:T(8,128)(2,1)S(1)}, u32[]{:S(2)}, u32[]{:S(2)}) collective-permute-start(bf16[128,1024]{1,0:T(8,128)(2,1)S(1)} %collective-permute-done.1.refs_2_), channel_id=1, source_target_pairs={{0,4},{4,0},{8,12},{12,8},{16,20},{20,16},{24,28},{28,24},{1,5},{5... | collective-permute-start | bytes 786440 | tf_op jit(solution)/shard_map/ppermute | solution.py:174
  12.0 13.6 %collective-permute-start.8 = (bf16[256,1024]{1,0:T(8,128)(2,1)S(1)}, bf16[256,1024]{1,0:T(8,128)(2,1)S(1)}, u32[]{:S(2)}, u32[]{:S(2)}) collective-permute-start(bf16[256,1024]{1,0:T(8,128)(2,1)S(1)} %shard_map.119.refs_0_), channel_id=1, source_target_pairs={{0,8},{4,12},{8,0},{12,4},{16,24},{20,28},{24,16},{28,20},{1,9},{5... | collective-permute-start | bytes 1572872 | tf_op jit(solution)/shard_map/ppermute | solution.py:174
  13.3 13.5 %collective-permute-start.10 = (bf16[256,1024]{1,0:T(8,128)(2,1)S(1)}, bf16[256,1024]{1,0:T(8,128)(2,1)S(1)}, u32[]{:S(2)}, u32[]{:S(2)}) collective-permute-start(bf16[256,1024]{1,0:T(8,128)(2,1)S(1)} %shard_map.119.refs_0_), channel_id=1, source_target_pairs={{0,16},{4,20},{8,24},{12,28},{16,0},{20,4},{24,8},{28,12},{1,17},{... | collective-permute-start | bytes 1572872 | tf_op jit(solution)/shard_map/ppermute | solution.py:174
  14.6 24.3 %collective-permute-start.12 = (bf16[256,1024]{1,0:T(8,128)(2,1)S(1)}, bf16[256,1024]{1,0:T(8,128)(2,1)}, u32[]{:S(2)}, u32[]{:S(2)}) collective-permute-start(bf16[256,1024]{1,0:T(8,128)(2,1)S(1)} %shard_map.119.refs_0_), channel_id=1, source_target_pairs={{0,24},{4,28},{8,16},{12,20},{16,8},{20,12},{24,0},{28,4},{1,25},{... | collective-permute-start | bytes 1572872 | tf_op jit(solution)/shard_map/ppermute | solution.py:174
  19.2 19.7 %collective-permute-start.7 = (bf16[256,1024]{1,0:T(8,128)(2,1)S(1)}, bf16[256,1024]{1,0:T(8,128)(2,1)S(1)}, u32[]{:S(2)}, u32[]{:S(2)}) collective-permute-start(bf16[256,1024]{1,0:T(8,128)(2,1)S(1)} %shard_map.119.refs_0_), channel_id=1, source_target_pairs={{0,4},{4,0},{8,12},{12,8},{16,20},{20,16},{24,28},{28,24},{1,5},{5... | collective-permute-start | bytes 1572872 | tf_op jit(solution)/shard_map/ppermute | solution.py:174
  25.7 13.2 %collective-permute-start.9 = (bf16[256,1024]{1,0:T(8,128)(2,1)S(1)}, bf16[256,1024]{1,0:T(8,128)(2,1)S(1)}, u32[]{:S(2)}, u32[]{:S(2)}) collective-permute-start(bf16[256,1024]{1,0:T(8,128)(2,1)S(1)} %collective-permute-done.8.refs_2_), channel_id=1, source_target_pairs={{0,4},{4,0},{8,12},{12,8},{16,20},{20,16},{24,28},{28,24},{1,5},{5... | collective-permute-start | bytes 1572872 | tf_op jit(solution)/shard_map/ppermute | solution.py:174
  26.8 14.3 %collective-permute-start.11 = (bf16[256,1024]{1,0:T(8,128)(2,1)S(1)}, bf16[256,1024]{1,0:T(8,128)(2,1)S(1)}, u32[]{:S(2)}, u32[]{:S(2)}) collective-permute-start(bf16[256,1024]{1,0:T(8,128)(2,1)S(1)} %collective-permute-done.10.refs_4_), channel_id=1, source_target_pairs={{0,4},{4,0},{8,12},{12,8},{16,20},{20,16},{24,28},{28,24},{1,5},{5... | collective-permute-start | bytes 1572872 | tf_op jit(solution)/shard_map/ppermute | solution.py:174
  75.3 9.1 %collective-permute-start.23 = (bf16[64,1024]{1,0:T(8,128)(2,1)S(1)}, bf16[64,1024]{1,0:T(8,128)(2,1)S(1)}, u32[]{:S(2)}, u32[]{:S(2)}) collective-permute-start(bf16[64,1024]{1,0:T(8,128)(2,1)S(1)} %get-tuple-element.69.refs_0_), channel_id=1, source_target_pairs={{0,4},{4,0},{8,12},{12,8},{16,20},{20,16},{24,28},{28,24},{1,5},{5... | collective-permute-start | bytes 393224 | tf_op jit(solution)/shard_map/ppermute | solution.py:174
  82.0 14.3 %collective-permute-start.33 = (bf16[256,512]{1,0:T(8,128)(2,1)S(1)}, bf16[256,512]{1,0:T(8,128)(2,1)S(1)}, u32[]{:S(2)}, u32[]{:S(2)}) collective-permute-start(bf16[256,512]{1,0:T(8,128)(2,1)S(1)} %get-tuple-element.68), channel_id=1, source_target_pairs={{0,2},{1,3},{2,0},{3,1},{4,6},{5,7},{6,4},{7,5},{8,10},{9,11},{10,... | collective-permute-start | bytes 786440 | tf_op jit(solution)/shard_map/ppermute | solution.py:174
  85.1 12.1 %collective-permute-start.34 = (bf16[256,512]{1,0:T(8,128)(2,1)S(1)}, bf16[256,512]{1,0:T(8,128)(2,1)S(1)}, u32[]{:S(2)}, u32[]{:S(2)}) collective-permute-start(bf16[256,512]{1,0:T(8,128)(2,1)S(1)} %get-tuple-element.79), channel_id=1, source_target_pairs={{0,1},{1,0},{2,3},{3,2},{4,5},{5,4},{6,7},{7,6},{8,9},{9,8},{10,11... | collective-permute-start | bytes 786440 | tf_op jit(solution)/shard_map/ppermute | solution.py:174
  85.4 21.8 %collective-permute-start.35 = (bf16[256,512]{1,0:T(8,128)(2,1)S(1)}, bf16[256,512]{1,0:T(8,128)(2,1)S(1)}, u32[]{:S(2)}, u32[]{:S(2)}) collective-permute-start(bf16[256,512]{1,0:T(8,128)(2,1)S(1)} %get-tuple-element.81), channel_id=1, source_target_pairs={{0,3},{1,2},{2,1},{3,0},{4,7},{5,6},{6,5},{7,4},{8,11},{9,10},{10,... | collective-permute-start | bytes 786440 | tf_op jit(solution)/shard_map/ppermute | solution.py:174
  86.8 20.4 %collective-permute-start.30 = (bf16[512,1024]{1,0:T(8,128)(2,1)S(1)}, bf16[512,1024]{1,0:T(8,128)(2,1)S(1)}, u32[]{:S(2)}, u32[]{:S(2)}) collective-permute-start(bf16[512,1024]{1,0:T(8,128)(2,1)S(1)} %copy-done.4), channel_id=1, source_target_pairs={{0,4},{4,0},{8,12},{12,8},{16,20},{20,16},{24,28},{28,24},{1,5},{5... | collective-permute-start | bytes 3145736 | tf_op jit(solution)/shard_map/ppermute | solution.py:174
  87.6 19.7 %collective-permute-start.31 = (bf16[512,1024]{1,0:T(8,128)(2,1)S(1)}, bf16[512,1024]{1,0:T(8,128)(2,1)S(1)}, u32[]{:S(2)}, u32[]{:S(2)}) collective-permute-start(bf16[512,1024]{1,0:T(8,128)(2,1)S(1)} %copy-done.5), channel_id=1, source_target_pairs={{0,4},{4,0},{8,12},{12,8},{16,20},{20,16},{24,28},{28,24},{1,5},{5... | collective-permute-start | bytes 3145736 | tf_op jit(solution)/shard_map/ppermute | solution.py:174
  96.3 11.0 %collective-permute-start.32 = (bf16[512,1024]{1,0:T(8,128)(2,1)S(1)}, bf16[512,1024]{1,0:T(8,128)(2,1)S(1)}, u32[]{:S(2)}, u32[]{:S(2)}) collective-permute-start(bf16[512,1024]{1,0:T(8,128)(2,1)S(1)} %copy-done.6), channel_id=1, source_target_pairs={{0,4},{4,0},{8,12},{12,8},{16,20},{20,16},{24,28},{28,24},{1,5},{5... | collective-permute-start | bytes 3145736 | tf_op jit(solution)/shard_map/ppermute | solution.py:174
  109.1 11.5 %collective-permute-start.40 = (bf16[256,512]{1,0:T(8,128)(2,1)S(1)}, bf16[256,512]{1,0:T(8,128)(2,1)S(1)}, u32[]{:S(2)}, u32[]{:S(2)}) collective-permute-start(bf16[256,512]{1,0:T(8,128)(2,1)S(1)} %add_convert_fusion.refs_0_), channel_id=1, source_target_pairs={{0,1},{1,0},{2,3},{3,2},{4,5},{5,4},{6,7},{7,6},{8,9},{9,8},{10,11... | collective-permute-start | bytes 786440 | tf_op jit(solution)/shard_map/ppermute | solution.py:174
  109.1 17.8 %collective-permute-start.42 = (bf16[256,512]{1,0:T(8,128)(2,1)S(1)}, bf16[256,512]{1,0:T(8,128)(2,1)S(1)}, u32[]{:S(2)}, u32[]{:S(2)}) collective-permute-start(bf16[256,512]{1,0:T(8,128)(2,1)S(1)} %add_convert_fusion.refs_0_), channel_id=1, source_target_pairs={{0,2},{1,3},{2,0},{3,1},{4,6},{5,7},{6,4},{7,5},{8,10},{9,11},{10,... | collective-permute-start | bytes 786440 | tf_op jit(solution)/shard_map/ppermute | solution.py:174
  115.3 10.1 %collective-permute-start.39 = (bf16[272,384]{1,0:T(8,128)(2,1)S(1)}, bf16[272,384]{1,0:T(8,128)(2,1)S(1)}, u32[]{:S(2)}, u32[]{:S(2)}) collective-permute-start(bf16[272,384]{1,0:T(8,128)(2,1)S(1)} %get-tuple-element.90), channel_id=1, source_target_pairs={{0,24},{4,28},{8,16},{12,20},{16,8},{20,12},{24,0},{28,4},{1,25},{... | collective-permute-start | bytes 626696 | tf_op jit(solution)/shard_map/ppermute | solution.py:174
  126.9 13.2 %collective-permute-start.47 = (bf16[256,512]{1,0:T(8,128)(2,1)S(1)}, bf16[256,512]{1,0:T(8,128)(2,1)S(1)}, u32[]{:S(2)}, u32[]{:S(2)}) collective-permute-start(bf16[256,512]{1,0:T(8,128)(2,1)S(1)} %add_convert_fusion.refs_0_), channel_id=1, source_target_pairs={{0,3},{1,2},{2,1},{3,0},{4,7},{5,6},{6,5},{7,4},{8,11},{9,10},{10,... | collective-permute-start | bytes 786440 | tf_op jit(solution)/shard_map/ppermute | solution.py:174
  130.8 14.8 %collective-permute-start.44 = (bf16[528,384]{1,0:T(8,128)(2,1)S(1)}, bf16[528,384]{1,0:T(8,128)(2,1)S(1)}, u32[]{:S(2)}, u32[]{:S(2)}) collective-permute-start(bf16[528,384]{1,0:T(8,128)(2,1)S(1)} %get-tuple-element.94), channel_id=1, source_target_pairs={{0,8},{4,12},{8,0},{12,4},{16,24},{20,28},{24,16},{28,20},{1,9},{5... | collective-permute-start | bytes 1216520 | tf_op jit(solution)/shard_map/ppermute | solution.py:174
  131.3 14.3 %collective-permute-start.45 = (bf16[528,384]{1,0:T(8,128)(2,1)S(1)}, bf16[528,384]{1,0:T(8,128)(2,1)S(1)}, u32[]{:S(2)}, u32[]{:S(2)}) collective-permute-start(bf16[528,384]{1,0:T(8,128)(2,1)S(1)} %get-tuple-element.95), channel_id=1, source_target_pairs={{0,16},{4,20},{8,24},{12,28},{16,0},{20,4},{24,8},{28,12},{1,17},{... | collective-permute-start | bytes 1216520 | tf_op jit(solution)/shard_map/ppermute | solution.py:174
  132.6 17.8 %collective-permute-start.46 = (bf16[528,384]{1,0:T(8,128)(2,1)S(1)}, bf16[528,384]{1,0:T(8,128)(2,1)S(1)}, u32[]{:S(2)}, u32[]{:S(2)}) collective-permute-start(bf16[528,384]{1,0:T(8,128)(2,1)S(1)} %get-tuple-element.96), channel_id=1, source_target_pairs={{0,24},{4,28},{8,16},{12,20},{16,8},{20,12},{24,0},{28,4},{1,25},{... | collective-permute-start | bytes 1216520 | tf_op jit(solution)/shard_map/ppermute | solution.py:174
  143.7 11.0 %collective-permute-start.49 = (bf16[272,384]{1,0:T(8,128)(2,1)S(1)}, bf16[272,384]{1,0:T(8,128)(2,1)S(1)}, u32[]{:S(2)}, u32[]{:S(2)}) collective-permute-start(bf16[272,384]{1,0:T(8,128)(2,1)S(1)} %get-tuple-element.100), channel_id=1, source_target_pairs={{0,8},{4,12},{8,0},{12,4},{16,24},{20,28},{24,16},{28,20},{1,9},{5... | collective-permute-start | bytes 626696 | tf_op jit(solution)/shard_map/ppermute | solution.py:174
  144.2 16.0 %collective-permute-start.50 = (bf16[272,384]{1,0:T(8,128)(2,1)S(1)}, bf16[272,384]{1,0:T(8,128)(2,1)S(1)}, u32[]{:S(2)}, u32[]{:S(2)}) collective-permute-start(bf16[272,384]{1,0:T(8,128)(2,1)S(1)} %get-tuple-element.101), channel_id=1, source_target_pairs={{0,16},{4,20},{8,24},{12,28},{16,0},{20,4},{24,8},{28,12},{1,17},{... | collective-permute-start | bytes 626696 | tf_op jit(solution)/shard_map/ppermute | solution.py:174
  150.4 9.9 %collective-permute-start.51 = (bf16[272,384]{1,0:T(8,128)(2,1)S(1)}, bf16[272,384]{1,0:T(8,128)(2,1)S(1)}, u32[]{:S(2)}, u32[]{:S(2)}) collective-permute-start(bf16[272,384]{1,0:T(8,128)(2,1)S(1)} %get-tuple-element.103), channel_id=1, source_target_pairs={{0,24},{4,28},{8,16},{12,20},{16,8},{20,12},{24,0},{28,4},{1,25},{... | collective-permute-start | bytes 626696 | tf_op jit(solution)/shard_map/ppermute | solution.py:174
  183.7 12.8 %collective-permute-start.66 = (bf16[256,512]{1,0:T(8,128)(2,1)S(1)}, bf16[256,512]{1,0:T(8,128)(2,1)S(1)}, u32[]{:S(2)}, u32[]{:S(2)}) collective-permute-start(bf16[256,512]{1,0:T(8,128)(2,1)S(1)} %get-tuple-element.106), channel_id=1, source_target_pairs={{0,2},{1,3},{2,0},{3,1},{4,6},{5,7},{6,4},{7,5},{8,10},{9,11},{10,... | collective-permute-start | bytes 786440 | tf_op jit(solution)/shard_map/ppermute | solution.py:174
  186.1 10.4 %collective-permute-start.67 = (bf16[256,512]{1,0:T(8,128)(2,1)S(1)}, bf16[256,512]{1,0:T(8,128)(2,1)S(1)}, u32[]{:S(2)}, u32[]{:S(2)}) collective-permute-start(bf16[256,512]{1,0:T(8,128)(2,1)S(1)} %get-tuple-element.109), channel_id=1, source_target_pairs={{0,1},{1,0},{2,3},{3,2},{4,5},{5,4},{6,7},{7,6},{8,9},{9,8},{10,11... | collective-permute-start | bytes 786440 | tf_op jit(solution)/shard_map/ppermute | solution.py:174
  186.6 21.7 %collective-permute-start.68 = (bf16[256,512]{1,0:T(8,128)(2,1)S(1)}, bf16[256,512]{1,0:T(8,128)(2,1)S(1)}, u32[]{:S(2)}, u32[]{:S(2)}) collective-permute-start(bf16[256,512]{1,0:T(8,128)(2,1)S(1)} %get-tuple-element.111), channel_id=1, source_target_pairs={{0,3},{1,2},{2,1},{3,0},{4,7},{5,6},{6,5},{7,4},{8,11},{9,10},{10,... | collective-permute-start | bytes 786440 | tf_op jit(solution)/shard_map/ppermute | solution.py:174
  208.6 14.2 %collective-permute-start.69 = (bf16[128,512]{1,0:T(8,128)(2,1)S(1)}, bf16[128,512]{1,0:T(8,128)(2,1)S(1)}, u32[]{:S(2)}, u32[]{:S(2)}) collective-permute-start(bf16[128,512]{1,0:T(8,128)(2,1)S(1)} %get-tuple-element.113), channel_id=1, source_target_pairs={{0,0},{1,8},{2,16},{3,24},{4,4},{5,12},{6,20},{7,28},{8,1},{9,9},{... | collective-permute-start | bytes 393224 | tf_op jit(solution)/shard_map/ppermute | solution.py:676
  210.5 15.1 %collective-permute-start.70 = (bf16[128,512]{1,0:T(8,128)(2,1)S(1)}, bf16[128,512]{1,0:T(8,128)(2,1)S(1)}, u32[]{:S(2)}, u32[]{:S(2)}) collective-permute-start(bf16[128,512]{1,0:T(8,128)(2,1)S(1)} %get-tuple-element.114), channel_id=1, source_target_pairs={{0,4},{1,12},{2,20},{3,28},{4,0},{5,8},{6,16},{7,24},{8,5},{9,13},... | collective-permute-start | bytes 393224 | tf_op jit(solution)/shard_map/ppermute | solution.py:676
  (50 other events, 381.9 us)

commit v7 on v5

--- a/solution.py
+++ b/solution.py
@@ -331,13 +331,31 @@
     quarters(whole, weight, outs)
 
 
-def latent_out_kernel(count, weight, *refs):
-    pieces, outs, whole = refs[:count], refs[count:-1], refs[-1]
-    chip, core, _ = place()
+def latent_out_kernel(count, parts, weight, *refs):
+    pieces, blocks, refs = refs[:count], refs[count : count + parts], refs[count + parts :]
+    outs, (whole, hidden) = refs[:-2], refs[-2:]
+    chip, core, tensor = place()
     for n, piece in enumerate(pieces):
         index = (count // 2) * (core ^ (n % 2)) + (chip ^ (n // 2))
         whole[:, aligned(index, HEAD_DIM)] = piece[...]
-    quarters(whole, weight, outs)
+    height = outs[0].shape[0]
+    for r, block in enumerate(blocks):
+        hidden[aligned(tensor ^ r, height), :] = block[...]
+    share = (tensor == chip).astype(jnp.float32)
+    for d, out in reversed(list(enumerate(outs))):
+        span = aligned(chip ^ d, height)
+        product = dot(whole[span, :], weight[...])
+        out[...] = (product + hidden[span, :].astype(jnp.float32) * share).astype(out.dtype)
+
+
+def column_kernel(*refs):
+    blocks, outs, whole = refs[: (len(refs) - 1) // 2], refs[(len(refs) - 1) // 2 : -1], refs[-1]
+    chip, _, tensor = place()
+    height = blocks[0].shape[0]
+    for d, block in enumerate(blocks):
+        whole[aligned(chip ^ d, height), :] = block[...].astype(jnp.float32)
+    for r, out in enumerate(outs):
+        out[...] = whole[aligned(tensor ^ r, height), :].astype(out.dtype)
 
 
 def arrange_kernel(*refs):
@@ -443,10 +461,10 @@
         attended[i * height : (i + 1) * height, :] = (numerator / denominator).astype(jnp.bfloat16)
 
 
-def final_kernel(own, hidden, *refs):
+def final_kernel(own, *refs):
     received, outs, whole = refs[:-3], refs[-3:-1], refs[-1]
     _, core, _ = place()
-    total = own[...] + hidden[...].astype(jnp.float32)
+    total = own[...]
     for block in received:
         total += block[...].astype(jnp.float32)
     whole[...] = total
@@ -542,17 +560,6 @@
     )
 
     spilled = [shifted(below, "seq", 1), shifted(above, "seq", -1)]
-    weights = []
-    for weight in (latent_query, latent_key, latent_value):
-        weights += [weight, core_swapped(after(weight, own))]
-    head_weights = call(
-        arrange_kernel,
-        [((2 * out_width, 3 * HEAD_DIM), bf16)] * chip_count,
-        *weights,
-        far=6,
-        scratch=[pltpu.SemaphoreType.DMA((6 * chip_count,))],
-    )
-    own, *head_weights = lax.optimization_barrier((own, *head_weights))
     own = own + jnp.concatenate(spilled, axis=0)
 
     total, *sent = call(
@@ -563,19 +570,33 @@
         scratch=[pltpu.VMEM((patch_count, local_width), bf16)],
         flops=2 * patch_count * local_width * out_width,
     )
-    for r, block in enumerate(sent, 1):
-        total = total + exchanged(block, "tensor", r).astype(f32)
+    received = [exchanged(block, "tensor", r) for r, block in enumerate(sent, 1)]
+
+    weights = []
+    for weight in (latent_query, latent_key, latent_value):
+        weights += [weight, core_swapped(after(weight, total))]
+    head_weights = call(
+        arrange_kernel,
+        [((2 * out_width, 3 * HEAD_DIM), bf16)] * chip_count,
+        *weights,
+        far=6,
+        scratch=[pltpu.SemaphoreType.DMA((6 * chip_count,))],
+    )
+    total, *head_weights = lax.optimization_barrier((total, *head_weights))
+    for share in received:
+        total = total + share.astype(f32)
     latent_in = total.astype(bf16)
 
     gain = norm_gain[None, :]
     groups = [[0], list(range(1, min(3, tensor_count))), list(range(3, tensor_count))]
     groups = [group for group in groups if group]
-    shares, arrived = [], []
+    shares, arrived, latent_blocks = [], [], [latent_in]
     for g, group in enumerate(groups):
         blocks = [latent_in]
         if g:
             start = after(latent_in, *arrived, *shares[:chip_count]) if g > 1 else latent_in
             arrived = [exchanged(start, "tensor", r) for r in group]
+            latent_blocks += arrived
             blocks = [after(block, *shares[:chip_count]) for block in arrived]
         height = len(group) * quarter
         share, *sent = call(
@@ -599,32 +620,34 @@
         flops=2 * patch_count * patch_count * HEAD_DIM,
     )
 
-    total, *sent = call(
-        functools.partial(latent_out_kernel, seq_count),
-        [((quarter, out_width), f32 if r == 0 else bf16) for r in range(tensor_count)],
+    own, *sent = call(
+        functools.partial(latent_out_kernel, seq_count, tensor_count),
+        [((quarter, out_width), bf16 if d else f32) for d in range(chip_count)],
         latent_out,
         *over_plane(attended),
-        scratch=[pltpu.VMEM((patch_count, local_width), bf16)],
+        *latent_blocks,
+        scratch=[
+            pltpu.VMEM((patch_count, local_width), bf16),
+            pltpu.VMEM((patch_count, out_width), bf16),
+        ],
         flops=2 * patch_count * local_width * out_width,
     )
-    pieces = call(
+
+    total, *sent = call(
+        column_kernel,
+        [((quarter, out_width), bf16 if r else f32) for r in range(tensor_count)],
+        own,
+        *[exchanged(block, "seq", 2 * d) for d, block in enumerate(sent, 1)],
+        scratch=[pltpu.VMEM((patch_count, out_width), f32)],
+    )
+    same, crossed = call(
         final_kernel,
         [((patch_dev, out_width), bf16)] * 2,
         total,
-        latent_in,
         *[exchanged(block, "tensor", r) for r, block in enumerate(sent, 1)],
         scratch=[pltpu.VMEM((quarter, out_width), f32)],
     )
-
-    moved = []
-    for flip in range(2):
-        route = [
-            (s * tensor_count + t, (2 * t + ((s % 2) ^ flip)) * tensor_count + s // 2)
-            for s in range(seq_count)
-            for t in range(tensor_count)
-        ]
-        moved.append(lax.ppermute(pieces[flip], ("seq", "tensor"), route))
-    same, crossed = moved
+    crossed = core_swapped(crossed)
     return jnp.concatenate(
         [jnp.where(core == 0, same, crossed), jnp.where(core == 0, crossed, same)], axis=1
     )

time: 223 us -> 219 us (0.982)
    ppermute x2 -> x0, waiting for transfers between devices: 11.8 us -> none  [per_device(): moved.append(lax.ppermute(pieces[flip], ('seq', 'tensor'), route))]
    ppermute x53 -> x57, waiting for transfers between devices: 86.5 us -> 96.1 us  [exchanged(): return lax.ppermute(block, axis, route)]
    ppermute x2 -> x0, starting transfers between devices: 5.88 us -> none  [per_device(): moved.append(lax.ppermute(pieces[flip], ('seq', 'tensor'), route))]
    ppermute x53 -> x57, starting transfers between devices: 78.4 us -> 83.4 us  [exchanged(): return lax.ppermute(block, axis, route)]
    pallas_call x11 -> x12, Pallas kernels: 23.8 us -> 23.9 us  [call(): pl.pallas_call(kernel, out_shape=shapes, in_specs=[pl.BlockSpec(memory_sp...]
  transfers between devices with their start and end apart: 57 -> 59, of which waited for: 28 -> 32; matrix products, arithmetic and copies ran while one was open for 1% -> 1% of each run, Pallas kernels for 4% -> 4%
where the time goes in v7:
time: 219 us; the launch traced here: 218 us
  waiting for transfers between devices  97.8 us (45%)
  starting transfers between devices  89.2 us (41%)
  Pallas kernels  23.9 us (11%)
  local copies, waits for them, and re-layouts  5.37 us (2%)
    ppermute x57, waiting for transfers between devices, exchanged(): return lax.ppermute(block, axis, route)  96.1 us
    ppermute x57, starting transfers between devices, exchanged(): return lax.ppermute(block, axis, route)  83.4 us
    pallas_call x12, Pallas kernels, call(): pl.pallas_call(kernel, out_shape=shapes, in_specs=[pl.BlockSpec(memory_sp...  23.9 us
    ppermute x2, starting transfers between devices, shifted(): return lax.ppermute(block, axis, route)  5.74 us
    unnamed x22, local copies, waits for them, and re-layouts  4.48 us
  transfers between devices with their start and end apart: 59, of which 32 were waited for; matrix products, arithmetic and copies ran while one was open for 1% of the time, Pallas kernels for 4%

profile of v7, /device:TPU:9, one launch (start us, length us, event | category | flops | bytes accessed | tf_op | source)
XLA Modules:
  0.0 218.3 jit_solution(10897711907494620735)
XLA Ops:
  4.2 3.2 %collective-permute-done.1.refs_2_ = bf16[128,1024]{1,0:T(8,128)(2,1)S(1)} collective-permute-done((bf16[128,1024]{1,0:T(8,128)(2,1)}, bf16[128,1024]{1,0:T(8,128)(2,1)S(1)}, u32[]{:S(2)}, u32[]{:S(2)}) %collective-permute-start.1) | collective-permute-done | bytes 262176 | tf_op jit(solution)/shard_map/ppermute | solution.py:174
  7.4 2.7 %collective-permute-start.2 = (bf16[128,1024]{1,0:T(8,128)(2,1)S(1)}, bf16[128,1024]{1,0:T(8,128)(2,1)S(1)}, u32[]{:S(2)}, u32[]{:S(2)}) collective-permute-start(bf16[128,1024]{1,0:T(8,128)(2,1)S(1)} %collective-permute-done.1.refs_2_), channel_id=1, source_target_pairs={{0,4},{4,0},{8,12},{12,8},{16,20},{20,16},{24,28},{28,24},{1,5},{5... | collective-permute-start | bytes 786440 | tf_op jit(solution)/shard_map/ppermute | solution.py:174
  15.9 2.1 collective-permute-start.4
  22.2 1.9 shard_map.118.query
  26.8 12.1 %collective-permute-start.11 = (bf16[256,1024]{1,0:T(8,128)(2,1)S(1)}, bf16[256,1024]{1,0:T(8,128)(2,1)S(1)}, u32[]{:S(2)}, u32[]{:S(2)}) collective-permute-start(bf16[256,1024]{1,0:T(8,128)(2,1)S(1)} %collective-permute-done.10.refs_4_), channel_id=1, source_target_pairs={{0,4},{4,0},{8,12},{12,8},{16,20},{20,16},{24,28},{28,24},{1,5},{5... | collective-permute-start | bytes 1572872 | tf_op jit(solution)/shard_map/ppermute | solution.py:174
  38.9 2.2 %collective-permute-done.11.refs_5_ = bf16[256,1024]{1,0:T(8,128)(2,1)S(1)} collective-permute-done((bf16[256,1024]{1,0:T(8,128)(2,1)S(1)}, bf16[256,1024]{1,0:T(8,128)(2,1)S(1)}, u32[]{:S(2)}, u32[]{:S(2)}) %collective-permute-start.11) | collective-permute-done | bytes 524320 | tf_op jit(solution)/shard_map/ppermute | solution.py:174
  41.4 10.2 %shard_map.120 = (bf16[128,1024]{1,0:T(8,128)(2,1)S(1)}, bf16[64,1024]{1,0:T(8,128)(2,1)S(1)}, bf16[64,1024]{1,0:T(8,128)(2,1)S(1)}) custom-call(s32[1,1024]{1,0:T(1,128)S(1)} %bitcast.7, bf16[256,1024]{1,0:T(8,128)(2,1)S(1)} %shard_map.118.query, bf16[1024,1024]{1,0:T(8,128)(2,1)S(1)} %copy-done.1, bf16[256,1024]{1,0:T(8,128)(2,1)S(1)} %shard_map.119.refs_0_, ...), custom_call_target="tpu_custom_call" | custom-call | flops 5368709120 | bytes 7344128 | tf_op jit(solution)/shard_map/pallas_call | solution.py:207
  51.6 2.3 %collective-permute-start.15 = (bf16[64,1024]{1,0:T(8,128)(2,1)S(1)}, bf16[64,1024]{1,0:T(8,128)(2,1)S(1)}, u32[]{:S(2)}, u32[]{:S(2)}) collective-permute-start(bf16[64,1024]{1,0:T(8,128)(2,1)S(1)} %get-tuple-element.61), channel_id=1, source_target_pairs={{4,0},{8,4},{12,8},{16,12},{20,16},{24,20},{28,24},{5,1},{9,5},{13... | collective-permute-start | bytes 393224 | tf_op jit(solution)/shard_map/ppermute | solution.py:22
  53.9 3.5 %collective-permute-start.14 = (bf16[64,1024]{1,0:T(8,128)(2,1)S(1)}, bf16[64,1024]{1,0:T(8,128)(2,1)S(1)}, u32[]{:S(2)}, u32[]{:S(2)}) collective-permute-start(bf16[64,1024]{1,0:T(8,128)(2,1)S(1)} %get-tuple-element.60), channel_id=1, source_target_pairs={{0,4},{4,8},{8,12},{12,16},{16,20},{20,24},{24,28},{1,5},{5,9},{9,... | collective-permute-start | bytes 393224 | tf_op jit(solution)/shard_map/ppermute | solution.py:22
  62.0 2.6 %collective-permute-start.16 = (bf16[128,1024]{1,0:T(8,128)(2,1)S(1)}, bf16[128,1024]{1,0:T(8,128)(2,1)S(1)}, u32[]{:S(2)}, u32[]{:S(2)}) collective-permute-start(bf16[128,1024]{1,0:T(8,128)(2,1)S(1)} %maximum_add_fusion.refs_0_), channel_id=1, source_target_pairs={{0,4},{4,0},{8,12},{12,8},{16,20},{20,16},{24,28},{28,24},{1,5},{5... | collective-permute-start | bytes 786440 | tf_op jit(solution)/shard_map/ppermute | solution.py:174
  66.3 3.0 %collective-permute-start.18 = (bf16[128,1024]{1,0:T(8,128)(2,1)S(1)}, bf16[128,1024]{1,0:T(8,128)(2,1)S(1)}, u32[]{:S(2)}, u32[]{:S(2)}) collective-permute-start(bf16[128,1024]{1,0:T(8,128)(2,1)S(1)} %collective-permute-done.17.refs_2_), channel_id=1, source_target_pairs={{0,4},{4,0},{8,12},{12,8},{16,20},{20,16},{24,28},{28,24},{1,5},{5... | collective-permute-start | bytes 786440 | tf_op jit(solution)/shard_map/ppermute | solution.py:174
  69.4 5.5 %collective-permute-start.20 = (bf16[128,1024]{1,0:T(8,128)(2,1)S(1)}, bf16[128,1024]{1,0:T(8,128)(2,1)S(1)}, u32[]{:S(2)}, u32[]{:S(2)}) collective-permute-start(bf16[128,1024]{1,0:T(8,128)(2,1)S(1)} %collective-permute-done.19.refs_4_), channel_id=1, source_target_pairs={{0,4},{4,0},{8,12},{12,8},{16,20},{20,16},{24,28},{28,24},{1,5},{5... | collective-permute-start | bytes 786440 | tf_op jit(solution)/shard_map/ppermute | solution.py:174
  84.6 13.1 %collective-permute-done.28 = bf16[256,512]{1,0:T(8,128)(2,1)S(1)} collective-permute-done((bf16[256,512]{1,0:T(8,128)(2,1)S(1)}, bf16[256,512]{1,0:T(8,128)(2,1)S(1)}, u32[]{:S(2)}, u32[]{:S(2)}) %collective-permute-start.28) | collective-permute-done | bytes 262176 | tf_op jit(solution)/shard_map/ppermute | solution.py:174
  97.7 4.7 %collective-permute-done.27 = bf16[256,512]{1,0:T(8,128)(2,1)S(1)} collective-permute-done((bf16[256,512]{1,0:T(8,128)(2,1)S(1)}, bf16[256,512]{1,0:T(8,128)(2,1)S(1)}, u32[]{:S(2)}, u32[]{:S(2)}) %collective-permute-start.27) | collective-permute-done | bytes 262176 | tf_op jit(solution)/shard_map/ppermute | solution.py:174
  103.6 2.1 collective-permute-start.33
  110.7 6.1 %collective-permute-done.33.refs_0_.refs_9_ = bf16[256,512]{1,0:T(8,128)(2,1)S(1)} collective-permute-done((bf16[256,512]{1,0:T(8,128)(2,1)S(1)}, bf16[256,512]{1,0:T(8,128)(2,1)S(1)}, u32[]{:S(2)}, u32[]{:S(2)}) %collective-permute-start.33) | collective-permute-done | bytes 262176 | tf_op jit(solution)/shard_map/ppermute | solution.py:174
  116.8 2.3 %collective-permute-done.32.refs_3_ = bf16[272,384]{1,0:T(8,128)(2,1)S(1)} collective-permute-done((bf16[272,384]{1,0:T(8,128)(2,1)S(1)}, bf16[272,384]{1,0:T(8,128)(2,1)S(1)}, u32[]{:S(2)}, u32[]{:S(2)}) %collective-permute-start.32) | collective-permute-done | bytes 208928 | tf_op jit(solution)/shard_map/ppermute | solution.py:174
  121.9 2.3 %shard_map.124 = (f32[520,384]{1,0:T(8,128)S(1)}, bf16[528,384]{1,0:T(8,128)(2,1)S(1)}, bf16[528,384]{1,0:T(8,128)(2,1)S(1)}, bf16[528,384]{1,0:T(8,128)(2,1)S(1)}) custom-call(f32[1,4096]{1,0:T(1,128)S(1)} %bitcast.4, bf16[256,512]{1,0:T(8,128)(2,1)S(1)} %collective-permute-done.33.refs_0_.refs_9_, bf16[256,512]{1,0:T(8,128)(2,1)S(1)} %collective-permute-done.34.refs_1_, ...), custom_call_target="tpu_custom_call" | custom-call | flops 1610612736 | bytes 6225920 | tf_op jit(solution)/shard_map/pallas_call | solution.py:207
  127.0 6.4 %collective-permute-done.40.refs_0_.refs_11_ = bf16[256,512]{1,0:T(8,128)(2,1)S(1)} collective-permute-done((bf16[256,512]{1,0:T(8,128)(2,1)S(1)}, bf16[256,512]{1,0:T(8,128)(2,1)S(1)}, u32[]{:S(2)}, u32[]{:S(2)}) %collective-permute-start.40) | collective-permute-done | bytes 262176 | tf_op jit(solution)/shard_map/ppermute | solution.py:174
  137.2 7.6 %collective-permute-done.39.refs_7_ = bf16[528,384]{1,0:T(8,128)(2,1)S(1)} collective-permute-done((bf16[528,384]{1,0:T(8,128)(2,1)S(1)}, bf16[528,384]{1,0:T(8,128)(2,1)S(1)}, u32[]{:S(2)}, u32[]{:S(2)}) %collective-permute-start.39) | collective-permute-done | bytes 405536 | tf_op jit(solution)/shard_map/ppermute | solution.py:174
  147.4 2.8 %collective-permute-done.42.refs_9_ = bf16[272,384]{1,0:T(8,128)(2,1)S(1)} collective-permute-done((bf16[272,384]{1,0:T(8,128)(2,1)S(1)}, bf16[272,384]{1,0:T(8,128)(2,1)S(1)}, u32[]{:S(2)}, u32[]{:S(2)}) %collective-permute-start.42) | collective-permute-done | bytes 208928 | tf_op jit(solution)/shard_map/ppermute | solution.py:174
  150.9 3.3 %collective-permute-done.44.refs_11_ = bf16[272,384]{1,0:T(8,128)(2,1)S(1)} collective-permute-done((bf16[272,384]{1,0:T(8,128)(2,1)S(1)}, bf16[272,384]{1,0:T(8,128)(2,1)S(1)}, u32[]{:S(2)}, u32[]{:S(2)}) %collective-permute-start.44) | collective-permute-done | bytes 208928 | tf_op jit(solution)/shard_map/ppermute | solution.py:174
  154.1 2.0 shard_map.126.refs_0_
  159.1 3.6 %collective-permute-start.45 = (bf16[1024,128]{1,0:T(8,128)(2,1)S(1)}, bf16[1024,128]{1,0:T(8,128)(2,1)S(1)}, u32[]{:S(2)}, u32[]{:S(2)}) collective-permute-start(bf16[1024,128]{1,0:T(8,128)(2,1)S(1)} %shard_map.126.refs_0_), channel_id=1, source_target_pairs={{0,4},{4,0},{8,12},{12,8},{16,20},{20,16},{24,28},{28,24},{1,5},{5... | collective-permute-start | bytes 786440 | tf_op jit(solution)/shard_map/ppermute | solution.py:174
  162.7 5.0 %collective-permute-start.47 = (bf16[1024,128]{1,0:T(8,128)(2,1)S(1)}, bf16[1024,128]{1,0:T(8,128)(2,1)S(1)}, u32[]{:S(2)}, u32[]{:S(2)}) collective-permute-start(bf16[1024,128]{1,0:T(8,128)(2,1)S(1)} %collective-permute-done.46.refs_2_), channel_id=1, source_target_pairs={{0,4},{4,0},{8,12},{12,8},{16,20},{20,16},{24,28},{28,24},{1,5},{5... | collective-permute-start | bytes 786440 | tf_op jit(solution)/shard_map/ppermute | solution.py:174
  167.7 4.5 %collective-permute-start.49 = (bf16[1024,128]{1,0:T(8,128)(2,1)S(1)}, bf16[1024,128]{1,0:T(8,128)(2,1)S(1)}, u32[]{:S(2)}, u32[]{:S(2)}) collective-permute-start(bf16[1024,128]{1,0:T(8,128)(2,1)S(1)} %collective-permute-done.48.refs_4_), channel_id=1, source_target_pairs={{0,4},{4,0},{8,12},{12,8},{16,20},{20,16},{24,28},{28,24},{1,5},{5... | collective-permute-start | bytes 786440 | tf_op jit(solution)/shard_map/ppermute | solution.py:174
  173.8 1.9 shard_map.127
  178.4 4.9 %collective-permute-done.52.refs_1_ = bf16[256,512]{1,0:T(8,128)(2,1)S(1)} collective-permute-done((bf16[256,512]{1,0:T(8,128)(2,1)S(1)}, bf16[256,512]{1,0:T(8,128)(2,1)S(1)}, u32[]{:S(2)}, u32[]{:S(2)}) %collective-permute-start.52) | collective-permute-done | bytes 262176 | tf_op jit(solution)/shard_map/ppermute | solution.py:174
  183.3 5.7 %collective-permute-done.54.refs_3_ = bf16[256,512]{1,0:T(8,128)(2,1)S(1)} collective-permute-done((bf16[256,512]{1,0:T(8,128)(2,1)S(1)}, bf16[256,512]{1,0:T(8,128)(2,1)S(1)}, u32[]{:S(2)}, u32[]{:S(2)}) %collective-permute-start.54) | collective-permute-done | bytes 262176 | tf_op jit(solution)/shard_map/ppermute | solution.py:174
  192.1 7.6 %collective-permute-done.55.refs_0_ = bf16[256,512]{1,0:T(8,128)(2,1)S(1)} collective-permute-done((bf16[256,512]{1,0:T(8,128)(2,1)S(1)}, bf16[256,512]{1,0:T(8,128)(2,1)S(1)}, u32[]{:S(2)}, u32[]{:S(2)}) %collective-permute-start.55) | collective-permute-done | bytes 262176 | tf_op jit(solution)/shard_map/ppermute | solution.py:174
  201.3 12.5 %collective-permute-done.57.refs_2_ = bf16[256,512]{1,0:T(8,128)(2,1)S(1)} collective-permute-done((bf16[256,512]{1,0:T(8,128)(2,1)S(1)}, bf16[256,512]{1,0:T(8,128)(2,1)S(1)}, u32[]{:S(2)}, u32[]{:S(2)}) %collective-permute-start.57) | collective-permute-done | bytes 262176 | tf_op jit(solution)/shard_map/ppermute | solution.py:174
  214.0 2.5 %collective-permute-start.58 = (bf16[128,512]{1,0:T(8,128)(2,1)S(1)}, bf16[128,512]{1,0:T(8,128)(2,1)S(1)}, u32[]{:S(2)}, u32[]{:S(2)}) collective-permute-start(bf16[128,512]{1,0:T(8,128)(2,1)S(1)} %get-tuple-element.106), channel_id=1, source_target_pairs={{0,4},{4,0},{8,12},{12,8},{16,20},{20,16},{24,28},{28,24},{1,5},{5... | collective-permute-start | bytes 393224 | tf_op jit(solution)/shard_map/ppermute | solution.py:174
  (129 shorter events, 65.8 us)
Async XLA Ops:
  1.2 12.1 %collective-permute-start.3 = (bf16[128,1024]{1,0:T(8,128)(2,1)}, bf16[128,1024]{1,0:T(8,128)(2,1)S(1)}, u32[]{:S(2)}, u32[]{:S(2)}) collective-permute-start(bf16[128,1024]{1,0:T(8,128)(2,1)} %refs_0_.3), channel_id=1, source_target_pairs={{0,16},{4,20},{8,24},{12,28},{16,0},{20,4},{24,8},{28,12},{1,17},{... | collective-permute-start | bytes 786440 | tf_op jit(solution)/shard_map/ppermute | solution.py:174
  2.5 12.1 %collective-permute-start.5 = (bf16[128,1024]{1,0:T(8,128)(2,1)}, bf16[128,1024]{1,0:T(8,128)(2,1)S(1)}, u32[]{:S(2)}, u32[]{:S(2)}) collective-permute-start(bf16[128,1024]{1,0:T(8,128)(2,1)} %refs_0_.3), channel_id=1, source_target_pairs={{0,24},{4,28},{8,16},{12,20},{16,8},{20,12},{24,0},{28,4},{1,25},{... | collective-permute-start | bytes 786440 | tf_op jit(solution)/shard_map/ppermute | solution.py:174
  2.6 13.3 %collective-permute-start = (bf16[128,1024]{1,0:T(8,128)(2,1)}, bf16[128,1024]{1,0:T(8,128)(2,1)S(1)}, u32[]{:S(2)}, u32[]{:S(2)}) collective-permute-start(bf16[128,1024]{1,0:T(8,128)(2,1)} %refs_0_.3), channel_id=1, source_target_pairs={{0,4},{4,0},{8,12},{12,8},{16,20},{20,16},{24,28},{28,24},{1,5},{5... | collective-permute-start | bytes 786440 | tf_op jit(solution)/shard_map/ppermute | solution.py:174
  7.4 10.7 %collective-permute-start.2 = (bf16[128,1024]{1,0:T(8,128)(2,1)S(1)}, bf16[128,1024]{1,0:T(8,128)(2,1)S(1)}, u32[]{:S(2)}, u32[]{:S(2)}) collective-permute-start(bf16[128,1024]{1,0:T(8,128)(2,1)S(1)} %collective-permute-done.1.refs_2_), channel_id=1, source_target_pairs={{0,4},{4,0},{8,12},{12,8},{16,20},{20,16},{24,28},{28,24},{1,5},{5... | collective-permute-start | bytes 786440 | tf_op jit(solution)/shard_map/ppermute | solution.py:174
  12.0 13.6 %collective-permute-start.8 = (bf16[256,1024]{1,0:T(8,128)(2,1)S(1)}, bf16[256,1024]{1,0:T(8,128)(2,1)S(1)}, u32[]{:S(2)}, u32[]{:S(2)}) collective-permute-start(bf16[256,1024]{1,0:T(8,128)(2,1)S(1)} %shard_map.119.refs_0_), channel_id=1, source_target_pairs={{0,8},{4,12},{8,0},{12,4},{16,24},{20,28},{24,16},{28,20},{1,9},{5... | collective-permute-start | bytes 1572872 | tf_op jit(solution)/shard_map/ppermute | solution.py:174
  13.3 13.5 %collective-permute-start.10 = (bf16[256,1024]{1,0:T(8,128)(2,1)S(1)}, bf16[256,1024]{1,0:T(8,128)(2,1)S(1)}, u32[]{:S(2)}, u32[]{:S(2)}) collective-permute-start(bf16[256,1024]{1,0:T(8,128)(2,1)S(1)} %shard_map.119.refs_0_), channel_id=1, source_target_pairs={{0,16},{4,20},{8,24},{12,28},{16,0},{20,4},{24,8},{28,12},{1,17},{... | collective-permute-start | bytes 1572872 | tf_op jit(solution)/shard_map/ppermute | solution.py:174
  14.6 24.3 %collective-permute-start.12 = (bf16[256,1024]{1,0:T(8,128)(2,1)S(1)}, bf16[256,1024]{1,0:T(8,128)(2,1)}, u32[]{:S(2)}, u32[]{:S(2)}) collective-permute-start(bf16[256,1024]{1,0:T(8,128)(2,1)S(1)} %shard_map.119.refs_0_), channel_id=1, source_target_pairs={{0,24},{4,28},{8,16},{12,20},{16,8},{20,12},{24,0},{28,4},{1,25},{... | collective-permute-start | bytes 1572872 | tf_op jit(solution)/shard_map/ppermute | solution.py:174
  19.2 19.7 %collective-permute-start.7 = (bf16[256,1024]{1,0:T(8,128)(2,1)S(1)}, bf16[256,1024]{1,0:T(8,128)(2,1)S(1)}, u32[]{:S(2)}, u32[]{:S(2)}) collective-permute-start(bf16[256,1024]{1,0:T(8,128)(2,1)S(1)} %shard_map.119.refs_0_), channel_id=1, source_target_pairs={{0,4},{4,0},{8,12},{12,8},{16,20},{20,16},{24,28},{28,24},{1,5},{5... | collective-permute-start | bytes 1572872 | tf_op jit(solution)/shard_map/ppermute | solution.py:174
  25.7 13.2 %collective-permute-start.9 = (bf16[256,1024]{1,0:T(8,128)(2,1)S(1)}, bf16[256,1024]{1,0:T(8,128)(2,1)S(1)}, u32[]{:S(2)}, u32[]{:S(2)}) collective-permute-start(bf16[256,1024]{1,0:T(8,128)(2,1)S(1)} %collective-permute-done.8.refs_2_), channel_id=1, source_target_pairs={{0,4},{4,0},{8,12},{12,8},{16,20},{20,16},{24,28},{28,24},{1,5},{5... | collective-permute-start | bytes 1572872 | tf_op jit(solution)/shard_map/ppermute | solution.py:174
  26.8 14.3 %collective-permute-start.11 = (bf16[256,1024]{1,0:T(8,128)(2,1)S(1)}, bf16[256,1024]{1,0:T(8,128)(2,1)S(1)}, u32[]{:S(2)}, u32[]{:S(2)}) collective-permute-start(bf16[256,1024]{1,0:T(8,128)(2,1)S(1)} %collective-permute-done.10.refs_4_), channel_id=1, source_target_pairs={{0,4},{4,0},{8,12},{12,8},{16,20},{20,16},{24,28},{28,24},{1,5},{5... | collective-permute-start | bytes 1572872 | tf_op jit(solution)/shard_map/ppermute | solution.py:174
  60.5 8.8 %collective-permute-start.19 = (bf16[128,1024]{1,0:T(8,128)(2,1)S(1)}, bf16[128,1024]{1,0:T(8,128)(2,1)S(1)}, u32[]{:S(2)}, u32[]{:S(2)}) collective-permute-start(bf16[128,1024]{1,0:T(8,128)(2,1)S(1)} %maximum_add_fusion.refs_0_), channel_id=1, source_target_pairs={{0,16},{4,20},{8,24},{12,28},{16,0},{20,4},{24,8},{28,12},{1,17},{... | collective-permute-start | bytes 786440 | tf_op jit(solution)/shard_map/ppermute | solution.py:174
  60.6 14.2 %collective-permute-start.21 = (bf16[128,1024]{1,0:T(8,128)(2,1)S(1)}, bf16[128,1024]{1,0:T(8,128)(2,1)S(1)}, u32[]{:S(2)}, u32[]{:S(2)}) collective-permute-start(bf16[128,1024]{1,0:T(8,128)(2,1)S(1)} %maximum_add_fusion.refs_0_), channel_id=1, source_target_pairs={{0,24},{4,28},{8,16},{12,20},{16,8},{20,12},{24,0},{28,4},{1,25},{... | collective-permute-start | bytes 786440 | tf_op jit(solution)/shard_map/ppermute | solution.py:174
  62.0 12.9 %collective-permute-start.16 = (bf16[128,1024]{1,0:T(8,128)(2,1)S(1)}, bf16[128,1024]{1,0:T(8,128)(2,1)S(1)}, u32[]{:S(2)}, u32[]{:S(2)}) collective-permute-start(bf16[128,1024]{1,0:T(8,128)(2,1)S(1)} %maximum_add_fusion.refs_0_), channel_id=1, source_target_pairs={{0,4},{4,0},{8,12},{12,8},{16,20},{20,16},{24,28},{28,24},{1,5},{5... | collective-permute-start | bytes 786440 | tf_op jit(solution)/shard_map/ppermute | solution.py:174
  78.7 19.0 %collective-permute-start.28 = (bf16[256,512]{1,0:T(8,128)(2,1)S(1)}, bf16[256,512]{1,0:T(8,128)(2,1)S(1)}, u32[]{:S(2)}, u32[]{:S(2)}) collective-permute-start(bf16[256,512]{1,0:T(8,128)(2,1)S(1)} %get-tuple-element.73), channel_id=1, source_target_pairs={{0,3},{1,2},{2,1},{3,0},{4,7},{5,6},{6,5},{7,4},{8,11},{9,10},{10,... | collective-permute-start | bytes 786440 | tf_op jit(solution)/shard_map/ppermute | solution.py:174
  80.0 22.4 %collective-permute-start.27 = (bf16[256,512]{1,0:T(8,128)(2,1)S(1)}, bf16[256,512]{1,0:T(8,128)(2,1)S(1)}, u32[]{:S(2)}, u32[]{:S(2)}) collective-permute-start(bf16[256,512]{1,0:T(8,128)(2,1)S(1)} %get-tuple-element.72), channel_id=1, source_target_pairs={{0,2},{1,3},{2,0},{3,1},{4,6},{5,7},{6,4},{7,5},{8,10},{9,11},{10,... | collective-permute-start | bytes 786440 | tf_op jit(solution)/shard_map/ppermute | solution.py:174
  81.1 21.4 %collective-permute-start.26 = (bf16[256,512]{1,0:T(8,128)(2,1)S(1)}, bf16[256,512]{1,0:T(8,128)(2,1)S(1)}, u32[]{:S(2)}, u32[]{:S(2)}) collective-permute-start(bf16[256,512]{1,0:T(8,128)(2,1)S(1)} %get-tuple-element.71), channel_id=1, source_target_pairs={{0,1},{1,0},{2,3},{3,2},{4,5},{5,4},{6,7},{7,6},{8,9},{9,8},{10,11... | collective-permute-start | bytes 786440 | tf_op jit(solution)/shard_map/ppermute | solution.py:174
  103.6 13.1 %collective-permute-start.33 = (bf16[256,512]{1,0:T(8,128)(2,1)S(1)}, bf16[256,512]{1,0:T(8,128)(2,1)S(1)}, u32[]{:S(2)}, u32[]{:S(2)}) collective-permute-start(bf16[256,512]{1,0:T(8,128)(2,1)S(1)} %add_convert_fusion.refs_0_.refs_8_), channel_id=1, source_target_pairs={{0,1},{1,0},{2,3},{3,2},{4,5},{5,4},{6,7},{7,6},{8,9},{9,8},{10,11... | collective-permute-start | bytes 786440 | tf_op jit(solution)/shard_map/ppermute | solution.py:174
  105.7 14.7 %collective-permute-start.35 = (bf16[256,512]{1,0:T(8,128)(2,1)S(1)}, bf16[256,512]{1,0:T(8,128)(2,1)S(1)}, u32[]{:S(2)}, u32[]{:S(2)}) collective-permute-start(bf16[256,512]{1,0:T(8,128)(2,1)S(1)} %add_convert_fusion.refs_0_.refs_8_), channel_id=1, source_target_pairs={{0,2},{1,3},{2,0},{3,1},{4,6},{5,7},{6,4},{7,5},{8,10},{9,11},{10,... | collective-permute-start | bytes 786440 | tf_op jit(solution)/shard_map/ppermute | solution.py:174
  108.0 8.8 %collective-permute-start.30 = (bf16[272,384]{1,0:T(8,128)(2,1)S(1)}, bf16[272,384]{1,0:T(8,128)(2,1)S(1)}, u32[]{:S(2)}, u32[]{:S(2)}) collective-permute-start(bf16[272,384]{1,0:T(8,128)(2,1)S(1)} %get-tuple-element.79), channel_id=1, source_target_pairs={{0,8},{4,12},{8,0},{12,4},{16,24},{20,28},{24,16},{28,20},{1,9},{5... | collective-permute-start | bytes 626696 | tf_op jit(solution)/shard_map/ppermute | solution.py:174
  109.7 9.3 %collective-permute-start.32 = (bf16[272,384]{1,0:T(8,128)(2,1)S(1)}, bf16[272,384]{1,0:T(8,128)(2,1)S(1)}, u32[]{:S(2)}, u32[]{:S(2)}) collective-permute-start(bf16[272,384]{1,0:T(8,128)(2,1)S(1)} %get-tuple-element.81), channel_id=1, source_target_pairs={{0,24},{4,28},{8,16},{12,20},{16,8},{20,12},{24,0},{28,4},{1,25},{... | collective-permute-start | bytes 626696 | tf_op jit(solution)/shard_map/ppermute | solution.py:174
  120.4 13.0 %collective-permute-start.40 = (bf16[256,512]{1,0:T(8,128)(2,1)S(1)}, bf16[256,512]{1,0:T(8,128)(2,1)S(1)}, u32[]{:S(2)}, u32[]{:S(2)}) collective-permute-start(bf16[256,512]{1,0:T(8,128)(2,1)S(1)} %add_convert_fusion.refs_0_.refs_8_), channel_id=1, source_target_pairs={{0,3},{1,2},{2,1},{3,0},{4,7},{5,6},{6,5},{7,4},{8,11},{9,10},{10,... | collective-permute-start | bytes 786440 | tf_op jit(solution)/shard_map/ppermute | solution.py:174
  124.3 12.9 %collective-permute-start.37 = (bf16[528,384]{1,0:T(8,128)(2,1)S(1)}, bf16[528,384]{1,0:T(8,128)(2,1)S(1)}, u32[]{:S(2)}, u32[]{:S(2)}) collective-permute-start(bf16[528,384]{1,0:T(8,128)(2,1)S(1)} %get-tuple-element.85), channel_id=1, source_target_pairs={{0,8},{4,12},{8,0},{12,4},{16,24},{20,28},{24,16},{28,20},{1,9},{5... | collective-permute-start | bytes 1216520 | tf_op jit(solution)/shard_map/ppermute | solution.py:174
  125.5 11.6 %collective-permute-start.38 = (bf16[528,384]{1,0:T(8,128)(2,1)S(1)}, bf16[528,384]{1,0:T(8,128)(2,1)S(1)}, u32[]{:S(2)}, u32[]{:S(2)}) collective-permute-start(bf16[528,384]{1,0:T(8,128)(2,1)S(1)} %get-tuple-element.86), channel_id=1, source_target_pairs={{0,16},{4,20},{8,24},{12,28},{16,0},{20,4},{24,8},{28,12},{1,17},{... | collective-permute-start | bytes 1216520 | tf_op jit(solution)/shard_map/ppermute | solution.py:174
  126.1 18.7 %collective-permute-start.39 = (bf16[528,384]{1,0:T(8,128)(2,1)S(1)}, bf16[528,384]{1,0:T(8,128)(2,1)S(1)}, u32[]{:S(2)}, u32[]{:S(2)}) collective-permute-start(bf16[528,384]{1,0:T(8,128)(2,1)S(1)} %get-tuple-element.87), channel_id=1, source_target_pairs={{0,24},{4,28},{8,16},{12,20},{16,8},{20,12},{24,0},{28,4},{1,25},{... | collective-permute-start | bytes 1216520 | tf_op jit(solution)/shard_map/ppermute | solution.py:174
  157.3 10.4 %collective-permute-start.48 = (bf16[1024,128]{1,0:T(8,128)(2,1)S(1)}, bf16[1024,128]{1,0:T(8,128)(2,1)S(1)}, u32[]{:S(2)}, u32[]{:S(2)}) collective-permute-start(bf16[1024,128]{1,0:T(8,128)(2,1)S(1)} %shard_map.126.refs_0_), channel_id=1, source_target_pairs={{0,16},{4,20},{8,24},{12,28},{16,0},{20,4},{24,8},{28,12},{1,17},{... | collective-permute-start | bytes 786440 | tf_op jit(solution)/shard_map/ppermute | solution.py:174
  158.3 13.9 %collective-permute-start.50 = (bf16[1024,128]{1,0:T(8,128)(2,1)S(1)}, bf16[1024,128]{1,0:T(8,128)(2,1)S(1)}, u32[]{:S(2)}, u32[]{:S(2)}) collective-permute-start(bf16[1024,128]{1,0:T(8,128)(2,1)S(1)} %shard_map.126.refs_0_), channel_id=1, source_target_pairs={{0,24},{4,28},{8,16},{12,20},{16,8},{20,12},{24,0},{28,4},{1,25},{... | collective-permute-start | bytes 786440 | tf_op jit(solution)/shard_map/ppermute | solution.py:174
  159.1 13.1 %collective-permute-start.45 = (bf16[1024,128]{1,0:T(8,128)(2,1)S(1)}, bf16[1024,128]{1,0:T(8,128)(2,1)S(1)}, u32[]{:S(2)}, u32[]{:S(2)}) collective-permute-start(bf16[1024,128]{1,0:T(8,128)(2,1)S(1)} %shard_map.126.refs_0_), channel_id=1, source_target_pairs={{0,4},{4,0},{8,12},{12,8},{16,20},{20,16},{24,28},{28,24},{1,5},{5... | collective-permute-start | bytes 786440 | tf_op jit(solution)/shard_map/ppermute | solution.py:174
  162.7 9.5 %collective-permute-start.47 = (bf16[1024,128]{1,0:T(8,128)(2,1)S(1)}, bf16[1024,128]{1,0:T(8,128)(2,1)S(1)}, u32[]{:S(2)}, u32[]{:S(2)}) collective-permute-start(bf16[1024,128]{1,0:T(8,128)(2,1)S(1)} %collective-permute-done.46.refs_2_), channel_id=1, source_target_pairs={{0,4},{4,0},{8,12},{12,8},{16,20},{20,16},{24,28},{28,24},{1,5},{5... | collective-permute-start | bytes 786440 | tf_op jit(solution)/shard_map/ppermute | solution.py:174
  177.2 11.8 %collective-permute-start.54 = (bf16[256,512]{1,0:T(8,128)(2,1)S(1)}, bf16[256,512]{1,0:T(8,128)(2,1)S(1)}, u32[]{:S(2)}, u32[]{:S(2)}) collective-permute-start(bf16[256,512]{1,0:T(8,128)(2,1)S(1)} %get-tuple-element.100), channel_id=1, source_target_pairs={{0,24},{4,28},{8,16},{12,20},{16,8},{20,12},{24,0},{28,4},{1,25},{... | collective-permute-start | bytes 786440 | tf_op jit(solution)/shard_map/ppermute | solution.py:174
  189.3 10.4 %collective-permute-start.55 = (bf16[256,512]{1,0:T(8,128)(2,1)S(1)}, bf16[256,512]{1,0:T(8,128)(2,1)S(1)}, u32[]{:S(2)}, u32[]{:S(2)}) collective-permute-start(bf16[256,512]{1,0:T(8,128)(2,1)S(1)} %get-tuple-element.102), channel_id=1, source_target_pairs={{0,1},{1,0},{2,3},{3,2},{4,5},{5,4},{6,7},{7,6},{8,9},{9,8},{10,11... | collective-permute-start | bytes 786440 | tf_op jit(solution)/shard_map/ppermute | solution.py:174
  190.9 10.4 %collective-permute-start.56 = (bf16[256,512]{1,0:T(8,128)(2,1)S(1)}, bf16[256,512]{1,0:T(8,128)(2,1)S(1)}, u32[]{:S(2)}, u32[]{:S(2)}) collective-permute-start(bf16[256,512]{1,0:T(8,128)(2,1)S(1)} %get-tuple-element.103), channel_id=1, source_target_pairs={{0,2},{1,3},{2,0},{3,1},{4,6},{5,7},{6,4},{7,5},{8,10},{9,11},{10,... | collective-permute-start | bytes 786440 | tf_op jit(solution)/shard_map/ppermute | solution.py:174
  190.9 22.9 %collective-permute-start.57 = (bf16[256,512]{1,0:T(8,128)(2,1)S(1)}, bf16[256,512]{1,0:T(8,128)(2,1)S(1)}, u32[]{:S(2)}, u32[]{:S(2)}) collective-permute-start(bf16[256,512]{1,0:T(8,128)(2,1)S(1)} %get-tuple-element.104), channel_id=1, source_target_pairs={{0,3},{1,2},{2,1},{3,0},{4,7},{5,6},{6,5},{7,4},{8,11},{9,10},{10,... | collective-permute-start | bytes 786440 | tf_op jit(solution)/shard_map/ppermute | solution.py:174
  (38 other events, 311.0 us)

commit v8 on v7

--- a/solution.py
+++ b/solution.py
@@ -223,25 +223,10 @@
         whole[aligned(index, piece.shape[0]), :] = piece[...]
 
 
-def stack_kernel(*refs):
-    sources, stacked, semaphores = refs[:-2], refs[-2], refs[-1]
-    height = sources[0].shape[0]
-    copies = fetched(
-        [(s, stacked.at[n * height : (n + 1) * height, :]) for n, s in enumerate(sources)],
-        semaphores,
-    )
-    for copy in copies:
-        copy.wait()
-
-
-def plane_rows(pieces, whole, part=0):
+def plane_rows(pieces, whole):
     chip, core, _ = place()
-    height = whole.shape[0] // len(pieces)
     return [
-        (
-            piece.at[part * height : (part + 1) * height, :],
-            whole.at[aligned(2 * (chip ^ (n // 2)) + (core ^ (n % 2)), height), :],
-        )
+        (piece, whole.at[aligned(2 * (chip ^ (n // 2)) + (core ^ (n % 2)), piece.shape[0]), :])
         for n, piece in enumerate(pieces)
     ]
 
@@ -260,14 +245,13 @@
 
 
 def cross_kernel(count, tile, slot_row, query, states, *refs):
-    pieces, (own, above, below, *scratch) = refs[:count], refs[count:]
+    pieces, (own, above, below, *scratch) = refs[: 2 * count], refs[2 * count :]
     held, key_weight, value_weight, totals, summed, semaphores = scratch
     slots, width = query.shape
     spill = above.shape[0]
     head_count = width // HEAD_DIM
     pairs = [(states, held)]
-    for part, weight in enumerate((key_weight, value_weight)):
-        pairs += plane_rows(pieces, weight, part)
+    pairs += plane_rows(pieces[:count], key_weight) + plane_rows(pieces[count:], value_weight)
     copies = fetched(pairs, semaphores)
     totals[...] = jnp.zeros_like(totals)
     summed[...] = jnp.zeros_like(summed)
@@ -331,31 +315,21 @@
     quarters(whole, weight, outs)
 
 
-def latent_out_kernel(count, parts, weight, *refs):
-    pieces, blocks, refs = refs[:count], refs[count : count + parts], refs[count + parts :]
-    outs, (whole, hidden) = refs[:-2], refs[-2:]
+def latent_out_kernel(count, *refs):
+    chips = count // 2
+    pieces, weights, refs = refs[:count], refs[count : count + chips], refs[count + chips :]
+    outs, (whole, held, products_of, semaphores) = refs[:chips], refs[chips:]
     chip, core, tensor = place()
+    copies = fetched([(weight, held.at[d]) for d, weight in enumerate(weights)], semaphores)
     for n, piece in enumerate(pieces):
-        index = (count // 2) * (core ^ (n % 2)) + (chip ^ (n // 2))
+        index = chips * (core ^ (n % 2)) + (chip ^ (n // 2))
         whole[:, aligned(index, HEAD_DIM)] = piece[...]
-    height = outs[0].shape[0]
-    for r, block in enumerate(blocks):
-        hidden[aligned(tensor ^ r, height), :] = block[...]
-    share = (tensor == chip).astype(jnp.float32)
-    for d, out in reversed(list(enumerate(outs))):
-        span = aligned(chip ^ d, height)
-        product = dot(whole[span, :], weight[...])
-        out[...] = (product + hidden[span, :].astype(jnp.float32) * share).astype(out.dtype)
-
-
-def column_kernel(*refs):
-    blocks, outs, whole = refs[: (len(refs) - 1) // 2], refs[(len(refs) - 1) // 2 : -1], refs[-1]
-    chip, _, tensor = place()
-    height = blocks[0].shape[0]
-    for d, block in enumerate(blocks):
-        whole[aligned(chip ^ d, height), :] = block[...].astype(jnp.float32)
+    height = whole.shape[0]
+    for d, copy in enumerate(copies):
+        copy.wait()
+        products_of[aligned(chip ^ d, height), :] = dot(whole[...], held[d])
     for r, out in enumerate(outs):
-        out[...] = whole[aligned(tensor ^ r, height), :].astype(out.dtype)
+        out[...] = products_of[aligned(tensor ^ r, height), :].astype(out.dtype)
 
 
 def arrange_kernel(*refs):
@@ -420,8 +394,9 @@
 
 
 def attention_kernel(groups, chips, depth, *refs):
-    shares, attended, (query, key, value) = refs[: len(groups) * chips], refs[-4], refs[-3:]
-    _, _, tensor = place()
+    shares, refs = refs[: len(groups) * chips], refs[len(groups) * chips :]
+    outs, (query, key, value, attended) = refs[:chips], refs[chips:]
+    chip, _, tensor = place()
     parts = sum(len(group) for group in groups)
     height = attended.shape[0] // parts
     own_place = diagonal(height)
@@ -459,6 +434,8 @@
             denominator += jnp.sum(raw, axis=1, keepdims=True)
             numerator += dot(raw.astype(jnp.bfloat16), value[span, :])
         attended[i * height : (i + 1) * height, :] = (numerator / denominator).astype(jnp.bfloat16)
+    for d, out in enumerate(outs):
+        out[...] = attended[aligned(chip ^ d, out.shape[0]), :]
 
 
 def final_kernel(own, *refs):
@@ -501,13 +478,16 @@
     out_width = cross_out.shape[1]
     quarter = patch_count // tensor_count
     bf16, f32 = jnp.bfloat16, jnp.float32
-    tile = min(256, byte_count)
-
-    def over_plane(block, earlier=()):
+    tile = min(1024, byte_count)
+
+    def over_plane(block, earlier=(), last_hop=None):
+        moved = [block]
+        for d in range(1, chip_count):
+            hop = last_hop(d) if last_hop else d
+            moved.append(exchanged(moved[d ^ hop], "seq", 2 * hop))
         pieces = []
-        for d in range(chip_count):
-            moved = exchanged(block, "seq", 2 * d) if d else block
-            pieces += [moved, core_swapped(after(moved, *earlier) if d else moved)]
+        for d, part in enumerate(moved):
+            pieces += [part, core_swapped(after(part, *earlier) if d else part)]
         return pieces
 
     slot_of = byte_patch - (seq * patch_dev - spill)
@@ -517,14 +497,6 @@
         jnp.concatenate([edge, patch_len, edge]), seq * patch_dev, slot_count
     ).astype(f32)[:, None]
     query_pieces = over_plane(cross_query)
-    (stacked,) = call(
-        stack_kernel,
-        [((2 * cross_key.shape[0], local_width), bf16)],
-        cross_key,
-        cross_value,
-        far=2,
-        scratch=[pltpu.SemaphoreType.DMA((2,))],
-    )
     (query_slots,) = call(
         functools.partial(query_kernel, seq_count),
         [((slot_count, local_width), bf16)],
@@ -540,14 +512,23 @@
         ],
         flops=2 * slot_count * byte_width * (byte_count + local_width),
     )
+    key_pieces = over_plane(cross_key, (query_slots,), lambda d: 1 << (d.bit_length() - 1))
+    value_pieces = over_plane(cross_value, (query_slots,), lambda d: d & -d)
+
+    near = (key_pieces[-2], value_pieces[-2])
+    weights = []
+    for weight in (latent_query, latent_key, latent_value):
+        weights += [weight, core_swapped(after(weight, *near))]
+    out_weights = [latent_out, exchanged(after(latent_out, *near), "seq", 2 * (chip_count - 1))]
     own, above, below = call(
         functools.partial(cross_kernel, seq_count, tile),
         [((height, local_width), bf16) for height in (patch_dev, spill, spill)],
         slot_row,
         query_slots,
         byte_states,
-        *over_plane(stacked, (query_slots,)),
-        far=1 + seq_count,
+        *key_pieces,
+        *value_pieces,
+        far=1 + 2 * seq_count,
         scratch=[
             pltpu.VMEM((byte_count, byte_width), bf16),
             pltpu.VMEM((byte_width, local_width), bf16),
@@ -560,6 +541,7 @@
     )
 
     spilled = [shifted(below, "seq", 1), shifted(above, "seq", -1)]
+    own, out_weights[-1] = lax.optimization_barrier((own, out_weights[-1]))
     own = own + jnp.concatenate(spilled, axis=0)
 
     total, *sent = call(
@@ -572,17 +554,17 @@
     )
     received = [exchanged(block, "tensor", r) for r, block in enumerate(sent, 1)]
 
-    weights = []
-    for weight in (latent_query, latent_key, latent_value):
-        weights += [weight, core_swapped(after(weight, total))]
     head_weights = call(
         arrange_kernel,
         [((2 * out_width, 3 * HEAD_DIM), bf16)] * chip_count,
-        *weights,
+        *[after(weight, total) for weight in weights],
         far=6,
         scratch=[pltpu.SemaphoreType.DMA((6 * chip_count,))],
     )
-    total, *head_weights = lax.optimization_barrier((total, *head_weights))
+    for d in range(1, chip_count - 1):
+        out_weights.insert(d, exchanged(after(latent_out, total), "seq", 2 * d))
+    total, *rest = lax.optimization_barrier((total, *head_weights, *out_weights))
+    head_weights, out_weights = rest[:chip_count], rest[chip_count:]
     for share in received:
         total = total + share.astype(f32)
     latent_in = total.astype(bf16)
@@ -590,13 +572,12 @@
     gain = norm_gain[None, :]
     groups = [[0], list(range(1, min(3, tensor_count))), list(range(3, tensor_count))]
     groups = [group for group in groups if group]
-    shares, arrived, latent_blocks = [], [], [latent_in]
+    shares, arrived = [], []
     for g, group in enumerate(groups):
         blocks = [latent_in]
         if g:
             start = after(latent_in, *arrived, *shares[:chip_count]) if g > 1 else latent_in
             arrived = [exchanged(start, "tensor", r) for r in group]
-            latent_blocks += arrived
             blocks = [after(block, *shares[:chip_count]) for block in arrived]
         height = len(group) * quarter
         share, *sent = call(
@@ -612,38 +593,45 @@
         if g > 1:
             sent = [after(part, *shares[(g - 1) * chip_count + 1 :]) for part in sent]
         shares += [share] + [exchanged(part, "seq", 2 * d) for d, part in enumerate(sent, 1)]
-    (attended,) = call(
+    attended = call(
         functools.partial(attention_kernel, groups, chip_count, out_width * seq_count),
-        [((patch_count, HEAD_DIM), bf16)],
+        [((quarter, HEAD_DIM), bf16)] * chip_count,
         *shares,
-        scratch=[pltpu.VMEM((patch_count, HEAD_DIM), bf16)] * 3,
+        scratch=[pltpu.VMEM((patch_count, HEAD_DIM), bf16)] * 4,
         flops=2 * patch_count * patch_count * HEAD_DIM,
     )
 
-    own, *sent = call(
-        functools.partial(latent_out_kernel, seq_count, tensor_count),
-        [((quarter, out_width), bf16 if d else f32) for d in range(chip_count)],
-        latent_out,
-        *over_plane(attended),
-        *latent_blocks,
+    route = [
+        (s * tensor_count + t, (2 * t + s % 2) * tensor_count + s // 2)
+        for s in range(seq_count)
+        for t in range(tensor_count)
+    ]
+    residual = lax.ppermute(after(latent_in, *arrived), ("seq", "tensor"), route)
+
+    pieces = []
+    for d, block in enumerate(attended):
+        moved = exchanged(block, "seq", 2 * d) if d else block
+        pieces += [moved, core_swapped(moved)]
+    pieces[0], residual = lax.optimization_barrier((pieces[0], residual))
+    total, *sent = call(
+        functools.partial(latent_out_kernel, seq_count),
+        [((quarter, out_width), bf16 if r else f32) for r in range(tensor_count)],
+        *pieces,
+        *out_weights,
+        far=chip_count,
         scratch=[
-            pltpu.VMEM((patch_count, local_width), bf16),
-            pltpu.VMEM((patch_count, out_width), bf16),
+            pltpu.VMEM((quarter, local_width), bf16),
+            pltpu.VMEM((chip_count, local_width, out_width), bf16),
+            pltpu.VMEM((patch_count, out_width), f32),
+            pltpu.SemaphoreType.DMA((chip_count,)),
         ],
-        flops=2 * patch_count * local_width * out_width,
-    )
-
-    total, *sent = call(
-        column_kernel,
-        [((quarter, out_width), bf16 if r else f32) for r in range(tensor_count)],
-        own,
-        *[exchanged(block, "seq", 2 * d) for d, block in enumerate(sent, 1)],
-        scratch=[pltpu.VMEM((patch_count, out_width), f32)],
+        flops=2 * quarter * local_width * out_width * chip_count,
     )
     same, crossed = call(
         final_kernel,
         [((patch_dev, out_width), bf16)] * 2,
         total,
+        residual,
         *[exchanged(block, "tensor", r) for r, block in enumerate(sent, 1)],
         scratch=[pltpu.VMEM((quarter, out_width), f32)],
     )

time: 219 us -> 213 us (0.973)
  Pallas kernels: 23.9 us -> 21.2 us
    ppermute x57 -> x64, starting transfers between devices: 83.4 us -> 77.9 us  [exchanged(): return lax.ppermute(block, axis, route)]
    ppermute x2, waiting for transfers between devices: 1.74 us -> 5.53 us  [shifted(): return lax.ppermute(block, axis, route)]
    ppermute x0 -> x1, starting transfers between devices: none -> 3.44 us  [per_device(): lax.ppermute(after(latent_in, *arrived), ('seq', 'tensor'), route)]
    ppermute x57 -> x64, waiting for transfers between devices: 96.1 us -> 93 us  [exchanged(): return lax.ppermute(block, axis, route)]
    pallas_call x12 -> x10, Pallas kernels: 23.9 us -> 21.2 us  [call(): pl.pallas_call(kernel, out_shape=shapes, in_specs=[pl.BlockSpec(memory_sp...]
  transfers between devices with their start and end apart: 59 -> 67, of which waited for: 32 -> 28; matrix products, arithmetic and copies ran while one was open for 1% -> 1% of each run, Pallas kernels for 4% -> 9%
where the time goes in v8:
time: 213 us; the launch traced here: 212 us
  waiting for transfers between devices  98.5 us (46%)
  starting transfers between devices  87.1 us (41%)
  Pallas kernels  21.2 us (10%)
  local copies, waits for them, and re-layouts  3.48 us (2%)
    ppermute x64, waiting for transfers between devices, exchanged(): return lax.ppermute(block, axis, route)  93 us
    ppermute x64, starting transfers between devices, exchanged(): return lax.ppermute(block, axis, route)  77.9 us
    pallas_call x10, Pallas kernels, call(): pl.pallas_call(kernel, out_shape=shapes, in_specs=[pl.BlockSpec(memory_sp...  21.2 us
    ppermute x2, starting transfers between devices, shifted(): return lax.ppermute(block, axis, route)  5.74 us
    ppermute x2, waiting for transfers between devices, shifted(): return lax.ppermute(block, axis, route)  5.53 us
  transfers between devices with their start and end apart: 67, of which 28 were waited for; matrix products, arithmetic and copies ran while one was open for 1% of the time, Pallas kernels for 9%

profile of v8, /device:TPU:9, one launch (start us, length us, event | category | flops | bytes accessed | tf_op | source)
XLA Modules:
  0.0 212.3 jit_solution(12013379362266606435)
XLA Ops:
  5.4 2.0 collective-permute-done.1.refs_2_
  8.6 7.4 %collective-permute-start.2 = (bf16[128,1024]{1,0:T(8,128)(2,1)S(1)}, bf16[128,1024]{1,0:T(8,128)(2,1)S(1)}, u32[]{:S(2)}, u32[]{:S(2)}) collective-permute-start(bf16[128,1024]{1,0:T(8,128)(2,1)S(1)} %collective-permute-done.1.refs_2_), channel_id=1, source_target_pairs={{0,4},{4,0},{8,12},{12,8},{16,20},{20,16},{24,28},{28,24},{1,5},{5... | collective-permute-start | bytes 786440 | tf_op jit(solution)/shard_map/ppermute | solution.py:174
  24.6 3.2 %collective-permute-start.7 = (bf16[128,1024]{1,0:T(8,128)(2,1)}, bf16[128,1024]{1,0:T(8,128)(2,1)S(1)}, u32[]{:S(2)}, u32[]{:S(2)}) collective-permute-start(bf16[128,1024]{1,0:T(8,128)(2,1)} %refs_0_.3), channel_id=1, source_target_pairs={{0,4},{4,0},{8,12},{12,8},{16,20},{20,16},{24,28},{28,24},{1,5},{5... | collective-permute-start | bytes 786440 | tf_op jit(solution)/shard_map/ppermute | solution.py:174
  30.4 2.0 shard_map.118.query
  33.1 1.8 collective-permute-start.21
  34.9 2.4 %collective-permute-start.13 = (bf16[128,1024]{1,0:T(8,128)(2,1)S(1)}, bf16[128,1024]{1,0:T(8,128)(2,1)S(1)}, u32[]{:S(2)}, u32[]{:S(2)}) collective-permute-start(bf16[128,1024]{1,0:T(8,128)(2,1)S(1)} %collective-permute-done.12.refs_6_), channel_id=1, source_target_pairs={{0,4},{4,0},{8,12},{12,8},{16,20},{20,16},{24,28},{28,24},{1,5},{5... | collective-permute-start | bytes 786440 | tf_op jit(solution)/shard_map/ppermute | solution.py:174
  39.6 7.3 %shard_map.119 = (bf16[128,1024]{1,0:T(8,128)(2,1)S(1)}, bf16[64,1024]{1,0:T(8,128)(2,1)S(1)}, bf16[64,1024]{1,0:T(8,128)(2,1)S(1)}) custom-call(s32[1,1024]{1,0:T(1,128)S(1)} %bitcast.7, bf16[256,1024]{1,0:T(8,128)(2,1)S(1)} %shard_map.118.query, bf16[1024,1024]{1,0:T(8,128)(2,1)S(1)} %copy-done.1, bf16[128,1024]{1,0:T(8,128)(2,1)S(1)} %copy-done.9, ...), custom_call_target="tpu_custom_call" | custom-call | flops 5368709120 | bytes 7344128 | tf_op jit(solution)/shard_map/pallas_call | solution.py:207
  46.9 2.3 %collective-permute-start.23 = (bf16[64,1024]{1,0:T(8,128)(2,1)S(1)}, bf16[64,1024]{1,0:T(8,128)(2,1)S(1)}, u32[]{:S(2)}, u32[]{:S(2)}) collective-permute-start(bf16[64,1024]{1,0:T(8,128)(2,1)S(1)} %get-tuple-element.86), channel_id=1, source_target_pairs={{4,0},{8,4},{12,8},{16,12},{20,16},{24,20},{28,24},{5,1},{9,5},{13... | collective-permute-start | bytes 393224 | tf_op jit(solution)/shard_map/ppermute | solution.py:22
  49.2 3.5 %collective-permute-start.22 = (bf16[64,1024]{1,0:T(8,128)(2,1)S(1)}, bf16[64,1024]{1,0:T(8,128)(2,1)S(1)}, u32[]{:S(2)}, u32[]{:S(2)}) collective-permute-start(bf16[64,1024]{1,0:T(8,128)(2,1)S(1)} %get-tuple-element.85), channel_id=1, source_target_pairs={{0,4},{4,8},{8,12},{12,16},{16,20},{20,24},{24,28},{1,5},{5,9},{9,... | collective-permute-start | bytes 393224 | tf_op jit(solution)/shard_map/ppermute | solution.py:22
  52.7 3.2 %collective-permute-done.21.refs_11_ = bf16[1024,512]{1,0:T(8,128)(2,1)S(1)} collective-permute-done((bf16[1024,512]{1,0:T(8,128)(2,1)S(1)}, bf16[1024,512]{1,0:T(8,128)(2,1)S(1)}, u32[]{:S(2)}, u32[]{:S(2)}) %collective-permute-start.21) | collective-permute-done | bytes 1048608 | tf_op jit(solution)/shard_map/ppermute | solution.py:174
  55.8 5.5 %collective-permute-done.23 = bf16[64,1024]{1,0:T(8,128)(2,1)S(1)} collective-permute-done((bf16[64,1024]{1,0:T(8,128)(2,1)S(1)}, bf16[64,1024]{1,0:T(8,128)(2,1)S(1)}, u32[]{:S(2)}, u32[]{:S(2)}) %collective-permute-start.23) | collective-permute-done | bytes 131104 | tf_op jit(solution)/shard_map/ppermute | solution.py:22
  61.4 2.8 %collective-permute-start.25 = (bf16[128,1024]{1,0:T(8,128)(2,1)S(1)}, bf16[128,1024]{1,0:T(8,128)(2,1)S(1)}, u32[]{:S(2)}, u32[]{:S(2)}) collective-permute-start(bf16[128,1024]{1,0:T(8,128)(2,1)S(1)} %maximum_add_fusion.refs_0_), channel_id=1, source_target_pairs={{0,8},{4,12},{8,0},{12,4},{16,24},{20,28},{24,16},{28,20},{1,9},{5... | collective-permute-start | bytes 786440 | tf_op jit(solution)/shard_map/ppermute | solution.py:174
  65.5 5.6 %collective-permute-done.25.refs_2_ = bf16[128,1024]{1,0:T(8,128)(2,1)S(1)} collective-permute-done((bf16[128,1024]{1,0:T(8,128)(2,1)S(1)}, bf16[128,1024]{1,0:T(8,128)(2,1)S(1)}, u32[]{:S(2)}, u32[]{:S(2)}) %collective-permute-start.25) | collective-permute-done | bytes 262176 | tf_op jit(solution)/shard_map/ppermute | solution.py:174
  71.1 6.4 %collective-permute-done.27.refs_4_ = bf16[128,1024]{1,0:T(8,128)(2,1)S(1)} collective-permute-done((bf16[128,1024]{1,0:T(8,128)(2,1)S(1)}, bf16[128,1024]{1,0:T(8,128)(2,1)S(1)}, u32[]{:S(2)}, u32[]{:S(2)}) %collective-permute-start.27) | collective-permute-done | bytes 262176 | tf_op jit(solution)/shard_map/ppermute | solution.py:174
  82.6 2.0 collective-permute-start.37
  86.0 19.1 %collective-permute-done.34.refs_9_ = bf16[1024,512]{1,0:T(8,128)(2,1)S(1)} collective-permute-done((bf16[1024,512]{1,0:T(8,128)(2,1)S(1)}, bf16[1024,512]{1,0:T(8,128)(2,1)S(1)}, u32[]{:S(2)}, u32[]{:S(2)}) %collective-permute-start.34) | collective-permute-done | bytes 1048608 | tf_op jit(solution)/shard_map/ppermute | solution.py:174
  113.3 6.1 %collective-permute-done.43.refs_0_ = bf16[256,512]{1,0:T(8,128)(2,1)S(1)} collective-permute-done((bf16[256,512]{1,0:T(8,128)(2,1)S(1)}, bf16[256,512]{1,0:T(8,128)(2,1)S(1)}, u32[]{:S(2)}, u32[]{:S(2)}) %collective-permute-start.43) | collective-permute-done | bytes 262176 | tf_op jit(solution)/shard_map/ppermute | solution.py:174
  119.4 2.8 %collective-permute-done.42.refs_3_ = bf16[272,384]{1,0:T(8,128)(2,1)S(1)} collective-permute-done((bf16[272,384]{1,0:T(8,128)(2,1)S(1)}, bf16[272,384]{1,0:T(8,128)(2,1)S(1)}, u32[]{:S(2)}, u32[]{:S(2)}) %collective-permute-start.42) | collective-permute-done | bytes 208928 | tf_op jit(solution)/shard_map/ppermute | solution.py:174
  125.5 2.3 %shard_map.123 = (f32[520,384]{1,0:T(8,128)S(1)}, bf16[528,384]{1,0:T(8,128)(2,1)S(1)}, bf16[528,384]{1,0:T(8,128)(2,1)S(1)}, bf16[528,384]{1,0:T(8,128)(2,1)S(1)}) custom-call(f32[1,4096]{1,0:T(1,128)S(1)} %bitcast.4, bf16[256,512]{1,0:T(8,128)(2,1)S(1)} %collective-permute-done.43.refs_0_, bf16[256,512]{1,0:T(8,128)(2,1)S(1)} %collective-permute-done.44.refs_1_, ...), custom_call_target="tpu_custom_call" | custom-call | flops 1610612736 | bytes 6225920 | tf_op jit(solution)/shard_map/pallas_call | solution.py:207
  130.6 6.5 %collective-permute-done.50.refs_0_ = bf16[256,512]{1,0:T(8,128)(2,1)S(1)} collective-permute-done((bf16[256,512]{1,0:T(8,128)(2,1)S(1)}, bf16[256,512]{1,0:T(8,128)(2,1)S(1)}, u32[]{:S(2)}, u32[]{:S(2)}) %collective-permute-start.50) | collective-permute-done | bytes 262176 | tf_op jit(solution)/shard_map/ppermute | solution.py:174
  140.8 7.2 %collective-permute-done.49.refs_7_ = bf16[528,384]{1,0:T(8,128)(2,1)S(1)} collective-permute-done((bf16[528,384]{1,0:T(8,128)(2,1)S(1)}, bf16[528,384]{1,0:T(8,128)(2,1)S(1)}, u32[]{:S(2)}, u32[]{:S(2)}) %collective-permute-start.49) | collective-permute-done | bytes 405536 | tf_op jit(solution)/shard_map/ppermute | solution.py:174
  150.7 3.4 %collective-permute-start.55 = (bf16[256,512]{1,0:T(8,128)(2,1)S(1)}, bf16[256,512]{1,0:T(8,128)(2,1)S(1)}, u32[]{:S(2)}, u32[]{:S(2)}) collective-permute-start(bf16[256,512]{1,0:T(8,128)(2,1)S(1)} %add_convert_fusion.refs_0_), channel_id=1, source_target_pairs={{0,0},{1,8},{2,16},{3,24},{4,4},{5,12},{6,20},{7,28},{8,1},{9,9},{... | collective-permute-start | bytes 786440 | tf_op jit(solution)/shard_map/ppermute | solution.py:609
  154.2 3.8 %collective-permute-done.54.refs_11_ = bf16[272,384]{1,0:T(8,128)(2,1)S(1)} collective-permute-done((bf16[272,384]{1,0:T(8,128)(2,1)S(1)}, bf16[272,384]{1,0:T(8,128)(2,1)S(1)}, u32[]{:S(2)}, u32[]{:S(2)}) %collective-permute-start.54) | collective-permute-done | bytes 208928 | tf_op jit(solution)/shard_map/ppermute | solution.py:174
  158.0 2.0 shard_map.125
  160.0 10.6 %collective-permute-start.57 = (bf16[256,128]{1,0:T(8,128)(2,1)S(1)}, bf16[256,128]{1,0:T(8,128)(2,1)S(1)}, u32[]{:S(2)}, u32[]{:S(2)}) collective-permute-start(bf16[256,128]{1,0:T(8,128)(2,1)S(1)} %get-tuple-element.133), channel_id=1, source_target_pairs={{0,8},{4,12},{8,0},{12,4},{16,24},{20,28},{24,16},{28,20},{1,9},{5... | collective-permute-start | bytes 196616 | tf_op jit(solution)/shard_map/ppermute | solution.py:174
  170.6 2.0 collective-permute-start.59
  173.7 2.7 %collective-permute-start.56 = (bf16[256,128]{1,0:T(8,128)(2,1)S(1)}, bf16[256,128]{1,0:T(8,128)(2,1)S(1)}, u32[]{:S(2)}, u32[]{:S(2)}) collective-permute-start(bf16[256,128]{1,0:T(8,128)(2,1)S(1)} %get-tuple-element.132.refs_0_), channel_id=1, source_target_pairs={{0,4},{4,0},{8,12},{12,8},{16,20},{20,16},{24,28},{28,24},{1,5},{5... | collective-permute-start | bytes 196616 | tf_op jit(solution)/shard_map/ppermute | solution.py:174
  178.0 2.2 %collective-permute-start.62 = (bf16[256,128]{1,0:T(8,128)(2,1)S(1)}, bf16[256,128]{1,0:T(8,128)(2,1)S(1)}, u32[]{:S(2)}, u32[]{:S(2)}) collective-permute-start(bf16[256,128]{1,0:T(8,128)(2,1)S(1)} %collective-permute-done.61.refs_6_), channel_id=1, source_target_pairs={{0,4},{4,0},{8,12},{12,8},{16,20},{20,16},{24,28},{28,24},{1,5},{5... | collective-permute-start | bytes 196616 | tf_op jit(solution)/shard_map/ppermute | solution.py:174
  181.1 2.3 %shard_map.126 = (f32[256,512]{1,0:T(8,128)S(1)}, bf16[256,512]{1,0:T(8,128)(2,1)S(1)}, bf16[256,512]{1,0:T(8,128)(2,1)S(1)}, bf16[256,512]{1,0:T(8,128)(2,1)S(1)}) custom-call(bf16[256,128]{1,0:T(8,128)(2,1)S(1)} %get-tuple-element.132.refs_0_, bf16[256,128]{1,0:T(8,128)(2,1)S(1)} %collective-permute-done.56.refs_1_, ...), custom_call_target="tpu_custom_call" | custom-call | flops 1073741824 | bytes 6029312 | tf_op jit(solution)/shard_map/pallas_call | solution.py:207
  186.1 7.1 %collective-permute-done.63.refs_1_ = bf16[256,512]{1,0:T(8,128)(2,1)S(1)} collective-permute-done((bf16[256,512]{1,0:T(8,128)(2,1)S(1)}, bf16[256,512]{1,0:T(8,128)(2,1)S(1)}, u32[]{:S(2)}, u32[]{:S(2)}) %collective-permute-start.63) | collective-permute-done | bytes 262176 | tf_op jit(solution)/shard_map/ppermute | solution.py:174
  193.2 3.1 %collective-permute-done.64.refs_2_ = bf16[256,512]{1,0:T(8,128)(2,1)S(1)} collective-permute-done((bf16[256,512]{1,0:T(8,128)(2,1)S(1)}, bf16[256,512]{1,0:T(8,128)(2,1)S(1)}, u32[]{:S(2)}, u32[]{:S(2)}) %collective-permute-start.64) | collective-permute-done | bytes 262176 | tf_op jit(solution)/shard_map/ppermute | solution.py:174
  196.3 12.5 %collective-permute-done.65.refs_3_ = bf16[256,512]{1,0:T(8,128)(2,1)S(1)} collective-permute-done((bf16[256,512]{1,0:T(8,128)(2,1)S(1)}, bf16[256,512]{1,0:T(8,128)(2,1)S(1)}, u32[]{:S(2)}, u32[]{:S(2)}) %collective-permute-start.65) | collective-permute-done | bytes 262176 | tf_op jit(solution)/shard_map/ppermute | solution.py:174
  (143 shorter events, 58.9 us)
Async XLA Ops:
  2.5 13.6 %collective-permute-start.5 = (bf16[128,1024]{1,0:T(8,128)(2,1)}, bf16[128,1024]{1,0:T(8,128)(2,1)S(1)}, u32[]{:S(2)}, u32[]{:S(2)}) collective-permute-start(bf16[128,1024]{1,0:T(8,128)(2,1)} %refs_0_.2), channel_id=1, source_target_pairs={{0,24},{4,28},{8,16},{12,20},{16,8},{20,12},{24,0},{28,4},{1,25},{... | collective-permute-start | bytes 786440 | tf_op jit(solution)/shard_map/ppermute | solution.py:174
  2.6 14.1 %collective-permute-start = (bf16[128,1024]{1,0:T(8,128)(2,1)}, bf16[128,1024]{1,0:T(8,128)(2,1)S(1)}, u32[]{:S(2)}, u32[]{:S(2)}) collective-permute-start(bf16[128,1024]{1,0:T(8,128)(2,1)} %refs_0_.2), channel_id=1, source_target_pairs={{0,4},{4,0},{8,12},{12,8},{16,20},{20,16},{24,28},{28,24},{1,5},{5... | collective-permute-start | bytes 786440 | tf_op jit(solution)/shard_map/ppermute | solution.py:174
  4.2 14.5 %collective-permute-start.8 = (bf16[128,1024]{1,0:T(8,128)(2,1)}, bf16[128,1024]{1,0:T(8,128)(2,1)S(1)}, u32[]{:S(2)}, u32[]{:S(2)}) collective-permute-start(bf16[128,1024]{1,0:T(8,128)(2,1)} %refs_0_.3), channel_id=1, source_target_pairs={{0,8},{4,12},{8,0},{12,4},{16,24},{20,28},{24,16},{28,20},{1,9},{5... | collective-permute-start | bytes 786440 | tf_op jit(solution)/shard_map/ppermute | solution.py:174
  7.4 13.2 %collective-permute-start.17 = (bf16[128,1024]{1,0:T(8,128)(2,1)}, bf16[128,1024]{1,0:T(8,128)(2,1)S(1)}, u32[]{:S(2)}, u32[]{:S(2)}) collective-permute-start(bf16[128,1024]{1,0:T(8,128)(2,1)} %refs_8_.1), channel_id=1, source_target_pairs={{0,16},{4,20},{8,24},{12,28},{16,0},{20,4},{24,8},{28,12},{1,17},{... | collective-permute-start | bytes 786440 | tf_op jit(solution)/shard_map/ppermute | solution.py:174
  8.6 12.8 %collective-permute-start.2 = (bf16[128,1024]{1,0:T(8,128)(2,1)S(1)}, bf16[128,1024]{1,0:T(8,128)(2,1)S(1)}, u32[]{:S(2)}, u32[]{:S(2)}) collective-permute-start(bf16[128,1024]{1,0:T(8,128)(2,1)S(1)} %collective-permute-done.1.refs_2_), channel_id=1, source_target_pairs={{0,4},{4,0},{8,12},{12,8},{16,20},{20,16},{24,28},{28,24},{1,5},{5... | collective-permute-start | bytes 786440 | tf_op jit(solution)/shard_map/ppermute | solution.py:174
  16.7 15.7 %collective-permute-start.10 = (bf16[128,1024]{1,0:T(8,128)(2,1)}, bf16[128,1024]{1,0:T(8,128)(2,1)S(1)}, u32[]{:S(2)}, u32[]{:S(2)}) collective-permute-start(bf16[128,1024]{1,0:T(8,128)(2,1)} %refs_0_.3), channel_id=1, source_target_pairs={{0,16},{4,20},{8,24},{12,28},{16,0},{20,4},{24,8},{28,12},{1,17},{... | collective-permute-start | bytes 786440 | tf_op jit(solution)/shard_map/ppermute | solution.py:174
  20.6 11.9 %collective-permute-start.12 = (bf16[128,1024]{1,0:T(8,128)(2,1)S(1)}, bf16[128,1024]{1,0:T(8,128)(2,1)S(1)}, u32[]{:S(2)}, u32[]{:S(2)}) collective-permute-start(bf16[128,1024]{1,0:T(8,128)(2,1)S(1)} %collective-permute-done.8.refs_2_), channel_id=1, source_target_pairs={{0,16},{4,20},{8,24},{12,28},{16,0},{20,4},{24,8},{28,12},{1,17},{... | collective-permute-start | bytes 786440 | tf_op jit(solution)/shard_map/ppermute | solution.py:174
  21.5 11.5 %collective-permute-start.19 = (bf16[128,1024]{1,0:T(8,128)(2,1)S(1)}, bf16[128,1024]{1,0:T(8,128)(2,1)S(1)}, u32[]{:S(2)}, u32[]{:S(2)}) collective-permute-start(bf16[128,1024]{1,0:T(8,128)(2,1)S(1)} %collective-permute-done.17.refs_12_), channel_id=1, source_target_pairs={{0,8},{4,12},{8,0},{12,4},{16,24},{20,28},{24,16},{28,20},{1,9},{5... | collective-permute-start | bytes 786440 | tf_op jit(solution)/shard_map/ppermute | solution.py:174
  24.6 10.3 %collective-permute-start.7 = (bf16[128,1024]{1,0:T(8,128)(2,1)}, bf16[128,1024]{1,0:T(8,128)(2,1)S(1)}, u32[]{:S(2)}, u32[]{:S(2)}) collective-permute-start(bf16[128,1024]{1,0:T(8,128)(2,1)} %refs_0_.3), channel_id=1, source_target_pairs={{0,4},{4,0},{8,12},{12,8},{16,20},{20,16},{24,28},{28,24},{1,5},{5... | collective-permute-start | bytes 786440 | tf_op jit(solution)/shard_map/ppermute | solution.py:174
  33.1 22.7 %collective-permute-start.21 = (bf16[1024,512]{1,0:T(8,128)(2,1)S(1)}, bf16[1024,512]{1,0:T(8,128)(2,1)S(1)}, u32[]{:S(2)}, u32[]{:S(2)}) collective-permute-start(bf16[1024,512]{1,0:T(8,128)(2,1)S(1)} %copy-done.5), channel_id=1, source_target_pairs={{0,24},{4,28},{8,16},{12,20},{16,8},{20,12},{24,0},{28,4},{1,25},{... | collective-permute-start | bytes 3145736 | tf_op jit(solution)/shard_map/ppermute | solution.py:174
  46.9 14.4 %collective-permute-start.23 = (bf16[64,1024]{1,0:T(8,128)(2,1)S(1)}, bf16[64,1024]{1,0:T(8,128)(2,1)S(1)}, u32[]{:S(2)}, u32[]{:S(2)}) collective-permute-start(bf16[64,1024]{1,0:T(8,128)(2,1)S(1)} %get-tuple-element.86), channel_id=1, source_target_pairs={{4,0},{8,4},{12,8},{16,12},{20,16},{24,20},{28,24},{5,1},{9,5},{13... | collective-permute-start | bytes 393224 | tf_op jit(solution)/shard_map/ppermute | solution.py:22
  49.2 12.2 %collective-permute-start.22 = (bf16[64,1024]{1,0:T(8,128)(2,1)S(1)}, bf16[64,1024]{1,0:T(8,128)(2,1)S(1)}, u32[]{:S(2)}, u32[]{:S(2)}) collective-permute-start(bf16[64,1024]{1,0:T(8,128)(2,1)S(1)} %get-tuple-element.85), channel_id=1, source_target_pairs={{0,4},{4,8},{8,12},{12,16},{16,20},{20,24},{24,28},{1,5},{5,9},{9,... | collective-permute-start | bytes 393224 | tf_op jit(solution)/shard_map/ppermute | solution.py:22
  61.4 9.6 %collective-permute-start.25 = (bf16[128,1024]{1,0:T(8,128)(2,1)S(1)}, bf16[128,1024]{1,0:T(8,128)(2,1)S(1)}, u32[]{:S(2)}, u32[]{:S(2)}) collective-permute-start(bf16[128,1024]{1,0:T(8,128)(2,1)S(1)} %maximum_add_fusion.refs_0_), channel_id=1, source_target_pairs={{0,8},{4,12},{8,0},{12,4},{16,24},{20,28},{24,16},{28,20},{1,9},{5... | collective-permute-start | bytes 786440 | tf_op jit(solution)/shard_map/ppermute | solution.py:174
  64.2 13.2 %collective-permute-start.27 = (bf16[128,1024]{1,0:T(8,128)(2,1)S(1)}, bf16[128,1024]{1,0:T(8,128)(2,1)S(1)}, u32[]{:S(2)}, u32[]{:S(2)}) collective-permute-start(bf16[128,1024]{1,0:T(8,128)(2,1)S(1)} %maximum_add_fusion.refs_0_), channel_id=1, source_target_pairs={{0,16},{4,20},{8,24},{12,28},{16,0},{20,4},{24,8},{28,12},{1,17},{... | collective-permute-start | bytes 786440 | tf_op jit(solution)/shard_map/ppermute | solution.py:174
  64.2 13.6 %collective-permute-start.29 = (bf16[128,1024]{1,0:T(8,128)(2,1)S(1)}, bf16[128,1024]{1,0:T(8,128)(2,1)S(1)}, u32[]{:S(2)}, u32[]{:S(2)}) collective-permute-start(bf16[128,1024]{1,0:T(8,128)(2,1)S(1)} %maximum_add_fusion.refs_0_), channel_id=1, source_target_pairs={{0,24},{4,28},{8,16},{12,20},{16,8},{20,12},{24,0},{28,4},{1,25},{... | collective-permute-start | bytes 786440 | tf_op jit(solution)/shard_map/ppermute | solution.py:174
  65.5 12.9 %collective-permute-start.24 = (bf16[128,1024]{1,0:T(8,128)(2,1)S(1)}, bf16[128,1024]{1,0:T(8,128)(2,1)S(1)}, u32[]{:S(2)}, u32[]{:S(2)}) collective-permute-start(bf16[128,1024]{1,0:T(8,128)(2,1)S(1)} %maximum_add_fusion.refs_0_), channel_id=1, source_target_pairs={{0,4},{4,0},{8,12},{12,8},{16,20},{20,16},{24,28},{28,24},{1,5},{5... | collective-permute-start | bytes 786440 | tf_op jit(solution)/shard_map/ppermute | solution.py:174
  80.7 24.4 %collective-permute-start.34 = (bf16[1024,512]{1,0:T(8,128)(2,1)S(1)}, bf16[1024,512]{1,0:T(8,128)(2,1)S(1)}, u32[]{:S(2)}, u32[]{:S(2)}) collective-permute-start(bf16[1024,512]{1,0:T(8,128)(2,1)S(1)} %copy-done.5), channel_id=1, source_target_pairs={{0,8},{4,12},{8,0},{12,4},{16,24},{20,28},{24,16},{28,20},{1,9},{5... | collective-permute-start | bytes 3145736 | tf_op jit(solution)/shard_map/ppermute | solution.py:174
  80.8 24.4 %collective-permute-start.35 = (bf16[1024,512]{1,0:T(8,128)(2,1)S(1)}, bf16[1024,512]{1,0:T(8,128)(2,1)S(1)}, u32[]{:S(2)}, u32[]{:S(2)}) collective-permute-start(bf16[1024,512]{1,0:T(8,128)(2,1)S(1)} %copy-done.5), channel_id=1, source_target_pairs={{0,16},{4,20},{8,24},{12,28},{16,0},{20,4},{24,8},{28,12},{1,17},{... | collective-permute-start | bytes 3145736 | tf_op jit(solution)/shard_map/ppermute | solution.py:174
  81.3 23.9 %collective-permute-start.38 = (bf16[256,512]{1,0:T(8,128)(2,1)S(1)}, bf16[256,512]{1,0:T(8,128)(2,1)S(1)}, u32[]{:S(2)}, u32[]{:S(2)}) collective-permute-start(bf16[256,512]{1,0:T(8,128)(2,1)S(1)} %get-tuple-element.106), channel_id=1, source_target_pairs={{0,3},{1,2},{2,1},{3,0},{4,7},{5,6},{6,5},{7,4},{8,11},{9,10},{10,... | collective-permute-start | bytes 786440 | tf_op jit(solution)/shard_map/ppermute | solution.py:174
  82.6 22.6 %collective-permute-start.37 = (bf16[256,512]{1,0:T(8,128)(2,1)S(1)}, bf16[256,512]{1,0:T(8,128)(2,1)S(1)}, u32[]{:S(2)}, u32[]{:S(2)}) collective-permute-start(bf16[256,512]{1,0:T(8,128)(2,1)S(1)} %get-tuple-element.105), channel_id=1, source_target_pairs={{0,2},{1,3},{2,0},{3,1},{4,6},{5,7},{6,4},{7,5},{8,10},{9,11},{10,... | collective-permute-start | bytes 786440 | tf_op jit(solution)/shard_map/ppermute | solution.py:174
  84.7 20.6 %collective-permute-start.36 = (bf16[256,512]{1,0:T(8,128)(2,1)S(1)}, bf16[256,512]{1,0:T(8,128)(2,1)S(1)}, u32[]{:S(2)}, u32[]{:S(2)}) collective-permute-start(bf16[256,512]{1,0:T(8,128)(2,1)S(1)} %get-tuple-element.104), channel_id=1, source_target_pairs={{0,1},{1,0},{2,3},{3,2},{4,5},{5,4},{6,7},{7,6},{8,9},{9,8},{10,11... | collective-permute-start | bytes 786440 | tf_op jit(solution)/shard_map/ppermute | solution.py:174
  106.7 12.7 %collective-permute-start.43 = (bf16[256,512]{1,0:T(8,128)(2,1)S(1)}, bf16[256,512]{1,0:T(8,128)(2,1)S(1)}, u32[]{:S(2)}, u32[]{:S(2)}) collective-permute-start(bf16[256,512]{1,0:T(8,128)(2,1)S(1)} %add_convert_fusion.refs_0_), channel_id=1, source_target_pairs={{0,1},{1,0},{2,3},{3,2},{4,5},{5,4},{6,7},{7,6},{8,9},{9,8},{10,11... | collective-permute-start | bytes 786440 | tf_op jit(solution)/shard_map/ppermute | solution.py:174
  108.3 15.6 %collective-permute-start.45 = (bf16[256,512]{1,0:T(8,128)(2,1)S(1)}, bf16[256,512]{1,0:T(8,128)(2,1)S(1)}, u32[]{:S(2)}, u32[]{:S(2)}) collective-permute-start(bf16[256,512]{1,0:T(8,128)(2,1)S(1)} %add_convert_fusion.refs_0_), channel_id=1, source_target_pairs={{0,2},{1,3},{2,0},{3,1},{4,6},{5,7},{6,4},{7,5},{8,10},{9,11},{10,... | collective-permute-start | bytes 786440 | tf_op jit(solution)/shard_map/ppermute | solution.py:174
  124.0 13.1 %collective-permute-start.50 = (bf16[256,512]{1,0:T(8,128)(2,1)S(1)}, bf16[256,512]{1,0:T(8,128)(2,1)S(1)}, u32[]{:S(2)}, u32[]{:S(2)}) collective-permute-start(bf16[256,512]{1,0:T(8,128)(2,1)S(1)} %add_convert_fusion.refs_0_), channel_id=1, source_target_pairs={{0,3},{1,2},{2,1},{3,0},{4,7},{5,6},{6,5},{7,4},{8,11},{9,10},{10,... | collective-permute-start | bytes 786440 | tf_op jit(solution)/shard_map/ppermute | solution.py:174
  127.8 13.0 %collective-permute-start.47 = (bf16[528,384]{1,0:T(8,128)(2,1)S(1)}, bf16[528,384]{1,0:T(8,128)(2,1)S(1)}, u32[]{:S(2)}, u32[]{:S(2)}) collective-permute-start(bf16[528,384]{1,0:T(8,128)(2,1)S(1)} %get-tuple-element.118), channel_id=1, source_target_pairs={{0,8},{4,12},{8,0},{12,4},{16,24},{20,28},{24,16},{28,20},{1,9},{5... | collective-permute-start | bytes 1216520 | tf_op jit(solution)/shard_map/ppermute | solution.py:174
  128.8 12.0 %collective-permute-start.48 = (bf16[528,384]{1,0:T(8,128)(2,1)S(1)}, bf16[528,384]{1,0:T(8,128)(2,1)S(1)}, u32[]{:S(2)}, u32[]{:S(2)}) collective-permute-start(bf16[528,384]{1,0:T(8,128)(2,1)S(1)} %get-tuple-element.119), channel_id=1, source_target_pairs={{0,16},{4,20},{8,24},{12,28},{16,0},{20,4},{24,8},{28,12},{1,17},{... | collective-permute-start | bytes 1216520 | tf_op jit(solution)/shard_map/ppermute | solution.py:174
  129.1 18.9 %collective-permute-start.49 = (bf16[528,384]{1,0:T(8,128)(2,1)S(1)}, bf16[528,384]{1,0:T(8,128)(2,1)S(1)}, u32[]{:S(2)}, u32[]{:S(2)}) collective-permute-start(bf16[528,384]{1,0:T(8,128)(2,1)S(1)} %get-tuple-element.120), channel_id=1, source_target_pairs={{0,24},{4,28},{8,16},{12,20},{16,8},{20,12},{24,0},{28,4},{1,25},{... | collective-permute-start | bytes 1216520 | tf_op jit(solution)/shard_map/ppermute | solution.py:174
  150.7 29.5 %collective-permute-start.55 = (bf16[256,512]{1,0:T(8,128)(2,1)S(1)}, bf16[256,512]{1,0:T(8,128)(2,1)S(1)}, u32[]{:S(2)}, u32[]{:S(2)}) collective-permute-start(bf16[256,512]{1,0:T(8,128)(2,1)S(1)} %add_convert_fusion.refs_0_), channel_id=1, source_target_pairs={{0,0},{1,8},{2,16},{3,24},{4,4},{5,12},{6,20},{7,28},{8,1},{9,9},{... | collective-permute-start | bytes 786440 | tf_op jit(solution)/shard_map/ppermute | solution.py:609
  160.0 16.4 %collective-permute-start.57 = (bf16[256,128]{1,0:T(8,128)(2,1)S(1)}, bf16[256,128]{1,0:T(8,128)(2,1)S(1)}, u32[]{:S(2)}, u32[]{:S(2)}) collective-permute-start(bf16[256,128]{1,0:T(8,128)(2,1)S(1)} %get-tuple-element.133), channel_id=1, source_target_pairs={{0,8},{4,12},{8,0},{12,4},{16,24},{20,28},{24,16},{28,20},{1,9},{5... | collective-permute-start | bytes 196616 | tf_op jit(solution)/shard_map/ppermute | solution.py:174
  183.4 9.8 %collective-permute-start.63 = (bf16[256,512]{1,0:T(8,128)(2,1)S(1)}, bf16[256,512]{1,0:T(8,128)(2,1)S(1)}, u32[]{:S(2)}, u32[]{:S(2)}) collective-permute-start(bf16[256,512]{1,0:T(8,128)(2,1)S(1)} %get-tuple-element.142), channel_id=1, source_target_pairs={{0,1},{1,0},{2,3},{3,2},{4,5},{5,4},{6,7},{7,6},{8,9},{9,8},{10,11... | collective-permute-start | bytes 786440 | tf_op jit(solution)/shard_map/ppermute | solution.py:174
  183.5 12.8 %collective-permute-start.64 = (bf16[256,512]{1,0:T(8,128)(2,1)S(1)}, bf16[256,512]{1,0:T(8,128)(2,1)S(1)}, u32[]{:S(2)}, u32[]{:S(2)}) collective-permute-start(bf16[256,512]{1,0:T(8,128)(2,1)S(1)} %get-tuple-element.143), channel_id=1, source_target_pairs={{0,2},{1,3},{2,0},{3,1},{4,6},{5,7},{6,4},{7,5},{8,10},{9,11},{10,... | collective-permute-start | bytes 786440 | tf_op jit(solution)/shard_map/ppermute | solution.py:174
  184.6 24.3 %collective-permute-start.65 = (bf16[256,512]{1,0:T(8,128)(2,1)S(1)}, bf16[256,512]{1,0:T(8,128)(2,1)S(1)}, u32[]{:S(2)}, u32[]{:S(2)}) collective-permute-start(bf16[256,512]{1,0:T(8,128)(2,1)S(1)} %get-tuple-element.144), channel_id=1, source_target_pairs={{0,3},{1,2},{2,1},{3,0},{4,7},{5,6},{6,5},{7,4},{8,11},{9,10},{10,... | collective-permute-start | bytes 786440 | tf_op jit(solution)/shard_map/ppermute | solution.py:174
  (46 other events, 408.6 us)

commit v9 on v8

--- a/solution.py
+++ b/solution.py
@@ -591,7 +591,7 @@
             flops=2 * height * 2 * out_width * 3 * HEAD_DIM * chip_count,
         )
         if g > 1:
-            sent = [after(part, *shares[(g - 1) * chip_count + 1 :]) for part in sent]
+            sent[2:] = [after(part, *shares[(g - 1) * chip_count + 1 :]) for part in sent[2:]]
         shares += [share] + [exchanged(part, "seq", 2 * d) for d, part in enumerate(sent, 1)]
     attended = call(
         functools.partial(attention_kernel, groups, chip_count, out_width * seq_count),

time: 213 us -> 210 us (0.986)
  starting transfers between devices: 87.1 us -> 84.6 us
    ppermute x64, starting transfers between devices: 77.9 us -> 75 us  [exchanged(): return lax.ppermute(block, axis, route)]
  transfers between devices with their start and end apart: 67 -> 67, of which waited for: 28 -> 30; matrix products, arithmetic and copies ran while one was open for 1% -> 1% of each run, Pallas kernels for 9% -> 9%
where the time goes in v9:
time: 210 us
  waiting for transfers between devices  98.4 us (47%)
  starting transfers between devices  84.6 us (40%)
  Pallas kernels  21.2 us (10%)
  local copies, waits for them, and re-layouts  3.48 us (2%)
    ppermute x64, waiting for transfers between devices, exchanged(): return lax.ppermute(block, axis, route)  92.8 us
    ppermute x64, starting transfers between devices, exchanged(): return lax.ppermute(block, axis, route)  75 us
    pallas_call x10, Pallas kernels, call(): pl.pallas_call(kernel, out_shape=shapes, in_specs=[pl.BlockSpec(memory_sp...  21.2 us
    ppermute x2, starting transfers between devices, shifted(): return lax.ppermute(block, axis, route)  5.74 us
    ppermute x2, waiting for transfers between devices, shifted(): return lax.ppermute(block, axis, route)  5.53 us
  transfers between devices with their start and end apart: 67, of which 30 were waited for; matrix products, arithmetic and copies ran while one was open for 1% of the time, Pallas kernels for 9%

profile of v9, /device:TPU:9, one launch (start us, length us, event | category | flops | bytes accessed | tf_op | source)
XLA Modules:
  0.0 209.6 jit_solution(7996485343850523105)
XLA Ops:
  5.4 2.0 collective-permute-done.1.refs_2_
  8.6 7.4 %collective-permute-start.2 = (bf16[128,1024]{1,0:T(8,128)(2,1)S(1)}, bf16[128,1024]{1,0:T(8,128)(2,1)S(1)}, u32[]{:S(2)}, u32[]{:S(2)}) collective-permute-start(bf16[128,1024]{1,0:T(8,128)(2,1)S(1)} %collective-permute-done.1.refs_2_), channel_id=1, source_target_pairs={{0,4},{4,0},{8,12},{12,8},{16,20},{20,16},{24,28},{28,24},{1,5},{5... | collective-permute-start | bytes 786440 | tf_op jit(solution)/shard_map/ppermute | solution.py:174
  24.6 3.2 %collective-permute-start.7 = (bf16[128,1024]{1,0:T(8,128)(2,1)}, bf16[128,1024]{1,0:T(8,128)(2,1)S(1)}, u32[]{:S(2)}, u32[]{:S(2)}) collective-permute-start(bf16[128,1024]{1,0:T(8,128)(2,1)} %refs_0_.3), channel_id=1, source_target_pairs={{0,4},{4,0},{8,12},{12,8},{16,20},{20,16},{24,28},{28,24},{1,5},{5... | collective-permute-start | bytes 786440 | tf_op jit(solution)/shard_map/ppermute | solution.py:174
  30.4 2.0 shard_map.118.query
  33.1 1.8 collective-permute-start.21
  34.9 2.4 %collective-permute-start.13 = (bf16[128,1024]{1,0:T(8,128)(2,1)S(1)}, bf16[128,1024]{1,0:T(8,128)(2,1)S(1)}, u32[]{:S(2)}, u32[]{:S(2)}) collective-permute-start(bf16[128,1024]{1,0:T(8,128)(2,1)S(1)} %collective-permute-done.12.refs_6_), channel_id=1, source_target_pairs={{0,4},{4,0},{8,12},{12,8},{16,20},{20,16},{24,28},{28,24},{1,5},{5... | collective-permute-start | bytes 786440 | tf_op jit(solution)/shard_map/ppermute | solution.py:174
  39.6 7.3 %shard_map.119 = (bf16[128,1024]{1,0:T(8,128)(2,1)S(1)}, bf16[64,1024]{1,0:T(8,128)(2,1)S(1)}, bf16[64,1024]{1,0:T(8,128)(2,1)S(1)}) custom-call(s32[1,1024]{1,0:T(1,128)S(1)} %bitcast.7, bf16[256,1024]{1,0:T(8,128)(2,1)S(1)} %shard_map.118.query, bf16[1024,1024]{1,0:T(8,128)(2,1)S(1)} %copy-done.1, bf16[128,1024]{1,0:T(8,128)(2,1)S(1)} %copy-done.9, ...), custom_call_target="tpu_custom_call" | custom-call | flops 5368709120 | bytes 7344128 | tf_op jit(solution)/shard_map/pallas_call | solution.py:207
  46.9 2.3 %collective-permute-start.23 = (bf16[64,1024]{1,0:T(8,128)(2,1)S(1)}, bf16[64,1024]{1,0:T(8,128)(2,1)S(1)}, u32[]{:S(2)}, u32[]{:S(2)}) collective-permute-start(bf16[64,1024]{1,0:T(8,128)(2,1)S(1)} %get-tuple-element.84), channel_id=1, source_target_pairs={{4,0},{8,4},{12,8},{16,12},{20,16},{24,20},{28,24},{5,1},{9,5},{13... | collective-permute-start | bytes 393224 | tf_op jit(solution)/shard_map/ppermute | solution.py:22
  49.2 3.5 %collective-permute-start.22 = (bf16[64,1024]{1,0:T(8,128)(2,1)S(1)}, bf16[64,1024]{1,0:T(8,128)(2,1)S(1)}, u32[]{:S(2)}, u32[]{:S(2)}) collective-permute-start(bf16[64,1024]{1,0:T(8,128)(2,1)S(1)} %get-tuple-element.83), channel_id=1, source_target_pairs={{0,4},{4,8},{8,12},{12,16},{16,20},{20,24},{24,28},{1,5},{5,9},{9,... | collective-permute-start | bytes 393224 | tf_op jit(solution)/shard_map/ppermute | solution.py:22
  52.7 3.2 %collective-permute-done.21.refs_11_ = bf16[1024,512]{1,0:T(8,128)(2,1)S(1)} collective-permute-done((bf16[1024,512]{1,0:T(8,128)(2,1)S(1)}, bf16[1024,512]{1,0:T(8,128)(2,1)S(1)}, u32[]{:S(2)}, u32[]{:S(2)}) %collective-permute-start.21) | collective-permute-done | bytes 1048608 | tf_op jit(solution)/shard_map/ppermute | solution.py:174
  55.8 5.5 %collective-permute-done.23 = bf16[64,1024]{1,0:T(8,128)(2,1)S(1)} collective-permute-done((bf16[64,1024]{1,0:T(8,128)(2,1)S(1)}, bf16[64,1024]{1,0:T(8,128)(2,1)S(1)}, u32[]{:S(2)}, u32[]{:S(2)}) %collective-permute-start.23) | collective-permute-done | bytes 131104 | tf_op jit(solution)/shard_map/ppermute | solution.py:22
  61.4 2.8 %collective-permute-start.25 = (bf16[128,1024]{1,0:T(8,128)(2,1)S(1)}, bf16[128,1024]{1,0:T(8,128)(2,1)S(1)}, u32[]{:S(2)}, u32[]{:S(2)}) collective-permute-start(bf16[128,1024]{1,0:T(8,128)(2,1)S(1)} %maximum_add_fusion.refs_0_), channel_id=1, source_target_pairs={{0,8},{4,12},{8,0},{12,4},{16,24},{20,28},{24,16},{28,20},{1,9},{5... | collective-permute-start | bytes 786440 | tf_op jit(solution)/shard_map/ppermute | solution.py:174
  65.5 5.6 %collective-permute-done.25.refs_2_ = bf16[128,1024]{1,0:T(8,128)(2,1)S(1)} collective-permute-done((bf16[128,1024]{1,0:T(8,128)(2,1)S(1)}, bf16[128,1024]{1,0:T(8,128)(2,1)S(1)}, u32[]{:S(2)}, u32[]{:S(2)}) %collective-permute-start.25) | collective-permute-done | bytes 262176 | tf_op jit(solution)/shard_map/ppermute | solution.py:174
  71.1 6.4 %collective-permute-done.27.refs_4_ = bf16[128,1024]{1,0:T(8,128)(2,1)S(1)} collective-permute-done((bf16[128,1024]{1,0:T(8,128)(2,1)S(1)}, bf16[128,1024]{1,0:T(8,128)(2,1)S(1)}, u32[]{:S(2)}, u32[]{:S(2)}) %collective-permute-start.27) | collective-permute-done | bytes 262176 | tf_op jit(solution)/shard_map/ppermute | solution.py:174
  82.6 2.0 collective-permute-start.37
  86.0 19.1 %collective-permute-done.34.refs_9_ = bf16[1024,512]{1,0:T(8,128)(2,1)S(1)} collective-permute-done((bf16[1024,512]{1,0:T(8,128)(2,1)S(1)}, bf16[1024,512]{1,0:T(8,128)(2,1)S(1)}, u32[]{:S(2)}, u32[]{:S(2)}) %collective-permute-start.34) | collective-permute-done | bytes 1048608 | tf_op jit(solution)/shard_map/ppermute | solution.py:174
  113.3 6.1 %collective-permute-done.43.refs_0_ = bf16[256,512]{1,0:T(8,128)(2,1)S(1)} collective-permute-done((bf16[256,512]{1,0:T(8,128)(2,1)S(1)}, bf16[256,512]{1,0:T(8,128)(2,1)S(1)}, u32[]{:S(2)}, u32[]{:S(2)}) %collective-permute-start.43) | collective-permute-done | bytes 262176 | tf_op jit(solution)/shard_map/ppermute | solution.py:174
  119.4 2.8 %collective-permute-done.42.refs_3_ = bf16[272,384]{1,0:T(8,128)(2,1)S(1)} collective-permute-done((bf16[272,384]{1,0:T(8,128)(2,1)S(1)}, bf16[272,384]{1,0:T(8,128)(2,1)S(1)}, u32[]{:S(2)}, u32[]{:S(2)}) %collective-permute-start.42) | collective-permute-done | bytes 208928 | tf_op jit(solution)/shard_map/ppermute | solution.py:174
  125.5 2.3 %shard_map.123 = (f32[520,384]{1,0:T(8,128)S(1)}, bf16[528,384]{1,0:T(8,128)(2,1)S(1)}, bf16[528,384]{1,0:T(8,128)(2,1)S(1)}, bf16[528,384]{1,0:T(8,128)(2,1)S(1)}) custom-call(f32[1,4096]{1,0:T(1,128)S(1)} %bitcast.4, bf16[256,512]{1,0:T(8,128)(2,1)S(1)} %collective-permute-done.43.refs_0_, bf16[256,512]{1,0:T(8,128)(2,1)S(1)} %collective-permute-done.44.refs_1_, ...), custom_call_target="tpu_custom_call" | custom-call | flops 1610612736 | bytes 6225920 | tf_op jit(solution)/shard_map/pallas_call | solution.py:207
  130.6 6.5 %collective-permute-done.50.refs_0_ = bf16[256,512]{1,0:T(8,128)(2,1)S(1)} collective-permute-done((bf16[256,512]{1,0:T(8,128)(2,1)S(1)}, bf16[256,512]{1,0:T(8,128)(2,1)S(1)}, u32[]{:S(2)}, u32[]{:S(2)}) %collective-permute-start.50) | collective-permute-done | bytes 262176 | tf_op jit(solution)/shard_map/ppermute | solution.py:174
  142.1 6.0 %collective-permute-done.49.refs_7_ = bf16[528,384]{1,0:T(8,128)(2,1)S(1)} collective-permute-done((bf16[528,384]{1,0:T(8,128)(2,1)S(1)}, bf16[528,384]{1,0:T(8,128)(2,1)S(1)}, u32[]{:S(2)}, u32[]{:S(2)}) %collective-permute-start.49) | collective-permute-done | bytes 405536 | tf_op jit(solution)/shard_map/ppermute | solution.py:174
  149.0 3.8 %collective-permute-start.55 = (bf16[256,512]{1,0:T(8,128)(2,1)S(1)}, bf16[256,512]{1,0:T(8,128)(2,1)S(1)}, u32[]{:S(2)}, u32[]{:S(2)}) collective-permute-start(bf16[256,512]{1,0:T(8,128)(2,1)S(1)} %add_convert_fusion.refs_0_), channel_id=1, source_target_pairs={{0,0},{1,8},{2,16},{3,24},{4,4},{5,12},{6,20},{7,28},{8,1},{9,9},{... | collective-permute-start | bytes 786440 | tf_op jit(solution)/shard_map/ppermute | solution.py:609
  153.9 3.2 %collective-permute-done.54.refs_11_ = bf16[272,384]{1,0:T(8,128)(2,1)S(1)} collective-permute-done((bf16[272,384]{1,0:T(8,128)(2,1)S(1)}, bf16[272,384]{1,0:T(8,128)(2,1)S(1)}, u32[]{:S(2)}, u32[]{:S(2)}) %collective-permute-start.54) | collective-permute-done | bytes 208928 | tf_op jit(solution)/shard_map/ppermute | solution.py:174
  157.1 2.0 shard_map.125
  159.1 9.7 %collective-permute-start.57 = (bf16[256,128]{1,0:T(8,128)(2,1)S(1)}, bf16[256,128]{1,0:T(8,128)(2,1)S(1)}, u32[]{:S(2)}, u32[]{:S(2)}) collective-permute-start(bf16[256,128]{1,0:T(8,128)(2,1)S(1)} %get-tuple-element.129), channel_id=1, source_target_pairs={{0,8},{4,12},{8,0},{12,4},{16,24},{20,28},{24,16},{28,20},{1,9},{5... | collective-permute-start | bytes 196616 | tf_op jit(solution)/shard_map/ppermute | solution.py:174
  168.8 2.0 collective-permute-start.59
  171.9 1.8 collective-permute-start.56
  175.2 2.2 %collective-permute-start.62 = (bf16[256,128]{1,0:T(8,128)(2,1)S(1)}, bf16[256,128]{1,0:T(8,128)(2,1)S(1)}, u32[]{:S(2)}, u32[]{:S(2)}) collective-permute-start(bf16[256,128]{1,0:T(8,128)(2,1)S(1)} %collective-permute-done.61.refs_6_), channel_id=1, source_target_pairs={{0,4},{4,0},{8,12},{12,8},{16,20},{20,16},{24,28},{28,24},{1,5},{5... | collective-permute-start | bytes 196616 | tf_op jit(solution)/shard_map/ppermute | solution.py:174
  178.3 2.3 %shard_map.126 = (f32[256,512]{1,0:T(8,128)S(1)}, bf16[256,512]{1,0:T(8,128)(2,1)S(1)}, bf16[256,512]{1,0:T(8,128)(2,1)S(1)}, bf16[256,512]{1,0:T(8,128)(2,1)S(1)}) custom-call(bf16[256,128]{1,0:T(8,128)(2,1)S(1)} %get-tuple-element.128.refs_0_, bf16[256,128]{1,0:T(8,128)(2,1)S(1)} %collective-permute-done.56.refs_1_, ...), custom_call_target="tpu_custom_call" | custom-call | flops 1073741824 | bytes 6029312 | tf_op jit(solution)/shard_map/pallas_call | solution.py:207
  183.4 7.3 %collective-permute-done.63.refs_1_ = bf16[256,512]{1,0:T(8,128)(2,1)S(1)} collective-permute-done((bf16[256,512]{1,0:T(8,128)(2,1)S(1)}, bf16[256,512]{1,0:T(8,128)(2,1)S(1)}, u32[]{:S(2)}, u32[]{:S(2)}) %collective-permute-start.63) | collective-permute-done | bytes 262176 | tf_op jit(solution)/shard_map/ppermute | solution.py:174
  190.6 3.1 %collective-permute-done.64.refs_2_ = bf16[256,512]{1,0:T(8,128)(2,1)S(1)} collective-permute-done((bf16[256,512]{1,0:T(8,128)(2,1)S(1)}, bf16[256,512]{1,0:T(8,128)(2,1)S(1)}, u32[]{:S(2)}, u32[]{:S(2)}) %collective-permute-start.64) | collective-permute-done | bytes 262176 | tf_op jit(solution)/shard_map/ppermute | solution.py:174
  193.7 12.4 %collective-permute-done.65.refs_3_ = bf16[256,512]{1,0:T(8,128)(2,1)S(1)} collective-permute-done((bf16[256,512]{1,0:T(8,128)(2,1)S(1)}, bf16[256,512]{1,0:T(8,128)(2,1)S(1)}, u32[]{:S(2)}, u32[]{:S(2)}) %collective-permute-start.65) | collective-permute-done | bytes 262176 | tf_op jit(solution)/shard_map/ppermute | solution.py:174
  (143 shorter events, 59.4 us)
Async XLA Ops:
  2.5 13.6 %collective-permute-start.5 = (bf16[128,1024]{1,0:T(8,128)(2,1)}, bf16[128,1024]{1,0:T(8,128)(2,1)S(1)}, u32[]{:S(2)}, u32[]{:S(2)}) collective-permute-start(bf16[128,1024]{1,0:T(8,128)(2,1)} %refs_0_.2), channel_id=1, source_target_pairs={{0,24},{4,28},{8,16},{12,20},{16,8},{20,12},{24,0},{28,4},{1,25},{... | collective-permute-start | bytes 786440 | tf_op jit(solution)/shard_map/ppermute | solution.py:174
  2.6 14.1 %collective-permute-start = (bf16[128,1024]{1,0:T(8,128)(2,1)}, bf16[128,1024]{1,0:T(8,128)(2,1)S(1)}, u32[]{:S(2)}, u32[]{:S(2)}) collective-permute-start(bf16[128,1024]{1,0:T(8,128)(2,1)} %refs_0_.2), channel_id=1, source_target_pairs={{0,4},{4,0},{8,12},{12,8},{16,20},{20,16},{24,28},{28,24},{1,5},{5... | collective-permute-start | bytes 786440 | tf_op jit(solution)/shard_map/ppermute | solution.py:174
  4.2 14.5 %collective-permute-start.8 = (bf16[128,1024]{1,0:T(8,128)(2,1)}, bf16[128,1024]{1,0:T(8,128)(2,1)S(1)}, u32[]{:S(2)}, u32[]{:S(2)}) collective-permute-start(bf16[128,1024]{1,0:T(8,128)(2,1)} %refs_0_.3), channel_id=1, source_target_pairs={{0,8},{4,12},{8,0},{12,4},{16,24},{20,28},{24,16},{28,20},{1,9},{5... | collective-permute-start | bytes 786440 | tf_op jit(solution)/shard_map/ppermute | solution.py:174
  7.4 13.2 %collective-permute-start.17 = (bf16[128,1024]{1,0:T(8,128)(2,1)}, bf16[128,1024]{1,0:T(8,128)(2,1)S(1)}, u32[]{:S(2)}, u32[]{:S(2)}) collective-permute-start(bf16[128,1024]{1,0:T(8,128)(2,1)} %refs_8_.1), channel_id=1, source_target_pairs={{0,16},{4,20},{8,24},{12,28},{16,0},{20,4},{24,8},{28,12},{1,17},{... | collective-permute-start | bytes 786440 | tf_op jit(solution)/shard_map/ppermute | solution.py:174
  8.6 12.8 %collective-permute-start.2 = (bf16[128,1024]{1,0:T(8,128)(2,1)S(1)}, bf16[128,1024]{1,0:T(8,128)(2,1)S(1)}, u32[]{:S(2)}, u32[]{:S(2)}) collective-permute-start(bf16[128,1024]{1,0:T(8,128)(2,1)S(1)} %collective-permute-done.1.refs_2_), channel_id=1, source_target_pairs={{0,4},{4,0},{8,12},{12,8},{16,20},{20,16},{24,28},{28,24},{1,5},{5... | collective-permute-start | bytes 786440 | tf_op jit(solution)/shard_map/ppermute | solution.py:174
  16.7 15.7 %collective-permute-start.10 = (bf16[128,1024]{1,0:T(8,128)(2,1)}, bf16[128,1024]{1,0:T(8,128)(2,1)S(1)}, u32[]{:S(2)}, u32[]{:S(2)}) collective-permute-start(bf16[128,1024]{1,0:T(8,128)(2,1)} %refs_0_.3), channel_id=1, source_target_pairs={{0,16},{4,20},{8,24},{12,28},{16,0},{20,4},{24,8},{28,12},{1,17},{... | collective-permute-start | bytes 786440 | tf_op jit(solution)/shard_map/ppermute | solution.py:174
  20.6 11.9 %collective-permute-start.12 = (bf16[128,1024]{1,0:T(8,128)(2,1)S(1)}, bf16[128,1024]{1,0:T(8,128)(2,1)S(1)}, u32[]{:S(2)}, u32[]{:S(2)}) collective-permute-start(bf16[128,1024]{1,0:T(8,128)(2,1)S(1)} %collective-permute-done.8.refs_2_), channel_id=1, source_target_pairs={{0,16},{4,20},{8,24},{12,28},{16,0},{20,4},{24,8},{28,12},{1,17},{... | collective-permute-start | bytes 786440 | tf_op jit(solution)/shard_map/ppermute | solution.py:174
  21.5 11.5 %collective-permute-start.19 = (bf16[128,1024]{1,0:T(8,128)(2,1)S(1)}, bf16[128,1024]{1,0:T(8,128)(2,1)S(1)}, u32[]{:S(2)}, u32[]{:S(2)}) collective-permute-start(bf16[128,1024]{1,0:T(8,128)(2,1)S(1)} %collective-permute-done.17.refs_12_), channel_id=1, source_target_pairs={{0,8},{4,12},{8,0},{12,4},{16,24},{20,28},{24,16},{28,20},{1,9},{5... | collective-permute-start | bytes 786440 | tf_op jit(solution)/shard_map/ppermute | solution.py:174
  24.6 10.3 %collective-permute-start.7 = (bf16[128,1024]{1,0:T(8,128)(2,1)}, bf16[128,1024]{1,0:T(8,128)(2,1)S(1)}, u32[]{:S(2)}, u32[]{:S(2)}) collective-permute-start(bf16[128,1024]{1,0:T(8,128)(2,1)} %refs_0_.3), channel_id=1, source_target_pairs={{0,4},{4,0},{8,12},{12,8},{16,20},{20,16},{24,28},{28,24},{1,5},{5... | collective-permute-start | bytes 786440 | tf_op jit(solution)/shard_map/ppermute | solution.py:174
  33.1 22.7 %collective-permute-start.21 = (bf16[1024,512]{1,0:T(8,128)(2,1)S(1)}, bf16[1024,512]{1,0:T(8,128)(2,1)S(1)}, u32[]{:S(2)}, u32[]{:S(2)}) collective-permute-start(bf16[1024,512]{1,0:T(8,128)(2,1)S(1)} %copy-done.5), channel_id=1, source_target_pairs={{0,24},{4,28},{8,16},{12,20},{16,8},{20,12},{24,0},{28,4},{1,25},{... | collective-permute-start | bytes 3145736 | tf_op jit(solution)/shard_map/ppermute | solution.py:174
  46.9 14.4 %collective-permute-start.23 = (bf16[64,1024]{1,0:T(8,128)(2,1)S(1)}, bf16[64,1024]{1,0:T(8,128)(2,1)S(1)}, u32[]{:S(2)}, u32[]{:S(2)}) collective-permute-start(bf16[64,1024]{1,0:T(8,128)(2,1)S(1)} %get-tuple-element.84), channel_id=1, source_target_pairs={{4,0},{8,4},{12,8},{16,12},{20,16},{24,20},{28,24},{5,1},{9,5},{13... | collective-permute-start | bytes 393224 | tf_op jit(solution)/shard_map/ppermute | solution.py:22
  49.2 12.2 %collective-permute-start.22 = (bf16[64,1024]{1,0:T(8,128)(2,1)S(1)}, bf16[64,1024]{1,0:T(8,128)(2,1)S(1)}, u32[]{:S(2)}, u32[]{:S(2)}) collective-permute-start(bf16[64,1024]{1,0:T(8,128)(2,1)S(1)} %get-tuple-element.83), channel_id=1, source_target_pairs={{0,4},{4,8},{8,12},{12,16},{16,20},{20,24},{24,28},{1,5},{5,9},{9,... | collective-permute-start | bytes 393224 | tf_op jit(solution)/shard_map/ppermute | solution.py:22
  64.2 13.2 %collective-permute-start.27 = (bf16[128,1024]{1,0:T(8,128)(2,1)S(1)}, bf16[128,1024]{1,0:T(8,128)(2,1)S(1)}, u32[]{:S(2)}, u32[]{:S(2)}) collective-permute-start(bf16[128,1024]{1,0:T(8,128)(2,1)S(1)} %maximum_add_fusion.refs_0_), channel_id=1, source_target_pairs={{0,16},{4,20},{8,24},{12,28},{16,0},{20,4},{24,8},{28,12},{1,17},{... | collective-permute-start | bytes 786440 | tf_op jit(solution)/shard_map/ppermute | solution.py:174
  64.2 13.6 %collective-permute-start.29 = (bf16[128,1024]{1,0:T(8,128)(2,1)S(1)}, bf16[128,1024]{1,0:T(8,128)(2,1)S(1)}, u32[]{:S(2)}, u32[]{:S(2)}) collective-permute-start(bf16[128,1024]{1,0:T(8,128)(2,1)S(1)} %maximum_add_fusion.refs_0_), channel_id=1, source_target_pairs={{0,24},{4,28},{8,16},{12,20},{16,8},{20,12},{24,0},{28,4},{1,25},{... | collective-permute-start | bytes 786440 | tf_op jit(solution)/shard_map/ppermute | solution.py:174
  65.5 12.9 %collective-permute-start.24 = (bf16[128,1024]{1,0:T(8,128)(2,1)S(1)}, bf16[128,1024]{1,0:T(8,128)(2,1)S(1)}, u32[]{:S(2)}, u32[]{:S(2)}) collective-permute-start(bf16[128,1024]{1,0:T(8,128)(2,1)S(1)} %maximum_add_fusion.refs_0_), channel_id=1, source_target_pairs={{0,4},{4,0},{8,12},{12,8},{16,20},{20,16},{24,28},{28,24},{1,5},{5... | collective-permute-start | bytes 786440 | tf_op jit(solution)/shard_map/ppermute | solution.py:174
  80.7 24.4 %collective-permute-start.34 = (bf16[1024,512]{1,0:T(8,128)(2,1)S(1)}, bf16[1024,512]{1,0:T(8,128)(2,1)S(1)}, u32[]{:S(2)}, u32[]{:S(2)}) collective-permute-start(bf16[1024,512]{1,0:T(8,128)(2,1)S(1)} %copy-done.5), channel_id=1, source_target_pairs={{0,8},{4,12},{8,0},{12,4},{16,24},{20,28},{24,16},{28,20},{1,9},{5... | collective-permute-start | bytes 3145736 | tf_op jit(solution)/shard_map/ppermute | solution.py:174
  80.8 24.4 %collective-permute-start.35 = (bf16[1024,512]{1,0:T(8,128)(2,1)S(1)}, bf16[1024,512]{1,0:T(8,128)(2,1)S(1)}, u32[]{:S(2)}, u32[]{:S(2)}) collective-permute-start(bf16[1024,512]{1,0:T(8,128)(2,1)S(1)} %copy-done.5), channel_id=1, source_target_pairs={{0,16},{4,20},{8,24},{12,28},{16,0},{20,4},{24,8},{28,12},{1,17},{... | collective-permute-start | bytes 3145736 | tf_op jit(solution)/shard_map/ppermute | solution.py:174
  81.3 23.9 %collective-permute-start.38 = (bf16[256,512]{1,0:T(8,128)(2,1)S(1)}, bf16[256,512]{1,0:T(8,128)(2,1)S(1)}, u32[]{:S(2)}, u32[]{:S(2)}) collective-permute-start(bf16[256,512]{1,0:T(8,128)(2,1)S(1)} %get-tuple-element.104), channel_id=1, source_target_pairs={{0,3},{1,2},{2,1},{3,0},{4,7},{5,6},{6,5},{7,4},{8,11},{9,10},{10,... | collective-permute-start | bytes 786440 | tf_op jit(solution)/shard_map/ppermute | solution.py:174
  82.6 22.6 %collective-permute-start.37 = (bf16[256,512]{1,0:T(8,128)(2,1)S(1)}, bf16[256,512]{1,0:T(8,128)(2,1)S(1)}, u32[]{:S(2)}, u32[]{:S(2)}) collective-permute-start(bf16[256,512]{1,0:T(8,128)(2,1)S(1)} %get-tuple-element.103), channel_id=1, source_target_pairs={{0,2},{1,3},{2,0},{3,1},{4,6},{5,7},{6,4},{7,5},{8,10},{9,11},{10,... | collective-permute-start | bytes 786440 | tf_op jit(solution)/shard_map/ppermute | solution.py:174
  84.7 20.6 %collective-permute-start.36 = (bf16[256,512]{1,0:T(8,128)(2,1)S(1)}, bf16[256,512]{1,0:T(8,128)(2,1)S(1)}, u32[]{:S(2)}, u32[]{:S(2)}) collective-permute-start(bf16[256,512]{1,0:T(8,128)(2,1)S(1)} %get-tuple-element.102), channel_id=1, source_target_pairs={{0,1},{1,0},{2,3},{3,2},{4,5},{5,4},{6,7},{7,6},{8,9},{9,8},{10,11... | collective-permute-start | bytes 786440 | tf_op jit(solution)/shard_map/ppermute | solution.py:174
  106.7 12.7 %collective-permute-start.43 = (bf16[256,512]{1,0:T(8,128)(2,1)S(1)}, bf16[256,512]{1,0:T(8,128)(2,1)S(1)}, u32[]{:S(2)}, u32[]{:S(2)}) collective-permute-start(bf16[256,512]{1,0:T(8,128)(2,1)S(1)} %add_convert_fusion.refs_0_), channel_id=1, source_target_pairs={{0,1},{1,0},{2,3},{3,2},{4,5},{5,4},{6,7},{7,6},{8,9},{9,8},{10,11... | collective-permute-start | bytes 786440 | tf_op jit(solution)/shard_map/ppermute | solution.py:174
  108.3 15.6 %collective-permute-start.45 = (bf16[256,512]{1,0:T(8,128)(2,1)S(1)}, bf16[256,512]{1,0:T(8,128)(2,1)S(1)}, u32[]{:S(2)}, u32[]{:S(2)}) collective-permute-start(bf16[256,512]{1,0:T(8,128)(2,1)S(1)} %add_convert_fusion.refs_0_), channel_id=1, source_target_pairs={{0,2},{1,3},{2,0},{3,1},{4,6},{5,7},{6,4},{7,5},{8,10},{9,11},{10,... | collective-permute-start | bytes 786440 | tf_op jit(solution)/shard_map/ppermute | solution.py:174
  124.0 13.1 %collective-permute-start.50 = (bf16[256,512]{1,0:T(8,128)(2,1)S(1)}, bf16[256,512]{1,0:T(8,128)(2,1)S(1)}, u32[]{:S(2)}, u32[]{:S(2)}) collective-permute-start(bf16[256,512]{1,0:T(8,128)(2,1)S(1)} %add_convert_fusion.refs_0_), channel_id=1, source_target_pairs={{0,3},{1,2},{2,1},{3,0},{4,7},{5,6},{6,5},{7,4},{8,11},{9,10},{10,... | collective-permute-start | bytes 786440 | tf_op jit(solution)/shard_map/ppermute | solution.py:174
  127.8 14.3 %collective-permute-start.47 = (bf16[528,384]{1,0:T(8,128)(2,1)S(1)}, bf16[528,384]{1,0:T(8,128)(2,1)S(1)}, u32[]{:S(2)}, u32[]{:S(2)}) collective-permute-start(bf16[528,384]{1,0:T(8,128)(2,1)S(1)} %get-tuple-element.116), channel_id=1, source_target_pairs={{0,8},{4,12},{8,0},{12,4},{16,24},{20,28},{24,16},{28,20},{1,9},{5... | collective-permute-start | bytes 1216520 | tf_op jit(solution)/shard_map/ppermute | solution.py:174
  128.8 13.3 %collective-permute-start.48 = (bf16[528,384]{1,0:T(8,128)(2,1)S(1)}, bf16[528,384]{1,0:T(8,128)(2,1)S(1)}, u32[]{:S(2)}, u32[]{:S(2)}) collective-permute-start(bf16[528,384]{1,0:T(8,128)(2,1)S(1)} %get-tuple-element.117), channel_id=1, source_target_pairs={{0,16},{4,20},{8,24},{12,28},{16,0},{20,4},{24,8},{28,12},{1,17},{... | collective-permute-start | bytes 1216520 | tf_op jit(solution)/shard_map/ppermute | solution.py:174
  129.1 19.0 %collective-permute-start.49 = (bf16[528,384]{1,0:T(8,128)(2,1)S(1)}, bf16[528,384]{1,0:T(8,128)(2,1)S(1)}, u32[]{:S(2)}, u32[]{:S(2)}) collective-permute-start(bf16[528,384]{1,0:T(8,128)(2,1)S(1)} %get-tuple-element.118), channel_id=1, source_target_pairs={{0,24},{4,28},{8,16},{12,20},{16,8},{20,12},{24,0},{28,4},{1,25},{... | collective-permute-start | bytes 1216520 | tf_op jit(solution)/shard_map/ppermute | solution.py:174
  140.8 12.0 %collective-permute-start.52 = (bf16[272,384]{1,0:T(8,128)(2,1)S(1)}, bf16[272,384]{1,0:T(8,128)(2,1)S(1)}, u32[]{:S(2)}, u32[]{:S(2)}) collective-permute-start(bf16[272,384]{1,0:T(8,128)(2,1)S(1)} %get-tuple-element.122), channel_id=1, source_target_pairs={{0,8},{4,12},{8,0},{12,4},{16,24},{20,28},{24,16},{28,20},{1,9},{5... | collective-permute-start | bytes 626696 | tf_op jit(solution)/shard_map/ppermute | solution.py:174
  141.7 12.2 %collective-permute-start.53 = (bf16[272,384]{1,0:T(8,128)(2,1)S(1)}, bf16[272,384]{1,0:T(8,128)(2,1)S(1)}, u32[]{:S(2)}, u32[]{:S(2)}) collective-permute-start(bf16[272,384]{1,0:T(8,128)(2,1)S(1)} %get-tuple-element.123), channel_id=1, source_target_pairs={{0,16},{4,20},{8,24},{12,28},{16,0},{20,4},{24,8},{28,12},{1,17},{... | collective-permute-start | bytes 626696 | tf_op jit(solution)/shard_map/ppermute | solution.py:174
  149.0 28.4 %collective-permute-start.55 = (bf16[256,512]{1,0:T(8,128)(2,1)S(1)}, bf16[256,512]{1,0:T(8,128)(2,1)S(1)}, u32[]{:S(2)}, u32[]{:S(2)}) collective-permute-start(bf16[256,512]{1,0:T(8,128)(2,1)S(1)} %add_convert_fusion.refs_0_), channel_id=1, source_target_pairs={{0,0},{1,8},{2,16},{3,24},{4,4},{5,12},{6,20},{7,28},{8,1},{9,9},{... | collective-permute-start | bytes 786440 | tf_op jit(solution)/shard_map/ppermute | solution.py:609
  159.1 14.6 %collective-permute-start.57 = (bf16[256,128]{1,0:T(8,128)(2,1)S(1)}, bf16[256,128]{1,0:T(8,128)(2,1)S(1)}, u32[]{:S(2)}, u32[]{:S(2)}) collective-permute-start(bf16[256,128]{1,0:T(8,128)(2,1)S(1)} %get-tuple-element.129), channel_id=1, source_target_pairs={{0,8},{4,12},{8,0},{12,4},{16,24},{20,28},{24,16},{28,20},{1,9},{5... | collective-permute-start | bytes 196616 | tf_op jit(solution)/shard_map/ppermute | solution.py:174
  180.7 12.9 %collective-permute-start.64 = (bf16[256,512]{1,0:T(8,128)(2,1)S(1)}, bf16[256,512]{1,0:T(8,128)(2,1)S(1)}, u32[]{:S(2)}, u32[]{:S(2)}) collective-permute-start(bf16[256,512]{1,0:T(8,128)(2,1)S(1)} %get-tuple-element.139), channel_id=1, source_target_pairs={{0,2},{1,3},{2,0},{3,1},{4,6},{5,7},{6,4},{7,5},{8,10},{9,11},{10,... | collective-permute-start | bytes 786440 | tf_op jit(solution)/shard_map/ppermute | solution.py:174
  182.0 24.1 %collective-permute-start.65 = (bf16[256,512]{1,0:T(8,128)(2,1)S(1)}, bf16[256,512]{1,0:T(8,128)(2,1)S(1)}, u32[]{:S(2)}, u32[]{:S(2)}) collective-permute-start(bf16[256,512]{1,0:T(8,128)(2,1)S(1)} %get-tuple-element.140), channel_id=1, source_target_pairs={{0,3},{1,2},{2,1},{3,0},{4,7},{5,6},{6,5},{7,4},{8,11},{9,10},{10,... | collective-permute-start | bytes 786440 | tf_op jit(solution)/shard_map/ppermute | solution.py:174
  (46 other events, 413.7 us)

commit v10 on v9

--- a/solution.py
+++ b/solution.py
@@ -438,10 +438,10 @@
         out[...] = attended[aligned(chip ^ d, out.shape[0]), :]
 
 
-def final_kernel(own, *refs):
+def final_kernel(own, latent, *refs):
     received, outs, whole = refs[:-3], refs[-3:-1], refs[-1]
-    _, core, _ = place()
-    total = own[...]
+    chip, core, tensor = place()
+    total = own[...] + jnp.where(chip == tensor, latent[...].astype(jnp.float32), 0.0)
     for block in received:
         total += block[...].astype(jnp.float32)
     whole[...] = total
@@ -572,12 +572,13 @@
     gain = norm_gain[None, :]
     groups = [[0], list(range(1, min(3, tensor_count))), list(range(3, tensor_count))]
     groups = [group for group in groups if group]
-    shares, arrived = [], []
+    shares, arrived, latent_blocks = [], [], [latent_in]
     for g, group in enumerate(groups):
         blocks = [latent_in]
         if g:
             start = after(latent_in, *arrived, *shares[:chip_count]) if g > 1 else latent_in
             arrived = [exchanged(start, "tensor", r) for r in group]
+            latent_blocks += arrived
             blocks = [after(block, *shares[:chip_count]) for block in arrived]
         height = len(group) * quarter
         share, *sent = call(
@@ -601,18 +602,10 @@
         flops=2 * patch_count * patch_count * HEAD_DIM,
     )
 
-    route = [
-        (s * tensor_count + t, (2 * t + s % 2) * tensor_count + s // 2)
-        for s in range(seq_count)
-        for t in range(tensor_count)
-    ]
-    residual = lax.ppermute(after(latent_in, *arrived), ("seq", "tensor"), route)
-
     pieces = []
     for d, block in enumerate(attended):
         moved = exchanged(block, "seq", 2 * d) if d else block
         pieces += [moved, core_swapped(moved)]
-    pieces[0], residual = lax.optimization_barrier((pieces[0], residual))
     total, *sent = call(
         functools.partial(latent_out_kernel, seq_count),
         [((quarter, out_width), bf16 if r else f32) for r in range(tensor_count)],
@@ -627,12 +620,23 @@
         ],
         flops=2 * quarter * local_width * out_width * chip_count,
     )
+    received = [exchanged(block, "tensor", r) for r, block in enumerate(sent, 1)]
+
+    residual = [latent_in]
+    for d in range(1, chip_count):
+        route = [
+            ((2 * t + k) * tensor_count + t, (2 * (t ^ d) + k) * tensor_count + t)
+            for t in range(tensor_count)
+            for k in range(2)
+        ]
+        block = after(latent_blocks[d], *(received[:1] if d == chip_count - 1 else [total]))
+        residual.append(lax.ppermute(block, ("seq", "tensor"), route))
     same, crossed = call(
         final_kernel,
         [((patch_dev, out_width), bf16)] * 2,
         total,
-        residual,
-        *[exchanged(block, "tensor", r) for r, block in enumerate(sent, 1)],
+        *residual,
+        *received,
         scratch=[pltpu.VMEM((quarter, out_width), f32)],
     )
     crossed = core_swapped(crossed)

time: 210 us -> 204 us (0.971)
  starting transfers between devices: 84.6 us -> 76 us
  waiting for transfers between devices: 98.4 us -> 101 us
    ppermute x64, starting transfers between devices: 75 us -> 67.7 us  [exchanged(): return lax.ppermute(block, axis, route)]
  transfers between devices with their start and end apart: 67 -> 69, of which waited for: 30 -> 31; matrix products, arithmetic and copies ran while one was open for 1% -> 1% of each run, Pallas kernels for 9% -> 8%
where the time goes in v10:
time: 204 us
  waiting for transfers between devices  101 us (50%)
  starting transfers between devices  76 us (37%)
  Pallas kernels  21.4 us (10%)
  local copies, waits for them, and re-layouts  3.48 us (2%)
    ppermute x64, waiting for transfers between devices, exchanged(): return lax.ppermute(block, axis, route)  93.2 us
    ppermute x64, starting transfers between devices, exchanged(): return lax.ppermute(block, axis, route)  67.7 us
    pallas_call x10, Pallas kernels, call(): pl.pallas_call(kernel, out_shape=shapes, in_specs=[pl.BlockSpec(memory_sp...  21.4 us
    ppermute x2, starting transfers between devices, shifted(): return lax.ppermute(block, axis, route)  5.74 us
    ppermute x2, waiting for transfers between devices, shifted(): return lax.ppermute(block, axis, route)  5.53 us
  transfers between devices with their start and end apart: 69, of which 31 were waited for; matrix products, arithmetic and copies ran while one was open for 1% of the time, Pallas kernels for 8%

profile of v10, /device:TPU:9, one launch (start us, length us, event | category | flops | bytes accessed | tf_op | source)
XLA Modules:
  0.0 203.6 jit_solution(4822042504448472878)
XLA Ops:
  5.4 2.0 collective-permute-done.1.refs_2_
  8.6 7.4 %collective-permute-start.2 = (bf16[128,1024]{1,0:T(8,128)(2,1)S(1)}, bf16[128,1024]{1,0:T(8,128)(2,1)S(1)}, u32[]{:S(2)}, u32[]{:S(2)}) collective-permute-start(bf16[128,1024]{1,0:T(8,128)(2,1)S(1)} %collective-permute-done.1.refs_2_), channel_id=1, source_target_pairs={{0,4},{4,0},{8,12},{12,8},{16,20},{20,16},{24,28},{28,24},{1,5},{5... | collective-permute-start | bytes 786440 | tf_op jit(solution)/shard_map/ppermute | solution.py:174
  24.6 3.2 %collective-permute-start.7 = (bf16[128,1024]{1,0:T(8,128)(2,1)}, bf16[128,1024]{1,0:T(8,128)(2,1)S(1)}, u32[]{:S(2)}, u32[]{:S(2)}) collective-permute-start(bf16[128,1024]{1,0:T(8,128)(2,1)} %refs_0_.3), channel_id=1, source_target_pairs={{0,4},{4,0},{8,12},{12,8},{16,20},{20,16},{24,28},{28,24},{1,5},{5... | collective-permute-start | bytes 786440 | tf_op jit(solution)/shard_map/ppermute | solution.py:174
  30.4 2.0 shard_map.118.query
  33.1 1.8 collective-permute-start.21
  34.9 2.4 %collective-permute-start.13 = (bf16[128,1024]{1,0:T(8,128)(2,1)S(1)}, bf16[128,1024]{1,0:T(8,128)(2,1)S(1)}, u32[]{:S(2)}, u32[]{:S(2)}) collective-permute-start(bf16[128,1024]{1,0:T(8,128)(2,1)S(1)} %collective-permute-done.12.refs_6_), channel_id=1, source_target_pairs={{0,4},{4,0},{8,12},{12,8},{16,20},{20,16},{24,28},{28,24},{1,5},{5... | collective-permute-start | bytes 786440 | tf_op jit(solution)/shard_map/ppermute | solution.py:174
  39.6 7.3 %shard_map.119 = (bf16[128,1024]{1,0:T(8,128)(2,1)S(1)}, bf16[64,1024]{1,0:T(8,128)(2,1)S(1)}, bf16[64,1024]{1,0:T(8,128)(2,1)S(1)}) custom-call(s32[1,1024]{1,0:T(1,128)S(1)} %bitcast.7, bf16[256,1024]{1,0:T(8,128)(2,1)S(1)} %shard_map.118.query, bf16[1024,1024]{1,0:T(8,128)(2,1)S(1)} %copy-done.1, bf16[128,1024]{1,0:T(8,128)(2,1)S(1)} %copy-done.9, ...), custom_call_target="tpu_custom_call" | custom-call | flops 5368709120 | bytes 7344128 | tf_op jit(solution)/shard_map/pallas_call | solution.py:207
  46.9 2.3 %collective-permute-start.23 = (bf16[64,1024]{1,0:T(8,128)(2,1)S(1)}, bf16[64,1024]{1,0:T(8,128)(2,1)S(1)}, u32[]{:S(2)}, u32[]{:S(2)}) collective-permute-start(bf16[64,1024]{1,0:T(8,128)(2,1)S(1)} %get-tuple-element.84), channel_id=1, source_target_pairs={{4,0},{8,4},{12,8},{16,12},{20,16},{24,20},{28,24},{5,1},{9,5},{13... | collective-permute-start | bytes 393224 | tf_op jit(solution)/shard_map/ppermute | solution.py:22
  49.2 3.5 %collective-permute-start.22 = (bf16[64,1024]{1,0:T(8,128)(2,1)S(1)}, bf16[64,1024]{1,0:T(8,128)(2,1)S(1)}, u32[]{:S(2)}, u32[]{:S(2)}) collective-permute-start(bf16[64,1024]{1,0:T(8,128)(2,1)S(1)} %get-tuple-element.83), channel_id=1, source_target_pairs={{0,4},{4,8},{8,12},{12,16},{16,20},{20,24},{24,28},{1,5},{5,9},{9,... | collective-permute-start | bytes 393224 | tf_op jit(solution)/shard_map/ppermute | solution.py:22
  52.7 3.2 %collective-permute-done.21.refs_11_ = bf16[1024,512]{1,0:T(8,128)(2,1)S(1)} collective-permute-done((bf16[1024,512]{1,0:T(8,128)(2,1)S(1)}, bf16[1024,512]{1,0:T(8,128)(2,1)S(1)}, u32[]{:S(2)}, u32[]{:S(2)}) %collective-permute-start.21) | collective-permute-done | bytes 1048608 | tf_op jit(solution)/shard_map/ppermute | solution.py:174
  55.8 5.5 %collective-permute-done.23 = bf16[64,1024]{1,0:T(8,128)(2,1)S(1)} collective-permute-done((bf16[64,1024]{1,0:T(8,128)(2,1)S(1)}, bf16[64,1024]{1,0:T(8,128)(2,1)S(1)}, u32[]{:S(2)}, u32[]{:S(2)}) %collective-permute-start.23) | collective-permute-done | bytes 131104 | tf_op jit(solution)/shard_map/ppermute | solution.py:22
  61.4 2.8 %collective-permute-start.25 = (bf16[128,1024]{1,0:T(8,128)(2,1)S(1)}, bf16[128,1024]{1,0:T(8,128)(2,1)S(1)}, u32[]{:S(2)}, u32[]{:S(2)}) collective-permute-start(bf16[128,1024]{1,0:T(8,128)(2,1)S(1)} %maximum_add_fusion.refs_0_), channel_id=1, source_target_pairs={{0,8},{4,12},{8,0},{12,4},{16,24},{20,28},{24,16},{28,20},{1,9},{5... | collective-permute-start | bytes 786440 | tf_op jit(solution)/shard_map/ppermute | solution.py:174
  65.5 5.6 %collective-permute-done.25.refs_2_ = bf16[128,1024]{1,0:T(8,128)(2,1)S(1)} collective-permute-done((bf16[128,1024]{1,0:T(8,128)(2,1)S(1)}, bf16[128,1024]{1,0:T(8,128)(2,1)S(1)}, u32[]{:S(2)}, u32[]{:S(2)}) %collective-permute-start.25) | collective-permute-done | bytes 262176 | tf_op jit(solution)/shard_map/ppermute | solution.py:174
  71.1 6.4 %collective-permute-done.27.refs_4_ = bf16[128,1024]{1,0:T(8,128)(2,1)S(1)} collective-permute-done((bf16[128,1024]{1,0:T(8,128)(2,1)S(1)}, bf16[128,1024]{1,0:T(8,128)(2,1)S(1)}, u32[]{:S(2)}, u32[]{:S(2)}) %collective-permute-start.27) | collective-permute-done | bytes 262176 | tf_op jit(solution)/shard_map/ppermute | solution.py:174
  82.6 2.0 collective-permute-start.37
  86.0 19.1 %collective-permute-done.34.refs_9_ = bf16[1024,512]{1,0:T(8,128)(2,1)S(1)} collective-permute-done((bf16[1024,512]{1,0:T(8,128)(2,1)S(1)}, bf16[1024,512]{1,0:T(8,128)(2,1)S(1)}, u32[]{:S(2)}, u32[]{:S(2)}) %collective-permute-start.34) | collective-permute-done | bytes 1048608 | tf_op jit(solution)/shard_map/ppermute | solution.py:174
  113.3 6.1 %collective-permute-done.43.refs_0_ = bf16[256,512]{1,0:T(8,128)(2,1)S(1)} collective-permute-done((bf16[256,512]{1,0:T(8,128)(2,1)S(1)}, bf16[256,512]{1,0:T(8,128)(2,1)S(1)}, u32[]{:S(2)}, u32[]{:S(2)}) %collective-permute-start.43) | collective-permute-done | bytes 262176 | tf_op jit(solution)/shard_map/ppermute | solution.py:174
  119.4 2.8 %collective-permute-done.42.refs_3_ = bf16[272,384]{1,0:T(8,128)(2,1)S(1)} collective-permute-done((bf16[272,384]{1,0:T(8,128)(2,1)S(1)}, bf16[272,384]{1,0:T(8,128)(2,1)S(1)}, u32[]{:S(2)}, u32[]{:S(2)}) %collective-permute-start.42) | collective-permute-done | bytes 208928 | tf_op jit(solution)/shard_map/ppermute | solution.py:174
  125.5 2.3 %shard_map.123 = (f32[520,384]{1,0:T(8,128)S(1)}, bf16[528,384]{1,0:T(8,128)(2,1)S(1)}, bf16[528,384]{1,0:T(8,128)(2,1)S(1)}, bf16[528,384]{1,0:T(8,128)(2,1)S(1)}) custom-call(f32[1,4096]{1,0:T(1,128)S(1)} %bitcast.4, bf16[256,512]{1,0:T(8,128)(2,1)S(1)} %collective-permute-done.43.refs_0_, bf16[256,512]{1,0:T(8,128)(2,1)S(1)} %collective-permute-done.44.refs_1_, ...), custom_call_target="tpu_custom_call" | custom-call | flops 1610612736 | bytes 6225920 | tf_op jit(solution)/shard_map/pallas_call | solution.py:207
  130.6 6.5 %collective-permute-done.50.refs_0_ = bf16[256,512]{1,0:T(8,128)(2,1)S(1)} collective-permute-done((bf16[256,512]{1,0:T(8,128)(2,1)S(1)}, bf16[256,512]{1,0:T(8,128)(2,1)S(1)}, u32[]{:S(2)}, u32[]{:S(2)}) %collective-permute-start.50) | collective-permute-done | bytes 262176 | tf_op jit(solution)/shard_map/ppermute | solution.py:174
  142.1 6.0 %collective-permute-done.49.refs_7_ = bf16[528,384]{1,0:T(8,128)(2,1)S(1)} collective-permute-done((bf16[528,384]{1,0:T(8,128)(2,1)S(1)}, bf16[528,384]{1,0:T(8,128)(2,1)S(1)}, u32[]{:S(2)}, u32[]{:S(2)}) %collective-permute-start.49) | collective-permute-done | bytes 405536 | tf_op jit(solution)/shard_map/ppermute | solution.py:174
  149.0 2.7 %collective-permute-done.52.refs_9_ = bf16[272,384]{1,0:T(8,128)(2,1)S(1)} collective-permute-done((bf16[272,384]{1,0:T(8,128)(2,1)S(1)}, bf16[272,384]{1,0:T(8,128)(2,1)S(1)}, u32[]{:S(2)}, u32[]{:S(2)}) %collective-permute-start.52) | collective-permute-done | bytes 208928 | tf_op jit(solution)/shard_map/ppermute | solution.py:174
  151.7 2.2 %collective-permute-done.53.refs_10_ = bf16[272,384]{1,0:T(8,128)(2,1)S(1)} collective-permute-done((bf16[272,384]{1,0:T(8,128)(2,1)S(1)}, bf16[272,384]{1,0:T(8,128)(2,1)S(1)}, u32[]{:S(2)}, u32[]{:S(2)}) %collective-permute-start.53) | collective-permute-done | bytes 208928 | tf_op jit(solution)/shard_map/ppermute | solution.py:174
  153.9 3.2 %collective-permute-done.54.refs_11_ = bf16[272,384]{1,0:T(8,128)(2,1)S(1)} collective-permute-done((bf16[272,384]{1,0:T(8,128)(2,1)S(1)}, bf16[272,384]{1,0:T(8,128)(2,1)S(1)}, u32[]{:S(2)}, u32[]{:S(2)}) %collective-permute-start.54) | collective-permute-done | bytes 208928 | tf_op jit(solution)/shard_map/ppermute | solution.py:174
  157.1 2.0 shard_map.125
  161.8 2.0 %collective-permute-start.55 = (bf16[256,128]{1,0:T(8,128)(2,1)S(1)}, bf16[256,128]{1,0:T(8,128)(2,1)S(1)}, u32[]{:S(2)}, u32[]{:S(2)}) collective-permute-start(bf16[256,128]{1,0:T(8,128)(2,1)S(1)} %get-tuple-element.126.refs_0_), channel_id=1, source_target_pairs={{0,4},{4,0},{8,12},{12,8},{16,20},{20,16},{24,28},{28,24},{1,5},{5... | collective-permute-start | bytes 196616 | tf_op jit(solution)/shard_map/ppermute | solution.py:174
  168.7 2.3 %shard_map.126 = (f32[256,512]{1,0:T(8,128)S(1)}, bf16[256,512]{1,0:T(8,128)(2,1)S(1)}, bf16[256,512]{1,0:T(8,128)(2,1)S(1)}, bf16[256,512]{1,0:T(8,128)(2,1)S(1)}) custom-call(bf16[256,128]{1,0:T(8,128)(2,1)S(1)} %get-tuple-element.126.refs_0_, bf16[256,128]{1,0:T(8,128)(2,1)S(1)} %collective-permute-done.55.refs_1_, ...), custom_call_target="tpu_custom_call" | custom-call | flops 1073741824 | bytes 6029312 | tf_op jit(solution)/shard_map/pallas_call | solution.py:207
  174.7 2.5 %collective-permute-start.67 = (bf16[256,512]{1,0:T(8,128)(2,1)S(1)}, bf16[256,512]{1,0:T(8,128)(2,1)S(1)}, u32[]{:S(2)}, u32[]{:S(2)}) collective-permute-start(bf16[256,512]{1,0:T(8,128)(2,1)S(1)} %get-tuple-element.140), channel_id=1, source_target_pairs={{0,3},{1,2},{2,1},{3,0},{4,7},{5,6},{6,5},{7,4},{8,11},{9,10},{10,... | collective-permute-start | bytes 786440 | tf_op jit(solution)/shard_map/ppermute | solution.py:174
  177.2 1.9 collective-permute-done.64.refs_3_
  179.7 1.9 collective-permute-done.62.refs_0_
  181.7 9.6 %collective-permute-done.66.refs_4_ = bf16[256,512]{1,0:T(8,128)(2,1)S(1)} collective-permute-done((bf16[256,512]{1,0:T(8,128)(2,1)S(1)}, bf16[256,512]{1,0:T(8,128)(2,1)S(1)}, u32[]{:S(2)}, u32[]{:S(2)}) %collective-permute-start.66) | collective-permute-done | bytes 262176 | tf_op jit(solution)/shard_map/ppermute | solution.py:174
  191.3 8.4 %collective-permute-done.67.refs_5_ = bf16[256,512]{1,0:T(8,128)(2,1)S(1)} collective-permute-done((bf16[256,512]{1,0:T(8,128)(2,1)S(1)}, bf16[256,512]{1,0:T(8,128)(2,1)S(1)}, u32[]{:S(2)}, u32[]{:S(2)}) %collective-permute-start.67) | collective-permute-done | bytes 262176 | tf_op jit(solution)/shard_map/ppermute | solution.py:174
  (147 shorter events, 64.4 us)
Async XLA Ops:
  2.5 13.6 %collective-permute-start.5 = (bf16[128,1024]{1,0:T(8,128)(2,1)}, bf16[128,1024]{1,0:T(8,128)(2,1)S(1)}, u32[]{:S(2)}, u32[]{:S(2)}) collective-permute-start(bf16[128,1024]{1,0:T(8,128)(2,1)} %refs_0_.2), channel_id=1, source_target_pairs={{0,24},{4,28},{8,16},{12,20},{16,8},{20,12},{24,0},{28,4},{1,25},{... | collective-permute-start | bytes 786440 | tf_op jit(solution)/shard_map/ppermute | solution.py:174
  2.6 14.1 %collective-permute-start = (bf16[128,1024]{1,0:T(8,128)(2,1)}, bf16[128,1024]{1,0:T(8,128)(2,1)S(1)}, u32[]{:S(2)}, u32[]{:S(2)}) collective-permute-start(bf16[128,1024]{1,0:T(8,128)(2,1)} %refs_0_.2), channel_id=1, source_target_pairs={{0,4},{4,0},{8,12},{12,8},{16,20},{20,16},{24,28},{28,24},{1,5},{5... | collective-permute-start | bytes 786440 | tf_op jit(solution)/shard_map/ppermute | solution.py:174
  4.2 14.5 %collective-permute-start.8 = (bf16[128,1024]{1,0:T(8,128)(2,1)}, bf16[128,1024]{1,0:T(8,128)(2,1)S(1)}, u32[]{:S(2)}, u32[]{:S(2)}) collective-permute-start(bf16[128,1024]{1,0:T(8,128)(2,1)} %refs_0_.3), channel_id=1, source_target_pairs={{0,8},{4,12},{8,0},{12,4},{16,24},{20,28},{24,16},{28,20},{1,9},{5... | collective-permute-start | bytes 786440 | tf_op jit(solution)/shard_map/ppermute | solution.py:174
  7.4 13.2 %collective-permute-start.17 = (bf16[128,1024]{1,0:T(8,128)(2,1)}, bf16[128,1024]{1,0:T(8,128)(2,1)S(1)}, u32[]{:S(2)}, u32[]{:S(2)}) collective-permute-start(bf16[128,1024]{1,0:T(8,128)(2,1)} %refs_8_.1), channel_id=1, source_target_pairs={{0,16},{4,20},{8,24},{12,28},{16,0},{20,4},{24,8},{28,12},{1,17},{... | collective-permute-start | bytes 786440 | tf_op jit(solution)/shard_map/ppermute | solution.py:174
  8.6 12.8 %collective-permute-start.2 = (bf16[128,1024]{1,0:T(8,128)(2,1)S(1)}, bf16[128,1024]{1,0:T(8,128)(2,1)S(1)}, u32[]{:S(2)}, u32[]{:S(2)}) collective-permute-start(bf16[128,1024]{1,0:T(8,128)(2,1)S(1)} %collective-permute-done.1.refs_2_), channel_id=1, source_target_pairs={{0,4},{4,0},{8,12},{12,8},{16,20},{20,16},{24,28},{28,24},{1,5},{5... | collective-permute-start | bytes 786440 | tf_op jit(solution)/shard_map/ppermute | solution.py:174
  16.7 15.7 %collective-permute-start.10 = (bf16[128,1024]{1,0:T(8,128)(2,1)}, bf16[128,1024]{1,0:T(8,128)(2,1)S(1)}, u32[]{:S(2)}, u32[]{:S(2)}) collective-permute-start(bf16[128,1024]{1,0:T(8,128)(2,1)} %refs_0_.3), channel_id=1, source_target_pairs={{0,16},{4,20},{8,24},{12,28},{16,0},{20,4},{24,8},{28,12},{1,17},{... | collective-permute-start | bytes 786440 | tf_op jit(solution)/shard_map/ppermute | solution.py:174
  20.6 11.9 %collective-permute-start.12 = (bf16[128,1024]{1,0:T(8,128)(2,1)S(1)}, bf16[128,1024]{1,0:T(8,128)(2,1)S(1)}, u32[]{:S(2)}, u32[]{:S(2)}) collective-permute-start(bf16[128,1024]{1,0:T(8,128)(2,1)S(1)} %collective-permute-done.8.refs_2_), channel_id=1, source_target_pairs={{0,16},{4,20},{8,24},{12,28},{16,0},{20,4},{24,8},{28,12},{1,17},{... | collective-permute-start | bytes 786440 | tf_op jit(solution)/shard_map/ppermute | solution.py:174
  21.5 11.5 %collective-permute-start.19 = (bf16[128,1024]{1,0:T(8,128)(2,1)S(1)}, bf16[128,1024]{1,0:T(8,128)(2,1)S(1)}, u32[]{:S(2)}, u32[]{:S(2)}) collective-permute-start(bf16[128,1024]{1,0:T(8,128)(2,1)S(1)} %collective-permute-done.17.refs_12_), channel_id=1, source_target_pairs={{0,8},{4,12},{8,0},{12,4},{16,24},{20,28},{24,16},{28,20},{1,9},{5... | collective-permute-start | bytes 786440 | tf_op jit(solution)/shard_map/ppermute | solution.py:174
  24.6 10.3 %collective-permute-start.7 = (bf16[128,1024]{1,0:T(8,128)(2,1)}, bf16[128,1024]{1,0:T(8,128)(2,1)S(1)}, u32[]{:S(2)}, u32[]{:S(2)}) collective-permute-start(bf16[128,1024]{1,0:T(8,128)(2,1)} %refs_0_.3), channel_id=1, source_target_pairs={{0,4},{4,0},{8,12},{12,8},{16,20},{20,16},{24,28},{28,24},{1,5},{5... | collective-permute-start | bytes 786440 | tf_op jit(solution)/shard_map/ppermute | solution.py:174
  33.1 22.7 %collective-permute-start.21 = (bf16[1024,512]{1,0:T(8,128)(2,1)S(1)}, bf16[1024,512]{1,0:T(8,128)(2,1)S(1)}, u32[]{:S(2)}, u32[]{:S(2)}) collective-permute-start(bf16[1024,512]{1,0:T(8,128)(2,1)S(1)} %copy-done.5), channel_id=1, source_target_pairs={{0,24},{4,28},{8,16},{12,20},{16,8},{20,12},{24,0},{28,4},{1,25},{... | collective-permute-start | bytes 3145736 | tf_op jit(solution)/shard_map/ppermute | solution.py:174
  46.9 14.4 %collective-permute-start.23 = (bf16[64,1024]{1,0:T(8,128)(2,1)S(1)}, bf16[64,1024]{1,0:T(8,128)(2,1)S(1)}, u32[]{:S(2)}, u32[]{:S(2)}) collective-permute-start(bf16[64,1024]{1,0:T(8,128)(2,1)S(1)} %get-tuple-element.84), channel_id=1, source_target_pairs={{4,0},{8,4},{12,8},{16,12},{20,16},{24,20},{28,24},{5,1},{9,5},{13... | collective-permute-start | bytes 393224 | tf_op jit(solution)/shard_map/ppermute | solution.py:22
  49.2 12.2 %collective-permute-start.22 = (bf16[64,1024]{1,0:T(8,128)(2,1)S(1)}, bf16[64,1024]{1,0:T(8,128)(2,1)S(1)}, u32[]{:S(2)}, u32[]{:S(2)}) collective-permute-start(bf16[64,1024]{1,0:T(8,128)(2,1)S(1)} %get-tuple-element.83), channel_id=1, source_target_pairs={{0,4},{4,8},{8,12},{12,16},{16,20},{20,24},{24,28},{1,5},{5,9},{9,... | collective-permute-start | bytes 393224 | tf_op jit(solution)/shard_map/ppermute | solution.py:22
  61.4 9.6 %collective-permute-start.25 = (bf16[128,1024]{1,0:T(8,128)(2,1)S(1)}, bf16[128,1024]{1,0:T(8,128)(2,1)S(1)}, u32[]{:S(2)}, u32[]{:S(2)}) collective-permute-start(bf16[128,1024]{1,0:T(8,128)(2,1)S(1)} %maximum_add_fusion.refs_0_), channel_id=1, source_target_pairs={{0,8},{4,12},{8,0},{12,4},{16,24},{20,28},{24,16},{28,20},{1,9},{5... | collective-permute-start | bytes 786440 | tf_op jit(solution)/shard_map/ppermute | solution.py:174
  64.2 13.2 %collective-permute-start.27 = (bf16[128,1024]{1,0:T(8,128)(2,1)S(1)}, bf16[128,1024]{1,0:T(8,128)(2,1)S(1)}, u32[]{:S(2)}, u32[]{:S(2)}) collective-permute-start(bf16[128,1024]{1,0:T(8,128)(2,1)S(1)} %maximum_add_fusion.refs_0_), channel_id=1, source_target_pairs={{0,16},{4,20},{8,24},{12,28},{16,0},{20,4},{24,8},{28,12},{1,17},{... | collective-permute-start | bytes 786440 | tf_op jit(solution)/shard_map/ppermute | solution.py:174
  64.2 13.6 %collective-permute-start.29 = (bf16[128,1024]{1,0:T(8,128)(2,1)S(1)}, bf16[128,1024]{1,0:T(8,128)(2,1)S(1)}, u32[]{:S(2)}, u32[]{:S(2)}) collective-permute-start(bf16[128,1024]{1,0:T(8,128)(2,1)S(1)} %maximum_add_fusion.refs_0_), channel_id=1, source_target_pairs={{0,24},{4,28},{8,16},{12,20},{16,8},{20,12},{24,0},{28,4},{1,25},{... | collective-permute-start | bytes 786440 | tf_op jit(solution)/shard_map/ppermute | solution.py:174
  65.5 12.9 %collective-permute-start.24 = (bf16[128,1024]{1,0:T(8,128)(2,1)S(1)}, bf16[128,1024]{1,0:T(8,128)(2,1)S(1)}, u32[]{:S(2)}, u32[]{:S(2)}) collective-permute-start(bf16[128,1024]{1,0:T(8,128)(2,1)S(1)} %maximum_add_fusion.refs_0_), channel_id=1, source_target_pairs={{0,4},{4,0},{8,12},{12,8},{16,20},{20,16},{24,28},{28,24},{1,5},{5... | collective-permute-start | bytes 786440 | tf_op jit(solution)/shard_map/ppermute | solution.py:174
  80.7 24.4 %collective-permute-start.34 = (bf16[1024,512]{1,0:T(8,128)(2,1)S(1)}, bf16[1024,512]{1,0:T(8,128)(2,1)S(1)}, u32[]{:S(2)}, u32[]{:S(2)}) collective-permute-start(bf16[1024,512]{1,0:T(8,128)(2,1)S(1)} %copy-done.5), channel_id=1, source_target_pairs={{0,8},{4,12},{8,0},{12,4},{16,24},{20,28},{24,16},{28,20},{1,9},{5... | collective-permute-start | bytes 3145736 | tf_op jit(solution)/shard_map/ppermute | solution.py:174
  80.8 24.4 %collective-permute-start.35 = (bf16[1024,512]{1,0:T(8,128)(2,1)S(1)}, bf16[1024,512]{1,0:T(8,128)(2,1)S(1)}, u32[]{:S(2)}, u32[]{:S(2)}) collective-permute-start(bf16[1024,512]{1,0:T(8,128)(2,1)S(1)} %copy-done.5), channel_id=1, source_target_pairs={{0,16},{4,20},{8,24},{12,28},{16,0},{20,4},{24,8},{28,12},{1,17},{... | collective-permute-start | bytes 3145736 | tf_op jit(solution)/shard_map/ppermute | solution.py:174
  81.3 23.9 %collective-permute-start.38 = (bf16[256,512]{1,0:T(8,128)(2,1)S(1)}, bf16[256,512]{1,0:T(8,128)(2,1)S(1)}, u32[]{:S(2)}, u32[]{:S(2)}) collective-permute-start(bf16[256,512]{1,0:T(8,128)(2,1)S(1)} %get-tuple-element.104), channel_id=1, source_target_pairs={{0,3},{1,2},{2,1},{3,0},{4,7},{5,6},{6,5},{7,4},{8,11},{9,10},{10,... | collective-permute-start | bytes 786440 | tf_op jit(solution)/shard_map/ppermute | solution.py:174
  82.6 22.6 %collective-permute-start.37 = (bf16[256,512]{1,0:T(8,128)(2,1)S(1)}, bf16[256,512]{1,0:T(8,128)(2,1)S(1)}, u32[]{:S(2)}, u32[]{:S(2)}) collective-permute-start(bf16[256,512]{1,0:T(8,128)(2,1)S(1)} %get-tuple-element.103), channel_id=1, source_target_pairs={{0,2},{1,3},{2,0},{3,1},{4,6},{5,7},{6,4},{7,5},{8,10},{9,11},{10,... | collective-permute-start | bytes 786440 | tf_op jit(solution)/shard_map/ppermute | solution.py:174
  84.7 20.6 %collective-permute-start.36 = (bf16[256,512]{1,0:T(8,128)(2,1)S(1)}, bf16[256,512]{1,0:T(8,128)(2,1)S(1)}, u32[]{:S(2)}, u32[]{:S(2)}) collective-permute-start(bf16[256,512]{1,0:T(8,128)(2,1)S(1)} %get-tuple-element.102), channel_id=1, source_target_pairs={{0,1},{1,0},{2,3},{3,2},{4,5},{5,4},{6,7},{7,6},{8,9},{9,8},{10,11... | collective-permute-start | bytes 786440 | tf_op jit(solution)/shard_map/ppermute | solution.py:174
  106.7 12.7 %collective-permute-start.43 = (bf16[256,512]{1,0:T(8,128)(2,1)S(1)}, bf16[256,512]{1,0:T(8,128)(2,1)S(1)}, u32[]{:S(2)}, u32[]{:S(2)}) collective-permute-start(bf16[256,512]{1,0:T(8,128)(2,1)S(1)} %add_convert_fusion.refs_0_.latent), channel_id=1, source_target_pairs={{0,1},{1,0},{2,3},{3,2},{4,5},{5,4},{6,7},{7,6},{8,9},{9,8},{10,11... | collective-permute-start | bytes 786440 | tf_op jit(solution)/shard_map/ppermute | solution.py:174
  108.3 15.6 %collective-permute-start.45 = (bf16[256,512]{1,0:T(8,128)(2,1)S(1)}, bf16[256,512]{1,0:T(8,128)(2,1)S(1)}, u32[]{:S(2)}, u32[]{:S(2)}) collective-permute-start(bf16[256,512]{1,0:T(8,128)(2,1)S(1)} %add_convert_fusion.refs_0_.latent), channel_id=1, source_target_pairs={{0,2},{1,3},{2,0},{3,1},{4,6},{5,7},{6,4},{7,5},{8,10},{9,11},{10,... | collective-permute-start | bytes 786440 | tf_op jit(solution)/shard_map/ppermute | solution.py:174
  124.0 13.1 %collective-permute-start.50 = (bf16[256,512]{1,0:T(8,128)(2,1)S(1)}, bf16[256,512]{1,0:T(8,128)(2,1)S(1)}, u32[]{:S(2)}, u32[]{:S(2)}) collective-permute-start(bf16[256,512]{1,0:T(8,128)(2,1)S(1)} %add_convert_fusion.refs_0_.latent), channel_id=1, source_target_pairs={{0,3},{1,2},{2,1},{3,0},{4,7},{5,6},{6,5},{7,4},{8,11},{9,10},{10,... | collective-permute-start | bytes 786440 | tf_op jit(solution)/shard_map/ppermute | solution.py:174
  127.8 14.3 %collective-permute-start.47 = (bf16[528,384]{1,0:T(8,128)(2,1)S(1)}, bf16[528,384]{1,0:T(8,128)(2,1)S(1)}, u32[]{:S(2)}, u32[]{:S(2)}) collective-permute-start(bf16[528,384]{1,0:T(8,128)(2,1)S(1)} %get-tuple-element.116), channel_id=1, source_target_pairs={{0,8},{4,12},{8,0},{12,4},{16,24},{20,28},{24,16},{28,20},{1,9},{5... | collective-permute-start | bytes 1216520 | tf_op jit(solution)/shard_map/ppermute | solution.py:174
  128.8 13.3 %collective-permute-start.48 = (bf16[528,384]{1,0:T(8,128)(2,1)S(1)}, bf16[528,384]{1,0:T(8,128)(2,1)S(1)}, u32[]{:S(2)}, u32[]{:S(2)}) collective-permute-start(bf16[528,384]{1,0:T(8,128)(2,1)S(1)} %get-tuple-element.117), channel_id=1, source_target_pairs={{0,16},{4,20},{8,24},{12,28},{16,0},{20,4},{24,8},{28,12},{1,17},{... | collective-permute-start | bytes 1216520 | tf_op jit(solution)/shard_map/ppermute | solution.py:174
  129.1 19.0 %collective-permute-start.49 = (bf16[528,384]{1,0:T(8,128)(2,1)S(1)}, bf16[528,384]{1,0:T(8,128)(2,1)S(1)}, u32[]{:S(2)}, u32[]{:S(2)}) collective-permute-start(bf16[528,384]{1,0:T(8,128)(2,1)S(1)} %get-tuple-element.118), channel_id=1, source_target_pairs={{0,24},{4,28},{8,16},{12,20},{16,8},{20,12},{24,0},{28,4},{1,25},{... | collective-permute-start | bytes 1216520 | tf_op jit(solution)/shard_map/ppermute | solution.py:174
  140.8 10.9 %collective-permute-start.52 = (bf16[272,384]{1,0:T(8,128)(2,1)S(1)}, bf16[272,384]{1,0:T(8,128)(2,1)S(1)}, u32[]{:S(2)}, u32[]{:S(2)}) collective-permute-start(bf16[272,384]{1,0:T(8,128)(2,1)S(1)} %get-tuple-element.122), channel_id=1, source_target_pairs={{0,8},{4,12},{8,0},{12,4},{16,24},{20,28},{24,16},{28,20},{1,9},{5... | collective-permute-start | bytes 626696 | tf_op jit(solution)/shard_map/ppermute | solution.py:174
  141.7 12.2 %collective-permute-start.53 = (bf16[272,384]{1,0:T(8,128)(2,1)S(1)}, bf16[272,384]{1,0:T(8,128)(2,1)S(1)}, u32[]{:S(2)}, u32[]{:S(2)}) collective-permute-start(bf16[272,384]{1,0:T(8,128)(2,1)S(1)} %get-tuple-element.123), channel_id=1, source_target_pairs={{0,16},{4,20},{8,24},{12,28},{16,0},{20,4},{24,8},{28,12},{1,17},{... | collective-permute-start | bytes 626696 | tf_op jit(solution)/shard_map/ppermute | solution.py:174
  174.6 16.7 %collective-permute-start.66 = (bf16[256,512]{1,0:T(8,128)(2,1)S(1)}, bf16[256,512]{1,0:T(8,128)(2,1)S(1)}, u32[]{:S(2)}, u32[]{:S(2)}) collective-permute-start(bf16[256,512]{1,0:T(8,128)(2,1)S(1)} %get-tuple-element.139), channel_id=1, source_target_pairs={{0,2},{1,3},{2,0},{3,1},{4,6},{5,7},{6,4},{7,5},{8,10},{9,11},{10,... | collective-permute-start | bytes 786440 | tf_op jit(solution)/shard_map/ppermute | solution.py:174
  174.7 25.0 %collective-permute-start.67 = (bf16[256,512]{1,0:T(8,128)(2,1)S(1)}, bf16[256,512]{1,0:T(8,128)(2,1)S(1)}, u32[]{:S(2)}, u32[]{:S(2)}) collective-permute-start(bf16[256,512]{1,0:T(8,128)(2,1)S(1)} %get-tuple-element.140), channel_id=1, source_target_pairs={{0,3},{1,2},{2,1},{3,0},{4,7},{5,6},{6,5},{7,4},{8,11},{9,10},{10,... | collective-permute-start | bytes 786440 | tf_op jit(solution)/shard_map/ppermute | solution.py:174
  179.1 20.6 %collective-permute-start.65 = (bf16[256,512]{1,0:T(8,128)(2,1)S(1)}, bf16[256,512]{1,0:T(8,128)(2,1)S(1)}, u32[]{:S(2)}, u32[]{:S(2)}) collective-permute-start(bf16[256,512]{1,0:T(8,128)(2,1)S(1)} %collective-permute-done.50.refs_0_), channel_id=1, source_target_pairs={{0,24},{4,28},{9,17},{13,21},{18,10},{22,14},{27,3},{31,7}} | collective-permute-start | bytes 786440 | tf_op jit(solution)/shard_map/ppermute | solution.py:633
  (48 other events, 423.5 us)

commit v11 on v10

--- a/solution.py
+++ b/solution.py
@@ -629,7 +629,7 @@
             for t in range(tensor_count)
             for k in range(2)
         ]
-        block = after(latent_blocks[d], *(received[:1] if d == chip_count - 1 else [total]))
+        block = after(latent_blocks[d], *(received[:1] if d > 1 else [total]))
         residual.append(lax.ppermute(block, ("seq", "tensor"), route))
     same, crossed = call(
         final_kernel,

time: 204 us -> 203 us (level)
  transfers between devices with their start and end apart: 69 -> 69, of which waited for: 31 -> 30; matrix products, arithmetic and copies ran while one was open for 1% -> 1% of each run, Pallas kernels for 8% -> 8%
where the time goes in v11:
time: 203 us; the launch traced here: 202 us
  waiting for transfers between devices  99.9 us (49%)
  starting transfers between devices  75.5 us (37%)
  Pallas kernels  21.4 us (11%)
  local copies, waits for them, and re-layouts  3.48 us (2%)
    ppermute x64, waiting for transfers between devices, exchanged(): return lax.ppermute(block, axis, route)  94.4 us
    ppermute x64, starting transfers between devices, exchanged(): return lax.ppermute(block, axis, route)  67.1 us
    pallas_call x10, Pallas kernels, call(): pl.pallas_call(kernel, out_shape=shapes, in_specs=[pl.BlockSpec(memory_sp...  21.4 us
    ppermute x2, starting transfers between devices, shifted(): return lax.ppermute(block, axis, route)  5.74 us
    ppermute x2, waiting for transfers between devices, shifted(): return lax.ppermute(block, axis, route)  5.53 us
  transfers between devices with their start and end apart: 69, of which 30 were waited for; matrix products, arithmetic and copies ran while one was open for 1% of the time, Pallas kernels for 8%

profile of v11, /device:TPU:9, one launch (start us, length us, event | category | flops | bytes accessed | tf_op | source)
XLA Modules:
  0.0 202.3 jit_solution(10544634016925825284)
XLA Ops:
  5.4 2.0 collective-permute-done.1.refs_2_
  8.6 7.4 %collective-permute-start.2 = (bf16[128,1024]{1,0:T(8,128)(2,1)S(1)}, bf16[128,1024]{1,0:T(8,128)(2,1)S(1)}, u32[]{:S(2)}, u32[]{:S(2)}) collective-permute-start(bf16[128,1024]{1,0:T(8,128)(2,1)S(1)} %collective-permute-done.1.refs_2_), channel_id=1, source_target_pairs={{0,4},{4,0},{8,12},{12,8},{16,20},{20,16},{24,28},{28,24},{1,5},{5... | collective-permute-start | bytes 786440 | tf_op jit(solution)/shard_map/ppermute | solution.py:174
  24.6 3.2 %collective-permute-start.7 = (bf16[128,1024]{1,0:T(8,128)(2,1)}, bf16[128,1024]{1,0:T(8,128)(2,1)S(1)}, u32[]{:S(2)}, u32[]{:S(2)}) collective-permute-start(bf16[128,1024]{1,0:T(8,128)(2,1)} %refs_0_.3), channel_id=1, source_target_pairs={{0,4},{4,0},{8,12},{12,8},{16,20},{20,16},{24,28},{28,24},{1,5},{5... | collective-permute-start | bytes 786440 | tf_op jit(solution)/shard_map/ppermute | solution.py:174
  30.4 2.0 shard_map.118.query
  33.1 1.8 collective-permute-start.21
  34.9 2.4 %collective-permute-start.13 = (bf16[128,1024]{1,0:T(8,128)(2,1)S(1)}, bf16[128,1024]{1,0:T(8,128)(2,1)S(1)}, u32[]{:S(2)}, u32[]{:S(2)}) collective-permute-start(bf16[128,1024]{1,0:T(8,128)(2,1)S(1)} %collective-permute-done.12.refs_6_), channel_id=1, source_target_pairs={{0,4},{4,0},{8,12},{12,8},{16,20},{20,16},{24,28},{28,24},{1,5},{5... | collective-permute-start | bytes 786440 | tf_op jit(solution)/shard_map/ppermute | solution.py:174
  39.6 7.3 %shard_map.119 = (bf16[128,1024]{1,0:T(8,128)(2,1)S(1)}, bf16[64,1024]{1,0:T(8,128)(2,1)S(1)}, bf16[64,1024]{1,0:T(8,128)(2,1)S(1)}) custom-call(s32[1,1024]{1,0:T(1,128)S(1)} %bitcast.7, bf16[256,1024]{1,0:T(8,128)(2,1)S(1)} %shard_map.118.query, bf16[1024,1024]{1,0:T(8,128)(2,1)S(1)} %copy-done.1, bf16[128,1024]{1,0:T(8,128)(2,1)S(1)} %copy-done.9, ...), custom_call_target="tpu_custom_call" | custom-call | flops 5368709120 | bytes 7344128 | tf_op jit(solution)/shard_map/pallas_call | solution.py:207
  46.9 2.3 %collective-permute-start.23 = (bf16[64,1024]{1,0:T(8,128)(2,1)S(1)}, bf16[64,1024]{1,0:T(8,128)(2,1)S(1)}, u32[]{:S(2)}, u32[]{:S(2)}) collective-permute-start(bf16[64,1024]{1,0:T(8,128)(2,1)S(1)} %get-tuple-element.84), channel_id=1, source_target_pairs={{4,0},{8,4},{12,8},{16,12},{20,16},{24,20},{28,24},{5,1},{9,5},{13... | collective-permute-start | bytes 393224 | tf_op jit(solution)/shard_map/ppermute | solution.py:22
  49.2 3.5 %collective-permute-start.22 = (bf16[64,1024]{1,0:T(8,128)(2,1)S(1)}, bf16[64,1024]{1,0:T(8,128)(2,1)S(1)}, u32[]{:S(2)}, u32[]{:S(2)}) collective-permute-start(bf16[64,1024]{1,0:T(8,128)(2,1)S(1)} %get-tuple-element.83), channel_id=1, source_target_pairs={{0,4},{4,8},{8,12},{12,16},{16,20},{20,24},{24,28},{1,5},{5,9},{9,... | collective-permute-start | bytes 393224 | tf_op jit(solution)/shard_map/ppermute | solution.py:22
  52.7 3.2 %collective-permute-done.21.refs_11_ = bf16[1024,512]{1,0:T(8,128)(2,1)S(1)} collective-permute-done((bf16[1024,512]{1,0:T(8,128)(2,1)S(1)}, bf16[1024,512]{1,0:T(8,128)(2,1)S(1)}, u32[]{:S(2)}, u32[]{:S(2)}) %collective-permute-start.21) | collective-permute-done | bytes 1048608 | tf_op jit(solution)/shard_map/ppermute | solution.py:174
  55.8 5.5 %collective-permute-done.23 = bf16[64,1024]{1,0:T(8,128)(2,1)S(1)} collective-permute-done((bf16[64,1024]{1,0:T(8,128)(2,1)S(1)}, bf16[64,1024]{1,0:T(8,128)(2,1)S(1)}, u32[]{:S(2)}, u32[]{:S(2)}) %collective-permute-start.23) | collective-permute-done | bytes 131104 | tf_op jit(solution)/shard_map/ppermute | solution.py:22
  61.4 2.8 %collective-permute-start.25 = (bf16[128,1024]{1,0:T(8,128)(2,1)S(1)}, bf16[128,1024]{1,0:T(8,128)(2,1)S(1)}, u32[]{:S(2)}, u32[]{:S(2)}) collective-permute-start(bf16[128,1024]{1,0:T(8,128)(2,1)S(1)} %maximum_add_fusion.refs_0_), channel_id=1, source_target_pairs={{0,8},{4,12},{8,0},{12,4},{16,24},{20,28},{24,16},{28,20},{1,9},{5... | collective-permute-start | bytes 786440 | tf_op jit(solution)/shard_map/ppermute | solution.py:174
  65.5 5.6 %collective-permute-done.25.refs_2_ = bf16[128,1024]{1,0:T(8,128)(2,1)S(1)} collective-permute-done((bf16[128,1024]{1,0:T(8,128)(2,1)S(1)}, bf16[128,1024]{1,0:T(8,128)(2,1)S(1)}, u32[]{:S(2)}, u32[]{:S(2)}) %collective-permute-start.25) | collective-permute-done | bytes 262176 | tf_op jit(solution)/shard_map/ppermute | solution.py:174
  71.1 6.4 %collective-permute-done.27.refs_4_ = bf16[128,1024]{1,0:T(8,128)(2,1)S(1)} collective-permute-done((bf16[128,1024]{1,0:T(8,128)(2,1)S(1)}, bf16[128,1024]{1,0:T(8,128)(2,1)S(1)}, u32[]{:S(2)}, u32[]{:S(2)}) %collective-permute-start.27) | collective-permute-done | bytes 262176 | tf_op jit(solution)/shard_map/ppermute | solution.py:174
  82.6 2.0 %collective-permute-start.37 = (bf16[256,512]{1,0:T(8,128)(2,1)S(1)}, bf16[256,512]{1,0:T(8,128)(2,1)S(1)}, u32[]{:S(2)}, u32[]{:S(2)}) collective-permute-start(bf16[256,512]{1,0:T(8,128)(2,1)S(1)} %get-tuple-element.103), channel_id=1, source_target_pairs={{0,2},{1,3},{2,0},{3,1},{4,6},{5,7},{6,4},{7,5},{8,10},{9,11},{10,... | collective-permute-start | bytes 786440 | tf_op jit(solution)/shard_map/ppermute | solution.py:174
  86.0 19.1 %collective-permute-done.34.refs_9_ = bf16[1024,512]{1,0:T(8,128)(2,1)S(1)} collective-permute-done((bf16[1024,512]{1,0:T(8,128)(2,1)S(1)}, bf16[1024,512]{1,0:T(8,128)(2,1)S(1)}, u32[]{:S(2)}, u32[]{:S(2)}) %collective-permute-start.34) | collective-permute-done | bytes 1048608 | tf_op jit(solution)/shard_map/ppermute | solution.py:174
  113.3 6.1 %collective-permute-done.43.refs_0_ = bf16[256,512]{1,0:T(8,128)(2,1)S(1)} collective-permute-done((bf16[256,512]{1,0:T(8,128)(2,1)S(1)}, bf16[256,512]{1,0:T(8,128)(2,1)S(1)}, u32[]{:S(2)}, u32[]{:S(2)}) %collective-permute-start.43) | collective-permute-done | bytes 262176 | tf_op jit(solution)/shard_map/ppermute | solution.py:174
  119.4 2.8 %collective-permute-done.42.refs_3_ = bf16[272,384]{1,0:T(8,128)(2,1)S(1)} collective-permute-done((bf16[272,384]{1,0:T(8,128)(2,1)S(1)}, bf16[272,384]{1,0:T(8,128)(2,1)S(1)}, u32[]{:S(2)}, u32[]{:S(2)}) %collective-permute-start.42) | collective-permute-done | bytes 208928 | tf_op jit(solution)/shard_map/ppermute | solution.py:174
  125.5 2.3 %shard_map.123 = (f32[520,384]{1,0:T(8,128)S(1)}, bf16[528,384]{1,0:T(8,128)(2,1)S(1)}, bf16[528,384]{1,0:T(8,128)(2,1)S(1)}, bf16[528,384]{1,0:T(8,128)(2,1)S(1)}) custom-call(f32[1,4096]{1,0:T(1,128)S(1)} %bitcast.4, bf16[256,512]{1,0:T(8,128)(2,1)S(1)} %collective-permute-done.43.refs_0_, bf16[256,512]{1,0:T(8,128)(2,1)S(1)} %collective-permute-done.44.refs_1_, ...), custom_call_target="tpu_custom_call" | custom-call | flops 1610612736 | bytes 6225920 | tf_op jit(solution)/shard_map/pallas_call | solution.py:207
  130.6 6.5 %collective-permute-done.50.refs_0_ = bf16[256,512]{1,0:T(8,128)(2,1)S(1)} collective-permute-done((bf16[256,512]{1,0:T(8,128)(2,1)S(1)}, bf16[256,512]{1,0:T(8,128)(2,1)S(1)}, u32[]{:S(2)}, u32[]{:S(2)}) %collective-permute-start.50) | collective-permute-done | bytes 262176 | tf_op jit(solution)/shard_map/ppermute | solution.py:174
  142.1 6.0 %collective-permute-done.49.refs_7_ = bf16[528,384]{1,0:T(8,128)(2,1)S(1)} collective-permute-done((bf16[528,384]{1,0:T(8,128)(2,1)S(1)}, bf16[528,384]{1,0:T(8,128)(2,1)S(1)}, u32[]{:S(2)}, u32[]{:S(2)}) %collective-permute-start.49) | collective-permute-done | bytes 405536 | tf_op jit(solution)/shard_map/ppermute | solution.py:174
  149.0 2.7 %collective-permute-done.52.refs_9_ = bf16[272,384]{1,0:T(8,128)(2,1)S(1)} collective-permute-done((bf16[272,384]{1,0:T(8,128)(2,1)S(1)}, bf16[272,384]{1,0:T(8,128)(2,1)S(1)}, u32[]{:S(2)}, u32[]{:S(2)}) %collective-permute-start.52) | collective-permute-done | bytes 208928 | tf_op jit(solution)/shard_map/ppermute | solution.py:174
  151.7 2.2 %collective-permute-done.53.refs_10_ = bf16[272,384]{1,0:T(8,128)(2,1)S(1)} collective-permute-done((bf16[272,384]{1,0:T(8,128)(2,1)S(1)}, bf16[272,384]{1,0:T(8,128)(2,1)S(1)}, u32[]{:S(2)}, u32[]{:S(2)}) %collective-permute-start.53) | collective-permute-done | bytes 208928 | tf_op jit(solution)/shard_map/ppermute | solution.py:174
  153.9 3.2 %collective-permute-done.54.refs_11_ = bf16[272,384]{1,0:T(8,128)(2,1)S(1)} collective-permute-done((bf16[272,384]{1,0:T(8,128)(2,1)S(1)}, bf16[272,384]{1,0:T(8,128)(2,1)S(1)}, u32[]{:S(2)}, u32[]{:S(2)}) %collective-permute-start.54) | collective-permute-done | bytes 208928 | tf_op jit(solution)/shard_map/ppermute | solution.py:174
  157.1 2.0 %shard_map.125 = (bf16[256,128]{1,0:T(8,128)(2,1)S(1)}, bf16[256,128]{1,0:T(8,128)(2,1)S(1)}, bf16[256,128]{1,0:T(8,128)(2,1)S(1)}, bf16[256,128]{1,0:T(8,128)(2,1)S(1)}) custom-call(f32[264,384]{1,0:T(8,128)S(1)} %get-tuple-element.109.refs_0_, bf16[272,384]{1,0:T(8,128)(2,1)S(1)} %collective-permute-done.40.refs_1_, ...), custom_call_target="tpu_custom_call" | custom-call | flops 268435456 | bytes 4341760 | tf_op jit(solution)/shard_map/pallas_call | solution.py:207
  161.8 2.0 %collective-permute-start.55 = (bf16[256,128]{1,0:T(8,128)(2,1)S(1)}, bf16[256,128]{1,0:T(8,128)(2,1)S(1)}, u32[]{:S(2)}, u32[]{:S(2)}) collective-permute-start(bf16[256,128]{1,0:T(8,128)(2,1)S(1)} %get-tuple-element.126.refs_0_), channel_id=1, source_target_pairs={{0,4},{4,0},{8,12},{12,8},{16,20},{20,16},{24,28},{28,24},{1,5},{5... | collective-permute-start | bytes 196616 | tf_op jit(solution)/shard_map/ppermute | solution.py:174
  168.7 2.3 %shard_map.126 = (f32[256,512]{1,0:T(8,128)S(1)}, bf16[256,512]{1,0:T(8,128)(2,1)S(1)}, bf16[256,512]{1,0:T(8,128)(2,1)S(1)}, bf16[256,512]{1,0:T(8,128)(2,1)S(1)}) custom-call(bf16[256,128]{1,0:T(8,128)(2,1)S(1)} %get-tuple-element.126.refs_0_, bf16[256,128]{1,0:T(8,128)(2,1)S(1)} %collective-permute-done.55.refs_1_, ...), custom_call_target="tpu_custom_call" | custom-call | flops 1073741824 | bytes 6029312 | tf_op jit(solution)/shard_map/pallas_call | solution.py:207
  174.0 1.9 collective-permute-start.67
  175.8 5.1 %collective-permute-done.63.refs_3_ = bf16[256,512]{1,0:T(8,128)(2,1)S(1)} collective-permute-done((bf16[256,512]{1,0:T(8,128)(2,1)S(1)}, bf16[256,512]{1,0:T(8,128)(2,1)S(1)}, u32[]{:S(2)}, u32[]{:S(2)}) %collective-permute-start.63) | collective-permute-done | bytes 262176 | tf_op jit(solution)/shard_map/ppermute | solution.py:174
  182.3 8.3 %collective-permute-done.66.refs_4_ = bf16[256,512]{1,0:T(8,128)(2,1)S(1)} collective-permute-done((bf16[256,512]{1,0:T(8,128)(2,1)S(1)}, bf16[256,512]{1,0:T(8,128)(2,1)S(1)}, u32[]{:S(2)}, u32[]{:S(2)}) %collective-permute-start.66) | collective-permute-done | bytes 262176 | tf_op jit(solution)/shard_map/ppermute | solution.py:174
  190.6 7.7 %collective-permute-done.67.refs_5_ = bf16[256,512]{1,0:T(8,128)(2,1)S(1)} collective-permute-done((bf16[256,512]{1,0:T(8,128)(2,1)S(1)}, bf16[256,512]{1,0:T(8,128)(2,1)S(1)}, u32[]{:S(2)}, u32[]{:S(2)}) %collective-permute-start.67) | collective-permute-done | bytes 262176 | tf_op jit(solution)/shard_map/ppermute | solution.py:174
  198.7 1.8 collective-permute-start.68
  (147 shorter events, 62.7 us)
Async XLA Ops:
  2.5 13.6 %collective-permute-start.5 = (bf16[128,1024]{1,0:T(8,128)(2,1)}, bf16[128,1024]{1,0:T(8,128)(2,1)S(1)}, u32[]{:S(2)}, u32[]{:S(2)}) collective-permute-start(bf16[128,1024]{1,0:T(8,128)(2,1)} %refs_0_.2), channel_id=1, source_target_pairs={{0,24},{4,28},{8,16},{12,20},{16,8},{20,12},{24,0},{28,4},{1,25},{... | collective-permute-start | bytes 786440 | tf_op jit(solution)/shard_map/ppermute | solution.py:174
  2.6 14.1 %collective-permute-start = (bf16[128,1024]{1,0:T(8,128)(2,1)}, bf16[128,1024]{1,0:T(8,128)(2,1)S(1)}, u32[]{:S(2)}, u32[]{:S(2)}) collective-permute-start(bf16[128,1024]{1,0:T(8,128)(2,1)} %refs_0_.2), channel_id=1, source_target_pairs={{0,4},{4,0},{8,12},{12,8},{16,20},{20,16},{24,28},{28,24},{1,5},{5... | collective-permute-start | bytes 786440 | tf_op jit(solution)/shard_map/ppermute | solution.py:174
  4.2 14.5 %collective-permute-start.8 = (bf16[128,1024]{1,0:T(8,128)(2,1)}, bf16[128,1024]{1,0:T(8,128)(2,1)S(1)}, u32[]{:S(2)}, u32[]{:S(2)}) collective-permute-start(bf16[128,1024]{1,0:T(8,128)(2,1)} %refs_0_.3), channel_id=1, source_target_pairs={{0,8},{4,12},{8,0},{12,4},{16,24},{20,28},{24,16},{28,20},{1,9},{5... | collective-permute-start | bytes 786440 | tf_op jit(solution)/shard_map/ppermute | solution.py:174
  7.4 13.2 %collective-permute-start.17 = (bf16[128,1024]{1,0:T(8,128)(2,1)}, bf16[128,1024]{1,0:T(8,128)(2,1)S(1)}, u32[]{:S(2)}, u32[]{:S(2)}) collective-permute-start(bf16[128,1024]{1,0:T(8,128)(2,1)} %refs_8_.1), channel_id=1, source_target_pairs={{0,16},{4,20},{8,24},{12,28},{16,0},{20,4},{24,8},{28,12},{1,17},{... | collective-permute-start | bytes 786440 | tf_op jit(solution)/shard_map/ppermute | solution.py:174
  8.6 12.8 %collective-permute-start.2 = (bf16[128,1024]{1,0:T(8,128)(2,1)S(1)}, bf16[128,1024]{1,0:T(8,128)(2,1)S(1)}, u32[]{:S(2)}, u32[]{:S(2)}) collective-permute-start(bf16[128,1024]{1,0:T(8,128)(2,1)S(1)} %collective-permute-done.1.refs_2_), channel_id=1, source_target_pairs={{0,4},{4,0},{8,12},{12,8},{16,20},{20,16},{24,28},{28,24},{1,5},{5... | collective-permute-start | bytes 786440 | tf_op jit(solution)/shard_map/ppermute | solution.py:174
  16.7 15.7 %collective-permute-start.10 = (bf16[128,1024]{1,0:T(8,128)(2,1)}, bf16[128,1024]{1,0:T(8,128)(2,1)S(1)}, u32[]{:S(2)}, u32[]{:S(2)}) collective-permute-start(bf16[128,1024]{1,0:T(8,128)(2,1)} %refs_0_.3), channel_id=1, source_target_pairs={{0,16},{4,20},{8,24},{12,28},{16,0},{20,4},{24,8},{28,12},{1,17},{... | collective-permute-start | bytes 786440 | tf_op jit(solution)/shard_map/ppermute | solution.py:174
  20.6 11.9 %collective-permute-start.12 = (bf16[128,1024]{1,0:T(8,128)(2,1)S(1)}, bf16[128,1024]{1,0:T(8,128)(2,1)S(1)}, u32[]{:S(2)}, u32[]{:S(2)}) collective-permute-start(bf16[128,1024]{1,0:T(8,128)(2,1)S(1)} %collective-permute-done.8.refs_2_), channel_id=1, source_target_pairs={{0,16},{4,20},{8,24},{12,28},{16,0},{20,4},{24,8},{28,12},{1,17},{... | collective-permute-start | bytes 786440 | tf_op jit(solution)/shard_map/ppermute | solution.py:174
  21.5 11.5 %collective-permute-start.19 = (bf16[128,1024]{1,0:T(8,128)(2,1)S(1)}, bf16[128,1024]{1,0:T(8,128)(2,1)S(1)}, u32[]{:S(2)}, u32[]{:S(2)}) collective-permute-start(bf16[128,1024]{1,0:T(8,128)(2,1)S(1)} %collective-permute-done.17.refs_12_), channel_id=1, source_target_pairs={{0,8},{4,12},{8,0},{12,4},{16,24},{20,28},{24,16},{28,20},{1,9},{5... | collective-permute-start | bytes 786440 | tf_op jit(solution)/shard_map/ppermute | solution.py:174
  24.6 10.3 %collective-permute-start.7 = (bf16[128,1024]{1,0:T(8,128)(2,1)}, bf16[128,1024]{1,0:T(8,128)(2,1)S(1)}, u32[]{:S(2)}, u32[]{:S(2)}) collective-permute-start(bf16[128,1024]{1,0:T(8,128)(2,1)} %refs_0_.3), channel_id=1, source_target_pairs={{0,4},{4,0},{8,12},{12,8},{16,20},{20,16},{24,28},{28,24},{1,5},{5... | collective-permute-start | bytes 786440 | tf_op jit(solution)/shard_map/ppermute | solution.py:174
  33.1 22.7 %collective-permute-start.21 = (bf16[1024,512]{1,0:T(8,128)(2,1)S(1)}, bf16[1024,512]{1,0:T(8,128)(2,1)S(1)}, u32[]{:S(2)}, u32[]{:S(2)}) collective-permute-start(bf16[1024,512]{1,0:T(8,128)(2,1)S(1)} %copy-done.5), channel_id=1, source_target_pairs={{0,24},{4,28},{8,16},{12,20},{16,8},{20,12},{24,0},{28,4},{1,25},{... | collective-permute-start | bytes 3145736 | tf_op jit(solution)/shard_map/ppermute | solution.py:174
  46.9 14.4 %collective-permute-start.23 = (bf16[64,1024]{1,0:T(8,128)(2,1)S(1)}, bf16[64,1024]{1,0:T(8,128)(2,1)S(1)}, u32[]{:S(2)}, u32[]{:S(2)}) collective-permute-start(bf16[64,1024]{1,0:T(8,128)(2,1)S(1)} %get-tuple-element.84), channel_id=1, source_target_pairs={{4,0},{8,4},{12,8},{16,12},{20,16},{24,20},{28,24},{5,1},{9,5},{13... | collective-permute-start | bytes 393224 | tf_op jit(solution)/shard_map/ppermute | solution.py:22
  49.2 12.2 %collective-permute-start.22 = (bf16[64,1024]{1,0:T(8,128)(2,1)S(1)}, bf16[64,1024]{1,0:T(8,128)(2,1)S(1)}, u32[]{:S(2)}, u32[]{:S(2)}) collective-permute-start(bf16[64,1024]{1,0:T(8,128)(2,1)S(1)} %get-tuple-element.83), channel_id=1, source_target_pairs={{0,4},{4,8},{8,12},{12,16},{16,20},{20,24},{24,28},{1,5},{5,9},{9,... | collective-permute-start | bytes 393224 | tf_op jit(solution)/shard_map/ppermute | solution.py:22
  64.2 13.2 %collective-permute-start.27 = (bf16[128,1024]{1,0:T(8,128)(2,1)S(1)}, bf16[128,1024]{1,0:T(8,128)(2,1)S(1)}, u32[]{:S(2)}, u32[]{:S(2)}) collective-permute-start(bf16[128,1024]{1,0:T(8,128)(2,1)S(1)} %maximum_add_fusion.refs_0_), channel_id=1, source_target_pairs={{0,16},{4,20},{8,24},{12,28},{16,0},{20,4},{24,8},{28,12},{1,17},{... | collective-permute-start | bytes 786440 | tf_op jit(solution)/shard_map/ppermute | solution.py:174
  64.2 13.6 %collective-permute-start.29 = (bf16[128,1024]{1,0:T(8,128)(2,1)S(1)}, bf16[128,1024]{1,0:T(8,128)(2,1)S(1)}, u32[]{:S(2)}, u32[]{:S(2)}) collective-permute-start(bf16[128,1024]{1,0:T(8,128)(2,1)S(1)} %maximum_add_fusion.refs_0_), channel_id=1, source_target_pairs={{0,24},{4,28},{8,16},{12,20},{16,8},{20,12},{24,0},{28,4},{1,25},{... | collective-permute-start | bytes 786440 | tf_op jit(solution)/shard_map/ppermute | solution.py:174
  65.5 12.9 %collective-permute-start.24 = (bf16[128,1024]{1,0:T(8,128)(2,1)S(1)}, bf16[128,1024]{1,0:T(8,128)(2,1)S(1)}, u32[]{:S(2)}, u32[]{:S(2)}) collective-permute-start(bf16[128,1024]{1,0:T(8,128)(2,1)S(1)} %maximum_add_fusion.refs_0_), channel_id=1, source_target_pairs={{0,4},{4,0},{8,12},{12,8},{16,20},{20,16},{24,28},{28,24},{1,5},{5... | collective-permute-start | bytes 786440 | tf_op jit(solution)/shard_map/ppermute | solution.py:174
  80.7 24.4 %collective-permute-start.34 = (bf16[1024,512]{1,0:T(8,128)(2,1)S(1)}, bf16[1024,512]{1,0:T(8,128)(2,1)S(1)}, u32[]{:S(2)}, u32[]{:S(2)}) collective-permute-start(bf16[1024,512]{1,0:T(8,128)(2,1)S(1)} %copy-done.5), channel_id=1, source_target_pairs={{0,8},{4,12},{8,0},{12,4},{16,24},{20,28},{24,16},{28,20},{1,9},{5... | collective-permute-start | bytes 3145736 | tf_op jit(solution)/shard_map/ppermute | solution.py:174
  80.8 24.4 %collective-permute-start.35 = (bf16[1024,512]{1,0:T(8,128)(2,1)S(1)}, bf16[1024,512]{1,0:T(8,128)(2,1)S(1)}, u32[]{:S(2)}, u32[]{:S(2)}) collective-permute-start(bf16[1024,512]{1,0:T(8,128)(2,1)S(1)} %copy-done.5), channel_id=1, source_target_pairs={{0,16},{4,20},{8,24},{12,28},{16,0},{20,4},{24,8},{28,12},{1,17},{... | collective-permute-start | bytes 3145736 | tf_op jit(solution)/shard_map/ppermute | solution.py:174
  81.3 23.9 %collective-permute-start.38 = (bf16[256,512]{1,0:T(8,128)(2,1)S(1)}, bf16[256,512]{1,0:T(8,128)(2,1)S(1)}, u32[]{:S(2)}, u32[]{:S(2)}) collective-permute-start(bf16[256,512]{1,0:T(8,128)(2,1)S(1)} %get-tuple-element.104), channel_id=1, source_target_pairs={{0,3},{1,2},{2,1},{3,0},{4,7},{5,6},{6,5},{7,4},{8,11},{9,10},{10,... | collective-permute-start | bytes 786440 | tf_op jit(solution)/shard_map/ppermute | solution.py:174
  82.6 22.6 %collective-permute-start.37 = (bf16[256,512]{1,0:T(8,128)(2,1)S(1)}, bf16[256,512]{1,0:T(8,128)(2,1)S(1)}, u32[]{:S(2)}, u32[]{:S(2)}) collective-permute-start(bf16[256,512]{1,0:T(8,128)(2,1)S(1)} %get-tuple-element.103), channel_id=1, source_target_pairs={{0,2},{1,3},{2,0},{3,1},{4,6},{5,7},{6,4},{7,5},{8,10},{9,11},{10,... | collective-permute-start | bytes 786440 | tf_op jit(solution)/shard_map/ppermute | solution.py:174
  84.7 20.6 %collective-permute-start.36 = (bf16[256,512]{1,0:T(8,128)(2,1)S(1)}, bf16[256,512]{1,0:T(8,128)(2,1)S(1)}, u32[]{:S(2)}, u32[]{:S(2)}) collective-permute-start(bf16[256,512]{1,0:T(8,128)(2,1)S(1)} %get-tuple-element.102), channel_id=1, source_target_pairs={{0,1},{1,0},{2,3},{3,2},{4,5},{5,4},{6,7},{7,6},{8,9},{9,8},{10,11... | collective-permute-start | bytes 786440 | tf_op jit(solution)/shard_map/ppermute | solution.py:174
  106.7 12.7 %collective-permute-start.43 = (bf16[256,512]{1,0:T(8,128)(2,1)S(1)}, bf16[256,512]{1,0:T(8,128)(2,1)S(1)}, u32[]{:S(2)}, u32[]{:S(2)}) collective-permute-start(bf16[256,512]{1,0:T(8,128)(2,1)S(1)} %add_convert_fusion.refs_0_.latent), channel_id=1, source_target_pairs={{0,1},{1,0},{2,3},{3,2},{4,5},{5,4},{6,7},{7,6},{8,9},{9,8},{10,11... | collective-permute-start | bytes 786440 | tf_op jit(solution)/shard_map/ppermute | solution.py:174
  108.3 15.6 %collective-permute-start.45 = (bf16[256,512]{1,0:T(8,128)(2,1)S(1)}, bf16[256,512]{1,0:T(8,128)(2,1)S(1)}, u32[]{:S(2)}, u32[]{:S(2)}) collective-permute-start(bf16[256,512]{1,0:T(8,128)(2,1)S(1)} %add_convert_fusion.refs_0_.latent), channel_id=1, source_target_pairs={{0,2},{1,3},{2,0},{3,1},{4,6},{5,7},{6,4},{7,5},{8,10},{9,11},{10,... | collective-permute-start | bytes 786440 | tf_op jit(solution)/shard_map/ppermute | solution.py:174
  124.0 13.1 %collective-permute-start.50 = (bf16[256,512]{1,0:T(8,128)(2,1)S(1)}, bf16[256,512]{1,0:T(8,128)(2,1)S(1)}, u32[]{:S(2)}, u32[]{:S(2)}) collective-permute-start(bf16[256,512]{1,0:T(8,128)(2,1)S(1)} %add_convert_fusion.refs_0_.latent), channel_id=1, source_target_pairs={{0,3},{1,2},{2,1},{3,0},{4,7},{5,6},{6,5},{7,4},{8,11},{9,10},{10,... | collective-permute-start | bytes 786440 | tf_op jit(solution)/shard_map/ppermute | solution.py:174
  127.8 14.3 %collective-permute-start.47 = (bf16[528,384]{1,0:T(8,128)(2,1)S(1)}, bf16[528,384]{1,0:T(8,128)(2,1)S(1)}, u32[]{:S(2)}, u32[]{:S(2)}) collective-permute-start(bf16[528,384]{1,0:T(8,128)(2,1)S(1)} %get-tuple-element.116), channel_id=1, source_target_pairs={{0,8},{4,12},{8,0},{12,4},{16,24},{20,28},{24,16},{28,20},{1,9},{5... | collective-permute-start | bytes 1216520 | tf_op jit(solution)/shard_map/ppermute | solution.py:174
  128.8 13.3 %collective-permute-start.48 = (bf16[528,384]{1,0:T(8,128)(2,1)S(1)}, bf16[528,384]{1,0:T(8,128)(2,1)S(1)}, u32[]{:S(2)}, u32[]{:S(2)}) collective-permute-start(bf16[528,384]{1,0:T(8,128)(2,1)S(1)} %get-tuple-element.117), channel_id=1, source_target_pairs={{0,16},{4,20},{8,24},{12,28},{16,0},{20,4},{24,8},{28,12},{1,17},{... | collective-permute-start | bytes 1216520 | tf_op jit(solution)/shard_map/ppermute | solution.py:174
  129.1 19.0 %collective-permute-start.49 = (bf16[528,384]{1,0:T(8,128)(2,1)S(1)}, bf16[528,384]{1,0:T(8,128)(2,1)S(1)}, u32[]{:S(2)}, u32[]{:S(2)}) collective-permute-start(bf16[528,384]{1,0:T(8,128)(2,1)S(1)} %get-tuple-element.118), channel_id=1, source_target_pairs={{0,24},{4,28},{8,16},{12,20},{16,8},{20,12},{24,0},{28,4},{1,25},{... | collective-permute-start | bytes 1216520 | tf_op jit(solution)/shard_map/ppermute | solution.py:174
  140.8 10.9 %collective-permute-start.52 = (bf16[272,384]{1,0:T(8,128)(2,1)S(1)}, bf16[272,384]{1,0:T(8,128)(2,1)S(1)}, u32[]{:S(2)}, u32[]{:S(2)}) collective-permute-start(bf16[272,384]{1,0:T(8,128)(2,1)S(1)} %get-tuple-element.122), channel_id=1, source_target_pairs={{0,8},{4,12},{8,0},{12,4},{16,24},{20,28},{24,16},{28,20},{1,9},{5... | collective-permute-start | bytes 626696 | tf_op jit(solution)/shard_map/ppermute | solution.py:174
  141.7 12.2 %collective-permute-start.53 = (bf16[272,384]{1,0:T(8,128)(2,1)S(1)}, bf16[272,384]{1,0:T(8,128)(2,1)S(1)}, u32[]{:S(2)}, u32[]{:S(2)}) collective-permute-start(bf16[272,384]{1,0:T(8,128)(2,1)S(1)} %get-tuple-element.123), channel_id=1, source_target_pairs={{0,16},{4,20},{8,24},{12,28},{16,0},{20,4},{24,8},{28,12},{1,17},{... | collective-permute-start | bytes 626696 | tf_op jit(solution)/shard_map/ppermute | solution.py:174
  173.9 16.7 %collective-permute-start.66 = (bf16[256,512]{1,0:T(8,128)(2,1)S(1)}, bf16[256,512]{1,0:T(8,128)(2,1)S(1)}, u32[]{:S(2)}, u32[]{:S(2)}) collective-permute-start(bf16[256,512]{1,0:T(8,128)(2,1)S(1)} %get-tuple-element.139), channel_id=1, source_target_pairs={{0,2},{1,3},{2,0},{3,1},{4,6},{5,7},{6,4},{7,5},{8,10},{9,11},{10,... | collective-permute-start | bytes 786440 | tf_op jit(solution)/shard_map/ppermute | solution.py:174
  174.0 24.3 %collective-permute-start.67 = (bf16[256,512]{1,0:T(8,128)(2,1)S(1)}, bf16[256,512]{1,0:T(8,128)(2,1)S(1)}, u32[]{:S(2)}, u32[]{:S(2)}) collective-permute-start(bf16[256,512]{1,0:T(8,128)(2,1)S(1)} %get-tuple-element.140), channel_id=1, source_target_pairs={{0,3},{1,2},{2,1},{3,0},{4,7},{5,6},{6,5},{7,4},{8,11},{9,10},{10,... | collective-permute-start | bytes 786440 | tf_op jit(solution)/shard_map/ppermute | solution.py:174
  180.9 17.3 %collective-permute-start.64 = (bf16[256,512]{1,0:T(8,128)(2,1)S(1)}, bf16[256,512]{1,0:T(8,128)(2,1)S(1)}, u32[]{:S(2)}, u32[]{:S(2)}) collective-permute-start(bf16[256,512]{1,0:T(8,128)(2,1)S(1)} %collective-permute-done.45.refs_2_), channel_id=1, source_target_pairs={{0,16},{4,20},{9,25},{13,29},{18,2},{22,6},{27,11},{31,15}} | collective-permute-start | bytes 786440 | tf_op jit(solution)/shard_map/ppermute | solution.py:633
  181.6 16.6 %collective-permute-start.65 = (bf16[256,512]{1,0:T(8,128)(2,1)S(1)}, bf16[256,512]{1,0:T(8,128)(2,1)S(1)}, u32[]{:S(2)}, u32[]{:S(2)}) collective-permute-start(bf16[256,512]{1,0:T(8,128)(2,1)S(1)} %collective-permute-done.50.refs_0_), channel_id=1, source_target_pairs={{0,24},{4,28},{9,17},{13,21},{18,10},{22,14},{27,3},{31,7}} | collective-permute-start | bytes 786440 | tf_op jit(solution)/shard_map/ppermute | solution.py:633
  (48 other events, 427.9 us)
